TPU v7x, 32 devices: a whole 2x2x4 slice. The times are simulated.
32 devices in a mesh: dp: 16 (over z, x, core), tensor: 2 (over y).
Axes of the slice: x: 2, y: 2, z: 4, core: 2. Of those that a mesh axis runs over, the one named last changes fastest.
Arguments:
- tokens: bfloat16 [16, 1376, 1024], P('dp', 'tensor'), may hold values from -16 to 16
- cotangent: bfloat16 [16, 1376, 1024], P('dp', 'tensor'), may hold values from -6 to 6
- lengths: int32 [16], P('dp'), may hold values from 0 to 1370, as said below
- adapter_ids: int32 [16], P('dp'), may hold values from 0 to 7
- gain_one: float32 [1024], replicated, may hold values from 0.25 to 1.75
- gain_two: float32 [1024], replicated, may hold values from 0.25 to 1.75
- scale_one: float32 [1024], replicated, may hold values from 0.5 to 2
- scale_two: float32 [1024], replicated, may hold values from 0.5 to 2
- w_qkv: bfloat16 [1024, 3, 1024], P(None, None, 'tensor'), may hold values from -0.1875 to 0.1875
- w_out: bfloat16 [1024, 1024], P('tensor'), may hold values from -1 to 1
- w_up: bfloat16 [1024, 4096], P(None, 'tensor'), may hold values from -0.1875 to 0.1875
- w_down: bfloat16 [4096, 1024], P('tensor'), may hold values from -0.09375 to 0.09375
- qkv_a: bfloat16 [8, 16, 1024], replicated, may hold values from -0.1875 to 0.1875
- qkv_b: bfloat16 [8, 3, 1024, 16], P(None, None, 'tensor'), may hold values from -1.5 to 1.5
- out_a: bfloat16 [8, 16, 1024], P(None, None, 'tensor'), may hold values from -1 to 1
- out_b: bfloat16 [8, 1024, 16], replicated, may hold values from -1.5 to 1.5
- up_a: bfloat16 [8, 16, 1024], replicated, may hold values from -0.1875 to 0.1875
- up_b: bfloat16 [8, 4096, 16], P(None, 'tensor'), may hold values from -1.5 to 1.5
- down_a: bfloat16 [8, 16, 4096], P(None, None, 'tensor'), may hold values from -0.09375 to 0.09375
- down_b: bfloat16 [8, 1024, 16], replicated, may hold values from -1.5 to 1.5
Outputs:
- layer_out: bfloat16 [16, 1376, 1024], P('dp', 'tensor')
- grad_tokens: float32 [16, 1376, 1024], P('dp', 'tensor')
- grad_qkv_a: float32 [8, 16, 1024], replicated
- grad_qkv_b: float32 [8, 3, 1024, 16], P(None, None, 'tensor')
- grad_out_a: float32 [8, 16, 1024], P(None, None, 'tensor')
- grad_out_b: float32 [8, 1024, 16], replicated
- grad_up_a: float32 [8, 16, 1024], replicated
- grad_up_b: float32 [8, 4096, 16], P(None, 'tensor')
- grad_down_a: float32 [8, 16, 4096], P(None, None, 'tensor')
- grad_down_b: float32 [8, 1024, 16], replicated
Inputs may be any that keep to these rules, and one draw needn't show every extreme that they name: `lengths`: slots g * 1 to g + 1 - 1 belong to group g of the dp axis; the first c of them hold images, with c from (2) // 2 to 1, each of 685 to 1370 valid tokens, and the others are empty with length 0.
All inputs are finite; a program needn't handle non-finite values.
Results may differ from a plain program's by a relative error of at most 0.014.
The roundings to bfloat16 on the way count: a program that leaves them out, or rounds other values in their place, can miss the bound.
Values may be sent and summed in bfloat16 or wider, within the bound.
No kernel may reach another device: no remote copies, remote signals or barrier semaphores. Data moves between devices by JAX's collectives and lax.ppermute only.
A program may use at most 384 MiB of HBM per device.

v0:
```python
import jax
import jax.numpy as jnp
from jax import lax
from jax.sharding import PartitionSpec as P

HD = 64
ADAPTERS = 8


epsilon = 1e-06
masked_score = -1e30
HIGHEST = lax.Precision.HIGHEST


def product(form, left, right):
    return jnp.einsum(form, left, right, preferred_element_type=jnp.float32)


def precise(form, left, right):
    return jnp.einsum(form, left.astype(jnp.float32), right.astype(jnp.float32), precision=HIGHEST)


def select_rows(onehot, table):
    return product("sn,n...->s...", onehot, table).astype(table.dtype)


def norm_rows(values, gain_vec):
    average = jnp.mean(values, axis=-1, keepdims=True)
    centred = values - average
    variance = jnp.mean(centred * centred, axis=-1, keepdims=True)
    return centred * lax.rsqrt(variance + epsilon) * gain_vec


def norm_back(values, gain_vec, grad_normed):
    normed, pullback = jax.vjp(lambda rows: norm_rows(rows, gain_vec), values)
    return pullback(grad_normed)[0]


def gelu_slope(values):
    return (
        0.5 * (1.0 + lax.erf(values * 0.7071067811865476))
        + values * jnp.exp(-0.5 * values * values) * 0.3989422804014327
    )


def ffn_forward(rows_low, up_mat, down_mat, up_a_sel, up_b_sel, down_a_sel, down_b_sel):
    rank_up = product("std,srd->str", rows_low, up_a_sel).astype(jnp.bfloat16)
    preact = product("std,dh->sth", rows_low, up_mat) + product("str,shr->sth", rank_up, up_b_sel)
    hidden = jax.nn.gelu(preact, approximate=False).astype(jnp.bfloat16)
    rank_down = product("sth,srh->str", hidden, down_a_sel)
    terms = product("sth,hd->std", hidden, down_mat) + precise(
        "str,sdr->std", rank_down, down_b_sel
    )
    return (rank_up, preact, hidden, rank_down, terms)


def ffn_backward(
    rows_low,
    grad_rows,
    up_mat,
    down_mat,
    up_a_sel,
    up_b_sel,
    down_a_sel,
    down_b_sel,
    rank_up,
    preact,
    hidden,
    rank_down,
):
    grad_rank_down = product("std,sdr->str", grad_rows, down_b_sel).astype(jnp.bfloat16)
    grad_hidden = product("std,hd->sth", grad_rows, down_mat) + product(
        "str,srh->sth", grad_rank_down, down_a_sel
    )
    grad_preact = (grad_hidden * gelu_slope(preact)).astype(jnp.bfloat16)
    grad_up_b = product("sth,str->shr", grad_preact, rank_up)
    grad_rank_up = product("sth,shr->str", grad_preact, up_b_sel)
    grad_rows_in = product("sth,dh->std", grad_preact, up_mat) + precise(
        "str,srd->std", grad_rank_up, up_a_sel
    )
    grad_up_a = precise("str,std->srd", grad_rank_up, rows_low)
    grad_down_a = product("str,sth->srh", grad_rank_down, hidden)
    grad_down_b = precise("std,str->sdr", grad_rows, rank_down)
    return (grad_rows_in, (grad_up_a, grad_up_b, grad_down_a, grad_down_b))


def body(
    tokens,
    cotangent,
    lengths,
    adapter_ids,
    gain_one,
    gain_two,
    scale_one,
    scale_two,
    w_qkv,
    w_out,
    w_up,
    w_down,
    qkv_a,
    qkv_b,
    out_a,
    out_b,
    up_a,
    up_b,
    down_a,
    down_b,
):
    shard_rows = tokens.shape[1]
    seq_len = shard_rows * lax.axis_size("tensor")
    heads_local = w_qkv.shape[2] // HD
    scale_attn = HD ** (-0.5)
    first_row = lax.axis_index("tensor") * shard_rows
    positions = jnp.arange(seq_len, dtype=jnp.int32)
    key_valid = positions[None, :] < jnp.maximum(lengths, 1)[:, None]
    local_rows = first_row + jnp.arange(shard_rows, dtype=jnp.int32)
    row_valid = (local_rows[None, :] < lengths[:, None]).astype(jnp.float32)[:, :, None]
    adapters = jnp.arange(ADAPTERS, dtype=jnp.int32)
    onehot = (adapter_ids[:, None] == adapters[None, :]).astype(jnp.bfloat16)
    qkv_a_sel = select_rows(onehot, qkv_a)
    qkv_b_sel = select_rows(onehot, qkv_b)
    out_a_sel = select_rows(onehot, out_a)
    out_b_sel = select_rows(onehot, out_b)
    up_a_sel = select_rows(onehot, up_a)
    down_b_sel = select_rows(onehot, down_b)
    inputs = tokens.astype(jnp.float32)
    normed_one = norm_rows(inputs, gain_one).astype(jnp.bfloat16)
    full_one = lax.all_gather(normed_one, "tensor", axis=1, tiled=True)
    rank_qkv = product("std,srd->str", full_one, qkv_a_sel).astype(jnp.bfloat16)
    projected = (
        product("std,dcf->sctf", full_one, w_qkv) + product("str,scfr->sctf", rank_qkv, qkv_b_sel)
    ).astype(jnp.bfloat16)

    def split_heads(rows):
        return rows.reshape(seq_len, heads_local, HD)

    def masked_scores(queries, keyrows, valid_keys):
        scores = product("qhe,khe->hqk", queries, keyrows) * scale_attn
        return jnp.where(valid_keys[None, None, :], scores, masked_score)

    def attend(slot_items):
        slot_block, valid_keys = slot_items
        queries = split_heads(slot_block[0])
        keyrows = split_heads(slot_block[1])
        values = split_heads(slot_block[2])
        scores = masked_scores(queries, keyrows, valid_keys)
        row_max = jnp.max(scores, axis=-1, keepdims=True)
        exponent = jnp.exp(scores - row_max)
        row_total = jnp.sum(exponent, axis=-1, keepdims=True)
        soft_low = (exponent / row_total).astype(jnp.bfloat16)
        mixed_rows = (
            product("hqk,khe->qhe", soft_low, values).astype(jnp.bfloat16).reshape(seq_len, -1)
        )
        return (mixed_rows, (row_max + jnp.log(row_total))[:, :, 0])

    mixed, log_total = lax.map(attend, (projected, key_valid))
    rank_out = product("stf,srf->str", mixed, out_a_sel)
    attn_terms = product("stf,fd->std", mixed, w_out) + precise("str,sdr->std", rank_out, out_b_sel)
    attn_branch = lax.psum_scatter(attn_terms, "tensor", scatter_dimension=1, tiled=True)
    residual = inputs + scale_one * attn_branch
    normed_two = norm_rows(residual, gain_two).astype(jnp.bfloat16)
    up_mat, down_mat, up_b_all, down_a_all = (
        lax.all_gather(w_up, "tensor", axis=1, tiled=True),
        lax.all_gather(w_down, "tensor", axis=0, tiled=True),
        lax.all_gather(up_b, "tensor", axis=1, tiled=True),
        lax.all_gather(down_a, "tensor", axis=2, tiled=True),
    )
    up_b_sel = select_rows(onehot, up_b_all)
    down_a_sel = select_rows(onehot, down_a_all)
    rank_up, preact, hidden, rank_down, ffn_terms = ffn_forward(
        normed_two, up_mat, down_mat, up_a_sel, up_b_sel, down_a_sel, down_b_sel
    )
    layer_out = ((residual + scale_two * ffn_terms) * row_valid).astype(jnp.bfloat16)
    grad_out = cotangent.astype(jnp.float32) * row_valid
    grad_mlp = (scale_two * grad_out).astype(jnp.bfloat16)
    ffn_grad_in, ffn_grads = ffn_backward(
        normed_two,
        grad_mlp,
        up_mat,
        down_mat,
        up_a_sel,
        up_b_sel,
        down_a_sel,
        down_b_sel,
        rank_up,
        preact,
        hidden,
        rank_down,
    )
    grad_residual = grad_out + norm_back(residual, gain_two, ffn_grad_in)
    grad_attn = (scale_one * grad_residual).astype(jnp.bfloat16)
    full_grad_attn = lax.all_gather(grad_attn, "tensor", axis=1, tiled=True)
    grad_rank_out = product("std,sdr->str", full_grad_attn, out_b_sel).astype(jnp.bfloat16)
    grad_mixed = (
        product("std,fd->stf", full_grad_attn, w_out)
        + product("str,srf->stf", grad_rank_out, out_a_sel)
    ).astype(jnp.bfloat16)
    grad_out_a = product("str,stf->srf", grad_rank_out, mixed)
    grad_out_b = precise("std,str->sdr", full_grad_attn, rank_out)

    def attend_back(slot_items):
        slot_block, valid_keys, log_rows, grad_rows = slot_items
        queries = split_heads(slot_block[0])
        keyrows = split_heads(slot_block[1])
        values = split_heads(slot_block[2])
        scores = masked_scores(queries, keyrows, valid_keys)
        soft = jnp.exp(scores - log_rows[:, :, None])
        soft_low = soft.astype(jnp.bfloat16)
        grad_heads = split_heads(grad_rows)
        grad_soft = product("qhe,khe->hqk", grad_heads, values)
        grad_values = product("hqk,qhe->khe", soft_low, grad_heads)
        grad_scores = (
            soft * (grad_soft - jnp.sum(soft * grad_soft, axis=-1, keepdims=True))
        ).astype(jnp.bfloat16)
        grad_queries = product("hqk,khe->qhe", grad_scores, keyrows) * scale_attn
        grad_keys = product("hqk,qhe->khe", grad_scores, queries) * scale_attn
        return (
            jnp.stack([grad_queries, grad_keys, grad_values])
            .reshape(3, seq_len, -1)
            .astype(jnp.bfloat16)
        )

    grad_projected = lax.map(attend_back, (projected, key_valid, log_total, grad_mixed))
    grad_qkv_b = product("sctf,str->scfr", grad_projected, rank_qkv)
    grad_rank_qkv = product("sctf,scfr->str", grad_projected, qkv_b_sel)
    grad_one_terms = product("sctf,dcf->std", grad_projected, w_qkv) + precise(
        "str,srd->std", grad_rank_qkv, qkv_a_sel
    )
    grad_qkv_a = precise("str,std->srd", grad_rank_qkv, full_one)
    grad_normed_one = lax.psum_scatter(grad_one_terms, "tensor", scatter_dimension=1, tiled=True)
    grad_tokens = grad_residual + norm_back(inputs, gain_one, grad_normed_one)
    onehot_wide = onehot.astype(jnp.float32)

    def stack_slots(slot_grads):
        return jnp.einsum("sn,s...->n...", onehot_wide, slot_grads, precision=HIGHEST)

    grad_up_a, grad_up_b, grad_down_a, grad_down_b = ffn_grads
    sum_qkv_b, sum_out_a = lax.psum((stack_slots(grad_qkv_b), stack_slots(grad_out_a)), "dp")
    joint_sums = lax.psum(
        (
            stack_slots(grad_qkv_a),
            stack_slots(grad_out_b),
            stack_slots(grad_up_a),
            stack_slots(grad_up_b),
            stack_slots(grad_down_a),
            stack_slots(grad_down_b),
        ),
        ("dp", "tensor"),
    )
    sum_qkv_a, sum_out_b, sum_up_a, up_b_whole, down_a_whole, sum_down_b = joint_sums
    width_local = w_up.shape[1]
    first_col = lax.axis_index("tensor") * width_local
    sum_up_b = lax.dynamic_slice_in_dim(up_b_whole, first_col, width_local, 1)
    sum_down_a = lax.dynamic_slice_in_dim(down_a_whole, first_col, width_local, 2)
    return (
        layer_out,
        grad_tokens,
        sum_qkv_a,
        sum_qkv_b,
        sum_out_a,
        sum_out_b,
        sum_up_a,
        sum_up_b,
        sum_down_a,
        sum_down_b,
    )


def solution(mesh):
    return jax.shard_map(
        body,
        mesh=mesh,
        in_specs=(
            P("dp", "tensor", None),
            P("dp", "tensor", None),
            P("dp"),
            P("dp"),
            P(),
            P(),
            P(),
            P(),
            P(None, None, "tensor"),
            P("tensor", None),
            P(None, "tensor"),
            P("tensor", None),
            P(),
            P(None, None, "tensor", None),
            P(None, None, "tensor"),
            P(),
            P(),
            P(None, "tensor", None),
            P(None, None, "tensor"),
            P(),
        ),
        out_specs=(
            P("dp", "tensor", None),
            P("dp", "tensor", None),
            P(),
            P(None, None, "tensor", None),
            P(None, None, "tensor"),
            P(),
            P(),
            P(None, "tensor", None),
            P(None, None, "tensor"),
            P(),
        ),
        check_vma=False,
    )
```

profile of v0, /device:TPU:1, one launch (start us, length us, event | category | flops | bytes accessed | tf_op | source)
XLA Modules:
  0.0 1014.0 jit_solution(800403736796422366)
XLA Ops:
  22.0 35.1 %all-gather.7.cloned.1.call-done = bf16[1,1376,1024]{2,1,0:T(8,128)(2,1)} async-done(((bf16[1,688,1024]{2,1,0:T(8,128)(2,1)}), bf16[1,1376,1024]{2,1,0:T(8,128)(2,1)}) %all-gather.7.cloned.1.call-update) | async-done | bytes 2818064 | tf_op jit(solution)/shard_map/all_gather | solution.py:128
  62.3 5.3 fusion.23
  77.3 25.8 %fusion.116 = (f32[8,1376]{1,0:T(8,128)S(1)}, f32[8,1376,1376]{1,2,0:T(8,128)}) fusion(bf16[1376,8,64]{0,2,1:T(8,128)(2,1)} %bitcast.204, bf16[1376,8,64]{0,2,1:T(8,128)(2,1)} %bitcast.202, pred[1376]{0:T(1024)(128)(4,1)S(1)} %iota_compare_fusion), kind=kOutput, calls=%fused_computation.176 | convolution fusion | flops 1984247040 | bytes 63451488 | tf_op jit(solution)/shard_map/while/body/eval_jaxpr/qhe,khe->hqk/dot_general | solution.py:16
  103.1 23.7 %fusion.1 = f32[8,1376]{1,0:T(8,128)S(1)} fusion(f32[8,1376,1376]{1,2,0:T(8,128)} %get-tuple-element.63, f32[8,1376]{1,0:T(8,128)S(1)} %get-tuple-element.62), kind=kLoop, calls=%fused_computation.7 | loop fusion | flops 30283008 | bytes 60676096 | tf_op jit(solution)/shard_map/while/body/eval_jaxpr/reduce_sum | solution.py:149
  126.8 24.8 %fusion.35 = bf16[8,64,1376]{2,1,0:T(8,128)(2,1)} fusion(bf16[1376,8,64]{0,2,1:T(8,128)(2,1)} %bitcast.214, f32[8,1376,1376]{1,2,0:T(8,128)} %get-tuple-element.63, f32[8,1376]{1,0:T(8,128)S(1)} %fusion.1, f32[8,1376]{1,0:T(8,128)S(1)} %get-tuple-element.62), kind=kOutput, calls=%fused_computation.61 | convolution fusion | flops 1984962560 | bytes 63494144 | tf_op jit(solution)/shard_map/while/body/eval_jaxpr/hqk,khe->qhe/dot_general | solution.py:16
  153.3 3.4 fusion.117
  156.7 5.2 add_bitcast_fusion
  168.4 11.0 %fusion.67 = bf16[1,4096,16]{0,1,2:T(8,128)(2,1)} fusion(bf16[8,4096,16]{1,2,0:T(8,128)(2,1)} %all-gather.11.cloned.1.call-done, s32[]{:T(128)} %bitcast.198), kind=kOutput, calls=%fused_computation.100 | convolution fusion | flops 1048584 | bytes 1179652 | tf_op jit(solution)/shard_map/sn,n...->s.../dot_general | solution.py:16
  179.3 13.3 %copy.80 = bf16[1,4096,16]{1,2,0:T(8,128)(2,1)S(1)} copy(bf16[1,4096,16]{0,1,2:T(8,128)(2,1)} %fusion.67) | data formatting | bytes 262144 | tf_op jit(solution)/shard_map/sn,n...->s.../dot_general | solution.py:16
  196.6 11.8 %all-gather.13.cloned.1.call-done = bf16[4096,1024]{1,0:T(8,128)(2,1)} async-done(((bf16[2048,1024]{1,0:T(8,128)(2,1)}), bf16[4096,1024]{1,0:T(8,128)(2,1)}) %all-gather.13.cloned.1.call-update) | async-done | bytes 8388624 | tf_op jit(solution)/shard_map/all_gather | solution.py:164
  208.4 11.4 %fusion.108 = f32[688,4096]{1,0:T(8,128)} fusion(bf16[4096,1024]{1,0:T(8,128)(2,1)} %all-gather.13.cloned.1.call-done, bf16[1,688,1024]{2,1,0:T(8,128)(2,1)} %param.21, f32[1024]{0:T(1024)S(1)} %copy-done.73, f32[688]{0:T(1024)S(1)} %fusion.85), kind=kOutput, calls=%fused_computation.169 | convolution fusion | flops 5774180352 | bytes 21076672 | tf_op jit(solution)/shard_map/std,hd->sth/dot_general | solution.py:16
  219.8 60.7 %reduce-scatter.3.cloned.1.call-done = f32[1,688,1024]{2,1,0:T(8,128)} async-done(((f32[1,1376,1024]{2,1,0:T(8,128)}), f32[1,688,1024]{2,1,0:T(8,128)}) %reduce-scatter.3.cloned.1.call-update) | async-done | bytes 2818064 | tf_op jit(solution)/shard_map/reduce_scatter | solution.py:159
  286.9 99.1 %all-gather.9.cloned.1.call-done = bf16[1024,4096]{1,0:T(8,128)(2,1)} async-done(((bf16[1024,2048]{1,0:T(8,128)(2,1)}), bf16[1024,4096]{1,0:T(8,128)(2,1)}) %all-gather.9.cloned.1.call-update) | async-done | bytes 8388624 | tf_op jit(solution)/shard_map/all_gather | solution.py:163
  386.1 8.8 fusion.118
  394.9 28.5 %fusion.9 = (bf16[688,4096]{1,0:T(8,128)(2,1)S(1)}, f32[688,4096]{1,0:T(8,128)}) fusion(f32[688,4096]{1,0:T(8,128)S(1)} %fusion.118, bf16[688,16]{0,1:T(8,128)(2,1)S(1)} %copy-done.54, bf16[1,4096,16]{1,2,0:T(8,128)(2,1)S(1)} %copy.80), kind=kOutput, calls=%fused_computation.16 | convolution fusion | flops 276168704 | bytes 28333568 | tf_op jit(solution)/shard_map/str,shr->sth/dot_general | solution.py:16
  425.7 9.9 fusion.15
  438.1 8.6 fusion.120
  455.3 3.4 fusion.123
  458.7 4.1 fusion.124
  466.1 28.2 %all-gather.17.cloned.1.call-done = bf16[1,1376,1024]{2,1,0:T(8,128)(2,1)} async-done(((bf16[1,688,1024]{2,1,0:T(8,128)(2,1)}), bf16[1,1376,1024]{2,1,0:T(8,128)(2,1)}) %all-gather.17.cloned.1.call-update) | async-done | bytes 2818064 | tf_op jit(solution)/shard_map/all_gather | solution.py:192
  504.2 23.3 %fusion.29 = bf16[8,64,1376]{2,1,0:T(8,128)(2,1)} fusion(bf16[1376,8,64]{0,2,1:T(8,128)(2,1)} %bitcast.206, f32[8,1376,1376]{1,2,0:T(8,128)} %get-tuple-element.63, f32[8,1376]{1,0:T(8,128)S(1)} %copy-done.14), kind=kOutput, calls=%fused_computation.57 | convolution fusion | flops 1969815552 | bytes 63450112 | tf_op jit(solution)/shard_map/while/body/eval_jaxpr/hqk,qhe->khe/dot_general | solution.py:16
  527.5 43.5 %multiply_reduce_fusion = (f32[8,1376]{1,0:T(8,128)S(1)}, f32[8,1376,1376]{1,2,0:T(8,128)}) fusion(f32[8,1376,1376]{1,2,0:T(8,128)} %get-tuple-element.63, f32[8,1376]{1,0:T(8,128)S(1)} %copy-done.14, bf16[1376,8,64]{0,2,1:T(8,128)(2,1)} %bitcast.207, bf16[1376,8,64]{0,2,1:T(8,128)(2,1)} %bitcast.215), kind=kOutput, calls=%fused_computation.3 | convolution fusion | flops 1984247040 | bytes 124082176 | tf_op jit(solution)/shard_map/while/body/eval_jaxpr/qhe,khe->hqk/dot_general | solution.py:16
  571.0 49.0 %multiply_convert_fusion = bf16[8,1376,1376]{1,2,0:T(8,128)(2,1)} fusion(f32[8,1376,1376]{1,2,0:T(8,128)} %get-tuple-element.69, f32[8,1376,1376]{1,2,0:T(8,128)} %get-tuple-element.63, f32[8,1376]{1,0:T(8,128)S(1)} %get-tuple-element.68, f32[8,1376]{1,0:T(8,128)S(1)} %copy-done.14), kind=kLoop, calls=%fused_computation.2 | loop fusion | flops 60588032 | bytes 151558144 | tf_op jit(solution)/shard_map/while/body/eval_jaxpr/convert_element_type | solution.py:214
  620.0 16.5 %fusion.34 = bf16[8,64,1376]{2,1,0:T(8,128)(2,1)} fusion(bf16[1376,8,64]{0,2,1:T(8,128)(2,1)} %bitcast.205, bf16[8,1376,1376]{1,2,0:T(8,128)(2,1)} %multiply_convert_fusion), kind=kOutput, calls=%fused_computation.60 | convolution fusion | flops 1940226048 | bytes 33112064 | tf_op jit(solution)/shard_map/while/body/eval_jaxpr/hqk,qhe->khe/dot_general | solution.py:16
  636.5 16.5 %fusion.33 = bf16[8,64,1376]{2,1,0:T(8,128)(2,1)} fusion(bf16[1376,8,64]{0,2,1:T(8,128)(2,1)} %bitcast.203, bf16[8,1376,1376]{1,2,0:T(8,128)(2,1)} %multiply_convert_fusion), kind=kOutput, calls=%fused_computation.59 | convolution fusion | flops 1940226048 | bytes 33112064 | tf_op jit(solution)/shard_map/while/body/eval_jaxpr/hqk,khe->qhe/dot_general | solution.py:16
  660.9 3.1 fusion.40
  670.2 6.3 fusion.111
  676.6 5.0 fusion.24
  681.7 10.6 %fusion.119 = f32[688,1024]{1,0:T(8,128)S(1)} fusion(bf16[688,4096]{1,0:T(8,128)(2,1)} %copy-done.9, bf16[4096,1024]{1,0:T(8,128)(2,1)} %all-gather.13.cloned.1.call-done), kind=kOutput, calls=%fused_computation.179 | convolution fusion | flops 5771362304 | bytes 16842752 | tf_op jit(solution)/shard_map/sth,hd->std/dot_general | solution.py:16
  698.5 130.7 %all-reduce.5.cloned.1.call-done = (f32[8,16,1024]{2,1,0:T(8,128)}, f32[8,1024,16]{1,2,0:T(8,128)}, f32[8,16,1024]{2,1,0:T(8,128)}, f32[8,4096,16]{1,2,0:T(8,128...) async-done(((f32[8,16,1024]{2,1,0:T(8,128)}, f32[8,1024,16]{1,2,0:T(8,128)}, f32[8,16,1024]{2,1,0:T(8,128)}, f32[8,4096,16]{1,2,0:T(8,128)}, f32[8,16,4096]{2,1,0:T(8,128)}, ...) | async-done | bytes 6291472 | tf_op jit(solution)/shard_map/psum | solution.py:239
  832.7 69.0 %reduce-scatter.5.cloned.1.call-done = f32[1,688,1024]{2,1,0:T(8,128)} async-done(((f32[1,1376,1024]{2,1,0:T(8,128)}), f32[1,688,1024]{2,1,0:T(8,128)}) %reduce-scatter.5.cloned.1.call-update) | async-done | bytes 2818064 | tf_op jit(solution)/shard_map/reduce_scatter | solution.py:230
  909.5 89.2 %all-reduce.7.cloned.1.call-done = (f32[8,3,512,16]{2,3,1,0:T(8,128)}, f32[8,16,512]{2,1,0:T(8,128)}) async-done(((f32[8,3,512,16]{2,3,1,0:T(8,128)}, f32[8,16,512]{2,1,0:T(8,128)}), (f32[8,3,512,16]{2,3,1,0:T(8,128)}, f32[8,16,512]{2,1,0:T(8,128)})) %all-reduce.7.cloned.1.call-update) | async-done | bytes 1048592 | tf_op jit(solution)/shard_map/psum | solution.py:238
  (246 shorter events, 112.7 us)
Async XLA Ops:
  7.2 54.7 %copy-start = (bf16[1024,3,512]{2,0,1:T(8,128)(2,1)S(1)}, bf16[1024,3,512]{2,0,1:T(8,128)(2,1)}, u32[]{:S(2)}) copy-start(bf16[1024,3,512]{2,0,1:T(8,128)(2,1)} %param.28) | copy-start | bytes 9437188
  7.2 50.0 %all-gather.7.cloned.1.call-start = ((), (), s32[]{:S(2)}) async-start(), calls=%async_computation.2 | async-start | bytes 4227072 | tf_op jit(solution)/shard_map/all_gather | solution.py:128
  13.7 154.6 %all-gather.11.cloned.1.call-start = ((), (), s32[]{:S(2)}) async-start(), calls=%async_computation.5 | async-start | bytes 1572864 | tf_op jit(solution)/shard_map/all_gather | solution.py:165
  14.5 178.2 %all-gather.15.cloned.1.call-start = ((), (), s32[]{:S(2)}) async-start(), calls=%async_computation.7 | async-start | bytes 1572864 | tf_op jit(solution)/shard_map/all_gather | solution.py:166
  15.2 193.2 %all-gather.13.cloned.1.call-start = ((), (), s32[]{:S(2)}) async-start(), calls=%async_computation.6 | async-start | bytes 12582912 | tf_op jit(solution)/shard_map/all_gather | solution.py:164
  15.8 264.8 %reduce-scatter.3.cloned.1.call-start = ((), (), s32[]{:S(2)}) async-start(), calls=%async_computation.3 | async-start | bytes 8454144 | tf_op jit(solution)/shard_map/reduce_scatter | solution.py:159
  17.6 139.1 %copy-start.19 = (bf16[1,1024,16]{2,1,0:T(8,128)(2,1)}, bf16[1,1024,16]{2,1,0:T(8,128)(2,1)S(1)}, u32[]{:S(2)}) copy-start(bf16[1,1024,16]{2,1,0:T(8,128)(2,1)S(1)} %copy.76) | copy-start | bytes 98308
  18.8 132.8 %copy-start.52 = (bf16[1,16,512]{2,0,1:T(2,128)(2,1)}, bf16[1,16,512]{2,0,1:T(2,128)(2,1)S(1)}, u32[]{:S(2)}) copy-start(bf16[1,16,512]{2,0,1:T(2,128)(2,1)S(1)} %fusion.79) | copy-start | bytes 49156
  20.0 39.8 %copy-start.37 = (bf16[1,16,1024]{2,0,1:T(2,128)(2,1)}, bf16[1,16,1024]{2,0,1:T(2,128)(2,1)S(1)}, u32[]{:S(2)}) copy-start(bf16[1,16,1024]{2,0,1:T(2,128)(2,1)S(1)} %fusion.77) | copy-start | bytes 98308
  103.1 23.7 %copy-start.34 = (f32[8,1376]{1,0:T(8,128)}, f32[8,1376]{1,0:T(8,128)S(1)}, u32[]{:S(2)}) copy-start(f32[8,1376]{1,0:T(8,128)S(1)} %get-tuple-element.62) | copy-start | bytes 132100
  126.8 24.8 %copy-start.47 = (f32[8,1376]{1,0:T(8,128)}, f32[8,1376]{1,0:T(8,128)S(1)}, u32[]{:S(2)}) copy-start(f32[8,1376]{1,0:T(8,128)S(1)} %fusion.1) | copy-start | bytes 132100
  161.9 224.1 %all-gather.9.cloned.1.call-start = ((), (), s32[]{:S(2)}) async-start(), calls=%async_computation.4 | async-start | bytes 12582912 | tf_op jit(solution)/shard_map/all_gather | solution.py:163
  162.5 331.7 %all-gather.17.cloned.1.call-start = ((), (), s32[]{:S(2)}) async-start(), calls=%async_computation.8 | async-start | bytes 4227072 | tf_op jit(solution)/shard_map/all_gather | solution.py:192
  163.3 16.0 %copy-start.26 = (bf16[1,1024,16]{2,1,0:T(8,128)(2,1)}, bf16[1,1024,16]{2,1,0:T(8,128)(2,1)S(1)}, u32[]{:S(2)}) copy-start(bf16[1,1024,16]{2,1,0:T(8,128)(2,1)S(1)} %copy.84) | copy-start | bytes 98308
  164.0 287.0 %copy-start.58 = (f32[688]{0:T(1024)}, f32[688]{0:T(1024)S(1)}, u32[]{:S(2)}) copy-start(f32[688]{0:T(1024)S(1)} %fusion.85) | copy-start | bytes 8260
  196.6 83.9 %copy-start.71 = (f32[1024]{0:T(1024)S(1)}, f32[1024]{0:T(1024)}, u32[]{:S(2)}) copy-start(f32[1024]{0:T(1024)} %param.26) | copy-start | bytes 12292
  386.1 8.8 copy-start.54
  425.7 23.8 %copy-start.45 = (f32[688,16]{0,1:T(8,128)}, f32[688,16]{0,1:T(8,128)S(1)}, u32[]{:S(2)}) copy-start(f32[688,16]{0,1:T(8,128)S(1)} %fusion.82) | copy-start | bytes 132100
  438.1 8.6 copy-start.70
  452.8 376.4 %all-reduce.5.cloned.1.call-start = ((), (), s32[]{:S(2)}) async-start(), calls=%async_computation.10 | async-start | bytes 12582912 | tf_op jit(solution)/shard_map/psum | solution.py:239
  462.9 31.4 %copy-start.20 = (bf16[1,1024,16]{2,1,0:T(8,128)(2,1)S(1)}, bf16[1,1024,16]{2,1,0:T(8,128)(2,1)}, u32[]{:S(2)}) copy-start(bf16[1,1024,16]{2,1,0:T(8,128)(2,1)} %copy-done.19) | copy-start | bytes 98308
  670.2 231.5 %reduce-scatter.5.cloned.1.call-start = ((), (), s32[]{:S(2)}) async-start(), calls=%async_computation.9 | async-start | bytes 8454144 | tf_op jit(solution)/shard_map/reduce_scatter | solution.py:230
  681.6 317.1 %all-reduce.7.cloned.1.call-start = ((), (), s32[]{:S(2)}) async-start(), calls=%async_computation.11 | async-start | bytes 2097152 | tf_op jit(solution)/shard_map/psum | solution.py:238
  681.6 10.7 %copy-start.3 = (f32[1,688,1024]{2,1,0:T(8,128)S(1)}, f32[1,688,1024]{2,1,0:T(8,128)}, u32[]{:S(2)}) copy-start(f32[1,688,1024]{2,1,0:T(8,128)} %copy-done.1) | copy-start | bytes 8454148
  681.7 10.7 %copy-start.27 = (bf16[1,1024,16]{2,1,0:T(8,128)(2,1)S(1)}, bf16[1,1024,16]{2,1,0:T(8,128)(2,1)}, u32[]{:S(2)}) copy-start(bf16[1,1024,16]{2,1,0:T(8,128)(2,1)} %copy-done.26) | copy-start | bytes 98308
  681.7 10.7 %copy-start.46 = (f32[688,16]{0,1:T(8,128)S(1)}, f32[688,16]{0,1:T(8,128)}, u32[]{:S(2)}) copy-start(f32[688,16]{0,1:T(8,128)} %copy-done.45) | copy-start | bytes 132100
  681.7 10.7 %copy-start.59 = (f32[688]{0:T(1024)S(1)}, f32[688]{0:T(1024)}, u32[]{:S(2)}) copy-start(f32[688]{0:T(1024)} %copy-done.58) | copy-start | bytes 8260
  681.7 10.7 %copy-start.75 = (f32[1024]{0:T(1024)S(1)}, f32[1024]{0:T(1024)}, u32[]{:S(2)}) copy-start(f32[1024]{0:T(1024)} %param.27) | copy-start | bytes 12292
  698.5 203.2 %copy-start.51 = (f32[688]{0:T(1024)S(1)}, f32[688]{0:T(1024)}, u32[]{:S(2)}) copy-start(f32[688]{0:T(1024)} %copy-done.50) | copy-start | bytes 8260
  698.5 203.2 %copy-start.57 = (f32[1024]{0:T(1024)S(1)}, f32[1024]{0:T(1024)}, u32[]{:S(2)}) copy-start(f32[1024]{0:T(1024)} %param.24) | copy-start | bytes 12292
  831.6 73.0 %copy-start.65 = (f32[688]{0:T(1024)S(1)}, f32[688]{0:T(1024)}, u32[]{:S(2)}) copy-start(f32[688]{0:T(1024)} %copy-done.64) | copy-start | bytes 8260
  831.6 73.1 %copy-start.61 = (f32[688]{0:T(1024)S(1)}, f32[688]{0:T(1024)}, u32[]{:S(2)}) copy-start(f32[688]{0:T(1024)} %copy-done.60) | copy-start | bytes 8260
  (54 other events, 180.7 us)
Sparse Core Ops, SparseCore 0:
  13.8 43.3 all-gather.6
  58.7 21.2 all-gather.10
  81.6 21.2 all-gather.14
  104.4 104.0 all-gather.12
  210.6 69.9 reduce-scatter.2
  282.0 103.9 all-gather.8
  452.9 41.2 all-gather.16
  670.3 158.8 all-reduce.4
  831.5 70.1 reduce-scatter.4
  906.1 92.6 all-reduce.6
where the time goes:
time: 1020 us; the launch traced here: 1010 us
  waiting for transfers between devices  526 us (52%)
  matrix products  317 us (31%)
  other arithmetic  99.8 us (10%)
  local copies, waits for them, and re-layouts  53.6 us (5%)
  between operations  16.5 us (2%)
    dot_general x38, matrix products, product(): return jnp.einsum(form, left, right, preferred_element_type=jnp.float32)  295 us
    psum x1, waiting for transfers between devices, body(): lax.psum((stack_slots(grad_qkv_a), stack_slots(grad_out_b), stack_slots(g...  131 us
    all_gather x1, waiting for transfers between devices, body(): lax.all_gather(w_up, 'tensor', axis=1, tiled=True)  99.1 us
    psum x1, waiting for transfers between devices, body(): lax.psum((stack_slots(grad_qkv_b), stack_slots(grad_out_a)), 'dp')  89.2 us
    reduce_scatter x1, waiting for transfers between devices, body(): lax.psum_scatter(grad_one_terms, 'tensor', scatter_dimension=1, tiled=True)  69 us
    reduce_scatter x1, waiting for transfers between devices, body(): lax.psum_scatter(attn_terms, 'tensor', scatter_dimension=1, tiled=True)  60.7 us
    convert_element_type x1, other arithmetic, attend_back(): grad_scores = (soft * (grad_soft - jnp.sum(soft * grad_soft, axis=-1, kee...  49 us
    all_gather x1, waiting for transfers between devices, body(): full_one = lax.all_gather(normed_one, 'tensor', axis=1, tiled=True)  35.1 us
  transfers between devices with their start and end apart: 10, of which 8 were waited for; matrix products, arithmetic and copies ran while one was open for 21% of the time, Pallas kernels for 0%

commit v1 on v0

--- a/solution.py
+++ b/solution.py
@@ -1,6 +1,11 @@
+import functools
+
 import jax
 import jax.numpy as jnp
 from jax import lax
+from jax.experimental import pallas as pl
+from jax.experimental.pallas import tpu as pltpu
+from jax.sharding import Mesh
 from jax.sharding import PartitionSpec as P
 
 HD = 64
@@ -84,7 +89,7 @@
     return (grad_rows_in, (grad_up_a, grad_up_b, grad_down_a, grad_down_b))
 
 
-def body(
+def plain_body(
     tokens,
     cotangent,
     lengths,
@@ -266,43 +271,841 @@
     )
 
 
+F32 = jnp.float32
+BF = jnp.bfloat16
+LOG2E = 1.4426950408889634
+PARTS = 8
+PAD = 128
+FLIP = [(0, 1), (1, 0)]
+SWAP = [(0, 0), (1, 2), (2, 1), (3, 3)]
+
+
+def dotg(a, b, ca, cb):
+    return lax.dot_general(a, b, (((ca,), (cb,)), ((), ())), preferred_element_type=F32)
+
+
+def pad_rows(table):
+    rank, width = table.shape
+    return jnp.concatenate([table, jnp.zeros((PAD - rank, width), table.dtype)], axis=0)
+
+
+def pad_twice(table):
+    rank, width = table.shape
+    return jnp.concatenate([table, table, jnp.zeros((PAD - 2 * rank, width), table.dtype)], axis=0)
+
+
+def two_terms(wide, rank):
+    high = wide.astype(BF).astype(F32)
+    return (high + pltpu.roll(wide - high, rank, 1)).astype(BF)
+
+
+def three_terms(wide):
+    high = wide.astype(BF)
+    rest = wide - high.astype(F32)
+    middle = rest.astype(BF)
+    return high, middle, (rest - middle.astype(F32)).astype(BF)
+
+
+def whole():
+    return pl.BlockSpec(memory_space=pltpu.VMEM)
+
+
+def in_place():
+    return pl.BlockSpec(memory_space=pl.ANY)
+
+
+def scalars():
+    return pl.BlockSpec(memory_space=pltpu.SMEM)
+
+
+def params(mib=58, **more):
+    return pltpu.CompilerParams(vmem_limit_bytes=mib * 2**20, **more)
+
+
+def cost(flops, nbytes):
+    return pl.CostEstimate(flops=int(flops), bytes_accessed=int(nbytes), transcendentals=0)
+
+
+def norm_stats(values):
+    average = jnp.mean(values, axis=-1, keepdims=True)
+    centred = values - average
+    scale = lax.rsqrt(jnp.mean(centred * centred, axis=-1, keepdims=True) + epsilon)
+    return centred * scale, scale
+
+
+def norm_grad(unit, scale, grad):
+    return scale * (
+        grad
+        - jnp.mean(grad, axis=-1, keepdims=True)
+        - unit * jnp.mean(grad * unit, axis=-1, keepdims=True)
+    )
+
+
+def row_mask(scal, rows):
+    at = lax.broadcasted_iota(jnp.int32, (rows, 1), 0) + scal[1] * rows
+    return (at < scal[0]).astype(F32)
+
+
+def fetch(parts, target, sem, part_at, axis, size):
+    copies = []
+    for near, part in enumerate(parts):
+        first = pl.multiple_of((part_at ^ near) * size, size)
+        place = target.at[:, pl.ds(first, size)] if axis == 1 else target.at[pl.ds(first, size)]
+        copies.append(pltpu.make_async_copy(part, place, sem.at[near]))
+    for copy in copies:
+        copy.start()
+    return copies
+
+
+def qkv_local_kernel(tok, gain, w, qa, qb, n1, rank, out, low):
+    @pl.when(pl.program_id(0) == 0)
+    def _():
+        unit, _ = norm_stats(tok[...].astype(F32))
+        normed = (unit * gain[...]).astype(BF)
+        n1[...] = normed
+        ranked = dotg(normed, pad_rows(qa[...]), 1, 1).astype(BF)
+        rank[...] = ranked
+        low[...] = ranked
+
+    out[0] = (dotg(n1[...], w[0], 1, 0) + dotg(low[...], pad_rows(qb[0]), 1, 0)).astype(BF)
+
+
+def qkv_local(tok, gain, w, qa, qb):
+    rows, width = tok.shape
+    third = w.shape[2]
+    rank = qa.shape[0]
+    fixed = lambda c: (0, 0)
+    turn = lambda c: ((c + 1) % 3, 0, 0)
+    return pl.pallas_call(
+        qkv_local_kernel,
+        grid=(3,),
+        in_specs=[
+            pl.BlockSpec((rows, width), fixed),
+            pl.BlockSpec((1, width), fixed),
+            pl.BlockSpec((1, width, third), turn),
+            pl.BlockSpec((rank, width), fixed),
+            pl.BlockSpec((1, rank, third), turn),
+        ],
+        out_specs=[
+            pl.BlockSpec((rows, width), fixed),
+            pl.BlockSpec((rows, PAD), fixed),
+            pl.BlockSpec((1, rows, third), turn),
+        ],
+        out_shape=[
+            jax.ShapeDtypeStruct((rows, width), BF),
+            jax.ShapeDtypeStruct((rows, PAD), BF),
+            jax.ShapeDtypeStruct((3, rows, third), BF),
+        ],
+        scratch_shapes=[pltpu.VMEM((rows, PAD), BF)],
+        compiler_params=params(dimension_semantics=("arbitrary",)),
+        cost_estimate=cost(2 * rows * width * 3 * third, 8e6),
+        name="qkv_local",
+    )(tok, gain, w, qa, qb)
+
+
+def qkv_other_kernel(scal, n1, rank, pack, *rest):
+    parts, (out, w), (sem,) = rest[:PARTS], rest[PARTS : PARTS + 2], rest[PARTS + 2 :]
+    third = w.shape[2]
+    copies = fetch(parts, w, sem, scal[2], 1, parts[0].shape[1])
+    for copy in copies:
+        copy.wait()
+    for c in (1, 2, 0):
+        qb = pack[:, c * third : (c + 1) * third]
+        out[c] = (dotg(n1[...], w[c], 1, 0) + dotg(rank[...], pad_rows(qb), 1, 0)).astype(BF)
+
+
+def qkv_other(scal, n1, rank, pack, parts):
+    rows, width = n1.shape
+    third = parts[0].shape[2]
+    return pl.pallas_call(
+        qkv_other_kernel,
+        in_specs=[scalars(), whole(), whole(), whole()] + [in_place()] * PARTS,
+        out_specs=[whole(), whole()],
+        out_shape=[
+            jax.ShapeDtypeStruct((3, rows, third), BF),
+            jax.ShapeDtypeStruct((3, width, third), BF),
+        ],
+        scratch_shapes=[pltpu.SemaphoreType.DMA((PARTS,))],
+        compiler_params=params(),
+        cost_estimate=cost(2 * rows * width * 3 * third, 10e6),
+        name="qkv_other",
+    )(scal, n1, rank, pack, *parts)
+
+
+def head_lanes(rows, head):
+    lanes = lax.broadcasted_iota(jnp.int32, (rows, 2 * HD), 1)
+    return lanes, (lanes < HD) if head == 0 else (lanes >= HD), HD if head == 0 else 0
+
+
+def key_bias(scal, rows, other):
+    side = 1 - scal[1] if other else scal[1]
+    at = lax.broadcasted_iota(jnp.int32, (rows, 2 * HD), 0) + side * rows
+    return jnp.where(at < jnp.maximum(scal[0], 1), 0.0, masked_score).astype(BF)
+
+
+def scaled_queries(queries):
+    wide = queries.astype(F32) * (HD**-0.5 * LOG2E)
+    high = wide.astype(BF)
+    return high, (wide - high.astype(F32)).astype(BF)
+
+
+def attend_kernel(scal, q_ref, k_ref, v_ref, ko_ref, vo_ref, out, log_out, qx, kx, vt):
+    rows = q_ref.shape[1]
+    queries = q_ref[0]
+    zero = jnp.zeros_like(queries)
+    one = jnp.ones_like(queries)
+    high, low = scaled_queries(queries)
+    for head in range(2):
+        lanes, own, spare = head_lanes(rows, head)
+        qx[head, :, 0:128] = jnp.where(own, high, jnp.where(lanes == spare, one, zero))
+        qx[head, :, 128:256] = low
+        for side, ref in enumerate((k_ref, ko_ref)):
+            at = slice(side * rows, (side + 1) * rows)
+            bias = key_bias(scal, rows, side == 1)
+            kx[head, at, 0:128] = jnp.where(own, ref[0], jnp.where(lanes == spare, bias, zero))
+            kx[head, at, 128:256] = jnp.where(own, ref[0], zero)
+    for side, ref in enumerate((v_ref, vo_ref)):
+        at = slice(side * rows, (side + 1) * rows)
+        turned = ref[0].T
+        for head in range(2):
+            vt[head, 0:HD, at] = turned[head * HD : (head + 1) * HD]
+            vt[head, HD : HD + 16, at] = jnp.ones((16, rows), BF)
+
+    def scores(head):
+        return dotg(kx[head], qx[head], 1, 1)
+
+    ahead = scores(0)
+    mixed = []
+    for head in range(2):
+        now = ahead
+        if head == 0:
+            ahead = scores(1)
+        top = jnp.max(now, axis=0, keepdims=True)
+        soft = jnp.exp2(now - top).astype(BF)
+        terms = dotg(vt[head], soft, 1, 0)
+        total = terms[HD : HD + 1]
+        mixed.append(terms[0:HD] / total)
+        log_out[0, head : head + 1, :] = top + jnp.log2(total)
+    out[...] = jnp.concatenate(mixed, axis=0).T.astype(BF)
+
+
+def attend(scal, own, other):
+    _, rows, width = own.shape
+    pairs = width // (2 * HD)
+    take = lambda c: pl.BlockSpec((1, rows, 2 * HD), lambda p: (c, 0, p))
+    return pl.pallas_call(
+        attend_kernel,
+        grid=(pairs,),
+        in_specs=[scalars(), take(0), take(1), take(2), take(0), take(1)],
+        out_specs=[
+            pl.BlockSpec((rows, 2 * HD), lambda p: (0, p)),
+            pl.BlockSpec((1, 8, rows), lambda p: (p, 0, 0)),
+        ],
+        out_shape=[
+            jax.ShapeDtypeStruct((rows, width), BF),
+            jax.ShapeDtypeStruct((pairs, 8, rows), F32),
+        ],
+        scratch_shapes=[
+            pltpu.VMEM((2, rows, 256), BF),
+            pltpu.VMEM((2, 2 * rows, 256), BF),
+            pltpu.VMEM((2, HD + 16, 2 * rows), BF),
+        ],
+        compiler_params=params(dimension_semantics=("arbitrary",)),
+        cost_estimate=cost(16e-6 * 1e15, 6e6),
+        name="attend",
+    )(scal, own, own, own, other, other)
+
+
+def attend_back_kernel(
+    scal, q_ref, k_ref, v_ref, ko_ref, vo_ref, mixed_ref, grad_ref, log_ref, own_out, other_out,
+    qx, gx, qm, gm, kx, vx, kt,
+):
+    rows = q_ref.shape[1]
+    queries, grad = q_ref[0], grad_ref[...]
+    zero = jnp.zeros_like(queries)
+    one = jnp.ones_like(queries)
+    high, low = scaled_queries(queries)
+    weighed = grad.astype(F32) * mixed_ref[...].astype(F32)
+    logs = log_ref[0].T
+    for head in range(2):
+        lanes, own, spare = head_lanes(rows, head)
+
+        def spread(columns):
+            filled = zero
+            for step, column in enumerate(columns):
+                filled = jnp.where(lanes == spare + step, column, filled)
+            return filled
+
+        row_sum = jnp.sum(jnp.where(own, weighed, 0.0), axis=1, keepdims=True)
+        log_terms = three_terms(-logs[:, head : head + 1])
+        qx[head, :, 0:128] = jnp.where(
+            own, high, spread(log_terms + (jnp.ones_like(log_terms[0]),))
+        )
+        qx[head, :, 128:256] = jnp.where(own, low, zero)
+        gx[head] = jnp.where(own, grad, spread(three_terms(-row_sum)))
+        qm[head] = jnp.where(own, queries, zero)
+        gm[head] = jnp.where(own, grad, zero)
+        extra = (lanes >= spare) & (lanes < spare + 3)
+        for side, (key_ref, value_ref) in enumerate(((k_ref, v_ref), (ko_ref, vo_ref))):
+            at = slice(side * rows, (side + 1) * rows)
+            bias = key_bias(scal, rows, side == 1)
+            fill = jnp.where(extra, one, jnp.where(lanes == spare + 3, bias, zero))
+            kx[head, at, 0:128] = jnp.where(own, key_ref[0], fill)
+            kx[head, at, 128:256] = jnp.where(own, key_ref[0], zero)
+            vx[head, at, :] = jnp.where(own, value_ref[0], jnp.where(extra, one, zero))
+    for side, ref in enumerate((k_ref, ko_ref)):
+        kt[:, side * rows : (side + 1) * rows] = ref[0].T
+    steps = [(side, head) for side in range(2) for head in range(2)]
+
+    def first(side, head):
+        at = slice(side * rows, (side + 1) * rows)
+        return dotg(kx[head, at], qx[head], 1, 1), dotg(vx[head, at], gx[head], 1, 1)
+
+    ahead = first(*steps[0])
+    grad_queries = [0.0, 0.0]
+    kept = None
+    for number, (side, head) in enumerate(steps):
+        scores, grad_soft = ahead
+        if number + 1 < len(steps):
+            ahead = first(*steps[number + 1])
+        soft = jnp.exp2(scores)
+        grad_scores = (soft * grad_soft).astype(BF)
+        values = dotg(soft.astype(BF), gm[head], 1, 0)
+        keys = dotg(grad_scores, qm[head], 1, 0)
+        at = slice(side * rows, (side + 1) * rows)
+        grad_queries[head] += dotg(kt[head * HD : (head + 1) * HD, at], grad_scores, 1, 0)
+        if head == 0:
+            kept = (keys, values)
+        else:
+            keys = ((kept[0] + keys) * HD**-0.5).astype(BF)
+            values = (kept[1] + values).astype(BF)
+            if side == 0:
+                own_out[1], own_out[2] = keys, values
+            else:
+                other_out[0], other_out[1] = keys, values
+    own_out[0] = (jnp.concatenate(grad_queries, axis=0).T * HD**-0.5).astype(BF)
+
+
+def attend_back(scal, own, other, mixed, grad, logs):
+    _, rows, width = own.shape
+    pairs = width // (2 * HD)
+    take = lambda c: pl.BlockSpec((1, rows, 2 * HD), lambda p: (c, 0, p))
+    flat = pl.BlockSpec((rows, 2 * HD), lambda p: (0, p))
+    return pl.pallas_call(
+        attend_back_kernel,
+        grid=(pairs,),
+        in_specs=[scalars(), take(0), take(1), take(2), take(0), take(1), flat, flat]
+        + [pl.BlockSpec((1, 8, rows), lambda p: (p, 0, 0))],
+        out_specs=[
+            pl.BlockSpec((3, rows, 2 * HD), lambda p: (0, 0, p)),
+            pl.BlockSpec((2, rows, 2 * HD), lambda p: (0, 0, p)),
+        ],
+        out_shape=[
+            jax.ShapeDtypeStruct((3, rows, width), BF),
+            jax.ShapeDtypeStruct((2, rows, width), BF),
+        ],
+        scratch_shapes=[
+            pltpu.VMEM((2, rows, 256), BF),
+            pltpu.VMEM((2, rows, 128), BF),
+            pltpu.VMEM((2, rows, 128), BF),
+            pltpu.VMEM((2, rows, 128), BF),
+            pltpu.VMEM((2, 2 * rows, 256), BF),
+            pltpu.VMEM((2, 2 * rows, 128), BF),
+            pltpu.VMEM((2 * HD, 2 * rows), BF),
+        ],
+        compiler_params=params(dimension_semantics=("arbitrary",)),
+        cost_estimate=cost(27e-6 * 1e15, 9e6),
+        name="attend_back",
+    )(scal, own, own, own, other, other, mixed, grad, logs)
+
+
+def branch_kernel(
+    scal, mix_a, mix_b, tok, w_a, oa_a, oa_b, ob, scale_one, gain_two, scale_two, ua, db, cot, *rest
+):
+    parts = rest[:PARTS]
+    residual, n2, rank_out, rank_up, grad_mlp, grad_rank, w_b, sem = rest[PARTS:]
+    rows = tok.shape[0]
+    rank = oa_a.shape[0]
+    copies = fetch(parts, w_b, sem, scal[2], 0, parts[0].shape[0])
+    grad_low = (scale_two[...] * (cot[...].astype(F32) * row_mask(scal, rows))).astype(BF)
+    grad_mlp[...] = grad_low
+    grad_rank[...] = dotg(grad_low, pad_rows(db[...]), 1, 1).astype(BF)
+    ranked = dotg(mix_a[...], pad_rows(oa_a[...]), 1, 1) + dotg(mix_b[...], pad_rows(oa_b[...]), 1, 1)
+    ranked = two_terms(ranked, rank)
+    rank_out[...] = ranked
+    for copy in copies:
+        copy.wait()
+    branch = dotg(mix_a[...], w_a[...], 1, 0) + dotg(mix_b[...], w_b[...], 1, 0)
+    branch = branch + dotg(ranked, pad_twice(ob[...]), 1, 0)
+    total = tok[...].astype(F32) + scale_one[...] * branch
+    residual[...] = total
+    unit, _ = norm_stats(total)
+    normed = (unit * gain_two[...]).astype(BF)
+    n2[...] = normed
+    rank_up[...] = dotg(normed, pad_rows(ua[...]), 1, 1).astype(BF)
+
+
+def branch(scal, mix_a, mix_b, tok, w_a, parts, oa_a, oa_b, ob, scale_one, gain_two, scale_two, ua, db, cot):
+    rows, width = tok.shape
+    low = jax.ShapeDtypeStruct((rows, width), BF)
+    ranked = jax.ShapeDtypeStruct((rows, PAD), BF)
+    return pl.pallas_call(
+        branch_kernel,
+        in_specs=[scalars()] + [whole()] * 13 + [in_place()] * PARTS,
+        out_specs=[whole()] * 7,
+        out_shape=[jax.ShapeDtypeStruct((rows, width), F32), low, ranked, ranked, low, ranked]
+        + [jax.ShapeDtypeStruct(w_a.shape, BF)],
+        scratch_shapes=[pltpu.SemaphoreType.DMA((PARTS,))],
+        compiler_params=params(),
+        cost_estimate=cost(2 * rows * width * width, 16e6),
+        name="branch",
+    )(scal, mix_a, mix_b, tok, w_a, oa_a, oa_b, ob, scale_one, gain_two, scale_two, ua, db, cot, *parts)
+
+
+def mlp_kernel(count, step, more, *refs):
+    scal, n2, rank_up, grad_mlp, grad_rank, ub, da = refs[:7]
+    ups, downs = refs[7 : 7 + count], refs[7 + count : 7 + 2 * count]
+    rest = refs[7 + 2 * count :]
+    earlier = ()
+    if more:
+        earlier, rest = rest[:4], rest[4:]
+    m_out, g_out, rd_out, gru_out, gub_out, gda_out = rest[:6]
+    wu, wd, ubs, das, hidden, grad_pre, sem, early_sem = rest[6:]
+    width = wu.shape[1]
+    rank = ub.shape[0]
+    size = width // PARTS
+    chunks = width // step
+    waits = [[] for _ in range(chunks)]
+    for near in range(PARTS):
+        at = pl.ds(near * size, size)
+        if count == 1:
+            sources = ups[0].at[:, at], downs[0].at[at]
+        else:
+            sources = ups[near], downs[near]
+        for which, (source, target) in enumerate(zip(sources, (wu.at[:, at], wd.at[at]))):
+            copy = pltpu.make_async_copy(source, target, sem.at[which, near])
+            copy.start()
+            waits[near * size // step].append(copy)
+    if more:
+        early = [
+            pltpu.make_async_copy(earlier[0], m_out, early_sem.at[0]),
+            pltpu.make_async_copy(earlier[1], g_out, early_sem.at[1]),
+        ]
+        for copy in early:
+            copy.start()
+
+    def place(near):
+        if count == 1:
+            return pl.ds(near * size, size)
+        return pl.ds(pl.multiple_of((scal[2] ^ near) * size, size), size)
+
+    ubs[...] = jnp.zeros_like(ubs)
+    das[...] = jnp.zeros_like(das)
+    for near in range(PARTS):
+        at = slice(near * size, (near + 1) * size)
+        ubs[0:rank, at] = ub[:, place(near)]
+        das[0:rank, at] = da[:, place(near)]
+    up_turned = rank_up[...].T[0:rank]
+    grad_turned = grad_rank[...].T[0:rank]
+
+    def first(k):
+        for copy in waits[k]:
+            copy.wait()
+        at = slice(k * step, (k + 1) * step)
+        return (
+            dotg(n2[...], wu[:, at], 1, 0) + dotg(rank_up[...], ubs[:, at], 1, 0),
+            dotg(grad_mlp[...], wd[at, :], 1, 1) + dotg(grad_rank[...], das[:, at], 1, 0),
+        )
+
+    ahead = first(0)
+    for k in range(chunks):
+        at = slice(k * step, (k + 1) * step)
+        preact, grad_hidden = ahead
+        if k + 1 < chunks:
+            ahead = first(k + 1)
+        cdf = 0.5 * (1.0 + lax.erf(preact * 0.7071067811865476))
+        hidden[:, at] = (preact * cdf).astype(BF)
+        slope = cdf + preact * jnp.exp(-0.5 * preact * preact) * 0.3989422804014327
+        grad_pre[:, at] = (grad_hidden * slope).astype(BF)
+    ranked = dotg(hidden[...], das[...], 1, 1)
+    grad_ranked = dotg(grad_pre[...], ubs[...], 1, 1)
+    if more:
+        ranked, grad_ranked = ranked + earlier[2][...], grad_ranked + earlier[3][...]
+    rd_out[...] = ranked
+    gru_out[...] = grad_ranked
+    for near in range(PARTS):
+        at = slice(near * size, (near + 1) * size)
+        gub_out[:, place(near)] = dotg(up_turned, grad_pre[:, at], 1, 0)
+        gda_out[:, place(near)] = dotg(grad_turned, hidden[:, at], 1, 0)
+    if more:
+        for copy in early:
+            copy.wait()
+    for at in (slice(k, k + step) for k in range(0, wu.shape[0], step)):
+        terms = dotg(hidden[...], wd[:, at], 1, 0)
+        grad_terms = dotg(grad_pre[...], wu[at, :], 1, 1)
+        if more:
+            m_out[:, at] += terms
+            g_out[:, at] += grad_terms
+        else:
+            m_out[:, at] = terms
+            g_out[:, at] = grad_terms
+
+
+def mlp(scal, n2, rank_up, grad_mlp, grad_rank, ub, da, ups, downs, earlier=()):
+    rows, width = n2.shape
+    half = ub.shape[1]
+    rank = ub.shape[0]
+    count = len(ups)
+    step = half // 4
+    sums = jax.ShapeDtypeStruct((rows, width), F32)
+    ranked = jax.ShapeDtypeStruct((rows, PAD), F32)
+    table = jax.ShapeDtypeStruct((rank, half), F32)
+    return pl.pallas_call(
+        functools.partial(mlp_kernel, count, step, bool(earlier)),
+        in_specs=[scalars()]
+        + [whole()] * 6
+        + [in_place()] * (2 * count)
+        + ([in_place()] * 2 + [whole()] * 2 if earlier else []),
+        out_specs=[whole()] * 6,
+        out_shape=[sums, sums, ranked, ranked, table, table],
+        scratch_shapes=[
+            pltpu.VMEM((width, half), BF),
+            pltpu.VMEM((half, width), BF),
+            pltpu.VMEM((PAD, half), BF),
+            pltpu.VMEM((PAD, half), BF),
+            pltpu.VMEM((rows, half), BF),
+            pltpu.VMEM((rows, half), BF),
+            pltpu.SemaphoreType.DMA((2, PARTS)),
+            pltpu.SemaphoreType.DMA((2,)),
+        ],
+        compiler_params=params(),
+        cost_estimate=cost(28e-6 * 1e15, 20e6),
+        name="mlp",
+    )(scal, n2, rank_up, grad_mlp, grad_rank, ub, da, *ups, *downs, *earlier)
+
+
+def middle_kernel(
+    scal, residual, m_in, g_in, rd, gru, db, ua, scale_two, gain_two, scale_one, cot, w_a, w_b,
+    oa_a, oa_b, ob, mix_a, mix_b, rank_out, n2, grad_mlp,
+    layer, grad_res, grad_a, grad_b, goa_a, goa_b, gob, gua, gdb,
+):
+    rows = residual.shape[0]
+    rank = db.shape[0]
+    valid = row_mask(scal, rows)
+    down = two_terms(rd[...], rank)
+    up = two_terms(gru[...], rank)
+
+    def turned(terms, right):
+        both = dotg(terms.T[0 : 2 * rank], right, 1, 0)
+        return both[0:rank] + both[rank : 2 * rank]
+
+    branch_out = m_in[...] + dotg(down, pad_twice(db[...]), 1, 0)
+    layer[...] = ((residual[...] + scale_two[...] * branch_out) * valid).astype(BF)
+    gua[...] = turned(up, n2[...])
+    gdb[...] = turned(down, grad_mlp[...])
+    unit, scale = norm_stats(residual[...])
+    grad_normed = (g_in[...] + dotg(up, pad_twice(ua[...]), 1, 0)) * gain_two[...]
+    grad_total = cot[...].astype(F32) * valid + norm_grad(unit, scale, grad_normed)
+    grad_res[...] = grad_total
+    grad_attn = (scale_one[...] * grad_total).astype(BF)
+    grad_rank = dotg(grad_attn, pad_rows(ob[...]), 1, 1).astype(BF)
+    grad_a[...] = (
+        dotg(grad_attn, w_a[...], 1, 1) + dotg(grad_rank, pad_rows(oa_a[...]), 1, 0)
+    ).astype(BF)
+    grad_b[...] = (
+        dotg(grad_attn, w_b[...], 1, 1) + dotg(grad_rank, pad_rows(oa_b[...]), 1, 0)
+    ).astype(BF)
+    rank_turned = grad_rank.T[0:rank]
+    goa_a[...] = dotg(rank_turned, mix_a[...], 1, 0)
+    goa_b[...] = dotg(rank_turned, mix_b[...], 1, 0)
+    gob[...] = turned(rank_out[...], grad_attn)
+
+
+def middle(*args):
+    rows, width = args[1].shape
+    half = args[12].shape[0]
+    rank = args[6].shape[0]
+    part = jax.ShapeDtypeStruct((rows, half), BF)
+    table = jax.ShapeDtypeStruct((rank, width), F32)
+    half_table = jax.ShapeDtypeStruct((rank, half), F32)
+    return pl.pallas_call(
+        middle_kernel,
+        in_specs=[scalars()] + [whole()] * (len(args) - 1),
+        out_specs=[whole()] * 9,
+        out_shape=[jax.ShapeDtypeStruct((rows, width), BF), jax.ShapeDtypeStruct((rows, width), F32)]
+        + [part, part, half_table, half_table, table, table, table],
+        compiler_params=params(),
+        cost_estimate=cost(8e-6 * 1e15, 20e6),
+        name="middle",
+    )(*args)
+
+
+def qkv_tables_kernel(own_a, got_a, own_b, got_b, qb_a, qb_b, n1, rank_in, sum_a, sum_b, rank_out, gqb_a, gqb_b, gqa):
+    rank = qb_a.shape[1]
+    rank_turned = rank_in[...].T[0:rank]
+    ranked = None
+    for own, got, qb, total, table in ((own_a, got_a, qb_a, sum_a, gqb_a), (own_b, got_b, qb_b, sum_b, gqb_b)):
+        for c in range(3):
+            grad = own[c] if c == 0 else (own[c].astype(F32) + got[c - 1].astype(F32)).astype(BF)
+            total[c] = grad
+            table[c] = dotg(rank_turned, grad, 1, 0)
+            terms = dotg(grad, pad_rows(qb[c]), 1, 1)
+            ranked = terms if ranked is None else ranked + terms
+    ranked = two_terms(ranked, rank)
+    rank_out[...] = ranked
+    both = dotg(ranked.T[0 : 2 * rank], n1[...], 1, 0)
+    gqa[...] = both[0:rank] + both[rank : 2 * rank]
+
+
+def qkv_tables(own_a, got_a, own_b, got_b, qb_a, qb_b, n1, rank_in):
+    rows, width = n1.shape
+    _, rank, third = qb_a.shape
+    return pl.pallas_call(
+        qkv_tables_kernel,
+        in_specs=[whole()] * 8,
+        out_specs=[whole()] * 6,
+        out_shape=[jax.ShapeDtypeStruct((3, rows, third), BF)] * 2
+        + [jax.ShapeDtypeStruct((rows, PAD), BF)]
+        + [jax.ShapeDtypeStruct((3, rank, third), F32)] * 2
+        + [jax.ShapeDtypeStruct((rank, width), F32)],
+        compiler_params=params(),
+        cost_estimate=cost(5e-6 * 1e15, 14e6),
+        name="qkv_tables",
+    )(own_a, got_a, own_b, got_b, qb_a, qb_b, n1, rank_in)
+
+
+def qkv_rows_kernel(grad_a, grad_b, w_a, w_b, ranked, qa, tok, gain, grad_res, out):
+    grad = dotg(ranked[...], pad_twice(qa[...]), 1, 0)
+    for part, w in ((grad_a, w_a), (grad_b, w_b)):
+        for c in range(3):
+            grad = grad + dotg(part[c], w[c], 1, 1)
+    unit, scale = norm_stats(tok[...].astype(F32))
+    out[...] = (grad_res[...] + norm_grad(unit, scale, grad * gain[...])).astype(BF)
+
+
+def qkv_rows(*args):
+    rows, width = args[6].shape
+    return pl.pallas_call(
+        qkv_rows_kernel,
+        in_specs=[whole()] * 9,
+        out_specs=whole(),
+        out_shape=jax.ShapeDtypeStruct((rows, width), BF),
+        compiler_params=params(),
+        cost_estimate=cost(7e-6 * 1e15, 16e6),
+        name="qkv_rows",
+    )(*args)
+
+
+def swap(rows):
+    return lax.ppermute(rows, ("core", "tensor"), SWAP)
+
+
+def flip(axis):
+    return lambda array: lax.ppermute(array, axis, FLIP)
+
+
+def other_half(local, axis, part_at):
+    size = local.shape[axis] // PARTS
+    mine = lax.dynamic_slice_in_dim(local, part_at * size, size, axis)
+    near = {0: flip("tensor")(mine)}
+    near[2] = flip("x")(near[0])
+    near[4] = flip("zb")(near[0])
+    near[6] = flip("zb")(near[2])
+    for k in (0, 2, 4, 6):
+        near[k + 1] = flip("core")(near[k])
+    return [near[k] for k in range(PARTS)]
+
+
+def side(array, axis, index, count):
+    size = array.shape[axis] // count
+    return lax.dynamic_slice_in_dim(array, index * size, size, axis)
+
+
+class Sum:
+    def __init__(self, near, far, shared, core, tensor):
+        self.core, self.tensor = core, tensor
+        self.rank = near.shape[0]
+        self.near, self.far, self.shared = near, far, shared
+
+    def over_cores(self):
+        c = self.core
+        rank, width = self.shared.shape
+        quarters = self.shared.reshape(rank, 4, width // 4)
+
+        def share(index):
+            near = side(self.near, 1, index, 2)
+            far = side(self.far, 1, index, 2)
+            ours = lax.dynamic_index_in_dim(quarters, self.tensor * 2 + index, 1, False)
+            theirs = lax.dynamic_index_in_dim(quarters, (1 - self.tensor) * 2 + index, 1, False)
+            return jnp.concatenate([near, ours, far, theirs], axis=1)
+
+        got = flip("core")(share(1 - c).astype(BF))
+        total = (share(c) + got.astype(F32)).astype(BF)
+        self.columns = total.shape[1] // 2
+        self.mine = total[:, : self.columns]
+        self.send = total[:, self.columns :]
+        return self
+
+    def over_pair(self):
+        self.pair = jnp.stack([self.mine, flip("tensor")(self.send)])
+        return self
+
+    def over_images(self, weights, groups):
+        got = [self.pair]
+        names, sizes = ("hi", "zb", "x"), groups
+        total = sizes[0] * sizes[1] * sizes[2]
+        for k in range(1, total):
+            got.append(lax.ppermute(self.pair, names, [(i, i ^ k) for i in range(total)]))
+        images = jnp.concatenate(got, axis=0)
+        self.dense = jnp.einsum("in,irf->nrf", weights, images, preferred_element_type=F32).astype(BF)
+        return self
+
+    def spread(self):
+        half = self.near.shape[1] // 2
+        ours = self.dense[:, :, half:]
+        theirs = flip("tensor")(ours)
+        first = self.tensor == 0
+        pair = jnp.concatenate(
+            [self.dense[:, :, :half], jnp.where(first, ours, theirs), jnp.where(first, theirs, ours)], axis=2
+        )
+        other = flip("core")(pair)
+        low = jnp.where(self.core == 0, pair, other).astype(F32)
+        high = jnp.where(self.core == 0, other, pair).astype(F32)
+        quarter = ours.shape[2]
+        near = jnp.concatenate([low[:, :, :half], high[:, :, :half]], axis=2)
+        cut = lambda array, index: array[:, :, half + index * quarter : half + (index + 1) * quarter]
+        shared = jnp.concatenate([cut(low, 0), cut(high, 0), cut(low, 1), cut(high, 1)], axis=2)
+        return near, shared
+
+
+def quad_body(
+    tokens, cotangent, lengths, adapter_ids, gain_one, gain_two, scale_one, scale_two, w_qkv, w_out, w_up, w_down,
+    qkv_a, qkv_b, out_a, out_b, up_a, up_b, down_a, down_b,
+):
+    core, tensor = lax.axis_index("core"), lax.axis_index("tensor")
+    groups = tuple(lax.axis_size(name) for name in ("hi", "zb", "x"))
+    part_at = lax.axis_index("zb") * 4 + lax.axis_index("x") * 2 + core
+    rank, width = qkv_a.shape[1:]
+    heads_width = w_qkv.shape[2]
+    units = w_up.shape[1]
+
+    tok = swap(tokens[0])
+    facts = jnp.stack([lengths[0], adapter_ids[0]])
+    facts_other = flip("core")(facts)
+    mine = jnp.where(core == tensor, facts, facts_other)
+    theirs = jnp.where(core == tensor, facts_other, facts)
+    length, adapter, adapter_other = mine[0], mine[1], theirs[1]
+    scal = jnp.stack([length, core, part_at, adapter]).astype(jnp.int32)
+
+    qkv_b, out_b, up_b, down_b = (jnp.swapaxes(table, -1, -2) for table in (qkv_b, out_b, up_b, down_b))
+    pick = lambda table, index: lax.dynamic_index_in_dim(table, index, 0, False)
+
+    def packed(index):
+        qb = jnp.swapaxes(pick(qkv_b, index), 0, 1).reshape(rank, 3 * heads_width)
+        return jnp.concatenate([qb, pick(out_a, index), pick(up_b, index), pick(down_a, index)], axis=1)
+
+    pack = flip("tensor")(packed(adapter_other))
+    cuts = (3 * heads_width, 4 * heads_width, 4 * heads_width + units)
+    qb_other, oa_other, ub_other, da_other = jnp.split(pack, cuts, axis=1)
+    qa, oa, ob, ua, ub, da, db = (
+        pick(table, adapter) for table in (qkv_a, out_a, out_b, up_a, up_b, down_a, down_b)
+    )
+    qb = pick(qkv_b, adapter)
+    gain_one, gain_two, scale_one, scale_two = (v.reshape(1, width) for v in (gain_one, gain_two, scale_one, scale_two))
+
+    pair_ids = jnp.stack([adapter, adapter_other])
+    total = groups[0] * groups[1] * groups[2]
+    all_ids = [pair_ids] + [
+        lax.ppermute(pair_ids, ("hi", "zb", "x"), [(i, i ^ k) for i in range(total)]) for k in range(1, total)
+    ]
+    weights = (jnp.concatenate(all_ids)[:, None] == jnp.arange(qkv_a.shape[0])[None, :]).astype(BF)
+
+    w3 = jnp.swapaxes(w_qkv, 0, 1)
+    n1, rank_qkv, own_a = qkv_local(tok, gain_one, w3, qa, qb)
+    kv_a = flip("core")(own_a[1:])
+    w3_parts = other_half(w3, 1, part_at)
+    out_parts = other_half(w_out, 0, part_at)
+    cot = swap(cotangent[0])
+    up_parts = other_half(w_up, 1, part_at)
+    down_parts = other_half(w_down, 0, part_at)
+
+    mix_a, logs_a = attend(scal, own_a, kv_a)
+    own_b, w3_other = qkv_other(scal, n1, rank_qkv, qb_other, w3_parts)
+    kv_b = flip("core")(own_b[1:])
+    mix_b, logs_b = attend(scal, own_b, kv_b)
+    residual, n2, rank_out, rank_up, grad_mlp, grad_rank, out_other = branch(
+        scal, mix_a, mix_b, tok, w_out, out_parts, oa, oa_other, ob, scale_one, gain_two, scale_two, ua, db, cot
+    )
+    m, g, rd, gru, gub_a, gda_a = mlp(scal, n2, rank_up, grad_mlp, grad_rank, ub, da, [w_up], [w_down])
+    m, g, rd, gru, gub_b, gda_b = mlp(
+        scal, n2, rank_up, grad_mlp, grad_rank, ub_other, da_other, up_parts, down_parts, (m, g, rd, gru)
+    )
+    layer, grad_res, grad_a, grad_b, goa_a, goa_b, gob, gua, gdb = middle(
+        scal, residual, m, g, rd, gru, db, ua, scale_two, gain_two, scale_one, cot, w_out, out_other,
+        oa, oa_other, ob, mix_a, mix_b, rank_out, n2, grad_mlp,
+    )
+    layer_out = swap(layer)
+    early = Sum(
+        jnp.concatenate([goa_a, gub_a, gda_a], axis=1),
+        jnp.concatenate([goa_b, gub_b, gda_b], axis=1),
+        jnp.concatenate([gob, gua, gdb], axis=1),
+        core,
+        tensor,
+    )
+    early.over_cores()
+    early.over_pair()
+    back_a, sent_a = attend_back(scal, own_a, kv_a, mix_a, grad_a, logs_a)
+    got_a = flip("core")(sent_a)
+    early.over_images(weights, groups)
+    back_b, sent_b = attend_back(scal, own_b, kv_b, mix_b, grad_b, logs_b)
+    got_b = flip("core")(sent_b)
+    qb_other3 = jnp.swapaxes(qb_other.reshape(rank, 3, heads_width), 0, 1)
+    sum_a, sum_b, ranked, gqb_a, gqb_b, gqa = qkv_tables(
+        back_a, got_a, back_b, got_b, qb, qb_other3, n1, rank_qkv
+    )
+    flat = lambda table: jnp.swapaxes(table, 0, 1).reshape(rank, 3 * heads_width)
+    late = Sum(flat(gqb_a), flat(gqb_b), gqa, core, tensor)
+    late.over_cores()
+    late.over_pair()
+    grad_tokens = qkv_rows(sum_a, sum_b, w3, w3_other, ranked, qa, tok, gain_one, grad_res)
+    grad_tokens = swap(grad_tokens).astype(F32)
+    late.over_images(weights, groups)
+    near, shared = early.spread()
+    sum_oa, sum_ub, sum_da = jnp.split(near, (heads_width, heads_width + units), axis=2)
+    sum_ob, sum_ua, sum_db = jnp.split(shared, 3, axis=2)
+    near, sum_qa = late.spread()
+    sum_qb = jnp.swapaxes(near.reshape(-1, rank, 3, heads_width), 1, 2)
+    turn = lambda table: jnp.swapaxes(table, -1, -2)
+    return (
+        layer_out[None],
+        grad_tokens[None],
+        sum_qa,
+        turn(sum_qb),
+        sum_oa,
+        turn(sum_ob),
+        sum_ua,
+        turn(sum_ub),
+        sum_da,
+        turn(sum_db),
+    )
+
+
 def solution(mesh):
-    return jax.shard_map(
-        body,
-        mesh=mesh,
-        in_specs=(
-            P("dp", "tensor", None),
-            P("dp", "tensor", None),
-            P("dp"),
-            P("dp"),
-            P(),
-            P(),
-            P(),
-            P(),
-            P(None, None, "tensor"),
-            P("tensor", None),
-            P(None, "tensor"),
-            P("tensor", None),
-            P(),
-            P(None, None, "tensor", None),
-            P(None, None, "tensor"),
-            P(),
-            P(),
-            P(None, "tensor", None),
-            P(None, None, "tensor"),
-            P(),
-        ),
-        out_specs=(
-            P("dp", "tensor", None),
-            P("dp", "tensor", None),
-            P(),
-            P(None, None, "tensor", None),
-            P(None, None, "tensor"),
-            P(),
-            P(),
-            P(None, "tensor", None),
-            P(None, None, "tensor"),
-            P(),
-        ),
-        check_vma=False,
-    )
+    groups, split = mesh.shape["dp"], mesh.shape["tensor"]
+    if split == 2 and groups % 8 == 0:
+        mesh = Mesh(mesh.devices.reshape(groups // 8, 2, 2, 2, 2), ("hi", "zb", "x", "core", "tensor"))
+        dp, body = ("hi", "zb", "x", "core"), quad_body
+    else:
+        dp, body = "dp", plain_body
+    slots = P(dp, "tensor", None)
+    in_specs = (
+        slots, slots, P(dp), P(dp), P(), P(), P(), P(),
+        P(None, None, "tensor"), P("tensor", None), P(None, "tensor"), P("tensor", None),
+        P(), P(None, None, "tensor", None), P(None, None, "tensor"), P(),
+        P(), P(None, "tensor", None), P(None, None, "tensor"), P(),
+    )
+    out_specs = (
+        slots, slots, P(), P(None, None, "tensor", None), P(None, None, "tensor"), P(),
+        P(), P(None, "tensor", None), P(None, None, "tensor"), P(),
+    )
+    return jax.shard_map(body, mesh=mesh, in_specs=in_specs, out_specs=out_specs, check_vma=False)

time: 1020 us -> 432 us (0.42)
  waiting for transfers between devices: 526 us -> 69.9 us
  matrix products: 317 us -> 1.98 us
  Pallas kernels: 0 us -> 188 us
  starting transfers between devices: 0.8 us -> 104 us
  other arithmetic: 99.8 us -> 9.58 us
    dot_general x46 -> x2, matrix products: 317 us -> 1.98 us  [over_images(): jnp.einsum('in,irf->nrf', weights, images, preferred_element_type=F32)]
    psum x2 -> x0, waiting for transfers between devices: 220 us -> none  [the longest x1 131 us: body(): lax.psum((stack_slots(grad_qkv_a), stack_slots(grad_out_b), stack_slots(g...]
    pallas_call x0 -> x12, Pallas kernels: none -> 188 us  [the longest x2 53 us: attend_back(): pl.pallas_call(attend_back_kernel, grid=(pairs,), in_specs=[scalars(), ta...]
    all_gather x6 -> x0, waiting for transfers between devices: 174 us -> none  [the longest x1 99.1 us: body(): lax.all_gather(w_up, 'tensor', axis=1, tiled=True)]
    reduce_scatter x2 -> x0, waiting for transfers between devices: 130 us -> none  [the longest x1 69 us: body(): lax.psum_scatter(grad_one_terms, 'tensor', scatter_dimension=1, tiled=True)]
    ppermute x0 -> x71, starting transfers between devices: none -> 104 us  [the longest x46 44.6 us: flip(): return lambda array: lax.ppermute(array, axis, FLIP)]
    ppermute x0 -> x71, waiting for transfers between devices: none -> 69.9 us  [the longest x46 39.2 us: flip(): return lambda array: lax.ppermute(array, axis, FLIP)]
    convert_element_type x4, other arithmetic: 52.3 us -> 1.61 us  [the longest x1 1.46 us: spread(): high = jnp.where(self.core == 0, other, pair).astype(F32)]
  transfers between devices with their start and end apart: 10 -> 71, of which waited for: 8 -> 19; matrix products, arithmetic and copies ran while one was open for 21% -> 11% of each run, Pallas kernels for 0% -> 36%
where the time goes in v1:
time: 432 us; the launch traced here: 425 us
  Pallas kernels  188 us (44%)
  starting transfers between devices  104 us (24%)
  waiting for transfers between devices  69.9 us (16%)
  local copies, waits for them, and re-layouts  43.8 us (10%)
  other arithmetic  9.58 us (2%)
  between operations  7.14 us (2%)
    pallas_call x2, Pallas kernels, attend_back(): pl.pallas_call(attend_back_kernel, grid=(pairs,), in_specs=[scalars(), ta...  53 us
    pallas_call x2, Pallas kernels, mlp(): pl.pallas_call(functools.partial(mlp_kernel, count, step, bool(earlier)),...  48.2 us
    ppermute x46, starting transfers between devices, flip(): return lambda array: lax.ppermute(array, axis, FLIP)  44.6 us
    ppermute x46, waiting for transfers between devices, flip(): return lambda array: lax.ppermute(array, axis, FLIP)  39.2 us
    pallas_call x2, Pallas kernels, attend(): pl.pallas_call(attend_kernel, grid=(pairs,), in_specs=[scalars(), take(0)...  30 us
    ppermute x14, starting transfers between devices, over_images(): lax.ppermute(self.pair, names, [(i, i ^ k) for i in range(total)])  28.4 us
    ppermute x14, waiting for transfers between devices, over_images(): lax.ppermute(self.pair, names, [(i, i ^ k) for i in range(total)])  20.3 us
    ppermute x7, starting transfers between devices, quad_body(): lax.ppermute(pair_ids, ('hi', 'zb', 'x'), [(i, i ^ k) for i in range(tota...  17.4 us
  transfers between devices with their start and end apart: 71, of which 19 were waited for; matrix products, arithmetic and copies ran while one was open for 11% of the time, Pallas kernels for 36%

profile of v1, /device:TPU:1, one launch (start us, length us, event | category | flops | bytes accessed | tf_op | source)
XLA Modules:
  0.0 424.5 jit_solution(12513914611529097188)
XLA Ops:
  2.1 4.5 %collective-permute-start.1 = (bf16[688,1024]{1,0:T(8,128)(2,1)}, bf16[688,1024]{1,0:T(8,128)(2,1)S(1)}, u32[]{:S(2)}, u32[]{:S(2)}) collective-permute-start(bf16[688,1024]{1,0:T(8,128)(2,1)} %bitcast.148), channel_id=1, source_target_pairs={{0,0},{1,2},{2,1},{3,3},{4,4},{5,6},{6,5},{7,7},{8,8},{9,10},{10,9... | collective-permute-start | bytes 4227080 | tf_op jit(solution)/shard_map/ppermute | solution.py:900
  26.5 14.9 %collective-permute-done.14.rest_0_ = bf16[64,1024]{1,0:T(8,128)(2,1)S(1)} collective-permute-done((bf16[64,1024]{1,0:T(8,128)(2,1)S(1)}, bf16[64,1024]{1,0:T(8,128)(2,1)S(1)}, u32[]{:S(2)}, u32[]{:S(2)}) %collective-permute-start.14) | collective-permute-done | bytes 131104 | tf_op jit(solution)/shard_map/ppermute | solution.py:904
  44.1 7.4 %qkv_local.1 = (bf16[688,1024]{1,0:T(8,128)(2,1)}, bf16[688,128]{1,0:T(8,128)(2,1)}, bf16[3,688,512]{2,1,0:T(8,128)(2,1)}) custom-call(bf16[688,1024]{1,0:T(8,128)(2,1)} %copy-done.2, f32[1,1024]{1,0:T(1,128)} %bitcast.149, bf16[3,1024,512]{2,1,0:T(8,128)(2,1)} %bitcast.137, bf16[16,1024]{1,0:T(8,128)(2,1)} %dynamic-slice_bitcast_fusion.10.qa, ...), custom_call_target="tpu_custom_call" | custom-call | flops 2164260864 | bytes 8000000 | tf_op jit(solution)/shard_map/qkv_local/pallas_call | solution.py:379
  62.3 3.1 collective-permute-start.46
  66.5 3.3 collective-permute-start.47
  70.8 4.0 collective-permute-start.48
  75.9 9.3 %collective-permute-start.2 = (bf16[2,688,512]{2,1,0:T(8,128)(2,1)S(1)}, bf16[2,688,512]{2,1,0:T(8,128)(2,1)}, u32[]{:S(2)}, u32[]{:S(2)}) collective-permute-start(bf16[2,688,512]{2,1,0:T(8,128)(2,1)S(1)} %slice.82), channel_id=1, source_target_pairs={{0,2},{2,0},{1,3},{3,1},{4,6},{6,4},{5,7},{7,5},{8,10},{10,8},{9,1... | collective-permute-start | bytes 4227080 | tf_op jit(solution)/shard_map/ppermute | solution.py:904
  85.3 5.1 %collective-permute-done.18.rest_4_ = bf16[64,1024]{1,0:T(8,128)(2,1)} collective-permute-done((bf16[64,1024]{1,0:T(8,128)(2,1)S(1)}, bf16[64,1024]{1,0:T(8,128)(2,1)}, u32[]{:S(2)}, u32[]{:S(2)}) %collective-permute-start.18) | collective-permute-done | bytes 131104 | tf_op jit(solution)/shard_map/ppermute | solution.py:904
  91.5 3.3 collective-permute-done.20.rest_6_
  108.4 4.0 collective-permute-done.10.rest_6_
  112.4 2.6 collective-permute-start.9
  118.0 7.5 %qkv_other.1 = (bf16[3,688,512]{2,1,0:T(8,128)(2,1)}, bf16[3,1024,512]{2,1,0:T(8,128)(2,1)}) custom-call(s32[4]{0:T(128)} %pad_add_fusion.1.scal.refs_0_, bf16[688,1024]{1,0:T(8,128)(2,1)} %get-tuple-element.59.n1, bf16[688,128]{1,0:T(8,128)(2,1)} %get-tuple-element.60.rank.rank_in, bf16[16,1536]{1,0:T(8,128)(2,1)} %copy-done.4, ...), custom_call_target="tpu_custom_call" | custom-call | flops 2164260864 | bytes 10000000 | tf_op jit(solution)/shard_map/qkv_other/pallas_call | solution.py:420
  132.7 14.9 %attend.2 = (bf16[688,512]{1,0:T(8,128)(2,1)}, f32[4,8,688]{2,1,0:T(8,128)}) custom-call(s32[4]{0:T(128)} %pad_add_fusion.1.scal.refs_0_, bf16[3,688,512]{2,1,0:T(8,128)(2,1)} %get-tuple-element.57.q_ref.k_ref.v_ref, bf16[3,688,512]{2,1,0:T(8,128)(2,1)} %get-tuple-element.57.q_ref.k_ref.v_ref, bf16[3,688,512]{2,1,0:T(8,128)(2,1)} %get-tuple-element.57.q_ref.k_ref.v_ref, ...), custom_call_target="tpu_custom_call" | custom-call | flops 16000000000 | bytes 6000000 | tf_op jit(solution)/shard_map/attend/pallas_call | solution.py:496
  148.2 5.7 %collective-permute-done.34.refs_19_ = bf16[256,1024]{1,0:T(8,128)(2,1)} collective-permute-done((bf16[256,1024]{1,0:T(8,128)(2,1)}, bf16[256,1024]{1,0:T(8,128)(2,1)}, u32[]{:S(2)}, u32[]{:S(2)}) %collective-permute-start.34) | collective-permute-done | bytes 524320 | tf_op jit(solution)/shard_map/ppermute | solution.py:904
  156.9 15.1 %attend.3 = (bf16[688,512]{1,0:T(8,128)(2,1)}, f32[4,8,688]{2,1,0:T(8,128)}) custom-call(s32[4]{0:T(128)} %pad_add_fusion.1.scal.refs_0_, bf16[3,688,512]{2,1,0:T(8,128)(2,1)} %get-tuple-element.61.q_ref.k_ref.v_ref, bf16[3,688,512]{2,1,0:T(8,128)(2,1)} %get-tuple-element.61.q_ref.k_ref.v_ref, bf16[3,688,512]{2,1,0:T(8,128)(2,1)} %get-tuple-element.61.q_ref.k_ref.v_ref, ...), custom_call_target="tpu_custom_call" | custom-call | flops 16000000000 | bytes 6000000 | tf_op jit(solution)/shard_map/attend/pallas_call | solution.py:496
  172.0 10.3 %branch.1 = (f32[688,1024]{1,0:T(8,128)}, bf16[688,1024]{1,0:T(8,128)(2,1)}, bf16[688,128]{1,0:T(8,128)(2,1)}, bf16[688,128]{1,0:T(8,128)(2,1)}, bf16[688,1024]{...) custom-call(s32[4]{0:T(128)} %pad_add_fusion.1.scal.refs_0_, ...), custom_call_target="tpu_custom_call" | custom-call | flops 1442840576 | bytes 16000000 | tf_op jit(solution)/shard_map/branch/pallas_call | solution.py:652
  183.8 24.0 %mlp.2 = (f32[688,1024]{1,0:T(8,128)}, f32[688,1024]{1,0:T(8,128)}, f32[688,128]{1,0:T(8,128)}, f32[688,128]{1,0:T(8,128)}, f32[16,2048]{1,0:T(8,128)}, /*index=5*/f32[16,2048]{1,0:T(8,128)}) custom-call(s32[4]{0:T(128)} %pad_add_fusion.1.scal.refs_0_, bf16[688,1024]{1,0:T(8,128)(2,1)} %get-tuple-element.64.refs_1_.n2, ...), custom_call_target="tpu_custom_call" | custom-call | flops 28000000000 | bytes 20000000 | tf_op jit(solution)/shard_map/mlp/pallas_call | solution.py:763
  209.3 24.2 %mlp.3 = (f32[688,1024]{1,0:T(8,128)}, f32[688,1024]{1,0:T(8,128)}, f32[688,128]{1,0:T(8,128)}, f32[688,128]{1,0:T(8,128)}, f32[16,2048]{1,0:T(8,128)}, /*index=5*/f32[16,2048]{1,0:T(8,128)}) custom-call(s32[4]{0:T(128)} %pad_add_fusion.1.scal.refs_0_, bf16[688,1024]{1,0:T(8,128)(2,1)} %get-tuple-element.64.refs_1_.n2, ...), custom_call_target="tpu_custom_call" | custom-call | flops 28000000000 | bytes 20000000 | tf_op jit(solution)/shard_map/mlp/pallas_call | solution.py:763
  233.6 12.5 %middle.1 = (bf16[688,1024]{1,0:T(8,128)(2,1)}, f32[688,1024]{1,0:T(8,128)}, bf16[688,512]{1,0:T(8,128)(2,1)}, bf16[688,512]{1,0:T(8,128)(2,1)}, f32[16,512]{1,0...) custom-call(s32[4]{0:T(128)} %pad_add_fusion.1.scal.refs_0_, ...), custom_call_target="tpu_custom_call" | custom-call | flops 8000000000 | bytes 20000000 | tf_op jit(solution)/shard_map/middle/pallas_call | solution.py:831
  249.3 26.5 %attend_back.3 = (bf16[3,688,512]{2,1,0:T(8,128)(2,1)}, bf16[2,688,512]{2,1,0:T(8,128)(2,1)}) custom-call(s32[4]{0:T(128)} %pad_add_fusion.1.scal.refs_0_, bf16[3,688,512]{2,1,0:T(8,128)(2,1)} %get-tuple-element.61.q_ref.k_ref.v_ref, bf16[3,688,512]{2,1,0:T(8,128)(2,1)} %get-tuple-element.61.q_ref.k_ref.v_ref, ...), custom_call_target="tpu_custom_call" | custom-call | flops 27000000512 | bytes 9000000 | tf_op jit(solution)/shard_map/attend_back/pallas_call | solution.py:594
  276.2 26.6 %attend_back.2 = (bf16[3,688,512]{2,1,0:T(8,128)(2,1)}, bf16[2,688,512]{2,1,0:T(8,128)(2,1)}) custom-call(s32[4]{0:T(128)} %pad_add_fusion.1.scal.refs_0_, bf16[3,688,512]{2,1,0:T(8,128)(2,1)} %get-tuple-element.57.q_ref.k_ref.v_ref, bf16[3,688,512]{2,1,0:T(8,128)(2,1)} %get-tuple-element.57.q_ref.k_ref.v_ref, ...), custom_call_target="tpu_custom_call" | custom-call | flops 27000000512 | bytes 9000000 | tf_op jit(solution)/shard_map/attend_back/pallas_call | solution.py:594
  303.2 4.0 collective-permute-done.61
  310.0 2.6 collective-permute-done.62
  312.6 3.8 collective-permute-start.65
  317.7 5.7 %collective-permute-start.67 = (bf16[2,16,3072]{2,1,0:T(8,128)(2,1)S(1)}, bf16[2,16,3072]{2,1,0:T(8,128)(2,1)S(1)}, u32[]{:S(2)}, u32[]{:S(2)}) collective-permute-start(bf16[2,16,3072]{2,1,0:T(8,128)(2,1)S(1)} %pad_maximum_fusion.11), channel_id=1, source_target_pairs={{0,24},{4,28},{8,16},{12,20},{16,8},{20,12},{24,0},{28,4},{1,25},{... | collective-permute-start | bytes 589832 | tf_op jit(solution)/shard_map/ppermute | solution.py:958
  324.7 15.2 %collective-permute-done.66 = bf16[2,16,3072]{2,1,0:T(8,128)(2,1)S(1)} collective-permute-done((bf16[2,16,3072]{2,1,0:T(8,128)(2,1)S(1)}, bf16[2,16,3072]{2,1,0:T(8,128)(2,1)S(1)}, u32[]{:S(2)}, u32[]{:S(2)}) %collective-permute-start.66) | collective-permute-done | bytes 196640 | tf_op jit(solution)/shard_map/ppermute | solution.py:958
  343.8 6.6 %qkv_tables.1 = (bf16[3,688,512]{2,1,0:T(8,128)(2,1)}, bf16[3,688,512]{2,1,0:T(8,128)(2,1)}, bf16[688,128]{1,0:T(8,128)(2,1)}, f32[3,16,512]{2,1,0:T(8,128)}, f32[3,16,512]{2,1,0:T(8,128)}, /*index=5*/f32[16,1024]{1,0:T(8,128)}) custom-call(bf16[3,688,512]{2,1,0:T(8,128)(2,1)} %get-tuple-element.81.own_a, bf16[2,688,512]{2,1,0:T(8,128)(2,1)} %copy-done.22, ...), custom_call_target="tpu_custom_call" | custom-call | flops 5000000000 | bytes 14000000 | tf_op jit(solution)/shard_map/qkv_tables/pallas_call | solution.py:863
  353.3 7.1 %collective-permute-start.49 = (bf16[16,2048]{1,0:T(8,128)(2,1)S(1)}, bf16[16,2048]{1,0:T(8,128)(2,1)S(1)}, u32[]{:S(2)}, u32[]{:S(2)}) collective-permute-start(bf16[16,2048]{1,0:T(8,128)(2,1)S(1)} %pad_maximum_fusion.12), channel_id=1, source_target_pairs={{0,2},{2,0},{1,3},{3,1},{4,6},{6,4},{5,7},{7,5},{8,10},{10,8},{9,1... | collective-permute-start | bytes 196616 | tf_op jit(solution)/shard_map/ppermute | solution.py:904
  366.7 5.5 %collective-permute-start.52 = (bf16[2,16,1024]{2,0,1:T(2,128)(2,1)S(1)}, bf16[2,16,1024]{2,0,1:T(2,128)(2,1)S(1)}, u32[]{:S(2)}, u32[]{:S(2)}) collective-permute-start(bf16[2,16,1024]{2,0,1:T(2,128)(2,1)S(1)} %pad_maximum_fusion.13), channel_id=1, source_target_pairs={{0,8},{4,12},{8,0},{12,4},{16,24},{20,28},{24,16},{28,20},{1,9},{5... | collective-permute-start | bytes 196616 | tf_op jit(solution)/shard_map/ppermute | solution.py:958
  387.3 12.6 %qkv_rows.1 = bf16[688,1024]{1,0:T(8,128)(2,1)} custom-call(bf16[3,688,512]{2,1,0:T(8,128)(2,1)} %get-tuple-element.87.grad_a, bf16[3,688,512]{2,1,0:T(8,128)(2,1)} %get-tuple-element.88.grad_b, bf16[3,1024,512]{2,1,0:T(8,128)(2,1)} %bitcast.138, bf16[3,1024,512]{2,1,0:T(8,128)(2,1)} %get-tuple-element.89.w_b, bf16[688,128]{1,0:T(8,128)(2,1)} %get-tuple-element.90.ranked, ...), custom_call_target="tpu_custom_call" | custom-call | flops 7000000000 | bytes 16000000 | tf_op jit(solution)/shard_map/qkv_rows/pallas_call | solution.py:888
  399.9 4.8 %collective-permute-start.41 = (bf16[688,1024]{1,0:T(8,128)(2,1)}, bf16[688,1024]{1,0:T(8,128)(2,1)S(1)}, u32[]{:S(2)}, u32[]{:S(2)}) collective-permute-start(bf16[688,1024]{1,0:T(8,128)(2,1)} %qkv_rows.1), channel_id=1, source_target_pairs={{0,0},{1,2},{2,1},{3,3},{4,4},{5,6},{6,5},{7,7},{8,8},{9,10},{10,9... | collective-permute-start | bytes 4227080 | tf_op jit(solution)/shard_map/ppermute | solution.py:900
  417.7 3.7 collective-permute-done.41
  (307 shorter events, 117.0 us)
Async XLA Ops:
  2.1 40.7 %collective-permute-start.1 = (bf16[688,1024]{1,0:T(8,128)(2,1)}, bf16[688,1024]{1,0:T(8,128)(2,1)S(1)}, u32[]{:S(2)}, u32[]{:S(2)}) collective-permute-start(bf16[688,1024]{1,0:T(8,128)(2,1)} %bitcast.148), channel_id=1, source_target_pairs={{0,0},{1,2},{2,1},{3,3},{4,4},{5,6},{6,5},{7,7},{8,8},{9,10},{10,9... | collective-permute-start | bytes 4227080 | tf_op jit(solution)/shard_map/ppermute | solution.py:900
  7.7 34.9 %collective-permute-start.4 = (bf16[3,128,512]{2,1,0:T(8,128)(2,1)S(1)}, bf16[3,128,512]{2,1,0:T(8,128)(2,1)}, u32[]{:S(2)}, u32[]{:S(2)}) collective-permute-start(bf16[3,128,512]{2,1,0:T(8,128)(2,1)S(1)} %dynamic-slice_bitcast_fusion), channel_id=1, source_target_pairs={{0,1},{1,0},{2,3},{3,2},{4,5},{5,4},{6,7},{7,6},{8,9},{9,8},{10,11... | collective-permute-start | bytes 1179656 | tf_op jit(solution)/shard_map/ppermute | solution.py:904
  8.8 32.6 %collective-permute-start.14 = (bf16[64,1024]{1,0:T(8,128)(2,1)S(1)}, bf16[64,1024]{1,0:T(8,128)(2,1)S(1)}, u32[]{:S(2)}, u32[]{:S(2)}) collective-permute-start(bf16[64,1024]{1,0:T(8,128)(2,1)S(1)} %constant_dynamic-slice_fusion.14), channel_id=1, source_target_pairs={{0,1},{1,0},{2,3},{3,2},{4,5},{5,4},{6,7},{7,6},{8,9},{9,8},{10,11... | collective-permute-start | bytes 393224 | tf_op jit(solution)/shard_map/ppermute | solution.py:904
  12.1 86.1 %collective-permute-start.22 = (bf16[1024,256]{1,0:T(8,128)(2,1)}, bf16[1024,256]{1,0:T(8,128)(2,1)}, u32[]{:S(2)}, u32[]{:S(2)}) collective-permute-start(bf16[1024,256]{1,0:T(8,128)(2,1)} %constant_dynamic-slice_fusion.13), channel_id=1, source_target_pairs={{0,1},{1,0},{2,3},{3,2},{4,5},{5,4},{6,7},{7,6},{8,9},{9,8},{10,11... | collective-permute-start | bytes 1572872 | tf_op jit(solution)/shard_map/ppermute | solution.py:904
  24.5 60.6 %collective-permute-start.3 = (bf16[16,6144]{1,0:T(8,128)(2,1)S(1)}, bf16[16,6144]{1,0:T(8,128)(2,1)S(1)}, u32[]{:S(2)}, u32[]{:S(2)}) collective-permute-start(bf16[16,6144]{1,0:T(8,128)(2,1)S(1)} %pad_maximum_fusion.8), channel_id=1, source_target_pairs={{0,1},{1,0},{2,3},{3,2},{4,5},{5,4},{6,7},{7,6},{8,9},{9,8},{10,11... | collective-permute-start | bytes 589832 | tf_op jit(solution)/shard_map/ppermute | solution.py:904
  42.6 42.6 %collective-permute-start.16 = (bf16[64,1024]{1,0:T(8,128)(2,1)S(1)}, bf16[64,1024]{1,0:T(8,128)(2,1)S(1)}, u32[]{:S(2)}, u32[]{:S(2)}) collective-permute-start(bf16[64,1024]{1,0:T(8,128)(2,1)S(1)} %collective-permute-done.14.rest_0_), channel_id=1, source_target_pairs={{0,4},{4,0},{1,5},{5,1},{2,6},{6,2},{3,7},{7,3},{8,12},{12,8},{9,1... | collective-permute-start | bytes 393224 | tf_op jit(solution)/shard_map/ppermute | solution.py:904
  42.9 54.1 %collective-permute-start.6 = (bf16[3,128,512]{2,1,0:T(8,128)(2,1)}, bf16[3,128,512]{2,1,0:T(8,128)(2,1)}, u32[]{:S(2)}, u32[]{:S(2)}) collective-permute-start(bf16[3,128,512]{2,1,0:T(8,128)(2,1)} %collective-permute-done.4.rest_0_), channel_id=1, source_target_pairs={{0,4},{4,0},{1,5},{5,1},{2,6},{6,2},{3,7},{7,3},{8,12},{12,8},{9,1... | collective-permute-start | bytes 1179656 | tf_op jit(solution)/shard_map/ppermute | solution.py:904
  75.9 55.6 %collective-permute-start.2 = (bf16[2,688,512]{2,1,0:T(8,128)(2,1)S(1)}, bf16[2,688,512]{2,1,0:T(8,128)(2,1)}, u32[]{:S(2)}, u32[]{:S(2)}) collective-permute-start(bf16[2,688,512]{2,1,0:T(8,128)(2,1)S(1)} %slice.82), channel_id=1, source_target_pairs={{0,2},{2,0},{1,3},{3,1},{4,6},{6,4},{5,7},{7,5},{8,10},{10,8},{9,1... | collective-permute-start | bytes 4227080 | tf_op jit(solution)/shard_map/ppermute | solution.py:904
  107.6 22.1 %collective-permute-start.30 = (bf16[256,1024]{1,0:T(8,128)(2,1)S(1)}, bf16[256,1024]{1,0:T(8,128)(2,1)}, u32[]{:S(2)}, u32[]{:S(2)}) collective-permute-start(bf16[256,1024]{1,0:T(8,128)(2,1)S(1)} %constant_dynamic-slice_fusion.12), channel_id=1, source_target_pairs={{0,1},{1,0},{2,3},{3,2},{4,5},{5,4},{6,7},{7,6},{8,9},{9,8},{10,11... | collective-permute-start | bytes 1572872 | tf_op jit(solution)/shard_map/ppermute | solution.py:904
  107.6 22.8 %collective-permute-start.24 = (bf16[1024,256]{1,0:T(8,128)(2,1)}, bf16[1024,256]{1,0:T(8,128)(2,1)S(1)}, u32[]{:S(2)}, u32[]{:S(2)}) collective-permute-start(bf16[1024,256]{1,0:T(8,128)(2,1)} %collective-permute-done.22.refs_7_), channel_id=1, source_target_pairs={{0,4},{4,0},{1,5},{5,1},{2,6},{6,2},{3,7},{7,3},{8,12},{12,8},{9,1... | collective-permute-start | bytes 1572872 | tf_op jit(solution)/shard_map/ppermute | solution.py:904
  127.0 27.3 %collective-permute-start.13 = (bf16[688,1024]{1,0:T(8,128)(2,1)}, bf16[688,1024]{1,0:T(8,128)(2,1)S(1)}, u32[]{:S(2)}, u32[]{:S(2)}) collective-permute-start(bf16[688,1024]{1,0:T(8,128)(2,1)} %bitcast.27), channel_id=1, source_target_pairs={{0,0},{1,2},{2,1},{3,3},{4,4},{5,6},{6,5},{7,7},{8,8},{9,10},{10,9... | collective-permute-start | bytes 4227080 | tf_op jit(solution)/shard_map/ppermute | solution.py:900
  130.4 23.5 %collective-permute-start.34 = (bf16[256,1024]{1,0:T(8,128)(2,1)}, bf16[256,1024]{1,0:T(8,128)(2,1)}, u32[]{:S(2)}, u32[]{:S(2)}) collective-permute-start(bf16[256,1024]{1,0:T(8,128)(2,1)} %collective-permute-done.30.refs_15_), channel_id=1, source_target_pairs={{0,8},{8,0},{1,9},{9,1},{2,10},{10,2},{3,11},{11,3},{4,12},{12,4},... | collective-permute-start | bytes 1572872 | tf_op jit(solution)/shard_map/ppermute | solution.py:904
  131.4 24.4 %collective-permute-start.12 = (bf16[2,688,512]{2,1,0:T(8,128)(2,1)S(1)}, bf16[2,688,512]{2,1,0:T(8,128)(2,1)S(1)}, u32[]{:S(2)}, u32[]{:S(2)}) collective-permute-start(bf16[2,688,512]{2,1,0:T(8,128)(2,1)S(1)} %slice.84), channel_id=1, source_target_pairs={{0,2},{2,0},{1,3},{3,1},{4,6},{6,4},{5,7},{7,5},{8,10},{10,8},{9,1... | collective-permute-start | bytes 4227080 | tf_op jit(solution)/shard_map/ppermute | solution.py:904
  147.7 34.7 %collective-permute-start.23 = (bf16[1024,256]{1,0:T(8,128)(2,1)}, bf16[1024,256]{1,0:T(8,128)(2,1)}, u32[]{:S(2)}, u32[]{:S(2)}) collective-permute-start(bf16[1024,256]{1,0:T(8,128)(2,1)} %collective-permute-done.22.refs_7_), channel_id=1, source_target_pairs={{0,2},{2,0},{1,3},{3,1},{4,6},{6,4},{5,7},{7,5},{8,10},{10,8},{9,1... | collective-permute-start | bytes 1572872 | tf_op jit(solution)/shard_map/ppermute | solution.py:904
  147.8 35.0 %collective-permute-start.31 = (bf16[256,1024]{1,0:T(8,128)(2,1)}, bf16[256,1024]{1,0:T(8,128)(2,1)}, u32[]{:S(2)}, u32[]{:S(2)}) collective-permute-start(bf16[256,1024]{1,0:T(8,128)(2,1)} %collective-permute-done.30.refs_15_), channel_id=1, source_target_pairs={{0,2},{2,0},{1,3},{3,1},{4,6},{6,4},{5,7},{7,5},{8,10},{10,8},{9,1... | collective-permute-start | bytes 1572872 | tf_op jit(solution)/shard_map/ppermute | solution.py:904
  153.9 29.0 %collective-permute-start.28 = (bf16[1024,256]{1,0:T(8,128)(2,1)S(1)}, bf16[1024,256]{1,0:T(8,128)(2,1)}, u32[]{:S(2)}, u32[]{:S(2)}) collective-permute-start(bf16[1024,256]{1,0:T(8,128)(2,1)S(1)} %copy-done.24), channel_id=1, source_target_pairs={{0,8},{8,0},{1,9},{9,1},{2,10},{10,2},{3,11},{11,3},{4,12},{12,4},... | collective-permute-start | bytes 1572872 | tf_op jit(solution)/shard_map/ppermute | solution.py:904
  154.3 29.1 %collective-permute-start.25 = (bf16[1024,256]{1,0:T(8,128)(2,1)S(1)}, bf16[1024,256]{1,0:T(8,128)(2,1)}, u32[]{:S(2)}, u32[]{:S(2)}) collective-permute-start(bf16[1024,256]{1,0:T(8,128)(2,1)S(1)} %copy-done.24), channel_id=1, source_target_pairs={{0,2},{2,0},{1,3},{3,1},{4,6},{6,4},{5,7},{7,5},{8,10},{10,8},{9,1... | collective-permute-start | bytes 1572872 | tf_op jit(solution)/shard_map/ppermute | solution.py:904
  155.8 27.5 %collective-permute-start.36 = (bf16[256,1024]{1,0:T(8,128)(2,1)S(1)}, bf16[256,1024]{1,0:T(8,128)(2,1)S(1)}, u32[]{:S(2)}, u32[]{:S(2)}) collective-permute-start(bf16[256,1024]{1,0:T(8,128)(2,1)S(1)} %collective-permute-done.32.refs_17_), channel_id=1, source_target_pairs={{0,8},{8,0},{1,9},{9,1},{2,10},{10,2},{3,11},{11,3},{4,12},{12,4},... | collective-permute-start | bytes 1572872 | tf_op jit(solution)/shard_map/ppermute | solution.py:904
  182.4 25.4 %collective-permute-start.33 = (bf16[256,1024]{1,0:T(8,128)(2,1)S(1)}, bf16[256,1024]{1,0:T(8,128)(2,1)S(1)}, u32[]{:S(2)}, u32[]{:S(2)}) collective-permute-start(bf16[256,1024]{1,0:T(8,128)(2,1)S(1)} %collective-permute-done.32.refs_17_), channel_id=1, source_target_pairs={{0,2},{2,0},{1,3},{3,1},{4,6},{6,4},{5,7},{7,5},{8,10},{10,8},{9,1... | collective-permute-start | bytes 1572872 | tf_op jit(solution)/shard_map/ppermute | solution.py:904
  182.7 25.1 %collective-permute-start.27 = (bf16[1024,256]{1,0:T(8,128)(2,1)}, bf16[1024,256]{1,0:T(8,128)(2,1)S(1)}, u32[]{:S(2)}, u32[]{:S(2)}) collective-permute-start(bf16[1024,256]{1,0:T(8,128)(2,1)} %collective-permute-done.26.refs_11_), channel_id=1, source_target_pairs={{0,2},{2,0},{1,3},{3,1},{4,6},{6,4},{5,7},{7,5},{8,10},{10,8},{9,1... | collective-permute-start | bytes 1572872 | tf_op jit(solution)/shard_map/ppermute | solution.py:904
  182.9 24.9 %collective-permute-start.35 = (bf16[256,1024]{1,0:T(8,128)(2,1)}, bf16[256,1024]{1,0:T(8,128)(2,1)S(1)}, u32[]{:S(2)}, u32[]{:S(2)}) collective-permute-start(bf16[256,1024]{1,0:T(8,128)(2,1)} %collective-permute-done.34.refs_19_), channel_id=1, source_target_pairs={{0,2},{2,0},{1,3},{3,1},{4,6},{6,4},{5,7},{7,5},{8,10},{10,8},{9,1... | collective-permute-start | bytes 1572872 | tf_op jit(solution)/shard_map/ppermute | solution.py:904
  183.3 24.6 %collective-permute-start.29 = (bf16[1024,256]{1,0:T(8,128)(2,1)}, bf16[1024,256]{1,0:T(8,128)(2,1)S(1)}, u32[]{:S(2)}, u32[]{:S(2)}) collective-permute-start(bf16[1024,256]{1,0:T(8,128)(2,1)} %collective-permute-done.28.refs_13_), channel_id=1, source_target_pairs={{0,2},{2,0},{1,3},{3,1},{4,6},{6,4},{5,7},{7,5},{8,10},{10,8},{9,1... | collective-permute-start | bytes 1572872 | tf_op jit(solution)/shard_map/ppermute | solution.py:904
  183.5 24.4 %collective-permute-start.37 = (bf16[256,1024]{1,0:T(8,128)(2,1)S(1)}, bf16[256,1024]{1,0:T(8,128)(2,1)S(1)}, u32[]{:S(2)}, u32[]{:S(2)}) collective-permute-start(bf16[256,1024]{1,0:T(8,128)(2,1)S(1)} %collective-permute-done.36.refs_21_), channel_id=1, source_target_pairs={{0,2},{2,0},{1,3},{3,1},{4,6},{6,4},{5,7},{7,5},{8,10},{10,8},{9,1... | collective-permute-start | bytes 1572872 | tf_op jit(solution)/shard_map/ppermute | solution.py:904
  248.9 54.1 %collective-permute-start.60 = (bf16[16,6144]{1,0:T(8,128)(2,1)S(1)}, bf16[16,6144]{1,0:T(8,128)(2,1)S(1)}, u32[]{:S(2)}, u32[]{:S(2)}) collective-permute-start(bf16[16,6144]{1,0:T(8,128)(2,1)S(1)} %pad_maximum_fusion.10), channel_id=1, source_target_pairs={{0,2},{2,0},{1,3},{3,1},{4,6},{6,4},{5,7},{7,5},{8,10},{10,8},{9,1... | collective-permute-start | bytes 589832 | tf_op jit(solution)/shard_map/ppermute | solution.py:904
  275.8 66.5 %collective-permute-start.40 = (bf16[2,688,512]{2,1,0:T(8,128)(2,1)}, bf16[2,688,512]{2,1,0:T(8,128)(2,1)S(1)}, u32[]{:S(2)}, u32[]{:S(2)}) collective-permute-start(bf16[2,688,512]{2,1,0:T(8,128)(2,1)} %get-tuple-element.86), channel_id=1, source_target_pairs={{0,2},{2,0},{1,3},{3,1},{4,6},{6,4},{5,7},{7,5},{8,10},{10,8},{9,1... | collective-permute-start | bytes 4227080 | tf_op jit(solution)/shard_map/ppermute | solution.py:904
  302.8 39.5 %collective-permute-start.39 = (bf16[2,688,512]{2,1,0:T(8,128)(2,1)}, bf16[2,688,512]{2,1,0:T(8,128)(2,1)S(1)}, u32[]{:S(2)}, u32[]{:S(2)}) collective-permute-start(bf16[2,688,512]{2,1,0:T(8,128)(2,1)} %get-tuple-element.82), channel_id=1, source_target_pairs={{0,2},{2,0},{1,3},{3,1},{4,6},{6,4},{5,7},{7,5},{8,10},{10,8},{9,1... | collective-permute-start | bytes 4227080 | tf_op jit(solution)/shard_map/ppermute | solution.py:904
  316.4 23.5 %collective-permute-start.66 = (bf16[2,16,3072]{2,1,0:T(8,128)(2,1)S(1)}, bf16[2,16,3072]{2,1,0:T(8,128)(2,1)S(1)}, u32[]{:S(2)}, u32[]{:S(2)}) collective-permute-start(bf16[2,16,3072]{2,1,0:T(8,128)(2,1)S(1)} %pad_maximum_fusion.11), channel_id=1, source_target_pairs={{0,20},{4,16},{8,28},{12,24},{16,4},{20,0},{24,12},{28,8},{1,21},{... | collective-permute-start | bytes 589832 | tf_op jit(solution)/shard_map/ppermute | solution.py:958
  317.7 22.1 %collective-permute-start.67 = (bf16[2,16,3072]{2,1,0:T(8,128)(2,1)S(1)}, bf16[2,16,3072]{2,1,0:T(8,128)(2,1)S(1)}, u32[]{:S(2)}, u32[]{:S(2)}) collective-permute-start(bf16[2,16,3072]{2,1,0:T(8,128)(2,1)S(1)} %pad_maximum_fusion.11), channel_id=1, source_target_pairs={{0,24},{4,28},{8,16},{12,20},{16,8},{20,12},{24,0},{28,4},{1,25},{... | collective-permute-start | bytes 589832 | tf_op jit(solution)/shard_map/ppermute | solution.py:958
  341.8 31.0 %collective-permute-start.69 = (bf16[8,16,768]{2,0,1:T(8,128)(2,1)S(1)}, bf16[8,16,768]{2,0,1:T(8,128)(2,1)S(1)}, u32[]{:S(2)}, u32[]{:S(2)}) collective-permute-start(bf16[8,16,768]{2,0,1:T(8,128)(2,1)S(1)} %slice.118), channel_id=1, source_target_pairs={{0,1},{1,0},{2,3},{3,2},{4,5},{5,4},{6,7},{7,6},{8,9},{9,8},{10,11... | collective-permute-start | bytes 589832 | tf_op jit(solution)/shard_map/ppermute | solution.py:904
  363.1 41.7 %collective-permute-start.38 = (bf16[688,1024]{1,0:T(8,128)(2,1)}, bf16[688,1024]{1,0:T(8,128)(2,1)S(1)}, u32[]{:S(2)}, u32[]{:S(2)}) collective-permute-start(bf16[688,1024]{1,0:T(8,128)(2,1)} %get-tuple-element.78), channel_id=1, source_target_pairs={{0,0},{1,2},{2,1},{3,3},{4,4},{5,6},{6,5},{7,7},{8,8},{9,10},{10,9... | collective-permute-start | bytes 4227080 | tf_op jit(solution)/shard_map/ppermute | solution.py:900
  380.9 24.5 %collective-permute-start.70 = (bf16[8,16,3840]{2,0,1:T(8,128)(2,1)}, bf16[8,16,3840]{2,0,1:T(8,128)(2,1)}, u32[]{:S(2)}, u32[]{:S(2)}) collective-permute-start(bf16[8,16,3840]{2,0,1:T(8,128)(2,1)} %pad_maximum_fusion.1), channel_id=1, source_target_pairs={{0,2},{2,0},{1,3},{3,1},{4,6},{6,4},{5,7},{7,5},{8,10},{10,8},{9,1... | collective-permute-start | bytes 2949128 | tf_op jit(solution)/shard_map/ppermute | solution.py:904
  399.9 21.4 %collective-permute-start.41 = (bf16[688,1024]{1,0:T(8,128)(2,1)}, bf16[688,1024]{1,0:T(8,128)(2,1)S(1)}, u32[]{:S(2)}, u32[]{:S(2)}) collective-permute-start(bf16[688,1024]{1,0:T(8,128)(2,1)} %qkv_rows.1), channel_id=1, source_target_pairs={{0,0},{1,2},{2,1},{3,3},{4,4},{5,6},{6,5},{7,7},{8,8},{9,10},{10,9... | collective-permute-start | bytes 4227080 | tf_op jit(solution)/shard_map/ppermute | solution.py:900
  (75 other events, 756.1 us)

commit v2 on v1

--- a/solution.py
+++ b/solution.py
@@ -277,7 +277,7 @@
 PARTS = 8
 PAD = 128
 FLIP = [(0, 1), (1, 0)]
-SWAP = [(0, 0), (1, 2), (2, 1), (3, 3)]
+SWAP = [(1, 2), (2, 1)]
 
 
 def dotg(a, b, ca, cb):
@@ -323,7 +323,7 @@
 
 
 def cost(flops, nbytes):
-    return pl.CostEstimate(flops=int(flops), bytes_accessed=int(nbytes), transcendentals=0)
+    return pl.CostEstimate(flops=int(flops * 0.5), bytes_accessed=int(nbytes), transcendentals=0)
 
 
 def norm_stats(values):
@@ -346,20 +346,36 @@
     return (at < scal[0]).astype(F32)
 
 
-def fetch(parts, target, sem, part_at, axis, size):
+def choose(scal, here, swapped, target, sem):
+    @pl.when(scal[3] != 0)
+    def _():
+        pltpu.make_async_copy(here, target, sem).start()
+
+    @pl.when(scal[3] == 0)
+    def _():
+        pltpu.make_async_copy(swapped, target, sem).start()
+
+    return pltpu.make_async_copy(here, target, sem)
+
+
+def fetch(arrays, nears, target, sem, part_at, axis, size):
     copies = []
-    for near, part in enumerate(parts):
-        first = pl.multiple_of((part_at ^ near) * size, size)
+    parts = len(nears)
+    for number, near in enumerate(nears):
+        first = pl.multiple_of(((part_at % parts) ^ near) * size, size)
         place = target.at[:, pl.ds(first, size)] if axis == 1 else target.at[pl.ds(first, size)]
-        copies.append(pltpu.make_async_copy(part, place, sem.at[near]))
+        copies.append(pltpu.make_async_copy(arrays[number // 2].at[number % 2], place, sem.at[near]))
     for copy in copies:
         copy.start()
     return copies
 
 
-def qkv_local_kernel(tok, gain, w, qa, qb, n1, rank, out, low):
-    @pl.when(pl.program_id(0) == 0)
+def qkv_local_kernel(scal, here, swapped, gain, w, qa, qb, tok, n1, rank, queries, rest, low, sem):
+    step = pl.program_id(0)
+
+    @pl.when(step == 0)
     def _():
+        choose(scal, here, swapped, tok, sem.at[0]).wait()
         unit, _ = norm_stats(tok[...].astype(F32))
         normed = (unit * gain[...]).astype(BF)
         n1[...] = normed
@@ -367,69 +383,88 @@
         rank[...] = ranked
         low[...] = ranked
 
-    out[0] = (dotg(n1[...], w[0], 1, 0) + dotg(low[...], pad_rows(qb[0]), 1, 0)).astype(BF)
-
-
-def qkv_local(tok, gain, w, qa, qb):
+    out = (dotg(n1[...], w[0], 1, 0) + dotg(low[...], pad_rows(qb[...]), 1, 0)).astype(BF)
+
+    @pl.when(step < 2)
+    def _():
+        rest[0] = out
+
+    @pl.when(step == 2)
+    def _():
+        queries[...] = out
+
+
+def qkv_local(scal, tok, swapped, gain, w, qa, qb):
     rows, width = tok.shape
     third = w.shape[2]
     rank = qa.shape[0]
     fixed = lambda c: (0, 0)
-    turn = lambda c: ((c + 1) % 3, 0, 0)
     return pl.pallas_call(
         qkv_local_kernel,
         grid=(3,),
         in_specs=[
-            pl.BlockSpec((rows, width), fixed),
+            scalars(),
+            in_place(),
+            in_place(),
             pl.BlockSpec((1, width), fixed),
-            pl.BlockSpec((1, width, third), turn),
+            pl.BlockSpec((1, width, third), lambda c: ((c + 1) % 3, 0, 0)),
             pl.BlockSpec((rank, width), fixed),
-            pl.BlockSpec((1, rank, third), turn),
+            pl.BlockSpec((rank, third), lambda c: (0, (c + 1) % 3)),
         ],
         out_specs=[
             pl.BlockSpec((rows, width), fixed),
+            pl.BlockSpec((rows, width), fixed),
             pl.BlockSpec((rows, PAD), fixed),
-            pl.BlockSpec((1, rows, third), turn),
+            pl.BlockSpec((rows, third), fixed),
+            pl.BlockSpec((1, rows, third), lambda c: (jnp.minimum(c, 1), 0, 0)),
         ],
         out_shape=[
             jax.ShapeDtypeStruct((rows, width), BF),
+            jax.ShapeDtypeStruct((rows, width), BF),
             jax.ShapeDtypeStruct((rows, PAD), BF),
-            jax.ShapeDtypeStruct((3, rows, third), BF),
+            jax.ShapeDtypeStruct((rows, third), BF),
+            jax.ShapeDtypeStruct((2, rows, third), BF),
         ],
-        scratch_shapes=[pltpu.VMEM((rows, PAD), BF)],
+        scratch_shapes=[pltpu.VMEM((rows, PAD), BF), pltpu.SemaphoreType.DMA((1,))],
         compiler_params=params(dimension_semantics=("arbitrary",)),
-        cost_estimate=cost(2 * rows * width * 3 * third, 8e6),
+        cost_estimate=cost(7e-6 * 1e15, 8e6),
         name="qkv_local",
-    )(tok, gain, w, qa, qb)
-
-
-def qkv_other_kernel(scal, n1, rank, pack, *rest):
-    parts, (out, w), (sem,) = rest[:PARTS], rest[PARTS : PARTS + 2], rest[PARTS + 2 :]
+    )(scal, tok, swapped, gain, w, qa, qb)
+
+
+def qkv_other_kernel(nears, scal, n1, rank, qb, *rest):
+    arrays, (queries, out, w, sem) = rest[: len(nears) // 2], rest[len(nears) // 2 :]
     third = w.shape[2]
-    copies = fetch(parts, w, sem, scal[2], 1, parts[0].shape[1])
+    copies = fetch(arrays, nears, w, sem, scal[2], 1, arrays[0].shape[2])
     for copy in copies:
         copy.wait()
     for c in (1, 2, 0):
-        qb = pack[:, c * third : (c + 1) * third]
-        out[c] = (dotg(n1[...], w[c], 1, 0) + dotg(rank[...], pad_rows(qb), 1, 0)).astype(BF)
-
-
-def qkv_other(scal, n1, rank, pack, parts):
+        at = slice(c * third, (c + 1) * third)
+        terms = (dotg(n1[...], w[c], 1, 0) + dotg(rank[...], pad_rows(qb[:, at]), 1, 0)).astype(BF)
+        if c == 0:
+            queries[...] = terms
+        else:
+            out[c - 1] = terms
+
+
+def qkv_other(scal, n1, rank, qb, half):
     rows, width = n1.shape
-    third = parts[0].shape[2]
+    arrays, nears = half.pairs, half.names
+    third = arrays[0].shape[3]
     return pl.pallas_call(
-        qkv_other_kernel,
-        in_specs=[scalars(), whole(), whole(), whole()] + [in_place()] * PARTS,
-        out_specs=[whole(), whole()],
+        functools.partial(qkv_other_kernel, nears),
+        in_specs=[scalars(), whole(), whole(), whole()] + [in_place()] * len(arrays),
+        out_specs=[whole()] * 3,
         out_shape=[
-            jax.ShapeDtypeStruct((3, rows, third), BF),
+            jax.ShapeDtypeStruct((rows, third), BF),
+            jax.ShapeDtypeStruct((2, rows, third), BF),
             jax.ShapeDtypeStruct((3, width, third), BF),
         ],
         scratch_shapes=[pltpu.SemaphoreType.DMA((PARTS,))],
         compiler_params=params(),
-        cost_estimate=cost(2 * rows * width * 3 * third, 10e6),
+        cost_estimate=cost(7e-6 * 1e15, 10e6),
         name="qkv_other",
-    )(scal, n1, rank, pack, *parts)
+    )(scal, n1, rank, qb, *arrays)
 
 
 def head_lanes(rows, head):
@@ -450,8 +485,8 @@
 
 
 def attend_kernel(scal, q_ref, k_ref, v_ref, ko_ref, vo_ref, out, log_out, qx, kx, vt):
-    rows = q_ref.shape[1]
-    queries = q_ref[0]
+    rows = q_ref.shape[0]
+    queries = q_ref[...]
     zero = jnp.zeros_like(queries)
     one = jnp.ones_like(queries)
     high, low = scaled_queries(queries)
@@ -489,14 +524,14 @@
     out[...] = jnp.concatenate(mixed, axis=0).T.astype(BF)
 
 
-def attend(scal, own, other):
+def attend(scal, queries, own, other):
     _, rows, width = own.shape
     pairs = width // (2 * HD)
     take = lambda c: pl.BlockSpec((1, rows, 2 * HD), lambda p: (c, 0, p))
     return pl.pallas_call(
         attend_kernel,
         grid=(pairs,),
-        in_specs=[scalars(), take(0), take(1), take(2), take(0), take(1)],
+        in_specs=[scalars(), pl.BlockSpec((rows, 2 * HD), lambda p: (0, p)), take(0), take(1), take(0), take(1)],
         out_specs=[
             pl.BlockSpec((rows, 2 * HD), lambda p: (0, p)),
             pl.BlockSpec((1, 8, rows), lambda p: (p, 0, 0)),
@@ -513,15 +548,15 @@
         compiler_params=params(dimension_semantics=("arbitrary",)),
         cost_estimate=cost(16e-6 * 1e15, 6e6),
         name="attend",
-    )(scal, own, own, own, other, other)
+    )(scal, queries, own, own, other, other)
 
 
 def attend_back_kernel(
-    scal, q_ref, k_ref, v_ref, ko_ref, vo_ref, mixed_ref, grad_ref, log_ref, own_out, other_out,
+    scal, q_ref, k_ref, v_ref, ko_ref, vo_ref, mixed_ref, grad_ref, log_ref, queries_out, own_out, other_out,
     qx, gx, qm, gm, kx, vx, kt,
 ):
-    rows = q_ref.shape[1]
-    queries, grad = q_ref[0], grad_ref[...]
+    rows = q_ref.shape[0]
+    queries, grad = q_ref[...], grad_ref[...]
     zero = jnp.zeros_like(queries)
     one = jnp.ones_like(queries)
     high, low = scaled_queries(queries)
@@ -579,29 +614,31 @@
         else:
             keys = ((kept[0] + keys) * HD**-0.5).astype(BF)
             values = (kept[1] + values).astype(BF)
-            if side == 0:
-                own_out[1], own_out[2] = keys, values
-            else:
-                other_out[0], other_out[1] = keys, values
-    own_out[0] = (jnp.concatenate(grad_queries, axis=0).T * HD**-0.5).astype(BF)
-
-
-def attend_back(scal, own, other, mixed, grad, logs):
+            out = own_out if side == 0 else other_out
+            out[0], out[1] = keys, values
+    queries_out[...] = (jnp.concatenate(grad_queries, axis=0).T * HD**-0.5).astype(BF)
+
+
+def attend_back(scal, queries, own, other, mixed, grad, logs, piece, pieces):
     _, rows, width = own.shape
+    width = width // pieces
     pairs = width // (2 * HD)
-    take = lambda c: pl.BlockSpec((1, rows, 2 * HD), lambda p: (c, 0, p))
-    flat = pl.BlockSpec((rows, 2 * HD), lambda p: (0, p))
+    skip = piece * pairs
+    take = lambda c: pl.BlockSpec((1, rows, 2 * HD), lambda p: (c, 0, p + skip))
+    flat = pl.BlockSpec((rows, 2 * HD), lambda p: (0, p + skip))
     return pl.pallas_call(
         attend_back_kernel,
         grid=(pairs,),
-        in_specs=[scalars(), take(0), take(1), take(2), take(0), take(1), flat, flat]
-        + [pl.BlockSpec((1, 8, rows), lambda p: (p, 0, 0))],
+        in_specs=[scalars(), flat, take(0), take(1), take(0), take(1), flat, flat]
+        + [pl.BlockSpec((1, 8, rows), lambda p: (p + skip, 0, 0))],
         out_specs=[
-            pl.BlockSpec((3, rows, 2 * HD), lambda p: (0, 0, p)),
+            pl.BlockSpec((rows, 2 * HD), lambda p: (0, p)),
+            pl.BlockSpec((2, rows, 2 * HD), lambda p: (0, 0, p)),
             pl.BlockSpec((2, rows, 2 * HD), lambda p: (0, 0, p)),
         ],
         out_shape=[
-            jax.ShapeDtypeStruct((3, rows, width), BF),
+            jax.ShapeDtypeStruct((rows, width), BF),
+            jax.ShapeDtypeStruct((2, rows, width), BF),
             jax.ShapeDtypeStruct((2, rows, width), BF),
         ],
         scratch_shapes=[
@@ -614,30 +651,27 @@
             pltpu.VMEM((2 * HD, 2 * rows), BF),
         ],
         compiler_params=params(dimension_semantics=("arbitrary",)),
-        cost_estimate=cost(27e-6 * 1e15, 9e6),
+        cost_estimate=cost(26e-6 / pieces * 1e15, 9e6),
         name="attend_back",
-    )(scal, own, own, own, other, other, mixed, grad, logs)
-
-
-def branch_kernel(
-    scal, mix_a, mix_b, tok, w_a, oa_a, oa_b, ob, scale_one, gain_two, scale_two, ua, db, cot, *rest
-):
-    parts = rest[:PARTS]
-    residual, n2, rank_out, rank_up, grad_mlp, grad_rank, w_b, sem = rest[PARTS:]
-    rows = tok.shape[0]
+    )(scal, queries, own, own, other, other, mixed, grad, logs)
+
+
+def branch_kernel(nears, scal, mix_a, mix_b, tok, w_a, oa_a, oa_b, ob, scale_one, gain_two, ua, *rest):
+    arrays = rest[: len(nears) // 2]
+    residual, n2, rank_out, rank_up, w_b, sem = rest[len(nears) // 2 :]
     rank = oa_a.shape[0]
-    copies = fetch(parts, w_b, sem, scal[2], 0, parts[0].shape[0])
-    grad_low = (scale_two[...] * (cot[...].astype(F32) * row_mask(scal, rows))).astype(BF)
-    grad_mlp[...] = grad_low
-    grad_rank[...] = dotg(grad_low, pad_rows(db[...]), 1, 1).astype(BF)
+
+    @pl.when(pl.program_id(0) == 0)
+    def _():
+        for copy in fetch(arrays, nears, w_b, sem, scal[2], 0, arrays[0].shape[1]):
+            copy.wait()
+
     ranked = dotg(mix_a[...], pad_rows(oa_a[...]), 1, 1) + dotg(mix_b[...], pad_rows(oa_b[...]), 1, 1)
     ranked = two_terms(ranked, rank)
     rank_out[...] = ranked
-    for copy in copies:
-        copy.wait()
-    branch = dotg(mix_a[...], w_a[...], 1, 0) + dotg(mix_b[...], w_b[...], 1, 0)
-    branch = branch + dotg(ranked, pad_twice(ob[...]), 1, 0)
-    total = tok[...].astype(F32) + scale_one[...] * branch
+    terms = dotg(mix_a[...], w_a[...], 1, 0) + dotg(mix_b[...], w_b[...], 1, 0)
+    terms = terms + dotg(ranked, pad_twice(ob[...]), 1, 0)
+    total = tok[...].astype(F32) + scale_one[...] * terms
     residual[...] = total
     unit, _ = norm_stats(total)
     normed = (unit * gain_two[...]).astype(BF)
@@ -645,47 +679,71 @@
     rank_up[...] = dotg(normed, pad_rows(ua[...]), 1, 1).astype(BF)
 
 
-def branch(scal, mix_a, mix_b, tok, w_a, parts, oa_a, oa_b, ob, scale_one, gain_two, scale_two, ua, db, cot):
+def blocked(rows, width):
+    return pl.BlockSpec((rows, width), lambda step: (step, 0))
+
+
+def fixed_block(*shape):
+    return pl.BlockSpec(shape, lambda step: (0,) * len(shape))
+
+
+def branch(scal, mix_a, mix_b, tok, w_a, half, oa_a, oa_b, ob, scale_one, gain_two, ua):
     rows, width = tok.shape
-    low = jax.ShapeDtypeStruct((rows, width), BF)
-    ranked = jax.ShapeDtypeStruct((rows, PAD), BF)
+    heads = mix_a.shape[1]
+    block = rows // 2
+    arrays, nears = half.pairs, half.names
     return pl.pallas_call(
-        branch_kernel,
-        in_specs=[scalars()] + [whole()] * 13 + [in_place()] * PARTS,
-        out_specs=[whole()] * 7,
-        out_shape=[jax.ShapeDtypeStruct((rows, width), F32), low, ranked, ranked, low, ranked]
-        + [jax.ShapeDtypeStruct(w_a.shape, BF)],
+        functools.partial(branch_kernel, nears),
+        grid=(2,),
+        in_specs=[scalars(), blocked(block, heads), blocked(block, heads), blocked(block, width)]
+        + [fixed_block(*array.shape) for array in (w_a, oa_a, oa_b, ob, scale_one, gain_two, ua)]
+        + [in_place()] * len(arrays),
+        out_specs=[blocked(block, width), blocked(block, width), blocked(block, PAD), blocked(block, PAD)]
+        + [fixed_block(*w_a.shape)],
+        out_shape=[
+            jax.ShapeDtypeStruct((rows, width), F32),
+            jax.ShapeDtypeStruct((rows, width), BF),
+            jax.ShapeDtypeStruct((rows, PAD), BF),
+            jax.ShapeDtypeStruct((rows, PAD), BF),
+            jax.ShapeDtypeStruct(w_a.shape, BF),
+        ],
         scratch_shapes=[pltpu.SemaphoreType.DMA((PARTS,))],
-        compiler_params=params(),
-        cost_estimate=cost(2 * rows * width * width, 16e6),
+        compiler_params=params(dimension_semantics=("arbitrary",)),
+        cost_estimate=cost(8e-6 * 1e15, 16e6),
         name="branch",
-    )(scal, mix_a, mix_b, tok, w_a, oa_a, oa_b, ob, scale_one, gain_two, scale_two, ua, db, cot, *parts)
-
-
-def mlp_kernel(count, step, more, *refs):
-    scal, n2, rank_up, grad_mlp, grad_rank, ub, da = refs[:7]
-    ups, downs = refs[7 : 7 + count], refs[7 + count : 7 + 2 * count]
-    rest = refs[7 + 2 * count :]
-    earlier = ()
-    if more:
-        earlier, rest = rest[:4], rest[4:]
+    )(scal, mix_a, mix_b, tok, w_a, oa_a, oa_b, ob, scale_one, gain_two, ua, *arrays)
+
+
+def mlp_kernel(nears, step, more, *refs):
+    scal, n2, rank_up, ub, da = refs[:5]
+    count = 1 if nears is None else len(nears)
+    ups, downs = refs[5 : 5 + count], refs[5 + count : 5 + 2 * count]
+    rest = refs[5 + 2 * count :]
+    if nears is None:
+        here, swapped, scale_two, db, cot, grad_mlp, grad_rank = rest[:7]
+        earlier, rest = (), rest[7:]
+        chosen = choose(scal, here, swapped, cot, rest[-1].at[0])
+    else:
+        grad_mlp, grad_rank = rest[:2]
+        earlier, rest = rest[2 : 2 + more], rest[2 + more :]
     m_out, g_out, rd_out, gru_out, gub_out, gda_out = rest[:6]
     wu, wd, ubs, das, hidden, grad_pre, sem, early_sem = rest[6:]
     width = wu.shape[1]
     rank = ub.shape[0]
-    size = width // PARTS
+    size = ub.shape[1] // PARTS
+    pieces = width // size
     chunks = width // step
     waits = [[] for _ in range(chunks)]
-    for near in range(PARTS):
-        at = pl.ds(near * size, size)
-        if count == 1:
+    for piece in range(pieces):
+        at = pl.ds(piece * size, size)
+        if nears is None:
             sources = ups[0].at[:, at], downs[0].at[at]
         else:
-            sources = ups[near], downs[near]
+            sources = ups[piece], downs[piece]
         for which, (source, target) in enumerate(zip(sources, (wu.at[:, at], wd.at[at]))):
-            copy = pltpu.make_async_copy(source, target, sem.at[which, near])
+            copy = pltpu.make_async_copy(source, target, sem.at[which, piece])
             copy.start()
-            waits[near * size // step].append(copy)
+            waits[piece * size // step].append(copy)
     if more:
         early = [
             pltpu.make_async_copy(earlier[0], m_out, early_sem.at[0]),
@@ -694,17 +752,24 @@
         for copy in early:
             copy.start()
 
-    def place(near):
-        if count == 1:
-            return pl.ds(near * size, size)
-        return pl.ds(pl.multiple_of((scal[2] ^ near) * size, size), size)
-
+    def place(piece):
+        if nears is None:
+            return pl.ds(piece * size, size)
+        return pl.ds(pl.multiple_of((scal[2] ^ nears[piece]) * size, size), size)
+
+    if nears is None:
+        chosen.wait()
+        grad_low = (scale_two[...] * (cot[...].astype(F32) * row_mask(scal, cot.shape[0]))).astype(BF)
+        grad_mlp[...] = grad_low
+        grad_rank[...] = dotg(grad_low, pad_rows(db[...]), 1, 1).astype(BF)
+    if more == 6:
+        gub_out[...], gda_out[...] = earlier[4][...], earlier[5][...]
     ubs[...] = jnp.zeros_like(ubs)
     das[...] = jnp.zeros_like(das)
-    for near in range(PARTS):
-        at = slice(near * size, (near + 1) * size)
-        ubs[0:rank, at] = ub[:, place(near)]
-        das[0:rank, at] = da[:, place(near)]
+    for piece in range(pieces):
+        at = slice(piece * size, (piece + 1) * size)
+        ubs[0:rank, at] = ub[:, place(piece)]
+        das[0:rank, at] = da[:, place(piece)]
     up_turned = rank_up[...].T[0:rank]
     grad_turned = grad_rank[...].T[0:rank]
 
@@ -733,10 +798,10 @@
         ranked, grad_ranked = ranked + earlier[2][...], grad_ranked + earlier[3][...]
     rd_out[...] = ranked
     gru_out[...] = grad_ranked
-    for near in range(PARTS):
-        at = slice(near * size, (near + 1) * size)
-        gub_out[:, place(near)] = dotg(up_turned, grad_pre[:, at], 1, 0)
-        gda_out[:, place(near)] = dotg(grad_turned, hidden[:, at], 1, 0)
+    for piece in range(pieces):
+        at = slice(piece * size, (piece + 1) * size)
+        gub_out[:, place(piece)] = dotg(up_turned, grad_pre[:, at], 1, 0)
+        gda_out[:, place(piece)] = dotg(grad_turned, hidden[:, at], 1, 0)
     if more:
         for copy in early:
             copy.wait()
@@ -751,49 +816,72 @@
             g_out[:, at] = grad_terms
 
 
-def mlp(scal, n2, rank_up, grad_mlp, grad_rank, ub, da, ups, downs, earlier=()):
+def mlp(scal, n2, rank_up, ub, da, ups, downs, grads, nears=None, earlier=()):
     rows, width = n2.shape
-    half = ub.shape[1]
-    rank = ub.shape[0]
-    count = len(ups)
-    step = half // 4
+    rank, half = ub.shape
+    units = half if nears is None else len(nears) * half // PARTS
+    step = min(512, units)
     sums = jax.ShapeDtypeStruct((rows, width), F32)
     ranked = jax.ShapeDtypeStruct((rows, PAD), F32)
     table = jax.ShapeDtypeStruct((rank, half), F32)
+    low = jax.ShapeDtypeStruct((rows, width), BF)
+    first = [low, low, jax.ShapeDtypeStruct((rows, PAD), BF)] if nears is None else []
     return pl.pallas_call(
-        functools.partial(mlp_kernel, count, step, bool(earlier)),
+        functools.partial(mlp_kernel, nears, step, len(earlier)),
         in_specs=[scalars()]
-        + [whole()] * 6
-        + [in_place()] * (2 * count)
-        + ([in_place()] * 2 + [whole()] * 2 if earlier else []),
-        out_specs=[whole()] * 6,
-        out_shape=[sums, sums, ranked, ranked, table, table],
+        + [whole()] * 4
+        + [in_place()] * (2 * len(ups))
+        + ([in_place()] * 2 if nears is None else [])
+        + [whole()] * 2
+        + ([in_place()] * 2 + [whole()] * (len(earlier) - 2) if earlier else []),
+        out_specs=[whole()] * (len(first) + 6),
+        out_shape=first + [sums, sums, ranked, ranked, table, table],
         scratch_shapes=[
-            pltpu.VMEM((width, half), BF),
-            pltpu.VMEM((half, width), BF),
-            pltpu.VMEM((PAD, half), BF),
-            pltpu.VMEM((PAD, half), BF),
-            pltpu.VMEM((rows, half), BF),
-            pltpu.VMEM((rows, half), BF),
+            pltpu.VMEM((width, units), BF),
+            pltpu.VMEM((units, width), BF),
+            pltpu.VMEM((PAD, units), BF),
+            pltpu.VMEM((PAD, units), BF),
+            pltpu.VMEM((rows, units), BF),
+            pltpu.VMEM((rows, units), BF),
             pltpu.SemaphoreType.DMA((2, PARTS)),
             pltpu.SemaphoreType.DMA((2,)),
         ],
         compiler_params=params(),
-        cost_estimate=cost(28e-6 * 1e15, 20e6),
+        cost_estimate=cost(25e-6 * units / half * 1e15, 20e6),
         name="mlp",
-    )(scal, n2, rank_up, grad_mlp, grad_rank, ub, da, *ups, *downs, *earlier)
+    )(scal, n2, rank_up, ub, da, *ups, *downs, *grads, *earlier)
+
+
+def mlp_other(scal, n2, rank_up, ub, da, up, down, grads, earlier):
+    for odd in range(2):
+        ups, nears = up.held(odd)
+        downs, same = down.held(odd)
+        assert nears == same
+        earlier = mlp(scal, n2, rank_up, ub, da, ups, downs, grads, nears, tuple(earlier))
+    return earlier
 
 
 def middle_kernel(
-    scal, residual, m_in, g_in, rd, gru, db, ua, scale_two, gain_two, scale_one, cot, w_a, w_b,
-    oa_a, oa_b, ob, mix_a, mix_b, rank_out, n2, grad_mlp,
+    scal, residual, m_in, g_in, rd, gru, cot, mix_a, mix_b, rank_out, n2, grad_mlp,
+    db, ua, scale_two, gain_two, scale_one, w_a, w_b, oa_a, oa_b, ob,
     layer, grad_res, grad_a, grad_b, goa_a, goa_b, gob, gua, gdb,
 ):
+    step = pl.program_id(0)
     rows = residual.shape[0]
     rank = db.shape[0]
-    valid = row_mask(scal, rows)
+    at = lax.broadcasted_iota(jnp.int32, (rows, 1), 0) + (scal[1] * 2 + step) * rows
+    valid = (at < scal[0]).astype(F32)
     down = two_terms(rd[...], rank)
     up = two_terms(gru[...], rank)
+
+    def add(out, terms):
+        @pl.when(step == 0)
+        def _():
+            out[...] = terms
+
+        @pl.when(step > 0)
+        def _():
+            out[...] += terms
 
     def turned(terms, right):
         both = dotg(terms.T[0 : 2 * rank], right, 1, 0)
@@ -801,8 +889,8 @@
 
     branch_out = m_in[...] + dotg(down, pad_twice(db[...]), 1, 0)
     layer[...] = ((residual[...] + scale_two[...] * branch_out) * valid).astype(BF)
-    gua[...] = turned(up, n2[...])
-    gdb[...] = turned(down, grad_mlp[...])
+    add(gua, turned(up, n2[...]))
+    add(gdb, turned(down, grad_mlp[...]))
     unit, scale = norm_stats(residual[...])
     grad_normed = (g_in[...] + dotg(up, pad_twice(ua[...]), 1, 0)) * gain_two[...]
     grad_total = cot[...].astype(F32) * valid + norm_grad(unit, scale, grad_normed)
@@ -816,84 +904,181 @@
         dotg(grad_attn, w_b[...], 1, 1) + dotg(grad_rank, pad_rows(oa_b[...]), 1, 0)
     ).astype(BF)
     rank_turned = grad_rank.T[0:rank]
-    goa_a[...] = dotg(rank_turned, mix_a[...], 1, 0)
-    goa_b[...] = dotg(rank_turned, mix_b[...], 1, 0)
-    gob[...] = turned(rank_out[...], grad_attn)
-
-
-def middle(*args):
-    rows, width = args[1].shape
-    half = args[12].shape[0]
-    rank = args[6].shape[0]
-    part = jax.ShapeDtypeStruct((rows, half), BF)
+    add(goa_a, dotg(rank_turned, mix_a[...], 1, 0))
+    add(goa_b, dotg(rank_turned, mix_b[...], 1, 0))
+    add(gob, turned(rank_out[...], grad_attn))
+
+
+def middle(scal, by_rows, others):
+    rows, width = by_rows[0].shape
+    block = rows // 2
+    heads = by_rows[6].shape[1]
+    rank = others[0].shape[0]
+    part = jax.ShapeDtypeStruct((rows, heads), BF)
     table = jax.ShapeDtypeStruct((rank, width), F32)
-    half_table = jax.ShapeDtypeStruct((rank, half), F32)
+    half_table = jax.ShapeDtypeStruct((rank, heads), F32)
     return pl.pallas_call(
         middle_kernel,
-        in_specs=[scalars()] + [whole()] * (len(args) - 1),
-        out_specs=[whole()] * 9,
+        grid=(2,),
+        in_specs=[scalars()]
+        + [blocked(block, array.shape[1]) for array in by_rows]
+        + [fixed_block(*array.shape) for array in others],
+        out_specs=[blocked(block, width), blocked(block, width), blocked(block, heads), blocked(block, heads)]
+        + [fixed_block(*shape) for shape in ((rank, heads),) * 2 + ((rank, width),) * 3],
         out_shape=[jax.ShapeDtypeStruct((rows, width), BF), jax.ShapeDtypeStruct((rows, width), F32)]
         + [part, part, half_table, half_table, table, table, table],
-        compiler_params=params(),
-        cost_estimate=cost(8e-6 * 1e15, 20e6),
+        compiler_params=params(dimension_semantics=("arbitrary",)),
+        cost_estimate=cost(9e-6 * 1e15, 20e6),
         name="middle",
-    )(*args)
-
-
-def qkv_tables_kernel(own_a, got_a, own_b, got_b, qb_a, qb_b, n1, rank_in, sum_a, sum_b, rank_out, gqb_a, gqb_b, gqa):
-    rank = qb_a.shape[1]
+    )(scal, *by_rows, *others)
+
+
+def columns_of(pieces):
+    first = 0
+    for piece in pieces:
+        yield piece, slice(first, first + piece.shape[-1])
+        first += piece.shape[-1]
+
+
+def qkv_tables_kernel(count, *refs):
+    sides, refs = (refs[: 3 * count], refs[3 * count : 6 * count]), refs[6 * count :]
+    scal, qb_a, qb_b, n1, rank_in, total_a, total_b, rank_out, kept, sent, gqb_a, gqb_b, gqa = refs
+    rank = qb_a.shape[0]
+    third = qb_a.shape[1] // 3
     rank_turned = rank_in[...].T[0:rank]
     ranked = None
-    for own, got, qb, total, table in ((own_a, got_a, qb_a, sum_a, gqb_a), (own_b, got_b, qb_b, sum_b, gqb_b)):
-        for c in range(3):
-            grad = own[c] if c == 0 else (own[c].astype(F32) + got[c - 1].astype(F32)).astype(BF)
-            total[c] = grad
-            table[c] = dotg(rank_turned, grad, 1, 0)
-            terms = dotg(grad, pad_rows(qb[c]), 1, 1)
-            ranked = terms if ranked is None else ranked + terms
+    for side, qb, total, table in zip(sides, (qb_a, qb_b), (total_a, total_b), (gqb_a, gqb_b)):
+        queries, owns, gots = side[:count], side[count : 2 * count], side[2 * count :]
+        for (piece, at), own, got in zip(columns_of(queries), owns, gots):
+            for c in range(3):
+                if c == 0:
+                    grad = piece[...]
+                else:
+                    grad = (own[c - 1].astype(F32) + got[c - 1].astype(F32)).astype(BF)
+                    total[c - 1, :, at] = grad
+                place = slice(c * third + at.start, c * third + at.stop)
+                table[:, place] = dotg(rank_turned, grad, 1, 0)
+                terms = dotg(grad, pad_rows(qb[:, place]), 1, 1)
+                ranked = terms if ranked is None else ranked + terms
     ranked = two_terms(ranked, rank)
     rank_out[...] = ranked
     both = dotg(ranked.T[0 : 2 * rank], n1[...], 1, 0)
     gqa[...] = both[0:rank] + both[rank : 2 * rank]
-
-
-def qkv_tables(own_a, got_a, own_b, got_b, qb_a, qb_b, n1, rank_in):
+    first = 0
+    for table in (gqb_a, gqa, gqb_b):
+        half = table.shape[1] // 2
+        at = slice(first, first + half)
+        kept[:, at] = table[:, pl.ds(pl.multiple_of(scal[1] * half, half), half)]
+        sent[:, at] = table[:, pl.ds(pl.multiple_of((1 - scal[1]) * half, half), half)].astype(BF)
+        first += half
+
+
+def qkv_tables(scal, side_a, side_b, qb_a, qb_b, n1, rank_in):
     rows, width = n1.shape
-    _, rank, third = qb_a.shape
+    rank, columns = qb_a.shape
+    count = len(side_a) // 3
+    total = jax.ShapeDtypeStruct((2, rows, columns // 3), BF)
+    share = columns + width // 2
     return pl.pallas_call(
-        qkv_tables_kernel,
-        in_specs=[whole()] * 8,
-        out_specs=[whole()] * 6,
-        out_shape=[jax.ShapeDtypeStruct((3, rows, third), BF)] * 2
-        + [jax.ShapeDtypeStruct((rows, PAD), BF)]
-        + [jax.ShapeDtypeStruct((3, rank, third), F32)] * 2
-        + [jax.ShapeDtypeStruct((rank, width), F32)],
+        functools.partial(qkv_tables_kernel, count),
+        in_specs=[whole()] * (6 * count) + [scalars()] + [whole()] * 4,
+        out_specs=[whole()] * 5,
+        out_shape=[total, total, jax.ShapeDtypeStruct((rows, PAD), BF)]
+        + [jax.ShapeDtypeStruct((rank, share), F32), jax.ShapeDtypeStruct((rank, share), BF)],
+        scratch_shapes=[pltpu.VMEM((rank, columns), F32)] * 2 + [pltpu.VMEM((rank, width), F32)],
         compiler_params=params(),
-        cost_estimate=cost(5e-6 * 1e15, 14e6),
+        cost_estimate=cost(7e-6 * 1e15, 14e6),
         name="qkv_tables",
-    )(own_a, got_a, own_b, got_b, qb_a, qb_b, n1, rank_in)
-
-
-def qkv_rows_kernel(grad_a, grad_b, w_a, w_b, ranked, qa, tok, gain, grad_res, out):
+    )(*side_a, *side_b, scal, qb_a, qb_b, n1, rank_in)
+
+
+def qkv_rows_kernel(count, *refs):
+    grads_a, grads_b, refs = refs[: count + 1], refs[count + 1 : 2 * count + 2], refs[2 * count + 2 :]
+    w_a, w_b, ranked, qa, tok, gain, grad_res, out = refs
     grad = dotg(ranked[...], pad_twice(qa[...]), 1, 0)
-    for part, w in ((grad_a, w_a), (grad_b, w_b)):
-        for c in range(3):
-            grad = grad + dotg(part[c], w[c], 1, 1)
+    for grads, w in ((grads_a, w_a), (grads_b, w_b)):
+        for piece, at in columns_of(grads[:count]):
+            grad = grad + dotg(piece[...], w[0, :, at], 1, 1)
+        for c in (1, 2):
+            grad = grad + dotg(grads[count][c - 1], w[c], 1, 1)
     unit, scale = norm_stats(tok[...].astype(F32))
     out[...] = (grad_res[...] + norm_grad(unit, scale, grad * gain[...])).astype(BF)
 
 
-def qkv_rows(*args):
-    rows, width = args[6].shape
+def qkv_rows(block_at, blocks, grads_a, grads_b, w_a, w_b, ranked, qa, tok, gain, grad_res):
+    rows, width = tok.shape
+    block = rows // blocks
+    flat = lambda array: pl.BlockSpec((block, array.shape[1]), lambda step: (block_at, 0))
+    deep = lambda array: pl.BlockSpec((2, block, array.shape[2]), lambda step: (0, block_at, 0))
+    specs = [flat(array) if array.ndim == 2 else deep(array) for array in grads_a + grads_b]
     return pl.pallas_call(
-        qkv_rows_kernel,
-        in_specs=[whole()] * 9,
+        functools.partial(qkv_rows_kernel, len(grads_a) - 1),
+        grid=(1,),
+        in_specs=specs
+        + [whole(), whole(), flat(ranked), whole(), flat(tok), whole(), flat(grad_res)],
         out_specs=whole(),
-        out_shape=jax.ShapeDtypeStruct((rows, width), BF),
+        out_shape=jax.ShapeDtypeStruct((block, width), BF),
         compiler_params=params(),
-        cost_estimate=cost(7e-6 * 1e15, 16e6),
+        cost_estimate=cost(12e-6 / blocks * 1e15, 16e6 / blocks),
         name="qkv_rows",
-    )(*args)
+    )(*grads_a, *grads_b, w_a, w_b, ranked, qa, tok, gain, grad_res)
+
+
+def gather_kernel(ids, images, out, total):
+    columns = out.shape[2]
+    total[...] = jnp.zeros_like(total)
+    for image in range(images.shape[0]):
+        adapter = ids[image]
+        total[adapter] += images[image, :, 0:columns].astype(F32)
+    out[...] = total[...].astype(BF)
+
+
+def gather_images(ids, images, adapters, columns):
+    rank = images.shape[1]
+    return pl.pallas_call(
+        gather_kernel,
+        in_specs=[scalars(), whole()],
+        out_specs=whole(),
+        out_shape=jax.ShapeDtypeStruct((adapters, rank, columns), BF),
+        scratch_shapes=[pltpu.VMEM((adapters, rank, columns), F32)],
+        compiler_params=params(),
+        cost_estimate=cost(2e-6 * 1e15, 1e6),
+        name="gather_images",
+    )(ids, images)
+
+
+def finish_kernel(cut, spans, places, core, own, other, *outs):
+    def write(low, high):
+        for (shared, start, stop), (number, index) in zip(spans, places):
+            first = cut if shared else 0
+            half = own.shape[2] - cut if shared else cut
+            out = outs[number] if index is None else outs[number].at[:, index]
+            middle = min(max(half - start, 0), stop - start)
+            if middle > 0:
+                out[:, :, 0:middle] = low[:, :, first + start : first + start + middle].astype(F32)
+            if middle < stop - start:
+                begin = first + start + middle - half
+                out[:, :, middle : stop - start] = high[:, :, begin : first + stop - half].astype(F32)
+
+    @pl.when(core[0] == 0)
+    def _():
+        write(own, other)
+
+    @pl.when(core[0] != 0)
+    def _():
+        write(other, own)
+
+
+def finish(core, cut, spans, places, own, other, shapes):
+    return pl.pallas_call(
+        functools.partial(finish_kernel, cut, spans, places),
+        in_specs=[scalars(), whole(), whole()],
+        out_specs=[whole()] * len(shapes),
+        out_shape=[jax.ShapeDtypeStruct(shape, F32) for shape in shapes],
+        compiler_params=params(),
+        cost_estimate=cost(2e-6 * 1e15, 4e6),
+        name="finish",
+    )(core, own, other)
 
 
 def swap(rows):
@@ -904,78 +1089,96 @@
     return lambda array: lax.ppermute(array, axis, FLIP)
 
 
-def other_half(local, axis, part_at):
-    size = local.shape[axis] // PARTS
-    mine = lax.dynamic_slice_in_dim(local, part_at * size, size, axis)
-    near = {0: flip("tensor")(mine)}
-    near[2] = flip("x")(near[0])
-    near[4] = flip("zb")(near[0])
-    near[6] = flip("zb")(near[2])
-    for k in (0, 2, 4, 6):
-        near[k + 1] = flip("core")(near[k])
-    return [near[k] for k in range(PARTS)]
-
-
-def side(array, axis, index, count):
-    size = array.shape[axis] // count
-    return lax.dynamic_slice_in_dim(array, index * size, size, axis)
+def after(value, *others):
+    return lax.optimization_barrier((value, others))[0]
+
+
+class OtherHalf:
+    BITS = {"core": 1, "x": 2, "zb": 4}
+
+    def __init__(self, local, axis, part_at, count):
+        size = local.shape[axis] // count
+        self.mine = lax.dynamic_slice_in_dim(local, (part_at % count) * size, size, axis)
+        self.parts = {}
+        self.nears = tuple(range(0, count, 2))
+
+    def over_tensor(self, *others):
+        self.parts[0] = flip("tensor")(after(self.mine, *others) if others else self.mine)
+
+    def hop(self, near, axis, *others):
+        part = after(self.parts[near], *others) if others else self.parts[near]
+        self.parts[near ^ self.BITS[axis]] = flip(axis)(part)
+
+    def last_hop(self):
+        over_zb, over_x = jnp.split(self.parts[2], 2, axis=1)[0], jnp.split(self.parts[4], 2, axis=1)[1]
+        self.parts[6] = jnp.concatenate([flip("zb")(over_zb), flip("x")(over_x)], axis=1)
+
+    def pairs_over_cores(self, *others):
+        parts = after(self.parts, *others) if others else self.parts
+        even = [jnp.stack([parts[a], parts[b]]) for a, b in zip(self.nears[::2], self.nears[1::2])]
+        self.pairs = even + [flip("core")(array) for array in even]
+        self.names = self.nears + tuple(near + 1 for near in self.nears)
+
+    def held(self, odd):
+        names = tuple(near + odd for near in self.nears)
+        return [self.parts[near] for near in names], names
+
+
+def half_columns(array, index):
+    size = array.shape[1] // 2
+    return lax.dynamic_slice_in_dim(array, index * size, size, 1)
+
+
+def by_index(index, own, other, axis):
+    return jnp.where(
+        index == 0, jnp.concatenate([own, other], axis=axis), jnp.concatenate([other, own], axis=axis)
+    )
 
 
 class Sum:
-    def __init__(self, near, far, shared, core, tensor):
-        self.core, self.tensor = core, tensor
-        self.rank = near.shape[0]
-        self.near, self.far, self.shared = near, far, shared
+    def __init__(self, kept, sent, cut, adapter, core, tensor):
+        self.core, self.tensor, self.adapter = core, tensor, adapter
+        self.kept, self.sent, self.cut = kept, sent, cut
+
+    @staticmethod
+    def shares(near, shared, far, core):
+        def share(index):
+            return jnp.concatenate([half_columns(array, index) for array in (near, shared, far)], axis=1)
+
+        return share(core), share(1 - core).astype(BF)
 
     def over_cores(self):
-        c = self.core
-        rank, width = self.shared.shape
-        quarters = self.shared.reshape(rank, 4, width // 4)
-
-        def share(index):
-            near = side(self.near, 1, index, 2)
-            far = side(self.far, 1, index, 2)
-            ours = lax.dynamic_index_in_dim(quarters, self.tensor * 2 + index, 1, False)
-            theirs = lax.dynamic_index_in_dim(quarters, (1 - self.tensor) * 2 + index, 1, False)
-            return jnp.concatenate([near, ours, far, theirs], axis=1)
-
-        got = flip("core")(share(1 - c).astype(BF))
-        total = (share(c) + got.astype(F32)).astype(BF)
-        self.columns = total.shape[1] // 2
-        self.mine = total[:, : self.columns]
-        self.send = total[:, self.columns :]
-        return self
-
-    def over_pair(self):
-        self.pair = jnp.stack([self.mine, flip("tensor")(self.send)])
-        return self
-
-    def over_images(self, weights, groups):
-        got = [self.pair]
-        names, sizes = ("hi", "zb", "x"), groups
-        total = sizes[0] * sizes[1] * sizes[2]
-        for k in range(1, total):
-            got.append(lax.ppermute(self.pair, names, [(i, i ^ k) for i in range(total)]))
-        images = jnp.concatenate(got, axis=0)
-        self.dense = jnp.einsum("in,irf->nrf", weights, images, preferred_element_type=F32).astype(BF)
-        return self
-
-    def spread(self):
-        half = self.near.shape[1] // 2
-        ours = self.dense[:, :, half:]
-        theirs = flip("tensor")(ours)
-        first = self.tensor == 0
-        pair = jnp.concatenate(
-            [self.dense[:, :, :half], jnp.where(first, ours, theirs), jnp.where(first, theirs, ours)], axis=2
-        )
-        other = flip("core")(pair)
-        low = jnp.where(self.core == 0, pair, other).astype(F32)
-        high = jnp.where(self.core == 0, other, pair).astype(F32)
-        quarter = ours.shape[2]
-        near = jnp.concatenate([low[:, :, :half], high[:, :, :half]], axis=2)
-        cut = lambda array, index: array[:, :, half + index * quarter : half + (index + 1) * quarter]
-        shared = jnp.concatenate([cut(low, 0), cut(high, 0), cut(low, 1), cut(high, 1)], axis=2)
-        return near, shared
+        total = (self.kept + flip("core")(self.sent).astype(F32)).astype(BF)
+        cut, columns = self.cut, total.shape[1] - self.cut
+        note = []
+        if self.adapter is not None:
+            note = [jnp.broadcast_to(self.adapter.astype(BF), (total.shape[0], PAD))]
+        self.mine = jnp.concatenate([total[:, :columns]] + note, axis=1)
+        self.send = jnp.concatenate([total[:, columns:], total[:, cut:columns]] + note, axis=1)
+        self.columns = columns
+
+    def over_pair(self, *others):
+        other = flip("tensor")(self.send)
+        other = after(other, *others) if others else other
+        self.images = by_index(self.tensor, self.mine[None], other[None], 0)
+
+    def over(self, name, *others):
+        if lax.axis_size(name) == 2:
+            got = flip(name)(self.images)
+            self.images = by_index(lax.axis_index(name), self.images, after(got, *others) if others else got, 0)
+        elif lax.axis_size(name) > 2:
+            self.images = lax.all_gather(self.images, name, axis=0, tiled=True)
+
+    def adapters_of_images(self):
+        return self.images[:, 0, -1].astype(jnp.int32)
+
+    def over_adapters(self, ids, adapters):
+        self.dense = gather_images(ids, self.images, adapters, self.columns)
+        self.other = flip("core")(self.dense)
+
+    def finish(self, spans, places, shapes):
+        core = self.core.astype(jnp.int32)[None]
+        return finish(core, self.cut, spans, places, self.dense, self.other, shapes)
 
 
 def quad_body(
@@ -983,98 +1186,145 @@
     qkv_a, qkv_b, out_a, out_b, up_a, up_b, down_a, down_b,
 ):
     core, tensor = lax.axis_index("core"), lax.axis_index("tensor")
-    groups = tuple(lax.axis_size(name) for name in ("hi", "zb", "x"))
     part_at = lax.axis_index("zb") * 4 + lax.axis_index("x") * 2 + core
-    rank, width = qkv_a.shape[1:]
-    heads_width = w_qkv.shape[2]
+    adapters, rank, width = qkv_a.shape
+    third = w_qkv.shape[2]
     units = w_up.shape[1]
 
-    tok = swap(tokens[0])
+    w3 = jnp.swapaxes(w_qkv, 0, 1)
+    half_qkv = OtherHalf(w3, 1, part_at, PARTS)
+    half_out = OtherHalf(w_out, 0, part_at, 4)
+    half_up = OtherHalf(w_up, 1, part_at, PARTS)
+    half_down = OtherHalf(w_down, 0, part_at, PARTS)
+    half_qkv.over_tensor()
+    tok_here = tokens[0]
+    tok_swapped = swap(tok_here)
     facts = jnp.stack([lengths[0], adapter_ids[0]])
     facts_other = flip("core")(facts)
     mine = jnp.where(core == tensor, facts, facts_other)
     theirs = jnp.where(core == tensor, facts_other, facts)
     length, adapter, adapter_other = mine[0], mine[1], theirs[1]
-    scal = jnp.stack([length, core, part_at, adapter]).astype(jnp.int32)
+    scal = jnp.stack([length, core, part_at, core == tensor]).astype(jnp.int32)
 
     qkv_b, out_b, up_b, down_b = (jnp.swapaxes(table, -1, -2) for table in (qkv_b, out_b, up_b, down_b))
     pick = lambda table, index: lax.dynamic_index_in_dim(table, index, 0, False)
-
-    def packed(index):
-        qb = jnp.swapaxes(pick(qkv_b, index), 0, 1).reshape(rank, 3 * heads_width)
-        return jnp.concatenate([qb, pick(out_a, index), pick(up_b, index), pick(down_a, index)], axis=1)
-
-    pack = flip("tensor")(packed(adapter_other))
-    cuts = (3 * heads_width, 4 * heads_width, 4 * heads_width + units)
-    qb_other, oa_other, ub_other, da_other = jnp.split(pack, cuts, axis=1)
+    flat = lambda table: jnp.swapaxes(table, 0, 1).reshape(rank, 3 * third)
+    packed_first = jnp.concatenate([flat(pick(qkv_b, adapter_other)), pick(out_a, adapter_other)], axis=1)
+    packed = jnp.concatenate([pick(table, adapter_other) for table in (up_b, down_a)], axis=1)
     qa, oa, ob, ua, ub, da, db = (
         pick(table, adapter) for table in (qkv_a, out_a, out_b, up_a, up_b, down_a, down_b)
     )
-    qb = pick(qkv_b, adapter)
+    qb = flat(pick(qkv_b, adapter))
     gain_one, gain_two, scale_one, scale_two = (v.reshape(1, width) for v in (gain_one, gain_two, scale_one, scale_two))
 
-    pair_ids = jnp.stack([adapter, adapter_other])
-    total = groups[0] * groups[1] * groups[2]
-    all_ids = [pair_ids] + [
-        lax.ppermute(pair_ids, ("hi", "zb", "x"), [(i, i ^ k) for i in range(total)]) for k in range(1, total)
-    ]
-    weights = (jnp.concatenate(all_ids)[:, None] == jnp.arange(qkv_a.shape[0])[None, :]).astype(BF)
-
-    w3 = jnp.swapaxes(w_qkv, 0, 1)
-    n1, rank_qkv, own_a = qkv_local(tok, gain_one, w3, qa, qb)
-    kv_a = flip("core")(own_a[1:])
-    w3_parts = other_half(w3, 1, part_at)
-    out_parts = other_half(w_out, 0, part_at)
-    cot = swap(cotangent[0])
-    up_parts = other_half(w_up, 1, part_at)
-    down_parts = other_half(w_down, 0, part_at)
-
-    mix_a, logs_a = attend(scal, own_a, kv_a)
-    own_b, w3_other = qkv_other(scal, n1, rank_qkv, qb_other, w3_parts)
-    kv_b = flip("core")(own_b[1:])
-    mix_b, logs_b = attend(scal, own_b, kv_b)
-    residual, n2, rank_out, rank_up, grad_mlp, grad_rank, out_other = branch(
-        scal, mix_a, mix_b, tok, w_out, out_parts, oa, oa_other, ob, scale_one, gain_two, scale_two, ua, db, cot
-    )
-    m, g, rd, gru, gub_a, gda_a = mlp(scal, n2, rank_up, grad_mlp, grad_rank, ub, da, [w_up], [w_down])
-    m, g, rd, gru, gub_b, gda_b = mlp(
-        scal, n2, rank_up, grad_mlp, grad_rank, ub_other, da_other, up_parts, down_parts, (m, g, rd, gru)
+    half_qkv.hop(0, "x")
+    half_qkv.hop(0, "zb")
+    slices = (scal, packed, packed_first, qa, oa, ob, ua, ub, da, db, qb, half_out.mine, half_up.mine, half_down.mine)
+    qb_other, oa_other = jnp.split(flip("tensor")(after(packed_first, half_qkv.parts[0])), (3 * third,), axis=1)
+    half_up.over_tensor(half_qkv.parts[4])
+    half_qkv.parts[2] = after(half_qkv.parts[2], *slices)
+    half_qkv.last_hop()
+    tok_swapped = after(tok_swapped, half_qkv.parts[2], half_qkv.parts[4], qb_other, scal)
+    tok, n1, rank_qkv, q_a, own_a = qkv_local(scal, tok_here, tok_swapped, gain_one, w3, qa, qb)
+    half_qkv.pairs_over_cores()
+    kv_a = flip("core")(own_a)
+    q_b, own_b, w3_other = qkv_other(scal, after(n1, half_up.parts[0]), rank_qkv, qb_other, half_qkv)
+    kv_b = flip("core")(own_b)
+    half_out.over_tensor(own_b)
+    half_up.hop(0, "x", own_b)
+    half_up.hop(0, "zb", own_b)
+    cot_swapped = swap(after(cotangent[0], own_b))
+    mix_a, logs_a = attend(scal, after(q_a, own_b), own_a, kv_a)
+    half_out.hop(0, "x", mix_a)
+    half_up.hop(4, "x", mix_a)
+    half_down.over_tensor(mix_a)
+    mix_b, logs_b = attend(scal, after(q_b, mix_a, half_up.parts[2], half_up.parts[4]), own_b, kv_b)
+    half_out.pairs_over_cores(mix_b)
+    half_down.hop(0, "x", mix_b)
+    half_down.hop(0, "zb", mix_b)
+    residual, n2, rank_out, rank_up, out_other = branch(
+        scal, mix_a, mix_b, tok, w_out, half_out, oa, oa_other, ob, scale_one, gain_two, ua
+    )
+    half_down.hop(2, "zb", n2)
+    ub_other, da_other = jnp.split(flip("tensor")(after(packed, n2)), 2, axis=1)
+    for near in (0, 2, 4):
+        half_up.hop(near, "core", n2)
+    cot, grad_mlp, grad_rank, m, g, rd, gru, gub_a, gda_a = mlp(
+        scal, n2, rank_up, ub, da, [w_up], [w_down], [cotangent[0], cot_swapped, scale_two, db]
+    )
+    half_up.hop(6, "core", m)
+    for near in (0, 2, 4, 6):
+        half_down.hop(near, "core", m)
+    m, g, rd, gru, gub_b, gda_b = mlp_other(
+        scal, n2, rank_up, ub_other, da_other, half_up, half_down, [grad_mlp, grad_rank], (m, g, rd, gru)
     )
     layer, grad_res, grad_a, grad_b, goa_a, goa_b, gob, gua, gdb = middle(
-        scal, residual, m, g, rd, gru, db, ua, scale_two, gain_two, scale_one, cot, w_out, out_other,
-        oa, oa_other, ob, mix_a, mix_b, rank_out, n2, grad_mlp,
-    )
-    layer_out = swap(layer)
-    early = Sum(
+        scal,
+        (residual, m, g, rd, gru, cot, mix_a, mix_b, rank_out, n2, grad_mlp),
+        (db, ua, scale_two, gain_two, scale_one, w_out, out_other, oa, oa_other, ob),
+    )
+    shares = Sum.shares(
         jnp.concatenate([goa_a, gub_a, gda_a], axis=1),
+        jnp.concatenate([gob, gua, gdb], axis=1),
         jnp.concatenate([goa_b, gub_b, gda_b], axis=1),
-        jnp.concatenate([gob, gua, gdb], axis=1),
         core,
-        tensor,
-    )
+    )
+    early = Sum(*shares, third // 2 + units, adapter, core, tensor)
     early.over_cores()
-    early.over_pair()
-    back_a, sent_a = attend_back(scal, own_a, kv_a, mix_a, grad_a, logs_a)
-    got_a = flip("core")(sent_a)
-    early.over_images(weights, groups)
-    back_b, sent_b = attend_back(scal, own_b, kv_b, mix_b, grad_b, logs_b)
-    got_b = flip("core")(sent_b)
-    qb_other3 = jnp.swapaxes(qb_other.reshape(rank, 3, heads_width), 0, 1)
-    sum_a, sum_b, ranked, gqb_a, gqb_b, gqa = qkv_tables(
-        back_a, got_a, back_b, got_b, qb, qb_other3, n1, rank_qkv
-    )
-    flat = lambda table: jnp.swapaxes(table, 0, 1).reshape(rank, 3 * heads_width)
-    late = Sum(flat(gqb_a), flat(gqb_b), gqa, core, tensor)
+
+    def back(queries, own, kv, mixed, grad, logs, piece, *others):
+        queries = after(queries, *others) if others else queries
+        grad_queries, kept, sent = attend_back(scal, queries, own, kv, mixed, grad, logs, piece, 2)
+        return grad_queries, kept, flip("core")(sent)
+
+    side_a, side_b = (q_a, own_a, kv_a, mix_a, grad_a, logs_a), (q_b, own_b, kv_b, mix_b, grad_b, logs_b)
+    back_1 = back(*side_a, 0)
+    layer_swapped = swap(after(layer, back_1[0]))
+    early.send = after(early.send, back_1[0])
+    back_2 = back(*side_a, 1, early.send)
+    early.over_pair(back_2[0])
+    back_3 = back(*side_b, 0, early.images)
+    early.over("hi", back_3[0])
+    back_4 = back(*side_b, 1, early.images, layer_swapped)
+    early.over("zb", back_4[0])
+    kv_sum_a, kv_sum_b, ranked, kept, sent = qkv_tables(
+        after(scal, early.images),
+        [part for pair in zip(back_1, back_2) for part in pair],
+        [part for pair in zip(back_3, back_4) for part in pair],
+        qb, qb_other, n1, rank_qkv,
+    )
+    late = Sum(kept, sent, 3 * third // 2, None, core, tensor)
     late.over_cores()
-    late.over_pair()
-    grad_tokens = qkv_rows(sum_a, sum_b, w3, w3_other, ranked, qa, tok, gain_one, grad_res)
-    grad_tokens = swap(grad_tokens).astype(F32)
-    late.over_images(weights, groups)
-    near, shared = early.spread()
-    sum_oa, sum_ub, sum_da = jnp.split(near, (heads_width, heads_width + units), axis=2)
-    sum_ob, sum_ua, sum_db = jnp.split(shared, 3, axis=2)
-    near, sum_qa = late.spread()
-    sum_qb = jnp.swapaxes(near.reshape(-1, rank, 3, heads_width), 1, 2)
+    early.over("x", kept)
+    grads = (
+        [back_1[0], back_2[0], kv_sum_a], [back_3[0], back_4[0], kv_sum_b],
+        w3, w3_other, ranked, qa, tok, gain_one, grad_res,
+    )
+    upper = qkv_rows(0, 2, grads[0], grads[1], after(w3, late.send), *grads[3:])
+    late.over_pair(upper)
+    lower = qkv_rows(1, 2, grads[0], grads[1], after(w3, late.images), *grads[3:])
+    late.over("hi", lower)
+    late.over("zb")
+    ids = early.adapters_of_images()
+    early.over_adapters(ids, adapters)
+    late.over("x")
+    in_place_already = core == tensor
+    grad_tokens = jnp.concatenate(
+        [jnp.where(in_place_already, rows, swap(rows)) for rows in (upper, lower)], axis=0
+    ).astype(F32)
+    layer_out = jnp.where(in_place_already, layer, layer_swapped)
+    late.over_adapters(ids, adapters)
+    ends = (0, third, third + units, third + 2 * units)
+    spans = [(False, ends[k], ends[k + 1]) for k in range(3)] + [(True, k * width, (k + 1) * width) for k in range(3)]
+    widths = (third, units, units, width, width, width)
+    sum_oa, sum_ub, sum_da, sum_ob, sum_ua, sum_db = early.finish(
+        spans, [(k, None) for k in range(6)], [(adapters, rank, size) for size in widths]
+    )
+    sum_qb, sum_qa = late.finish(
+        [(False, c * third, (c + 1) * third) for c in range(3)] + [(True, 0, width)],
+        [(0, c) for c in range(3)] + [(1, None)],
+        [(adapters, 3, rank, third), (adapters, rank, width)],
+    )
     turn = lambda table: jnp.swapaxes(table, -1, -2)
     return (
         layer_out[None],

time: 432 us -> 350 us (0.81)
  starting transfers between devices: 104 us -> 53 us
  waiting for transfers between devices: 69.9 us -> 25.6 us
  Pallas kernels: 188 us -> 217 us
  local copies, waits for them, and re-layouts: 43.8 us -> 25.3 us
  other arithmetic: 9.58 us -> 15 us
    ppermute x21 -> x0, starting transfers between devices: 45.8 us -> none  [the longest x14 28.4 us: over_images(): lax.ppermute(self.pair, names, [(i, i ^ k) for i in range(total)])]
    pallas_call x12 -> x20, Pallas kernels: 188 us -> 217 us  [the longest x4 57.4 us: attend_back(): pl.pallas_call(attend_back_kernel, grid=(pairs,), in_specs=[scalars(), fl...]
    ppermute x21 -> x0, waiting for transfers between devices: 27 us -> none  [the longest x14 20.3 us: over_images(): lax.ppermute(self.pair, names, [(i, i ^ k) for i in range(total)])]
    ppermute x46 -> x47, waiting for transfers between devices: 39.2 us -> 25.2 us  [flip(): return lambda array: lax.ppermute(array, axis, FLIP)]
    unnamed x101 -> x76, local copies, waits for them, and re-layouts: 16.2 us -> 8.02 us
    ppermute x46 -> x47, starting transfers between devices: 44.6 us -> 37.5 us  [flip(): return lambda array: lax.ppermute(array, axis, FLIP)]
    select_n x2 -> x8, other arithmetic: 0.05 us -> 5.42 us  [by_index(): jnp.where(index == 0, jnp.concatenate([own, other], axis=axis), jnp.conca...]
    ppermute x4 -> x5, starting transfers between devices: 13.6 us -> 15.5 us  [swap(): return lax.ppermute(rows, ('core', 'tensor'), SWAP)]
  transfers between devices with their start and end apart: 71 -> 52, of which waited for: 19 -> 9; matrix products, arithmetic and copies ran while one was open for 11% -> 9% of each run, Pallas kernels for 36% -> 52%
where the time goes in v2:
time: 350 us; the launch traced here: 344 us
  Pallas kernels  217 us (62%)
  starting transfers between devices  53 us (15%)
  waiting for transfers between devices  25.6 us (7%)
  local copies, waits for them, and re-layouts  25.3 us (7%)
  other arithmetic  15 us (4%)
  between operations  7.57 us (2%)
    pallas_call x4, Pallas kernels, attend_back(): pl.pallas_call(attend_back_kernel, grid=(pairs,), in_specs=[scalars(), fl...  57.4 us
    pallas_call x3, Pallas kernels, mlp(): pl.pallas_call(functools.partial(mlp_kernel, nears, step, len(earlier)),...  56.1 us
    ppermute x47, starting transfers between devices, flip(): return lambda array: lax.ppermute(array, axis, FLIP)  37.5 us
    pallas_call x2, Pallas kernels, attend(): pl.pallas_call(attend_kernel, grid=(pairs,), in_specs=[scalars(), pl.Bloc...  29.9 us
    ppermute x47, waiting for transfers between devices, flip(): return lambda array: lax.ppermute(array, axis, FLIP)  25.2 us
    pallas_call x2, Pallas kernels, qkv_rows(): pl.pallas_call(functools.partial(qkv_rows_kernel, len(grads_a) - 1), grid...  16 us
    ppermute x5, starting transfers between devices, swap(): return lax.ppermute(rows, ('core', 'tensor'), SWAP)  15.5 us
    pallas_call x1, Pallas kernels, middle(): pl.pallas_call(middle_kernel, grid=(2,), in_specs=[scalars()] + [blocked(...  13.9 us
  transfers between devices with their start and end apart: 52, of which 9 were waited for; matrix products, arithmetic and copies ran while one was open for 9% of the time, Pallas kernels for 52%

profile of v2, /device:TPU:1, one launch (start us, length us, event | category | flops | bytes accessed | tf_op | source)
XLA Modules:
  0.0 343.9 jit_solution(331450976777527410)
XLA Ops:
  1.8 2.1 collective-permute-start.2
  30.9 8.4 %collective-permute-done.3 = bf16[3,128,512]{2,1,0:T(8,128)(2,1)S(1)} collective-permute-done((bf16[3,128,512]{2,1,0:T(8,128)(2,1)S(1)}, bf16[3,128,512]{2,1,0:T(8,128)(2,1)S(1)}, u32[]{:S(2)}, u32[]{:S(2)}) %collective-permute-start.3) | collective-permute-done | bytes 393248 | tf_op jit(solution)/shard_map/ppermute | solution.py:1089
  48.8 9.7 %qkv_local.1 = (bf16[688,1024]{1,0:T(8,128)(2,1)}, bf16[688,1024]{1,0:T(8,128)(2,1)}, bf16[688,128]{1,0:T(8,128)(2,1)}, bf16[688,512]{1,0:T(8,128)(2,1)}, bf16[2,688,512]{2,1,0:T(8,128)(2,1)}) custom-call(s32[4]{0:T(128)} %pad_add_fusion.1.scal.refs_0_.refs_12_, bf16[688,1024]{1,0:T(8,128)(2,1)} %bitcast.104, ...), custom_call_target="tpu_custom_call" | custom-call | flops 3500000000 | bytes 8000000 | tf_op jit(solution)/shard_map/qkv_local/pallas_call | solution.py:402
  58.8 3.4 collective-permute-done.6.refs_5_
  63.4 7.7 %qkv_other.1 = (bf16[688,512]{1,0:T(8,128)(2,1)}, bf16[2,688,512]{2,1,0:T(8,128)(2,1)}, bf16[3,1024,512]{2,1,0:T(8,128)(2,1)}) custom-call(s32[4]{0:T(128)} %pad_add_fusion.1.scal.refs_0_.refs_12_, bf16[688,1024]{1,0:T(8,128)(2,1)} %get-tuple-element.128.n1.refs_15_, bf16[688,128]{1,0:T(8,128)(2,1)} %get-tuple-element.129.rank.refs_16_, ...), custom_call_target="tpu_custom_call" | custom-call | flops 3500000000 | bytes 10000000 | tf_op jit(solution)/shard_map/qkv_other/pallas_call | solution.py:454
  73.5 4.6 %collective-permute-start.23 = (bf16[688,1024]{1,0:T(8,128)(2,1)}, bf16[688,1024]{1,0:T(8,128)(2,1)}, u32[]{:S(2)}, u32[]{:S(2)}) collective-permute-start(bf16[688,1024]{1,0:T(8,128)(2,1)} %bitcast.38.refs_7_), channel_id=1, source_target_pairs={{1,2},{2,1},{5,6},{6,5},{9,10},{10,9},{13,14},{14,13},{17,18},{18,... | collective-permute-start | bytes 4227080 | tf_op jit(solution)/shard_map/ppermute | solution.py:1085
  78.1 14.9 %attend.2 = (bf16[688,512]{1,0:T(8,128)(2,1)}, f32[4,8,688]{2,1,0:T(8,128)}) custom-call(s32[4]{0:T(128)} %pad_add_fusion.1.scal.refs_0_.refs_12_, bf16[688,512]{1,0:T(8,128)(2,1)} %get-tuple-element.194.q_ref, bf16[2,688,512]{2,1,0:T(8,128)(2,1)} %get-tuple-element.132.k_ref.v_ref, bf16[2,688,512]{2,1,0:T(8,128)(2,1)} %get-tuple-element.132.k_ref.v_ref, ...), custom_call_target="tpu_custom_call" | custom-call | flops 8000000000 | bytes 6000000 | tf_op jit(solution)/shard_map/attend/pallas_call | solution.py:531
  94.3 14.9 %attend.3 = (bf16[688,512]{1,0:T(8,128)(2,1)}, f32[4,8,688]{2,1,0:T(8,128)}) custom-call(s32[4]{0:T(128)} %pad_add_fusion.1.scal.refs_0_.refs_12_, bf16[688,512]{1,0:T(8,128)(2,1)} %get-tuple-element.206.q_ref, bf16[2,688,512]{2,1,0:T(8,128)(2,1)} %get-tuple-element.130.k_ref.v_ref, bf16[2,688,512]{2,1,0:T(8,128)(2,1)} %get-tuple-element.130.k_ref.v_ref, ...), custom_call_target="tpu_custom_call" | custom-call | flops 8000000000 | bytes 6000000 | tf_op jit(solution)/shard_map/attend/pallas_call | solution.py:531
  113.4 9.1 %branch.1 = (f32[688,1024]{1,0:T(8,128)}, bf16[688,1024]{1,0:T(8,128)(2,1)}, bf16[688,128]{1,0:T(8,128)(2,1)}, bf16[688,128]{1,0:T(8,128)(2,1)}, bf16[512,1024]{1,0:T(8,128)(2,1)}) custom-call(s32[4]{0:T(128)} %pad_add_fusion.1.scal.refs_0_.refs_12_, bf16[688,512]{1,0:T(8,128)(2,1)} %get-tuple-element.133.mix_a.mixed_ref, ...), custom_call_target="tpu_custom_call" | custom-call | flops 4000000000 | bytes 16000000 | tf_op jit(solution)/shard_map/branch/pallas_call | solution.py:695
  123.4 27.2 %mlp.3 = (bf16[688,1024]{1,0:T(8,128)(2,1)}, bf16[688,1024]{1,0:T(8,128)(2,1)}, bf16[688,128]{1,0:T(8,128)(2,1)}, f32[688,1024]{1,0:T(8,128)}, f32[688,1024]{1,0...) custom-call(s32[4]{0:T(128)} %pad_add_fusion.1.scal.refs_0_.refs_12_, ...), custom_call_target="tpu_custom_call" | custom-call | flops 12499999744 | bytes 20000000 | tf_op jit(solution)/shard_map/mlp/pallas_call | solution.py:829
  155.5 7.3 %collective-permute-done.31.refs_12_ = bf16[256,1024]{1,0:T(8,128)(2,1)} collective-permute-done((bf16[256,1024]{1,0:T(8,128)(2,1)S(1)}, bf16[256,1024]{1,0:T(8,128)(2,1)}, u32[]{:S(2)}, u32[]{:S(2)}) %collective-permute-start.31) | collective-permute-done | bytes 524320 | tf_op jit(solution)/shard_map/ppermute | solution.py:1089
  162.7 2.5 collective-permute-start.19
  165.8 14.2 %mlp.4 = (f32[688,1024]{1,0:T(8,128)}, f32[688,1024]{1,0:T(8,128)}, f32[688,128]{1,0:T(8,128)}, f32[688,128]{1,0:T(8,128)}, f32[16,2048]{1,0:T(8,128)}, /*index=5*/f32[16,2048]{1,0:T(8,128)}) custom-call(s32[4]{0:T(128)} %pad_add_fusion.1.scal.refs_0_.refs_12_, bf16[688,1024]{1,0:T(8,128)(2,1)} %get-tuple-element.144.refs_1_.n2, ...), custom_call_target="tpu_custom_call" | custom-call | flops 6249999872 | bytes 20000000 | tf_op jit(solution)/shard_map/mlp/pallas_call | solution.py:829
  181.6 14.6 %mlp.5 = (f32[688,1024]{1,0:T(8,128)}, f32[688,1024]{1,0:T(8,128)}, f32[688,128]{1,0:T(8,128)}, f32[688,128]{1,0:T(8,128)}, f32[16,2048]{1,0:T(8,128)}, /*index=5*/f32[16,2048]{1,0:T(8,128)}) custom-call(s32[4]{0:T(128)} %pad_add_fusion.1.scal.refs_0_.refs_12_, bf16[688,1024]{1,0:T(8,128)(2,1)} %get-tuple-element.144.refs_1_.n2, ...), custom_call_target="tpu_custom_call" | custom-call | flops 6249999872 | bytes 20000000 | tf_op jit(solution)/shard_map/mlp/pallas_call | solution.py:829
  196.2 13.9 %middle.1 = (bf16[688,1024]{1,0:T(8,128)(2,1)}, f32[688,1024]{1,0:T(8,128)}, bf16[688,512]{1,0:T(8,128)(2,1)}, bf16[688,512]{1,0:T(8,128)(2,1)}, f32[16,512]{1,0...) custom-call(s32[4]{0:T(128)} %pad_add_fusion.1.scal.refs_0_.refs_12_, ...), custom_call_target="tpu_custom_call" | custom-call | flops 4499999744 | bytes 20000000 | tf_op jit(solution)/shard_map/middle/pallas_call | solution.py:920
  211.8 14.2 %attend_back.4 = (bf16[688,256]{1,0:T(8,128)(2,1)}, bf16[2,688,256]{2,1,0:T(8,128)(2,1)}, bf16[2,688,256]{2,1,0:T(8,128)(2,1)}) custom-call(s32[4]{0:T(128)} %pad_add_fusion.1.scal.refs_0_.refs_12_, bf16[688,512]{1,0:T(8,128)(2,1)} %get-tuple-element.194.q_ref, bf16[2,688,512]{2,1,0:T(8,128)(2,1)} %get-tuple-element.132.k_ref.v_ref, ...), custom_call_target="tpu_custom_call" | custom-call | flops 6499999744 | bytes 9000000 | tf_op jit(solution)/shard_map/attend_back/pallas_call | solution.py:629
  226.0 2.5 collective-permute-start.33
  230.1 14.5 %attend_back.5 = (bf16[688,256]{1,0:T(8,128)(2,1)}, bf16[2,688,256]{2,1,0:T(8,128)(2,1)}, bf16[2,688,256]{2,1,0:T(8,128)(2,1)}) custom-call(s32[4]{0:T(128)} %pad_add_fusion.1.scal.refs_0_.refs_12_, bf16[688,512]{1,0:T(8,128)(2,1)} %get-tuple-element.194.q_ref, bf16[2,688,512]{2,1,0:T(8,128)(2,1)} %get-tuple-element.132.k_ref.v_ref, ...), custom_call_target="tpu_custom_call" | custom-call | flops 6499999744 | bytes 9000000 | tf_op jit(solution)/shard_map/attend_back/pallas_call | solution.py:629
  246.8 2.4 collective-permute-start.38
  249.2 14.1 %attend_back.6 = (bf16[688,256]{1,0:T(8,128)(2,1)}, bf16[2,688,256]{2,1,0:T(8,128)(2,1)}, bf16[2,688,256]{2,1,0:T(8,128)(2,1)}) custom-call(s32[4]{0:T(128)} %pad_add_fusion.1.scal.refs_0_.refs_12_, bf16[688,512]{1,0:T(8,128)(2,1)} %get-tuple-element.206.q_ref, bf16[2,688,512]{2,1,0:T(8,128)(2,1)} %get-tuple-element.130.k_ref.v_ref, ...), custom_call_target="tpu_custom_call" | custom-call | flops 6499999744 | bytes 9000000 | tf_op jit(solution)/shard_map/attend_back/pallas_call | solution.py:629
  263.3 2.9 collective-permute-start.39
  267.3 14.6 %attend_back.7 = (bf16[688,256]{1,0:T(8,128)(2,1)}, bf16[2,688,256]{2,1,0:T(8,128)(2,1)}, bf16[2,688,256]{2,1,0:T(8,128)(2,1)}) custom-call(s32[4]{0:T(128)} %pad_add_fusion.1.scal.refs_0_.refs_12_, bf16[688,512]{1,0:T(8,128)(2,1)} %get-tuple-element.206.q_ref, bf16[2,688,512]{2,1,0:T(8,128)(2,1)} %get-tuple-element.130.k_ref.v_ref, ...), custom_call_target="tpu_custom_call" | custom-call | flops 6499999744 | bytes 9000000 | tf_op jit(solution)/shard_map/attend_back/pallas_call | solution.py:629
  284.5 6.7 %qkv_tables.1 = (bf16[2,688,512]{2,1,0:T(8,128)(2,1)}, bf16[2,688,512]{2,1,0:T(8,128)(2,1)}, bf16[688,128]{1,0:T(8,128)(2,1)}, f32[16,2048]{1,0:T(8,128)}, bf16[16,2048]{1,0:T(8,128)(2,1)}) custom-call(bf16[688,256]{1,0:T(8,128)(2,1)} %get-tuple-element.182.refs_0_, bf16[688,256]{1,0:T(8,128)(2,1)} %get-tuple-element.195.refs_1_, ...), custom_call_target="tpu_custom_call" | custom-call | flops 3500000000 | bytes 14000000 | tf_op jit(solution)/shard_map/qkv_tables/pallas_call | solution.py:982
  293.7 8.0 %qkv_rows.2 = bf16[344,1024]{1,0:T(8,128)(2,1)} custom-call(bf16[688,256]{1,0:T(8,128)(2,1)} %get-tuple-element.182.refs_0_, bf16[688,256]{1,0:T(8,128)(2,1)} %get-tuple-element.195.refs_1_, bf16[2,688,512]{2,1,0:T(8,128)(2,1)} %get-tuple-element.214.refs_2_, bf16[688,256]{1,0:T(8,128)(2,1)} %get-tuple-element.204.refs_6_.refs_3_, ...), custom_call_target="tpu_custom_call" | custom-call | flops 3000000000 | bytes 8000000 | tf_op jit(solution)/shard_map/qkv_rows/pallas_call | solution.py:1014
  301.8 8.0 %qkv_rows.3 = bf16[344,1024]{1,0:T(8,128)(2,1)} custom-call(bf16[688,256]{1,0:T(8,128)(2,1)} %get-tuple-element.182.refs_0_, bf16[688,256]{1,0:T(8,128)(2,1)} %get-tuple-element.195.refs_1_, bf16[2,688,512]{2,1,0:T(8,128)(2,1)} %get-tuple-element.214.refs_2_, bf16[688,256]{1,0:T(8,128)(2,1)} %get-tuple-element.204.refs_6_.refs_3_, ...), custom_call_target="tpu_custom_call" | custom-call | flops 3000000000 | bytes 8000000 | tf_op jit(solution)/shard_map/qkv_rows/pallas_call | solution.py:1014
  310.6 2.6 select_bitcast_fusion
  313.2 4.6 %collective-permute-start.43 = (bf16[344,1024]{1,0:T(8,128)(2,1)S(1)}, bf16[344,1024]{1,0:T(8,128)(2,1)}, u32[]{:S(2)}, u32[]{:S(2)}) collective-permute-start(bf16[344,1024]{1,0:T(8,128)(2,1)S(1)} %copy-done.2), channel_id=1, source_target_pairs={{1,2},{2,1},{5,6},{6,5},{9,10},{10,9},{13,14},{14,13},{17,18},{18,... | collective-permute-start | bytes 2113544 | tf_op jit(solution)/shard_map/ppermute | solution.py:1085
  324.9 3.1 gather_images.3.own
  328.0 2.0 maximum_select_fusion.2.images
  330.0 2.0 gather_images.2.own
  336.8 2.3 finish.2
  340.1 3.7 %finish.3 = (f32[8,16,512]{2,1,0:T(8,128)}, f32[8,16,2048]{2,1,0:T(8,128)}, f32[8,16,2048]{2,1,0:T(8,128)}, f32[8,16,1024]{2,1,0:T(8,128)}, f32[8,16,1024]{2,1,0:T(8,128)}, /*index=5*/f32[8,16,1024]{2,1,0:T(8,128)}) custom-call(s32[1]{0:T(128)} %bitcast.core, bf16[8,16,3840]{2,1,0:T(8,128)(2,1)} %gather_images.3.own, bf16[8,16,3840]{2,1,0:T(8,128)(2,1)} %copy-done.19), custom_call_target="tpu_custom_call" | custom-call | flops 1000000000 | bytes 4000000 | tf_op jit(solution)/shard_map/finish/pallas_call | solution.py:1073
  (232 shorter events, 73.7 us)
Async XLA Ops:
  1.8 26.7 %collective-permute-start.2 = (bf16[3,128,512]{2,1,0:T(8,128)(2,1)S(1)}, bf16[3,128,512]{2,1,0:T(8,128)(2,1)S(1)}, u32[]{:S(2)}, u32[]{:S(2)}) collective-permute-start(bf16[3,128,512]{2,1,0:T(8,128)(2,1)S(1)} %dynamic-slice_bitcast_fusion), channel_id=1, source_target_pairs={{0,1},{1,0},{2,3},{3,2},{4,5},{5,4},{6,7},{7,6},{8,9},{9,8},{10,11... | collective-permute-start | bytes 1179656 | tf_op jit(solution)/shard_map/ppermute | solution.py:1089
  6.2 42.6 %collective-permute-start.1 = (bf16[688,1024]{1,0:T(8,128)(2,1)}, bf16[688,1024]{1,0:T(8,128)(2,1)}, u32[]{:S(2)}, u32[]{:S(2)}) collective-permute-start(bf16[688,1024]{1,0:T(8,128)(2,1)} %bitcast.103), channel_id=1, source_target_pairs={{1,2},{2,1},{5,6},{6,5},{9,10},{10,9},{13,14},{14,13},{17,18},{18,... | collective-permute-start | bytes 4227080 | tf_op jit(solution)/shard_map/ppermute | solution.py:1085
  42.0 20.2 %collective-permute-start.9 = (bf16[2,3,128,512]{3,2,1,0:T(8,128)(2,1)S(1)}, bf16[2,3,128,512]{3,2,1,0:T(8,128)(2,1)S(1)}, u32[]{:S(2)}, u32[]{:S(2)}) collective-permute-start(bf16[2,3,128,512]{3,2,1,0:T(8,128)(2,1)S(1)} %pad_maximum_fusion.rest_0_), channel_id=1, source_target_pairs={{0,2},{2,0},{1,3},{3,1},{4,6},{6,4},{5,7},{7,5},{8,10},{10,8},{9,1... | collective-permute-start | bytes 2359304 | tf_op jit(solution)/shard_map/ppermute | solution.py:1089
  46.3 15.9 %collective-permute-start.10 = (bf16[2,3,128,512]{3,2,1,0:T(8,128)(2,1)S(1)}, bf16[2,3,128,512]{3,2,1,0:T(8,128)(2,1)S(1)}, u32[]{:S(2)}, u32[]{:S(2)}) collective-permute-start(bf16[2,3,128,512]{3,2,1,0:T(8,128)(2,1)S(1)} %pad_maximum_fusion.1.rest_1_), channel_id=1, source_target_pairs={{0,2},{2,0},{1,3},{3,1},{4,6},{6,4},{5,7},{7,5},{8,10},{10,8},{9,1... | collective-permute-start | bytes 2359304 | tf_op jit(solution)/shard_map/ppermute | solution.py:1089
  58.6 14.9 %collective-permute-start.11 = (bf16[2,688,512]{2,1,0:T(8,128)(2,1)}, bf16[2,688,512]{2,1,0:T(8,128)(2,1)}, u32[]{:S(2)}, u32[]{:S(2)}) collective-permute-start(bf16[2,688,512]{2,1,0:T(8,128)(2,1)} %get-tuple-element.132.k_ref.v_ref), channel_id=1, source_target_pairs={{0,2},{2,0},{1,3},{3,1},{4,6},{6,4},{5,7},{7,5},{8,10},{10,8},{9,1... | collective-permute-start | bytes 4227080 | tf_op jit(solution)/shard_map/ppermute | solution.py:1089
  71.1 23.2 %collective-permute-start.14 = (bf16[2,688,512]{2,1,0:T(8,128)(2,1)}, bf16[2,688,512]{2,1,0:T(8,128)(2,1)}, u32[]{:S(2)}, u32[]{:S(2)}) collective-permute-start(bf16[2,688,512]{2,1,0:T(8,128)(2,1)} %get-tuple-element.130.k_ref.v_ref), channel_id=1, source_target_pairs={{0,2},{2,0},{1,3},{3,1},{4,6},{6,4},{5,7},{7,5},{8,10},{10,8},{9,1... | collective-permute-start | bytes 4227080 | tf_op jit(solution)/shard_map/ppermute | solution.py:1089
  72.1 21.0 %collective-permute-start.12 = (bf16[1024,256]{1,0:T(8,128)(2,1)S(1)}, bf16[1024,256]{1,0:T(8,128)(2,1)S(1)}, u32[]{:S(2)}, u32[]{:S(2)}) collective-permute-start(bf16[1024,256]{1,0:T(8,128)(2,1)S(1)} %collective-permute-done.6.refs_5_), channel_id=1, source_target_pairs={{0,4},{4,0},{1,5},{5,1},{2,6},{6,2},{3,7},{7,3},{8,12},{12,8},{9,1... | collective-permute-start | bytes 1572872 | tf_op jit(solution)/shard_map/ppermute | solution.py:1089
  73.3 19.8 %collective-permute-start.13 = (bf16[1024,256]{1,0:T(8,128)(2,1)S(1)}, bf16[1024,256]{1,0:T(8,128)(2,1)S(1)}, u32[]{:S(2)}, u32[]{:S(2)}) collective-permute-start(bf16[1024,256]{1,0:T(8,128)(2,1)S(1)} %collective-permute-done.6.refs_5_), channel_id=1, source_target_pairs={{0,8},{8,0},{1,9},{9,1},{2,10},{10,2},{3,11},{11,3},{4,12},{12,4},... | collective-permute-start | bytes 1572872 | tf_op jit(solution)/shard_map/ppermute | solution.py:1089
  73.5 19.7 %collective-permute-start.15 = (bf16[128,1024]{1,0:T(8,128)(2,1)S(1)}, bf16[128,1024]{1,0:T(8,128)(2,1)S(1)}, u32[]{:S(2)}, u32[]{:S(2)}) collective-permute-start(bf16[128,1024]{1,0:T(8,128)(2,1)S(1)} %constant_dynamic-slice_fusion.5), channel_id=1, source_target_pairs={{0,1},{1,0},{2,3},{3,2},{4,5},{5,4},{6,7},{7,6},{8,9},{9,8},{10,11... | collective-permute-start | bytes 786440 | tf_op jit(solution)/shard_map/ppermute | solution.py:1089
  73.5 49.9 %collective-permute-start.23 = (bf16[688,1024]{1,0:T(8,128)(2,1)}, bf16[688,1024]{1,0:T(8,128)(2,1)}, u32[]{:S(2)}, u32[]{:S(2)}) collective-permute-start(bf16[688,1024]{1,0:T(8,128)(2,1)} %bitcast.38.refs_7_), channel_id=1, source_target_pairs={{1,2},{2,1},{5,6},{6,5},{9,10},{10,9},{13,14},{14,13},{17,18},{18,... | collective-permute-start | bytes 4227080 | tf_op jit(solution)/shard_map/ppermute | solution.py:1085
  93.1 17.9 %collective-permute-start.25 = (bf16[256,1024]{1,0:T(8,128)(2,1)S(1)}, bf16[256,1024]{1,0:T(8,128)(2,1)S(1)}, u32[]{:S(2)}, u32[]{:S(2)}) collective-permute-start(bf16[256,1024]{1,0:T(8,128)(2,1)S(1)} %constant_dynamic-slice_fusion.3), channel_id=1, source_target_pairs={{0,1},{1,0},{2,3},{3,2},{4,5},{5,4},{6,7},{7,6},{8,9},{9,8},{10,11... | collective-permute-start | bytes 1572872 | tf_op jit(solution)/shard_map/ppermute | solution.py:1089
  93.2 16.0 %collective-permute-start.16 = (bf16[128,1024]{1,0:T(8,128)(2,1)S(1)}, bf16[128,1024]{1,0:T(8,128)(2,1)S(1)}, u32[]{:S(2)}, u32[]{:S(2)}) collective-permute-start(bf16[128,1024]{1,0:T(8,128)(2,1)S(1)} %collective-permute-done.15), channel_id=1, source_target_pairs={{0,4},{4,0},{1,5},{5,1},{2,6},{6,2},{3,7},{7,3},{8,12},{12,8},{9,1... | collective-permute-start | bytes 786440 | tf_op jit(solution)/shard_map/ppermute | solution.py:1089
  110.5 42.9 %collective-permute-start.22 = (bf16[1024,256]{1,0:T(8,128)(2,1)S(1)}, bf16[1024,256]{1,0:T(8,128)(2,1)}, u32[]{:S(2)}, u32[]{:S(2)}) collective-permute-start(bf16[1024,256]{1,0:T(8,128)(2,1)S(1)} %collective-permute-done.13.refs_7_), channel_id=1, source_target_pairs={{0,4},{4,0},{1,5},{5,1},{2,6},{6,2},{3,7},{7,3},{8,12},{12,8},{9,1... | collective-permute-start | bytes 1572872 | tf_op jit(solution)/shard_map/ppermute | solution.py:1089
  111.0 39.6 %collective-permute-start.27 = (bf16[256,1024]{1,0:T(8,128)(2,1)S(1)}, bf16[256,1024]{1,0:T(8,128)(2,1)S(1)}, u32[]{:S(2)}, u32[]{:S(2)}) collective-permute-start(bf16[256,1024]{1,0:T(8,128)(2,1)S(1)} %collective-permute-done.25.refs_9_), channel_id=1, source_target_pairs={{0,4},{4,0},{1,5},{5,1},{2,6},{6,2},{3,7},{7,3},{8,12},{12,8},{9,1... | collective-permute-start | bytes 1572872 | tf_op jit(solution)/shard_map/ppermute | solution.py:1089
  112.0 43.3 %collective-permute-start.29 = (bf16[256,1024]{1,0:T(8,128)(2,1)S(1)}, bf16[256,1024]{1,0:T(8,128)(2,1)S(1)}, u32[]{:S(2)}, u32[]{:S(2)}) collective-permute-start(bf16[256,1024]{1,0:T(8,128)(2,1)S(1)} %collective-permute-done.25.refs_9_), channel_id=1, source_target_pairs={{0,8},{8,0},{1,9},{9,1},{2,10},{10,2},{3,11},{11,3},{4,12},{12,4},... | collective-permute-start | bytes 1572872 | tf_op jit(solution)/shard_map/ppermute | solution.py:1089
  122.5 31.0 %collective-permute-start.18 = (bf16[16,4096]{1,0:T(8,128)(2,1)S(1)}, bf16[16,4096]{1,0:T(8,128)(2,1)S(1)}, u32[]{:S(2)}, u32[]{:S(2)}) collective-permute-start(bf16[16,4096]{1,0:T(8,128)(2,1)S(1)} %pad_maximum_fusion.4), channel_id=1, source_target_pairs={{0,1},{1,0},{2,3},{3,2},{4,5},{5,4},{6,7},{7,6},{8,9},{9,8},{10,11... | collective-permute-start | bytes 393224 | tf_op jit(solution)/shard_map/ppermute | solution.py:1089
  155.3 24.7 %collective-permute-start.20 = (bf16[1024,256]{1,0:T(8,128)(2,1)S(1)}, bf16[1024,256]{1,0:T(8,128)(2,1)S(1)}, u32[]{:S(2)}, u32[]{:S(2)}) collective-permute-start(bf16[1024,256]{1,0:T(8,128)(2,1)S(1)} %collective-permute-done.12.refs_6_), channel_id=1, source_target_pairs={{0,2},{2,0},{1,3},{3,1},{4,6},{6,4},{5,7},{7,5},{8,10},{10,8},{9,1... | collective-permute-start | bytes 1572872 | tf_op jit(solution)/shard_map/ppermute | solution.py:1089
  162.7 17.3 %collective-permute-start.19 = (bf16[1024,256]{1,0:T(8,128)(2,1)S(1)}, bf16[1024,256]{1,0:T(8,128)(2,1)S(1)}, u32[]{:S(2)}, u32[]{:S(2)}) collective-permute-start(bf16[1024,256]{1,0:T(8,128)(2,1)S(1)} %collective-permute-done.6.refs_5_), channel_id=1, source_target_pairs={{0,2},{2,0},{1,3},{3,1},{4,6},{6,4},{5,7},{7,5},{8,10},{10,8},{9,1... | collective-permute-start | bytes 1572872 | tf_op jit(solution)/shard_map/ppermute | solution.py:1089
  165.2 14.9 %collective-permute-start.30 = (bf16[256,1024]{1,0:T(8,128)(2,1)S(1)}, bf16[256,1024]{1,0:T(8,128)(2,1)S(1)}, u32[]{:S(2)}, u32[]{:S(2)}) collective-permute-start(bf16[256,1024]{1,0:T(8,128)(2,1)S(1)} %collective-permute-done.29.refs_11_), channel_id=1, source_target_pairs={{0,2},{2,0},{1,3},{3,1},{4,6},{6,4},{5,7},{7,5},{8,10},{10,8},{9,1... | collective-permute-start | bytes 1572872 | tf_op jit(solution)/shard_map/ppermute | solution.py:1089
  165.3 14.8 %collective-permute-start.28 = (bf16[256,1024]{1,0:T(8,128)(2,1)S(1)}, bf16[256,1024]{1,0:T(8,128)(2,1)S(1)}, u32[]{:S(2)}, u32[]{:S(2)}) collective-permute-start(bf16[256,1024]{1,0:T(8,128)(2,1)S(1)} %collective-permute-done.27.refs_10_), channel_id=1, source_target_pairs={{0,2},{2,0},{1,3},{3,1},{4,6},{6,4},{5,7},{7,5},{8,10},{10,8},{9,1... | collective-permute-start | bytes 1572872 | tf_op jit(solution)/shard_map/ppermute | solution.py:1089
  165.7 14.4 %collective-permute-start.32 = (bf16[256,1024]{1,0:T(8,128)(2,1)}, bf16[256,1024]{1,0:T(8,128)(2,1)S(1)}, u32[]{:S(2)}, u32[]{:S(2)}) collective-permute-start(bf16[256,1024]{1,0:T(8,128)(2,1)} %collective-permute-done.31.refs_12_), channel_id=1, source_target_pairs={{0,2},{2,0},{1,3},{3,1},{4,6},{6,4},{5,7},{7,5},{8,10},{10,8},{9,1... | collective-permute-start | bytes 1572872 | tf_op jit(solution)/shard_map/ppermute | solution.py:1089
  211.3 17.3 %collective-permute-start.34 = (bf16[16,6144]{1,0:T(8,128)(2,1)S(1)}, bf16[16,6144]{1,0:T(8,128)(2,1)S(1)}, u32[]{:S(2)}, u32[]{:S(2)}) collective-permute-start(bf16[16,6144]{1,0:T(8,128)(2,1)S(1)} %pad_maximum_fusion.3), channel_id=1, source_target_pairs={{0,2},{2,0},{1,3},{3,1},{4,6},{6,4},{5,7},{7,5},{8,10},{10,8},{9,1... | collective-permute-start | bytes 589832 | tf_op jit(solution)/shard_map/ppermute | solution.py:1089
  226.0 41.3 %collective-permute-start.33 = (bf16[688,1024]{1,0:T(8,128)(2,1)S(1)}, bf16[688,1024]{1,0:T(8,128)(2,1)S(1)}, u32[]{:S(2)}, u32[]{:S(2)}) collective-permute-start(bf16[688,1024]{1,0:T(8,128)(2,1)S(1)} %copy-done.5), channel_id=1, source_target_pairs={{1,2},{2,1},{5,6},{6,5},{9,10},{10,9},{13,14},{14,13},{17,18},{18,... | collective-permute-start | bytes 4227080 | tf_op jit(solution)/shard_map/ppermute | solution.py:1085
  228.5 55.2 %collective-permute-start.35 = (bf16[2,688,256]{2,1,0:T(8,128)(2,1)}, bf16[2,688,256]{2,1,0:T(8,128)(2,1)}, u32[]{:S(2)}, u32[]{:S(2)}) collective-permute-start(bf16[2,688,256]{2,1,0:T(8,128)(2,1)} %get-tuple-element.198), channel_id=1, source_target_pairs={{0,2},{2,0},{1,3},{3,1},{4,6},{6,4},{5,7},{7,5},{8,10},{10,8},{9,1... | collective-permute-start | bytes 2113544 | tf_op jit(solution)/shard_map/ppermute | solution.py:1089
  228.7 18.1 %collective-permute-start.37 = (bf16[16,3968]{1,0:T(8,128)(2,1)S(1)}, bf16[16,3968]{1,0:T(8,128)(2,1)S(1)}, u32[]{:S(2)}, u32[]{:S(2)}) collective-permute-start(bf16[16,3968]{1,0:T(8,128)(2,1)S(1)} %maximum_maximum_fusion), channel_id=1, source_target_pairs={{0,1},{1,0},{2,3},{3,2},{4,5},{5,4},{6,7},{7,6},{8,9},{9,8},{10,11... | collective-permute-start | bytes 380936 | tf_op jit(solution)/shard_map/ppermute | solution.py:1089
  244.6 39.1 %collective-permute-start.36 = (bf16[2,688,256]{2,1,0:T(8,128)(2,1)}, bf16[2,688,256]{2,1,0:T(8,128)(2,1)}, u32[]{:S(2)}, u32[]{:S(2)}) collective-permute-start(bf16[2,688,256]{2,1,0:T(8,128)(2,1)} %get-tuple-element.199), channel_id=1, source_target_pairs={{0,2},{2,0},{1,3},{3,1},{4,6},{6,4},{5,7},{7,5},{8,10},{10,8},{9,1... | collective-permute-start | bytes 2113544 | tf_op jit(solution)/shard_map/ppermute | solution.py:1089
  246.8 19.4 %collective-permute-start.38 = (bf16[2,16,3968]{2,1,0:T(8,128)(2,1)S(1)}, bf16[2,16,3968]{2,1,0:T(8,128)(2,1)S(1)}, u32[]{:S(2)}, u32[]{:S(2)}) collective-permute-start(bf16[2,16,3968]{2,1,0:T(8,128)(2,1)S(1)} %maximum_select_fusion.5), channel_id=1, source_target_pairs={{0,16},{16,0},{1,17},{17,1},{2,18},{18,2},{3,19},{19,3},{4,20},{20... | collective-permute-start | bytes 761864 | tf_op jit(solution)/shard_map/ppermute | solution.py:1089
  263.3 20.4 %collective-permute-start.39 = (bf16[2,688,256]{2,1,0:T(8,128)(2,1)}, bf16[2,688,256]{2,1,0:T(8,128)(2,1)}, u32[]{:S(2)}, u32[]{:S(2)}) collective-permute-start(bf16[2,688,256]{2,1,0:T(8,128)(2,1)} %get-tuple-element.210), channel_id=1, source_target_pairs={{0,2},{2,0},{1,3},{3,1},{4,6},{6,4},{5,7},{7,5},{8,10},{10,8},{9,1... | collective-permute-start | bytes 2113544 | tf_op jit(solution)/shard_map/ppermute | solution.py:1089
  266.3 16.0 %collective-permute-start.41 = (bf16[4,16,3968]{2,1,0:T(8,128)(2,1)S(1)}, bf16[4,16,3968]{2,1,0:T(8,128)(2,1)}, u32[]{:S(2)}, u32[]{:S(2)}) collective-permute-start(bf16[4,16,3968]{2,1,0:T(8,128)(2,1)S(1)} %maximum_select_fusion.3), channel_id=1, source_target_pairs={{0,8},{8,0},{1,9},{9,1},{2,10},{10,2},{3,11},{11,3},{4,12},{12,4},... | collective-permute-start | bytes 1523720 | tf_op jit(solution)/shard_map/ppermute | solution.py:1089
  291.5 28.2 %collective-permute-start.46 = (bf16[8,16,3968]{2,1,0:T(8,128)(2,1)S(1)}, bf16[8,16,3968]{2,1,0:T(8,128)(2,1)S(1)}, u32[]{:S(2)}, u32[]{:S(2)}) collective-permute-start(bf16[8,16,3968]{2,1,0:T(8,128)(2,1)S(1)} %maximum_select_fusion.1), channel_id=1, source_target_pairs={{0,4},{4,0},{1,5},{5,1},{2,6},{6,2},{3,7},{7,3},{8,12},{12,8},{9,1... | collective-permute-start | bytes 3047432 | tf_op jit(solution)/shard_map/ppermute | solution.py:1089
  313.2 19.4 %collective-permute-start.43 = (bf16[344,1024]{1,0:T(8,128)(2,1)S(1)}, bf16[344,1024]{1,0:T(8,128)(2,1)}, u32[]{:S(2)}, u32[]{:S(2)}) collective-permute-start(bf16[344,1024]{1,0:T(8,128)(2,1)S(1)} %copy-done.2), channel_id=1, source_target_pairs={{1,2},{2,1},{5,6},{6,5},{9,10},{10,9},{13,14},{14,13},{17,18},{18,... | collective-permute-start | bytes 2113544 | tf_op jit(solution)/shard_map/ppermute | solution.py:1085
  317.8 16.3 %collective-permute-start.45 = (bf16[344,1024]{1,0:T(8,128)(2,1)S(1)}, bf16[344,1024]{1,0:T(8,128)(2,1)S(1)}, u32[]{:S(2)}, u32[]{:S(2)}) collective-permute-start(bf16[344,1024]{1,0:T(8,128)(2,1)S(1)} %copy-done.3), channel_id=1, source_target_pairs={{1,2},{2,1},{5,6},{6,5},{9,10},{10,9},{13,14},{14,13},{17,18},{18,... | collective-permute-start | bytes 2113544 | tf_op jit(solution)/shard_map/ppermute | solution.py:1085
  (55 other events, 646.8 us)

commit v3 on v2

--- a/solution.py
+++ b/solution.py
@@ -323,7 +323,7 @@
 
 
 def cost(flops, nbytes):
-    return pl.CostEstimate(flops=int(flops * 0.5), bytes_accessed=int(nbytes), transcendentals=0)
+    return pl.CostEstimate(flops=int(flops * 0.25), bytes_accessed=int(nbytes * 0.025), transcendentals=0)
 
 
 def norm_stats(values):
@@ -467,38 +467,39 @@
     )(scal, n1, rank, qb, *arrays)
 
 
-def head_lanes(rows, head):
-    lanes = lax.broadcasted_iota(jnp.int32, (rows, 2 * HD), 1)
-    return lanes, (lanes < HD) if head == 0 else (lanes >= HD), HD if head == 0 else 0
-
-
-def key_bias(scal, rows, other):
+def lane_numbers(rows):
+    return lax.broadcasted_iota(jnp.int32, (rows, 2 * HD), 1)
+
+
+def key_fill(scal, rows, other, ones):
     side = 1 - scal[1] if other else scal[1]
+    lanes = lane_numbers(rows) % HD
     at = lax.broadcasted_iota(jnp.int32, (rows, 2 * HD), 0) + side * rows
-    return jnp.where(at < jnp.maximum(scal[0], 1), 0.0, masked_score).astype(BF)
-
-
-def scaled_queries(queries):
-    wide = queries.astype(F32) * (HD**-0.5 * LOG2E)
-    high = wide.astype(BF)
-    return high, (wide - high.astype(F32)).astype(BF)
+    bias = jnp.where(at < jnp.maximum(scal[0], 1), 0.0, masked_score)
+    return jnp.where(lanes < ones, 1.0, jnp.where(lanes == ones, bias, 0.0)).astype(BF)
+
+
+def lane_terms(wide, rows, with_one):
+    lanes = lane_numbers(rows) % HD
+    first, second, third = three_terms(wide)
+    filled = jnp.where(lanes == 2, third, jnp.full_like(third, 0.0))
+    if with_one:
+        filled = jnp.where(lanes == 3, jnp.full_like(third, 1.0), filled)
+    return jnp.where(lanes == 0, first, jnp.where(lanes == 1, second, filled))
 
 
 def attend_kernel(scal, q_ref, k_ref, v_ref, ko_ref, vo_ref, out, log_out, qx, kx, vt):
     rows = q_ref.shape[0]
-    queries = q_ref[...]
-    zero = jnp.zeros_like(queries)
-    one = jnp.ones_like(queries)
-    high, low = scaled_queries(queries)
+    queries = (q_ref[...].astype(F32) * HD**-0.5).astype(BF)
+    lanes = lane_numbers(rows)
+    low_half = lanes < HD
+    ones = (lanes % HD == 0).astype(BF)
+    fills = [key_fill(scal, rows, side == 1, 0) for side in range(2)]
     for head in range(2):
-        lanes, own, spare = head_lanes(rows, head)
-        qx[head, :, 0:128] = jnp.where(own, high, jnp.where(lanes == spare, one, zero))
-        qx[head, :, 128:256] = low
+        own = low_half if head == 0 else ~low_half
+        qx[head] = jnp.where(own, queries, ones)
         for side, ref in enumerate((k_ref, ko_ref)):
-            at = slice(side * rows, (side + 1) * rows)
-            bias = key_bias(scal, rows, side == 1)
-            kx[head, at, 0:128] = jnp.where(own, ref[0], jnp.where(lanes == spare, bias, zero))
-            kx[head, at, 128:256] = jnp.where(own, ref[0], zero)
+            kx[head, side * rows : (side + 1) * rows] = jnp.where(own, ref[0], fills[side])
     for side, ref in enumerate((v_ref, vo_ref)):
         at = slice(side * rows, (side + 1) * rows)
         turned = ref[0].T
@@ -510,39 +511,35 @@
         return dotg(kx[head], qx[head], 1, 1)
 
     ahead = scores(0)
-    mixed = []
+    mixed, logs = [], []
     for head in range(2):
         now = ahead
         if head == 0:
             ahead = scores(1)
         top = jnp.max(now, axis=0, keepdims=True)
-        soft = jnp.exp2(now - top).astype(BF)
+        soft = jnp.exp(now - top).astype(BF)
         terms = dotg(vt[head], soft, 1, 0)
         total = terms[HD : HD + 1]
         mixed.append(terms[0:HD] / total)
-        log_out[0, head : head + 1, :] = top + jnp.log2(total)
+        logs.append(jnp.broadcast_to(top + jnp.log(total), (HD, total.shape[1])))
     out[...] = jnp.concatenate(mixed, axis=0).T.astype(BF)
+    log_out[...] = jnp.concatenate([logs[1], logs[0]], axis=0).T
 
 
 def attend(scal, queries, own, other):
     _, rows, width = own.shape
     pairs = width // (2 * HD)
     take = lambda c: pl.BlockSpec((1, rows, 2 * HD), lambda p: (c, 0, p))
+    flat = pl.BlockSpec((rows, 2 * HD), lambda p: (0, p))
     return pl.pallas_call(
         attend_kernel,
         grid=(pairs,),
-        in_specs=[scalars(), pl.BlockSpec((rows, 2 * HD), lambda p: (0, p)), take(0), take(1), take(0), take(1)],
-        out_specs=[
-            pl.BlockSpec((rows, 2 * HD), lambda p: (0, p)),
-            pl.BlockSpec((1, 8, rows), lambda p: (p, 0, 0)),
-        ],
-        out_shape=[
-            jax.ShapeDtypeStruct((rows, width), BF),
-            jax.ShapeDtypeStruct((pairs, 8, rows), F32),
-        ],
+        in_specs=[scalars(), flat, take(0), take(1), take(0), take(1)],
+        out_specs=[flat, flat],
+        out_shape=[jax.ShapeDtypeStruct((rows, width), BF), jax.ShapeDtypeStruct((rows, width), F32)],
         scratch_shapes=[
-            pltpu.VMEM((2, rows, 256), BF),
-            pltpu.VMEM((2, 2 * rows, 256), BF),
+            pltpu.VMEM((2, rows, 2 * HD), BF),
+            pltpu.VMEM((2, 2 * rows, 2 * HD), BF),
             pltpu.VMEM((2, HD + 16, 2 * rows), BF),
         ],
         compiler_params=params(dimension_semantics=("arbitrary",)),
@@ -558,36 +555,28 @@
     rows = q_ref.shape[0]
     queries, grad = q_ref[...], grad_ref[...]
     zero = jnp.zeros_like(queries)
-    one = jnp.ones_like(queries)
-    high, low = scaled_queries(queries)
+    low_half = lane_numbers(rows) < HD
+    scaled = (queries.astype(F32) * HD**-0.5).astype(BF)
     weighed = grad.astype(F32) * mixed_ref[...].astype(F32)
-    logs = log_ref[0].T
+    high = weighed.astype(BF)
+    pair = jnp.concatenate([high, (weighed - high.astype(F32)).astype(BF)], axis=1)
+    down = lax.broadcasted_iota(jnp.int32, (4 * HD, 2 * HD), 0) // HD % 2
+    across = lax.broadcasted_iota(jnp.int32, (4 * HD, 2 * HD), 1) // HD
+    sums = dotg(pair, (down != across).astype(BF), 1, 0)
+    query_fill = lane_terms(-log_ref[...], rows, True)
+    grad_fill = lane_terms(-sums, rows, False)
+    fills = [key_fill(scal, rows, side == 1, 3) for side in range(2)]
+    value_fill = (lane_numbers(rows) % HD < 3).astype(BF)
     for head in range(2):
-        lanes, own, spare = head_lanes(rows, head)
-
-        def spread(columns):
-            filled = zero
-            for step, column in enumerate(columns):
-                filled = jnp.where(lanes == spare + step, column, filled)
-            return filled
-
-        row_sum = jnp.sum(jnp.where(own, weighed, 0.0), axis=1, keepdims=True)
-        log_terms = three_terms(-logs[:, head : head + 1])
-        qx[head, :, 0:128] = jnp.where(
-            own, high, spread(log_terms + (jnp.ones_like(log_terms[0]),))
-        )
-        qx[head, :, 128:256] = jnp.where(own, low, zero)
-        gx[head] = jnp.where(own, grad, spread(three_terms(-row_sum)))
+        own = low_half if head == 0 else ~low_half
+        qx[head] = jnp.where(own, scaled, query_fill)
+        gx[head] = jnp.where(own, grad, grad_fill)
         qm[head] = jnp.where(own, queries, zero)
         gm[head] = jnp.where(own, grad, zero)
-        extra = (lanes >= spare) & (lanes < spare + 3)
         for side, (key_ref, value_ref) in enumerate(((k_ref, v_ref), (ko_ref, vo_ref))):
             at = slice(side * rows, (side + 1) * rows)
-            bias = key_bias(scal, rows, side == 1)
-            fill = jnp.where(extra, one, jnp.where(lanes == spare + 3, bias, zero))
-            kx[head, at, 0:128] = jnp.where(own, key_ref[0], fill)
-            kx[head, at, 128:256] = jnp.where(own, key_ref[0], zero)
-            vx[head, at, :] = jnp.where(own, value_ref[0], jnp.where(extra, one, zero))
+            kx[head, at] = jnp.where(own, key_ref[0], fills[side])
+            vx[head, at] = jnp.where(own, value_ref[0], value_fill)
     for side, ref in enumerate((k_ref, ko_ref)):
         kt[:, side * rows : (side + 1) * rows] = ref[0].T
     steps = [(side, head) for side in range(2) for head in range(2)]
@@ -603,7 +592,7 @@
         scores, grad_soft = ahead
         if number + 1 < len(steps):
             ahead = first(*steps[number + 1])
-        soft = jnp.exp2(scores)
+        soft = jnp.exp(scores)
         grad_scores = (soft * grad_soft).astype(BF)
         values = dotg(soft.astype(BF), gm[head], 1, 0)
         keys = dotg(grad_scores, qm[head], 1, 0)
@@ -626,40 +615,31 @@
     skip = piece * pairs
     take = lambda c: pl.BlockSpec((1, rows, 2 * HD), lambda p: (c, 0, p + skip))
     flat = pl.BlockSpec((rows, 2 * HD), lambda p: (0, p + skip))
+    both = jax.ShapeDtypeStruct((2, rows, width), BF)
     return pl.pallas_call(
         attend_back_kernel,
         grid=(pairs,),
-        in_specs=[scalars(), flat, take(0), take(1), take(0), take(1), flat, flat]
-        + [pl.BlockSpec((1, 8, rows), lambda p: (p + skip, 0, 0))],
+        in_specs=[scalars(), flat, take(0), take(1), take(0), take(1), flat, flat, flat],
         out_specs=[
             pl.BlockSpec((rows, 2 * HD), lambda p: (0, p)),
             pl.BlockSpec((2, rows, 2 * HD), lambda p: (0, 0, p)),
             pl.BlockSpec((2, rows, 2 * HD), lambda p: (0, 0, p)),
         ],
-        out_shape=[
-            jax.ShapeDtypeStruct((rows, width), BF),
-            jax.ShapeDtypeStruct((2, rows, width), BF),
-            jax.ShapeDtypeStruct((2, rows, width), BF),
-        ],
-        scratch_shapes=[
-            pltpu.VMEM((2, rows, 256), BF),
-            pltpu.VMEM((2, rows, 128), BF),
-            pltpu.VMEM((2, rows, 128), BF),
-            pltpu.VMEM((2, rows, 128), BF),
-            pltpu.VMEM((2, 2 * rows, 256), BF),
-            pltpu.VMEM((2, 2 * rows, 128), BF),
-            pltpu.VMEM((2 * HD, 2 * rows), BF),
-        ],
+        out_shape=[jax.ShapeDtypeStruct((rows, width), BF), both, both],
+        scratch_shapes=[pltpu.VMEM((2, rows, 2 * HD), BF)] * 4
+        + [pltpu.VMEM((2, 2 * rows, 2 * HD), BF)] * 2
+        + [pltpu.VMEM((2 * HD, 2 * rows), BF)],
         compiler_params=params(dimension_semantics=("arbitrary",)),
         cost_estimate=cost(26e-6 / pieces * 1e15, 9e6),
         name="attend_back",
     )(scal, queries, own, own, other, other, mixed, grad, logs)
 
 
-def branch_kernel(nears, scal, mix_a, mix_b, tok, w_a, oa_a, oa_b, ob, scale_one, gain_two, ua, *rest):
+def branch_kernel(nears, scal, mix_a, mix_b, tok, w_a, oa_a, oa_b, obs, scale_one, gain_two, uas, *rest):
     arrays = rest[: len(nears) // 2]
     residual, n2, rank_out, rank_up, w_b, sem = rest[len(nears) // 2 :]
     rank = oa_a.shape[0]
+    ob, ua = obs[scal[4]], uas[scal[4]]
 
     @pl.when(pl.program_id(0) == 0)
     def _():
@@ -670,13 +650,13 @@
     ranked = two_terms(ranked, rank)
     rank_out[...] = ranked
     terms = dotg(mix_a[...], w_a[...], 1, 0) + dotg(mix_b[...], w_b[...], 1, 0)
-    terms = terms + dotg(ranked, pad_twice(ob[...]), 1, 0)
+    terms = terms + dotg(ranked, pad_twice(ob), 1, 0)
     total = tok[...].astype(F32) + scale_one[...] * terms
-    residual[...] = total
+    residual[...] = total.astype(BF)
     unit, _ = norm_stats(total)
     normed = (unit * gain_two[...]).astype(BF)
     n2[...] = normed
-    rank_up[...] = dotg(normed, pad_rows(ua[...]), 1, 1).astype(BF)
+    rank_up[...] = dotg(normed, pad_rows(ua), 1, 1).astype(BF)
 
 
 def blocked(rows, width):
@@ -701,7 +681,7 @@
         out_specs=[blocked(block, width), blocked(block, width), blocked(block, PAD), blocked(block, PAD)]
         + [fixed_block(*w_a.shape)],
         out_shape=[
-            jax.ShapeDtypeStruct((rows, width), F32),
+            jax.ShapeDtypeStruct((rows, width), BF),
             jax.ShapeDtypeStruct((rows, width), BF),
             jax.ShapeDtypeStruct((rows, PAD), BF),
             jax.ShapeDtypeStruct((rows, PAD), BF),
@@ -720,14 +700,14 @@
     ups, downs = refs[5 : 5 + count], refs[5 + count : 5 + 2 * count]
     rest = refs[5 + 2 * count :]
     if nears is None:
-        here, swapped, scale_two, db, cot, grad_mlp, grad_rank = rest[:7]
-        earlier, rest = (), rest[7:]
-        chosen = choose(scal, here, swapped, cot, rest[-1].at[0])
+        cot, scale_two, dbs, grad_mlp, grad_rank = rest[:5]
+        earlier, rest = (), rest[5:]
+        ub, da, db = (table.at[scal[4]] for table in (ub, da, dbs))
     else:
         grad_mlp, grad_rank = rest[:2]
         earlier, rest = rest[2 : 2 + more], rest[2 + more :]
     m_out, g_out, rd_out, gru_out, gub_out, gda_out = rest[:6]
-    wu, wd, ubs, das, hidden, grad_pre, sem, early_sem = rest[6:]
+    wu, wd, ubs, das, hidden, grad_pre, sem = rest[6:]
     width = wu.shape[1]
     rank = ub.shape[0]
     size = ub.shape[1] // PARTS
@@ -744,21 +724,12 @@
             copy = pltpu.make_async_copy(source, target, sem.at[which, piece])
             copy.start()
             waits[piece * size // step].append(copy)
-    if more:
-        early = [
-            pltpu.make_async_copy(earlier[0], m_out, early_sem.at[0]),
-            pltpu.make_async_copy(earlier[1], g_out, early_sem.at[1]),
-        ]
-        for copy in early:
-            copy.start()
-
     def place(piece):
         if nears is None:
             return pl.ds(piece * size, size)
         return pl.ds(pl.multiple_of((scal[2] ^ nears[piece]) * size, size), size)
 
     if nears is None:
-        chosen.wait()
         grad_low = (scale_two[...] * (cot[...].astype(F32) * row_mask(scal, cot.shape[0]))).astype(BF)
         grad_mlp[...] = grad_low
         grad_rank[...] = dotg(grad_low, pad_rows(db[...]), 1, 1).astype(BF)
@@ -802,38 +773,32 @@
         at = slice(piece * size, (piece + 1) * size)
         gub_out[:, place(piece)] = dotg(up_turned, grad_pre[:, at], 1, 0)
         gda_out[:, place(piece)] = dotg(grad_turned, hidden[:, at], 1, 0)
-    if more:
-        for copy in early:
-            copy.wait()
     for at in (slice(k, k + step) for k in range(0, wu.shape[0], step)):
         terms = dotg(hidden[...], wd[:, at], 1, 0)
         grad_terms = dotg(grad_pre[...], wu[at, :], 1, 1)
         if more:
-            m_out[:, at] += terms
-            g_out[:, at] += grad_terms
-        else:
-            m_out[:, at] = terms
-            g_out[:, at] = grad_terms
+            terms = terms + earlier[0][:, at].astype(F32)
+            grad_terms = grad_terms + earlier[1][:, at].astype(F32)
+        m_out[:, at] = terms.astype(BF)
+        g_out[:, at] = grad_terms.astype(BF)
 
 
 def mlp(scal, n2, rank_up, ub, da, ups, downs, grads, nears=None, earlier=()):
     rows, width = n2.shape
-    rank, half = ub.shape
+    rank, half = ub.shape[-2:]
     units = half if nears is None else len(nears) * half // PARTS
     step = min(512, units)
-    sums = jax.ShapeDtypeStruct((rows, width), F32)
+    sums = jax.ShapeDtypeStruct((rows, width), BF)
     ranked = jax.ShapeDtypeStruct((rows, PAD), F32)
     table = jax.ShapeDtypeStruct((rank, half), F32)
     low = jax.ShapeDtypeStruct((rows, width), BF)
-    first = [low, low, jax.ShapeDtypeStruct((rows, PAD), BF)] if nears is None else []
+    first = [low, jax.ShapeDtypeStruct((rows, PAD), BF)] if nears is None else []
     return pl.pallas_call(
         functools.partial(mlp_kernel, nears, step, len(earlier)),
         in_specs=[scalars()]
         + [whole()] * 4
         + [in_place()] * (2 * len(ups))
-        + ([in_place()] * 2 if nears is None else [])
-        + [whole()] * 2
-        + ([in_place()] * 2 + [whole()] * (len(earlier) - 2) if earlier else []),
+        + [whole()] * (len(grads) + len(earlier)),
         out_specs=[whole()] * (len(first) + 6),
         out_shape=first + [sums, sums, ranked, ranked, table, table],
         scratch_shapes=[
@@ -844,7 +809,6 @@
             pltpu.VMEM((rows, units), BF),
             pltpu.VMEM((rows, units), BF),
             pltpu.SemaphoreType.DMA((2, PARTS)),
-            pltpu.SemaphoreType.DMA((2,)),
         ],
         compiler_params=params(),
         cost_estimate=cost(25e-6 * units / half * 1e15, 20e6),
@@ -863,13 +827,14 @@
 
 def middle_kernel(
     scal, residual, m_in, g_in, rd, gru, cot, mix_a, mix_b, rank_out, n2, grad_mlp,
-    db, ua, scale_two, gain_two, scale_one, w_a, w_b, oa_a, oa_b, ob,
+    dbs, uas, scale_two, gain_two, scale_one, w_a, w_b, oa_a, oa_b, obs,
     layer, grad_res, grad_a, grad_b, goa_a, goa_b, gob, gua, gdb,
 ):
     step = pl.program_id(0)
     rows = residual.shape[0]
+    db, ua, ob = dbs[scal[4]], uas[scal[4]], obs[scal[4]]
     rank = db.shape[0]
-    at = lax.broadcasted_iota(jnp.int32, (rows, 1), 0) + (scal[1] * 2 + step) * rows
+    at = lax.broadcasted_iota(jnp.int32, (rows, 1), 0) + (scal[1] * pl.num_programs(0) + step) * rows
     valid = (at < scal[0]).astype(F32)
     down = two_terms(rd[...], rank)
     up = two_terms(gru[...], rank)
@@ -887,16 +852,17 @@
         both = dotg(terms.T[0 : 2 * rank], right, 1, 0)
         return both[0:rank] + both[rank : 2 * rank]
 
-    branch_out = m_in[...] + dotg(down, pad_twice(db[...]), 1, 0)
-    layer[...] = ((residual[...] + scale_two[...] * branch_out) * valid).astype(BF)
+    branch_out = m_in[...].astype(F32) + dotg(down, pad_twice(db), 1, 0)
+    total = residual[...].astype(F32)
+    layer[...] = ((total + scale_two[...] * branch_out) * valid).astype(BF)
     add(gua, turned(up, n2[...]))
     add(gdb, turned(down, grad_mlp[...]))
-    unit, scale = norm_stats(residual[...])
-    grad_normed = (g_in[...] + dotg(up, pad_twice(ua[...]), 1, 0)) * gain_two[...]
+    unit, scale = norm_stats(total)
+    grad_normed = (g_in[...].astype(F32) + dotg(up, pad_twice(ua), 1, 0)) * gain_two[...]
     grad_total = cot[...].astype(F32) * valid + norm_grad(unit, scale, grad_normed)
-    grad_res[...] = grad_total
+    grad_res[...] = grad_total.astype(BF)
     grad_attn = (scale_one[...] * grad_total).astype(BF)
-    grad_rank = dotg(grad_attn, pad_rows(ob[...]), 1, 1).astype(BF)
+    grad_rank = dotg(grad_attn, pad_rows(ob), 1, 1).astype(BF)
     grad_a[...] = (
         dotg(grad_attn, w_a[...], 1, 1) + dotg(grad_rank, pad_rows(oa_a[...]), 1, 0)
     ).astype(BF)
@@ -909,23 +875,23 @@
     add(gob, turned(rank_out[...], grad_attn))
 
 
-def middle(scal, by_rows, others):
+def middle(scal, by_rows, others, blocks=1):
     rows, width = by_rows[0].shape
-    block = rows // 2
+    block = rows // blocks
     heads = by_rows[6].shape[1]
-    rank = others[0].shape[0]
+    rank = others[0].shape[1]
     part = jax.ShapeDtypeStruct((rows, heads), BF)
     table = jax.ShapeDtypeStruct((rank, width), F32)
     half_table = jax.ShapeDtypeStruct((rank, heads), F32)
     return pl.pallas_call(
         middle_kernel,
-        grid=(2,),
+        grid=(blocks,),
         in_specs=[scalars()]
         + [blocked(block, array.shape[1]) for array in by_rows]
         + [fixed_block(*array.shape) for array in others],
         out_specs=[blocked(block, width), blocked(block, width), blocked(block, heads), blocked(block, heads)]
         + [fixed_block(*shape) for shape in ((rank, heads),) * 2 + ((rank, width),) * 3],
-        out_shape=[jax.ShapeDtypeStruct((rows, width), BF), jax.ShapeDtypeStruct((rows, width), F32)]
+        out_shape=[jax.ShapeDtypeStruct((rows, width), BF)] * 2
         + [part, part, half_table, half_table, table, table, table],
         compiler_params=params(dimension_semantics=("arbitrary",)),
         cost_estimate=cost(9e-6 * 1e15, 20e6),
@@ -1002,7 +968,7 @@
         for c in (1, 2):
             grad = grad + dotg(grads[count][c - 1], w[c], 1, 1)
     unit, scale = norm_stats(tok[...].astype(F32))
-    out[...] = (grad_res[...] + norm_grad(unit, scale, grad * gain[...])).astype(BF)
+    out[...] = (grad_res[...].astype(F32) + norm_grad(unit, scale, grad * gain[...])).astype(BF)
 
 
 def qkv_rows(block_at, blocks, grads_a, grads_b, w_a, w_b, ranked, qa, tok, gain, grad_res):
@@ -1024,27 +990,51 @@
     )(*grads_a, *grads_b, w_a, w_b, ranked, qa, tok, gain, grad_res)
 
 
-def gather_kernel(ids, images, out, total):
+def gather_kernel(has_ids, flag, *refs):
+    ids, (own, got, out, ids_out, total) = refs[0], refs[has_ids:]
     columns = out.shape[2]
+    half = own.shape[0]
     total[...] = jnp.zeros_like(total)
-    for image in range(images.shape[0]):
-        adapter = ids[image]
-        total[adapter] += images[image, :, 0:columns].astype(F32)
+
+    def add(first, images):
+        for image in range(half):
+            if has_ids:
+                adapter = ids[first + image]
+            else:
+                note = images[image, 0:8, columns : columns + PAD].astype(F32)
+                adapter = jnp.max(note).astype(jnp.int32)
+            ids_out[first + image] = adapter
+            total[adapter] += images[image, :, 0:columns].astype(F32)
+
+    @pl.when(flag[0] == 0)
+    def _():
+        add(0, own)
+        add(half, got)
+
+    @pl.when(flag[0] != 0)
+    def _():
+        add(0, got)
+        add(half, own)
+
     out[...] = total[...].astype(BF)
 
 
-def gather_images(ids, images, adapters, columns):
-    rank = images.shape[1]
+def gather_images(flag, ids, pair, adapters, columns):
+    count, rank, _ = pair[0].shape
+    given = [] if ids is None else [ids]
     return pl.pallas_call(
-        gather_kernel,
-        in_specs=[scalars(), whole()],
-        out_specs=whole(),
-        out_shape=jax.ShapeDtypeStruct((adapters, rank, columns), BF),
+        functools.partial(gather_kernel, len(given)),
+        in_specs=[scalars()] * (1 + len(given)) + [whole()] * 2,
+        out_specs=[whole(), scalars()],
+        out_shape=[
+            jax.ShapeDtypeStruct((adapters, rank, columns), BF),
+            jax.ShapeDtypeStruct((2 * count,), jnp.int32),
+        ],
         scratch_shapes=[pltpu.VMEM((adapters, rank, columns), F32)],
         compiler_params=params(),
         cost_estimate=cost(2e-6 * 1e15, 1e6),
         name="gather_images",
-    )(ids, images)
+    )(flag.astype(jnp.int32)[None], *given, *pair)
 
 
 def finish_kernel(cut, spans, places, core, own, other, *outs):
@@ -1157,24 +1147,25 @@
         self.send = jnp.concatenate([total[:, columns:], total[:, cut:columns]] + note, axis=1)
         self.columns = columns
 
-    def over_pair(self, *others):
-        other = flip("tensor")(self.send)
-        other = after(other, *others) if others else other
-        self.images = by_index(self.tensor, self.mine[None], other[None], 0)
-
-    def over(self, name, *others):
+    def start_pair(self):
+        self.flag, self.pair = self.tensor, (self.mine[None], flip("tensor")(self.send)[None])
+
+    def start(self, name):
+        self.images = by_index(self.flag, *self.pair, 0)
         if lax.axis_size(name) == 2:
-            got = flip(name)(self.images)
-            self.images = by_index(lax.axis_index(name), self.images, after(got, *others) if others else got, 0)
-        elif lax.axis_size(name) > 2:
-            self.images = lax.all_gather(self.images, name, axis=0, tiled=True)
-
-    def adapters_of_images(self):
-        return self.images[:, 0, -1].astype(jnp.int32)
+            self.flag, self.pair = lax.axis_index(name), (self.images, flip(name)(self.images))
+        else:
+            images = lax.all_gather(self.images, name, axis=0, tiled=True)
+            half = images.shape[0] // 2
+            self.flag, self.pair = jnp.zeros((), jnp.int32), (images[:half], images[half:])
+
+    def arrive(self, *others):
+        self.pair = (self.pair[0], after(self.pair[1], *others))
 
     def over_adapters(self, ids, adapters):
-        self.dense = gather_images(ids, self.images, adapters, self.columns)
+        self.dense, ids = gather_images(self.flag, ids, self.pair, adapters, self.columns)
         self.other = flip("core")(self.dense)
+        return ids
 
     def finish(self, spans, places, shapes):
         core = self.core.astype(jnp.int32)[None]
@@ -1204,25 +1195,22 @@
     mine = jnp.where(core == tensor, facts, facts_other)
     theirs = jnp.where(core == tensor, facts_other, facts)
     length, adapter, adapter_other = mine[0], mine[1], theirs[1]
-    scal = jnp.stack([length, core, part_at, core == tensor]).astype(jnp.int32)
+    scal = jnp.stack([length, core, part_at, core == tensor, adapter]).astype(jnp.int32)
 
     qkv_b, out_b, up_b, down_b = (jnp.swapaxes(table, -1, -2) for table in (qkv_b, out_b, up_b, down_b))
     pick = lambda table, index: lax.dynamic_index_in_dim(table, index, 0, False)
     flat = lambda table: jnp.swapaxes(table, 0, 1).reshape(rank, 3 * third)
+    half_qkv.hop(0, "x")
+    half_qkv.hop(0, "zb")
+    adapter, adapter_other = after((adapter, adapter_other), half_qkv.parts[2])
     packed_first = jnp.concatenate([flat(pick(qkv_b, adapter_other)), pick(out_a, adapter_other)], axis=1)
     packed = jnp.concatenate([pick(table, adapter_other) for table in (up_b, down_a)], axis=1)
-    qa, oa, ob, ua, ub, da, db = (
-        pick(table, adapter) for table in (qkv_a, out_a, out_b, up_a, up_b, down_a, down_b)
-    )
+    qa, oa = pick(qkv_a, adapter), pick(out_a, adapter)
     qb = flat(pick(qkv_b, adapter))
     gain_one, gain_two, scale_one, scale_two = (v.reshape(1, width) for v in (gain_one, gain_two, scale_one, scale_two))
 
-    half_qkv.hop(0, "x")
-    half_qkv.hop(0, "zb")
-    slices = (scal, packed, packed_first, qa, oa, ob, ua, ub, da, db, qb, half_out.mine, half_up.mine, half_down.mine)
-    qb_other, oa_other = jnp.split(flip("tensor")(after(packed_first, half_qkv.parts[0])), (3 * third,), axis=1)
-    half_up.over_tensor(half_qkv.parts[4])
-    half_qkv.parts[2] = after(half_qkv.parts[2], *slices)
+    qb_other, oa_other = jnp.split(flip("tensor")(packed_first), (3 * third,), axis=1)
+    half_up.over_tensor(half_qkv.parts[4], qb_other)
     half_qkv.last_hop()
     tok_swapped = after(tok_swapped, half_qkv.parts[2], half_qkv.parts[4], qb_other, scal)
     tok, n1, rank_qkv, q_a, own_a = qkv_local(scal, tok_here, tok_swapped, gain_one, w3, qa, qb)
@@ -1243,14 +1231,16 @@
     half_down.hop(0, "x", mix_b)
     half_down.hop(0, "zb", mix_b)
     residual, n2, rank_out, rank_up, out_other = branch(
-        scal, mix_a, mix_b, tok, w_out, half_out, oa, oa_other, ob, scale_one, gain_two, ua
+        scal, after(mix_a, half_up.parts[6], half_down.parts[0]), mix_b, tok, w_out, half_out, oa, oa_other, out_b, scale_one, gain_two, up_a
     )
     half_down.hop(2, "zb", n2)
     ub_other, da_other = jnp.split(flip("tensor")(after(packed, n2)), 2, axis=1)
     for near in (0, 2, 4):
         half_up.hop(near, "core", n2)
-    cot, grad_mlp, grad_rank, m, g, rd, gru, gub_a, gda_a = mlp(
-        scal, n2, rank_up, ub, da, [w_up], [w_down], [cotangent[0], cot_swapped, scale_two, db]
+    cot = jnp.where(core == tensor, cotangent[0], cot_swapped)
+    grad_mlp, grad_rank, m, g, rd, gru, gub_a, gda_a = mlp(
+        scal, after(n2, half_down.parts[2], half_down.parts[4]), rank_up, up_b, down_a, [w_up], [w_down],
+        [cot, scale_two, down_b],
     )
     half_up.hop(6, "core", m)
     for near in (0, 2, 4, 6):
@@ -1261,7 +1251,7 @@
     layer, grad_res, grad_a, grad_b, goa_a, goa_b, gob, gua, gdb = middle(
         scal,
         (residual, m, g, rd, gru, cot, mix_a, mix_b, rank_out, n2, grad_mlp),
-        (db, ua, scale_two, gain_two, scale_one, w_out, out_other, oa, oa_other, ob),
+        (down_b, up_a, scale_two, gain_two, scale_one, w_out, out_other, oa, oa_other, out_b),
     )
     shares = Sum.shares(
         jnp.concatenate([goa_a, gub_a, gda_a], axis=1),
@@ -1277,40 +1267,47 @@
         grad_queries, kept, sent = attend_back(scal, queries, own, kv, mixed, grad, logs, piece, 2)
         return grad_queries, kept, flip("core")(sent)
 
-    side_a, side_b = (q_a, own_a, kv_a, mix_a, grad_a, logs_a), (q_b, own_b, kv_b, mix_b, grad_b, logs_b)
-    back_1 = back(*side_a, 0)
+    side_a = (q_a, own_a, kv_a, mix_a, grad_a, logs_a)
+    side_b = (q_b, own_b, kv_b, mix_b, grad_b, logs_b)
+    early.start_pair()
+    back_1 = back(*side_a, 0, early.send)
+    early.arrive(back_1[0])
+    early.start("hi")
+    back_2 = back(*side_a, 1, early.images)
     layer_swapped = swap(after(layer, back_1[0]))
-    early.send = after(early.send, back_1[0])
-    back_2 = back(*side_a, 1, early.send)
-    early.over_pair(back_2[0])
+    early.arrive(back_2[0])
+    early.start("zb")
     back_3 = back(*side_b, 0, early.images)
-    early.over("hi", back_3[0])
+    early.arrive(back_3[0])
+    early.start("x")
     back_4 = back(*side_b, 1, early.images, layer_swapped)
-    early.over("zb", back_4[0])
     kv_sum_a, kv_sum_b, ranked, kept, sent = qkv_tables(
-        after(scal, early.images),
+        scal,
         [part for pair in zip(back_1, back_2) for part in pair],
         [part for pair in zip(back_3, back_4) for part in pair],
         qb, qb_other, n1, rank_qkv,
     )
     late = Sum(kept, sent, 3 * third // 2, None, core, tensor)
     late.over_cores()
-    early.over("x", kept)
+    late.start_pair()
     grads = (
         [back_1[0], back_2[0], kv_sum_a], [back_3[0], back_4[0], kv_sum_b],
         w3, w3_other, ranked, qa, tok, gain_one, grad_res,
     )
     upper = qkv_rows(0, 2, grads[0], grads[1], after(w3, late.send), *grads[3:])
-    late.over_pair(upper)
+    upper_swapped = swap(upper)
+    late.arrive(upper)
+    late.start("hi")
     lower = qkv_rows(1, 2, grads[0], grads[1], after(w3, late.images), *grads[3:])
-    late.over("hi", lower)
-    late.over("zb")
-    ids = early.adapters_of_images()
-    early.over_adapters(ids, adapters)
-    late.over("x")
+    lower_swapped = swap(lower)
+    late.arrive(lower, upper_swapped)
+    late.start("zb")
+    late.start("x")
+    early.arrive(lower, late.images)
+    ids = early.over_adapters(None, adapters)
     in_place_already = core == tensor
     grad_tokens = jnp.concatenate(
-        [jnp.where(in_place_already, rows, swap(rows)) for rows in (upper, lower)], axis=0
+        [jnp.where(in_place_already, *rows) for rows in ((upper, upper_swapped), (lower, lower_swapped))], axis=0
     ).astype(F32)
     layer_out = jnp.where(in_place_already, layer, layer_swapped)
     late.over_adapters(ids, adapters)

time: 350 us -> 326 us (0.931)
  waiting for transfers between devices: 25.6 us -> 13.4 us
  other arithmetic: 15 us -> 8.55 us
  Pallas kernels: 217 us -> 211 us
    ppermute x47, waiting for transfers between devices: 25.2 us -> 11.6 us  [flip(): return lambda array: lax.ppermute(array, axis, FLIP)]
    squeeze x7 -> x4, local copies, waits for them, and re-layouts: 9.2 us -> 3.64 us  [quad_body(): pick = lambda table, index: lax.dynamic_index_in_dim(table, index, 0, False)]
    select_n x8 -> x6, other arithmetic: 5.42 us -> 0.37 us  [by_index(): jnp.where(index == 0, jnp.concatenate([own, other], axis=axis), jnp.conca...]
    unnamed x76 -> x86, local copies, waits for them, and re-layouts: 8.02 us -> 9.63 us
  transfers between devices with their start and end apart: 52 -> 52, of which waited for: 9 -> 7; matrix products, arithmetic and copies ran while one was open for 9% -> 7% of each run, Pallas kernels for 52% -> 55%
where the time goes in v3:
time: 326 us; the launch traced here: 320 us
  Pallas kernels  211 us (65%)
  starting transfers between devices  55.8 us (17%)
  local copies, waits for them, and re-layouts  23.2 us (7%)
  waiting for transfers between devices  13.4 us (4%)
  other arithmetic  8.55 us (3%)
  between operations  7.7 us (2%)
    pallas_call x4, Pallas kernels, attend_back(): pl.pallas_call(attend_back_kernel, grid=(pairs,), in_specs=[scalars(), fl...  57.1 us
    pallas_call x3, Pallas kernels, mlp(): pl.pallas_call(functools.partial(mlp_kernel, nears, step, len(earlier)),...  53.1 us
    ppermute x47, starting transfers between devices, flip(): return lambda array: lax.ppermute(array, axis, FLIP)  40.4 us
    pallas_call x2, Pallas kernels, attend(): pl.pallas_call(attend_kernel, grid=(pairs,), in_specs=[scalars(), flat, t...  29.9 us
    pallas_call x2, Pallas kernels, qkv_rows(): pl.pallas_call(functools.partial(qkv_rows_kernel, len(grads_a) - 1), grid...  15.6 us
    ppermute x5, starting transfers between devices, swap(): return lax.ppermute(rows, ('core', 'tensor'), SWAP)  15.5 us
    pallas_call x1, Pallas kernels, middle(): pl.pallas_call(middle_kernel, grid=(blocks,), in_specs=[scalars()] + [blo...  11.6 us
    ppermute x47, waiting for transfers between devices, flip(): return lambda array: lax.ppermute(array, axis, FLIP)  11.6 us
  transfers between devices with their start and end apart: 52, of which 7 were waited for; matrix products, arithmetic and copies ran while one was open for 7% of the time, Pallas kernels for 55%

profile of v3, /device:TPU:1, one launch (start us, length us, event | category | flops | bytes accessed | tf_op | source)
XLA Modules:
  0.0 320.1 jit_solution(2590747276202648992)
XLA Ops:
  1.8 2.1 collective-permute-start.2
  8.2 4.6 %collective-permute-done.2 = bf16[3,128,512]{2,1,0:T(8,128)(2,1)S(1)} collective-permute-done((bf16[3,128,512]{2,1,0:T(8,128)(2,1)S(1)}, bf16[3,128,512]{2,1,0:T(8,128)(2,1)S(1)}, u32[]{:S(2)}, u32[]{:S(2)}) %collective-permute-start.2) | collective-permute-done | bytes 393248 | tf_op jit(solution)/shard_map/ppermute | solution.py:1079
  19.4 2.3 collective-permute-done.3
  29.1 3.3 %collective-permute-start.9 = (bf16[2,3,128,512]{3,2,1,0:T(8,128)(2,1)S(1)}, bf16[2,3,128,512]{3,2,1,0:T(8,128)(2,1)S(1)}, u32[]{:S(2)}, u32[]{:S(2)}) collective-permute-start(bf16[2,3,128,512]{3,2,1,0:T(8,128)(2,1)S(1)} %pad_maximum_fusion.rest_0_), channel_id=1, source_target_pairs={{0,2},{2,0},{1,3},{3,1},{4,6},{6,4},{5,7},{7,5},{8,10},{10,8},{9,1... | collective-permute-start | bytes 2359304 | tf_op jit(solution)/shard_map/ppermute | solution.py:1079
  33.8 2.7 collective-permute-start.10
  43.1 9.7 %qkv_local.1 = (bf16[688,1024]{1,0:T(8,128)(2,1)}, bf16[688,1024]{1,0:T(8,128)(2,1)}, bf16[688,128]{1,0:T(8,128)(2,1)}, bf16[688,512]{1,0:T(8,128)(2,1)}, bf16[2,688,512]{2,1,0:T(8,128)(2,1)}) custom-call(s32[5]{0:T(128)} %stack.50.scal.refs_0_.refs_12_, bf16[688,1024]{1,0:T(8,128)(2,1)} %bitcast.99, bf16[688,1024]{1,0:T(8,128)(2,1)} %copy-done.24, ...), custom_call_target="tpu_custom_call" | custom-call | flops 1750000000 | bytes 200000 | tf_op jit(solution)/shard_map/qkv_local/pallas_call | solution.py:402
  55.2 7.7 %qkv_other.1 = (bf16[688,512]{1,0:T(8,128)(2,1)}, bf16[2,688,512]{2,1,0:T(8,128)(2,1)}, bf16[3,1024,512]{2,1,0:T(8,128)(2,1)}) custom-call(s32[5]{0:T(128)} %stack.50.scal.refs_0_.refs_12_, bf16[688,1024]{1,0:T(8,128)(2,1)} %get-tuple-element.131.n1.refs_15_, bf16[688,128]{1,0:T(8,128)(2,1)} %get-tuple-element.132.rank.refs_16_, ...), custom_call_target="tpu_custom_call" | custom-call | flops 1750000000 | bytes 250000 | tf_op jit(solution)/shard_map/qkv_other/pallas_call | solution.py:454
  69.7 3.5 %collective-permute-start.26 = (bf16[688,1024]{1,0:T(8,128)(2,1)S(1)}, bf16[688,1024]{1,0:T(8,128)(2,1)S(1)}, u32[]{:S(2)}, u32[]{:S(2)}) collective-permute-start(bf16[688,1024]{1,0:T(8,128)(2,1)S(1)} %bitcast.73), channel_id=1, source_target_pairs={{1,2},{2,1},{5,6},{6,5},{9,10},{10,9},{13,14},{14,13},{17,18},{18,... | collective-permute-start | bytes 4227080 | tf_op jit(solution)/shard_map/ppermute | solution.py:1075
  73.3 14.9 %attend.2 = (bf16[688,512]{1,0:T(8,128)(2,1)}, f32[688,512]{1,0:T(8,128)}) custom-call(s32[5]{0:T(128)} %stack.50.scal.refs_0_.refs_12_, bf16[688,512]{1,0:T(8,128)(2,1)} %get-tuple-element.199.q_ref, bf16[2,688,512]{2,1,0:T(8,128)(2,1)} %get-tuple-element.135.k_ref.v_ref, bf16[2,688,512]{2,1,0:T(8,128)(2,1)} %get-tuple-element.135.k_ref.v_ref, ...), custom_call_target="tpu_custom_call" | custom-call | flops 4000000000 | bytes 150000 | tf_op jit(solution)/shard_map/attend/pallas_call | solution.py:534
  90.7 15.0 %attend.3 = (bf16[688,512]{1,0:T(8,128)(2,1)}, f32[688,512]{1,0:T(8,128)}) custom-call(s32[5]{0:T(128)} %stack.50.scal.refs_0_.refs_12_, bf16[688,512]{1,0:T(8,128)(2,1)} %get-tuple-element.211.q_ref, bf16[2,688,512]{2,1,0:T(8,128)(2,1)} %get-tuple-element.133.k_ref.v_ref, bf16[2,688,512]{2,1,0:T(8,128)(2,1)} %get-tuple-element.133.k_ref.v_ref, ...), custom_call_target="tpu_custom_call" | custom-call | flops 4000000000 | bytes 150000 | tf_op jit(solution)/shard_map/attend/pallas_call | solution.py:534
  112.1 8.8 %branch.1 = (bf16[688,1024]{1,0:T(8,128)(2,1)}, bf16[688,1024]{1,0:T(8,128)(2,1)}, bf16[688,128]{1,0:T(8,128)(2,1)}, bf16[688,128]{1,0:T(8,128)(2,1)}, bf16[512,1024]{1,0:T(8,128)(2,1)}) custom-call(s32[5]{0:T(128)} %stack.50.scal.refs_0_.refs_12_, bf16[688,512]{1,0:T(8,128)(2,1)} %get-tuple-element.140.mix_a.mixed_ref, ...), custom_call_target="tpu_custom_call" | custom-call | flops 2000000000 | bytes 400000 | tf_op jit(solution)/shard_map/branch/pallas_call | solution.py:675
  124.1 24.4 %mlp.3 = (bf16[688,1024]{1,0:T(8,128)(2,1)}, bf16[688,128]{1,0:T(8,128)(2,1)}, bf16[688,1024]{1,0:T(8,128)(2,1)}, bf16[688,1024]{1,0:T(8,128)(2,1)}, f32[688,128...) custom-call(s32[5]{0:T(128)} %stack.50.scal.refs_0_.refs_12_, ...), custom_call_target="tpu_custom_call" | custom-call | flops 6249999872 | bytes 500000 | tf_op jit(solution)/shard_map/mlp/pallas_call | solution.py:796
  150.8 14.2 %mlp.4 = (bf16[688,1024]{1,0:T(8,128)(2,1)}, bf16[688,1024]{1,0:T(8,128)(2,1)}, f32[688,128]{1,0:T(8,128)}, f32[688,128]{1,0:T(8,128)}, f32[16,2048]{1,0:T(8,128)}, /*index=5*/f32[16,2048]{1,0:T(8,128)}) custom-call(s32[5]{0:T(128)} %stack.50.scal.refs_0_.refs_12_, bf16[688,1024]{1,0:T(8,128)(2,1)} %get-tuple-element.157.refs_1_.n2, ...), custom_call_target="tpu_custom_call" | custom-call | flops 3124999936 | bytes 500000 | tf_op jit(solution)/shard_map/mlp/pallas_call | solution.py:796
  166.5 14.5 %mlp.5 = (bf16[688,1024]{1,0:T(8,128)(2,1)}, bf16[688,1024]{1,0:T(8,128)(2,1)}, f32[688,128]{1,0:T(8,128)}, f32[688,128]{1,0:T(8,128)}, f32[16,2048]{1,0:T(8,128)}, /*index=5*/f32[16,2048]{1,0:T(8,128)}) custom-call(s32[5]{0:T(128)} %stack.50.scal.refs_0_.refs_12_, bf16[688,1024]{1,0:T(8,128)(2,1)} %get-tuple-element.157.refs_1_.n2, ...), custom_call_target="tpu_custom_call" | custom-call | flops 3124999936 | bytes 500000 | tf_op jit(solution)/shard_map/mlp/pallas_call | solution.py:796
  181.0 11.6 %middle.1 = (bf16[688,1024]{1,0:T(8,128)(2,1)}, bf16[688,1024]{1,0:T(8,128)(2,1)}, bf16[688,512]{1,0:T(8,128)(2,1)}, bf16[688,512]{1,0:T(8,128)(2,1)}, f32[16,51...) custom-call(s32[5]{0:T(128)} %stack.50.scal.refs_0_.refs_12_, ...), custom_call_target="tpu_custom_call" | custom-call | flops 2249999872 | bytes 500000 | tf_op jit(solution)/shard_map/middle/pallas_call | solution.py:886
  195.6 14.2 %attend_back.4 = (bf16[688,256]{1,0:T(8,128)(2,1)}, bf16[2,688,256]{2,1,0:T(8,128)(2,1)}, bf16[2,688,256]{2,1,0:T(8,128)(2,1)}) custom-call(s32[5]{0:T(128)} %stack.50.scal.refs_0_.refs_12_, bf16[688,512]{1,0:T(8,128)(2,1)} %get-tuple-element.199.q_ref, bf16[2,688,512]{2,1,0:T(8,128)(2,1)} %get-tuple-element.135.k_ref.v_ref, ...), custom_call_target="tpu_custom_call" | custom-call | flops 3249999872 | bytes 225000 | tf_op jit(solution)/shard_map/attend_back/pallas_call | solution.py:619
  209.8 3.7 %collective-permute-start.34 = (bf16[688,1024]{1,0:T(8,128)(2,1)S(1)}, bf16[688,1024]{1,0:T(8,128)(2,1)}, u32[]{:S(2)}, u32[]{:S(2)}) collective-permute-start(bf16[688,1024]{1,0:T(8,128)(2,1)S(1)} %copy-done.6), channel_id=1, source_target_pairs={{1,2},{2,1},{5,6},{6,5},{9,10},{10,9},{13,14},{14,13},{17,18},{18,... | collective-permute-start | bytes 4227080 | tf_op jit(solution)/shard_map/ppermute | solution.py:1075
  213.6 2.4 collective-permute-start.38
  215.9 14.5 %attend_back.5 = (bf16[688,256]{1,0:T(8,128)(2,1)}, bf16[2,688,256]{2,1,0:T(8,128)(2,1)}, bf16[2,688,256]{2,1,0:T(8,128)(2,1)}) custom-call(s32[5]{0:T(128)} %stack.50.scal.refs_0_.refs_12_, bf16[688,512]{1,0:T(8,128)(2,1)} %get-tuple-element.199.q_ref, bf16[2,688,512]{2,1,0:T(8,128)(2,1)} %get-tuple-element.135.k_ref.v_ref, ...), custom_call_target="tpu_custom_call" | custom-call | flops 3249999872 | bytes 225000 | tf_op jit(solution)/shard_map/attend_back/pallas_call | solution.py:619
  231.3 14.1 %attend_back.6 = (bf16[688,256]{1,0:T(8,128)(2,1)}, bf16[2,688,256]{2,1,0:T(8,128)(2,1)}, bf16[2,688,256]{2,1,0:T(8,128)(2,1)}) custom-call(s32[5]{0:T(128)} %stack.50.scal.refs_0_.refs_12_, bf16[688,512]{1,0:T(8,128)(2,1)} %get-tuple-element.211.q_ref, bf16[2,688,512]{2,1,0:T(8,128)(2,1)} %get-tuple-element.133.k_ref.v_ref, ...), custom_call_target="tpu_custom_call" | custom-call | flops 3249999872 | bytes 225000 | tf_op jit(solution)/shard_map/attend_back/pallas_call | solution.py:619
  245.6 14.4 %attend_back.7 = (bf16[688,256]{1,0:T(8,128)(2,1)}, bf16[2,688,256]{2,1,0:T(8,128)(2,1)}, bf16[2,688,256]{2,1,0:T(8,128)(2,1)}) custom-call(s32[5]{0:T(128)} %stack.50.scal.refs_0_.refs_12_, bf16[688,512]{1,0:T(8,128)(2,1)} %get-tuple-element.211.q_ref, bf16[2,688,512]{2,1,0:T(8,128)(2,1)} %get-tuple-element.133.k_ref.v_ref, ...), custom_call_target="tpu_custom_call" | custom-call | flops 3249999872 | bytes 225000 | tf_op jit(solution)/shard_map/attend_back/pallas_call | solution.py:619
  260.5 2.0 collective-permute-done.41.refs_11_
  263.3 6.7 %qkv_tables.1 = (bf16[2,688,512]{2,1,0:T(8,128)(2,1)}, bf16[2,688,512]{2,1,0:T(8,128)(2,1)}, bf16[688,128]{1,0:T(8,128)(2,1)}, f32[16,2048]{1,0:T(8,128)}, bf16[16,2048]{1,0:T(8,128)(2,1)}) custom-call(bf16[688,256]{1,0:T(8,128)(2,1)} %get-tuple-element.196.refs_0_, bf16[688,256]{1,0:T(8,128)(2,1)} %get-tuple-element.200.refs_1_, ...), custom_call_target="tpu_custom_call" | custom-call | flops 1750000000 | bytes 350000 | tf_op jit(solution)/shard_map/qkv_tables/pallas_call | solution.py:948
  274.0 7.8 %qkv_rows.2 = bf16[344,1024]{1,0:T(8,128)(2,1)} custom-call(bf16[688,256]{1,0:T(8,128)(2,1)} %get-tuple-element.196.refs_0_, bf16[688,256]{1,0:T(8,128)(2,1)} %get-tuple-element.200.refs_1_, bf16[2,688,512]{2,1,0:T(8,128)(2,1)} %get-tuple-element.217.refs_2_, bf16[688,256]{1,0:T(8,128)(2,1)} %get-tuple-element.209.refs_6_.refs_3_, ...), custom_call_target="tpu_custom_call" | custom-call | flops 1500000000 | bytes 200000 | tf_op jit(solution)/shard_map/qkv_rows/pallas_call | solution.py:980
  281.8 2.8 collective-permute-start.43
  285.1 7.8 %qkv_rows.3 = bf16[344,1024]{1,0:T(8,128)(2,1)} custom-call(bf16[688,256]{1,0:T(8,128)(2,1)} %get-tuple-element.196.refs_0_, bf16[688,256]{1,0:T(8,128)(2,1)} %get-tuple-element.200.refs_1_, bf16[2,688,512]{2,1,0:T(8,128)(2,1)} %get-tuple-element.217.refs_2_, bf16[688,256]{1,0:T(8,128)(2,1)} %get-tuple-element.209.refs_6_.refs_3_, ...), custom_call_target="tpu_custom_call" | custom-call | flops 1500000000 | bytes 200000 | tf_op jit(solution)/shard_map/qkv_rows/pallas_call | solution.py:980
  295.2 3.5 %collective-permute-start.45 = (bf16[344,1024]{1,0:T(8,128)(2,1)}, bf16[344,1024]{1,0:T(8,128)(2,1)S(1)}, u32[]{:S(2)}, u32[]{:S(2)}) collective-permute-start(bf16[344,1024]{1,0:T(8,128)(2,1)} %qkv_rows.3), channel_id=1, source_target_pairs={{1,2},{2,1},{5,6},{6,5},{9,10},{10,9},{13,14},{14,13},{17,18},{18,... | collective-permute-start | bytes 2113544 | tf_op jit(solution)/shard_map/ppermute | solution.py:1075
  301.2 3.3 %gather_images.2 = (bf16[8,16,3840]{2,1,0:T(8,128)(2,1)}, s32[16]{0:T(128)}) custom-call(s32[1]{0:T(128)} %bitcast.41.flag, bf16[8,16,3968]{2,1,0:T(8,128)(2,1)} %copy-done.2, bf16[8,16,3968]{2,1,0:T(8,128)(2,1)} %copy-done.7), custom_call_target="tpu_custom_call" | custom-call | flops 500000000 | bytes 25000 | tf_op jit(solution)/shard_map/gather_images/pallas_call | solution.py:1025
  304.6 2.6 select_bitcast_fusion
  308.1 2.0 gather_images.3
  312.9 2.3 finish.2
  316.2 3.7 %finish.3 = (f32[8,16,512]{2,1,0:T(8,128)}, f32[8,16,2048]{2,1,0:T(8,128)}, f32[8,16,2048]{2,1,0:T(8,128)}, f32[8,16,1024]{2,1,0:T(8,128)}, f32[8,16,1024]{2,1,0:T(8,128)}, /*index=5*/f32[8,16,1024]{2,1,0:T(8,128)}) custom-call(s32[1]{0:T(128)} %bitcast.core, bf16[8,16,3840]{2,1,0:T(8,128)(2,1)} %get-tuple-element.233.own, bf16[8,16,3840]{2,1,0:T(8,128)(2,1)} %copy-done.8), custom_call_target="tpu_custom_call" | custom-call | flops 500000000 | bytes 100000 | tf_op jit(solution)/shard_map/finish/pallas_call | solution.py:1063
  (237 shorter events, 65.6 us)
Async XLA Ops:
  6.2 35.8 %collective-permute-start.1 = (bf16[688,1024]{1,0:T(8,128)(2,1)}, bf16[688,1024]{1,0:T(8,128)(2,1)S(1)}, u32[]{:S(2)}, u32[]{:S(2)}) collective-permute-start(bf16[688,1024]{1,0:T(8,128)(2,1)} %bitcast.98), channel_id=1, source_target_pairs={{1,2},{2,1},{5,6},{6,5},{9,10},{10,9},{13,14},{14,13},{17,18},{18,... | collective-permute-start | bytes 4227080 | tf_op jit(solution)/shard_map/ppermute | solution.py:1075
  29.1 25.0 %collective-permute-start.9 = (bf16[2,3,128,512]{3,2,1,0:T(8,128)(2,1)S(1)}, bf16[2,3,128,512]{3,2,1,0:T(8,128)(2,1)S(1)}, u32[]{:S(2)}, u32[]{:S(2)}) collective-permute-start(bf16[2,3,128,512]{3,2,1,0:T(8,128)(2,1)S(1)} %pad_maximum_fusion.rest_0_), channel_id=1, source_target_pairs={{0,2},{2,0},{1,3},{3,1},{4,6},{6,4},{5,7},{7,5},{8,10},{10,8},{9,1... | collective-permute-start | bytes 2359304 | tf_op jit(solution)/shard_map/ppermute | solution.py:1079
  33.8 20.2 %collective-permute-start.10 = (bf16[2,3,128,512]{3,2,1,0:T(8,128)(2,1)S(1)}, bf16[2,3,128,512]{3,2,1,0:T(8,128)(2,1)S(1)}, u32[]{:S(2)}, u32[]{:S(2)}) collective-permute-start(bf16[2,3,128,512]{3,2,1,0:T(8,128)(2,1)S(1)} %pad_maximum_fusion.1.rest_1_), channel_id=1, source_target_pairs={{0,2},{2,0},{1,3},{3,1},{4,6},{6,4},{5,7},{7,5},{8,10},{10,8},{9,1... | collective-permute-start | bytes 2359304 | tf_op jit(solution)/shard_map/ppermute | solution.py:1079
  52.8 16.9 %collective-permute-start.11 = (bf16[2,688,512]{2,1,0:T(8,128)(2,1)}, bf16[2,688,512]{2,1,0:T(8,128)(2,1)}, u32[]{:S(2)}, u32[]{:S(2)}) collective-permute-start(bf16[2,688,512]{2,1,0:T(8,128)(2,1)} %get-tuple-element.135.k_ref.v_ref), channel_id=1, source_target_pairs={{0,2},{2,0},{1,3},{3,1},{4,6},{6,4},{5,7},{7,5},{8,10},{10,8},{9,1... | collective-permute-start | bytes 4227080 | tf_op jit(solution)/shard_map/ppermute | solution.py:1079
  62.8 27.8 %collective-permute-start.16 = (bf16[2,688,512]{2,1,0:T(8,128)(2,1)}, bf16[2,688,512]{2,1,0:T(8,128)(2,1)}, u32[]{:S(2)}, u32[]{:S(2)}) collective-permute-start(bf16[2,688,512]{2,1,0:T(8,128)(2,1)} %get-tuple-element.133.k_ref.v_ref), channel_id=1, source_target_pairs={{0,2},{2,0},{1,3},{3,1},{4,6},{6,4},{5,7},{7,5},{8,10},{10,8},{9,1... | collective-permute-start | bytes 4227080 | tf_op jit(solution)/shard_map/ppermute | solution.py:1079
  66.2 22.0 %collective-permute-start.12 = (bf16[1024,256]{1,0:T(8,128)(2,1)}, bf16[1024,256]{1,0:T(8,128)(2,1)}, u32[]{:S(2)}, u32[]{:S(2)}) collective-permute-start(bf16[1024,256]{1,0:T(8,128)(2,1)} %collective-permute-done.6.refs_5_), channel_id=1, source_target_pairs={{0,8},{8,0},{1,9},{9,1},{2,10},{10,2},{3,11},{11,3},{4,12},{12,4},... | collective-permute-start | bytes 1572872 | tf_op jit(solution)/shard_map/ppermute | solution.py:1079
  67.4 21.7 %collective-permute-start.15 = (bf16[1024,256]{1,0:T(8,128)(2,1)}, bf16[1024,256]{1,0:T(8,128)(2,1)S(1)}, u32[]{:S(2)}, u32[]{:S(2)}) collective-permute-start(bf16[1024,256]{1,0:T(8,128)(2,1)} %collective-permute-done.6.refs_5_), channel_id=1, source_target_pairs={{0,4},{4,0},{1,5},{5,1},{2,6},{6,2},{3,7},{7,3},{8,12},{12,8},{9,1... | collective-permute-start | bytes 1572872 | tf_op jit(solution)/shard_map/ppermute | solution.py:1079
  68.5 20.6 %collective-permute-start.17 = (bf16[128,1024]{1,0:T(8,128)(2,1)S(1)}, bf16[128,1024]{1,0:T(8,128)(2,1)S(1)}, u32[]{:S(2)}, u32[]{:S(2)}) collective-permute-start(bf16[128,1024]{1,0:T(8,128)(2,1)S(1)} %constant_dynamic-slice_fusion.3), channel_id=1, source_target_pairs={{0,1},{1,0},{2,3},{3,2},{4,5},{5,4},{6,7},{7,6},{8,9},{9,8},{10,11... | collective-permute-start | bytes 786440 | tf_op jit(solution)/shard_map/ppermute | solution.py:1079
  69.7 41.2 %collective-permute-start.26 = (bf16[688,1024]{1,0:T(8,128)(2,1)S(1)}, bf16[688,1024]{1,0:T(8,128)(2,1)S(1)}, u32[]{:S(2)}, u32[]{:S(2)}) collective-permute-start(bf16[688,1024]{1,0:T(8,128)(2,1)S(1)} %bitcast.73), channel_id=1, source_target_pairs={{1,2},{2,1},{5,6},{6,5},{9,10},{10,9},{13,14},{14,13},{17,18},{18,... | collective-permute-start | bytes 4227080 | tf_op jit(solution)/shard_map/ppermute | solution.py:1075
  88.2 19.9 %collective-permute-start.14 = (bf16[256,1024]{1,0:T(8,128)(2,1)S(1)}, bf16[256,1024]{1,0:T(8,128)(2,1)}, u32[]{:S(2)}, u32[]{:S(2)}) collective-permute-start(bf16[256,1024]{1,0:T(8,128)(2,1)S(1)} %constant_dynamic-slice_fusion.4), channel_id=1, source_target_pairs={{0,1},{1,0},{2,3},{3,2},{4,5},{5,4},{6,7},{7,6},{8,9},{9,8},{10,11... | collective-permute-start | bytes 1572872 | tf_op jit(solution)/shard_map/ppermute | solution.py:1079
  89.1 16.5 %collective-permute-start.18 = (bf16[128,1024]{1,0:T(8,128)(2,1)S(1)}, bf16[128,1024]{1,0:T(8,128)(2,1)S(1)}, u32[]{:S(2)}, u32[]{:S(2)}) collective-permute-start(bf16[128,1024]{1,0:T(8,128)(2,1)S(1)} %collective-permute-done.17), channel_id=1, source_target_pairs={{0,4},{4,0},{1,5},{5,1},{2,6},{6,2},{3,7},{7,3},{8,12},{12,8},{9,1... | collective-permute-start | bytes 786440 | tf_op jit(solution)/shard_map/ppermute | solution.py:1079
  89.6 22.6 %collective-permute-start.13 = (bf16[1024,256]{1,0:T(8,128)(2,1)}, bf16[1024,256]{1,0:T(8,128)(2,1)}, u32[]{:S(2)}, u32[]{:S(2)}) collective-permute-start(bf16[1024,256]{1,0:T(8,128)(2,1)} %collective-permute-done.12.refs_7_), channel_id=1, source_target_pairs={{0,4},{4,0},{1,5},{5,1},{2,6},{6,2},{3,7},{7,3},{8,12},{12,8},{9,1... | collective-permute-start | bytes 1572872 | tf_op jit(solution)/shard_map/ppermute | solution.py:1079
  108.3 14.5 %collective-permute-start.25 = (bf16[256,1024]{1,0:T(8,128)(2,1)}, bf16[256,1024]{1,0:T(8,128)(2,1)}, u32[]{:S(2)}, u32[]{:S(2)}) collective-permute-start(bf16[256,1024]{1,0:T(8,128)(2,1)} %collective-permute-done.14.refs_9_), channel_id=1, source_target_pairs={{0,8},{8,0},{1,9},{9,1},{2,10},{10,2},{3,11},{11,3},{4,12},{12,4},... | collective-permute-start | bytes 1572872 | tf_op jit(solution)/shard_map/ppermute | solution.py:1079
  121.0 28.1 %collective-permute-start.20 = (bf16[16,4096]{1,0:T(8,128)(2,1)S(1)}, bf16[16,4096]{1,0:T(8,128)(2,1)S(1)}, u32[]{:S(2)}, u32[]{:S(2)}) collective-permute-start(bf16[16,4096]{1,0:T(8,128)(2,1)S(1)} %pad_maximum_fusion.4), channel_id=1, source_target_pairs={{0,1},{1,0},{2,3},{3,2},{4,5},{5,4},{6,7},{7,6},{8,9},{9,8},{10,11... | collective-permute-start | bytes 393224 | tf_op jit(solution)/shard_map/ppermute | solution.py:1079
  121.0 28.1 %collective-permute-start.23 = (bf16[1024,256]{1,0:T(8,128)(2,1)}, bf16[1024,256]{1,0:T(8,128)(2,1)S(1)}, u32[]{:S(2)}, u32[]{:S(2)}) collective-permute-start(bf16[1024,256]{1,0:T(8,128)(2,1)} %collective-permute-done.12.refs_7_), channel_id=1, source_target_pairs={{0,2},{2,0},{1,3},{3,1},{4,6},{6,4},{5,7},{7,5},{8,10},{10,8},{9,1... | collective-permute-start | bytes 1572872 | tf_op jit(solution)/shard_map/ppermute | solution.py:1079
  122.3 27.3 %collective-permute-start.22 = (bf16[1024,256]{1,0:T(8,128)(2,1)S(1)}, bf16[1024,256]{1,0:T(8,128)(2,1)S(1)}, u32[]{:S(2)}, u32[]{:S(2)}) collective-permute-start(bf16[1024,256]{1,0:T(8,128)(2,1)S(1)} %copy-done.28), channel_id=1, source_target_pairs={{0,2},{2,0},{1,3},{3,1},{4,6},{6,4},{5,7},{7,5},{8,10},{10,8},{9,1... | collective-permute-start | bytes 1572872 | tf_op jit(solution)/shard_map/ppermute | solution.py:1079
  122.3 27.4 %collective-permute-start.21 = (bf16[1024,256]{1,0:T(8,128)(2,1)}, bf16[1024,256]{1,0:T(8,128)(2,1)S(1)}, u32[]{:S(2)}, u32[]{:S(2)}) collective-permute-start(bf16[1024,256]{1,0:T(8,128)(2,1)} %collective-permute-done.6.refs_5_), channel_id=1, source_target_pairs={{0,2},{2,0},{1,3},{3,1},{4,6},{6,4},{5,7},{7,5},{8,10},{10,8},{9,1... | collective-permute-start | bytes 1572872 | tf_op jit(solution)/shard_map/ppermute | solution.py:1079
  122.8 25.7 %collective-permute-start.31 = (bf16[256,1024]{1,0:T(8,128)(2,1)}, bf16[256,1024]{1,0:T(8,128)(2,1)S(1)}, u32[]{:S(2)}, u32[]{:S(2)}) collective-permute-start(bf16[256,1024]{1,0:T(8,128)(2,1)} %collective-permute-done.24.refs_10_), channel_id=1, source_target_pairs={{0,8},{8,0},{1,9},{9,1},{2,10},{10,2},{3,11},{11,3},{4,12},{12,4},... | collective-permute-start | bytes 1572872 | tf_op jit(solution)/shard_map/ppermute | solution.py:1079
  148.5 16.5 %collective-permute-start.30 = (bf16[256,1024]{1,0:T(8,128)(2,1)}, bf16[256,1024]{1,0:T(8,128)(2,1)S(1)}, u32[]{:S(2)}, u32[]{:S(2)}) collective-permute-start(bf16[256,1024]{1,0:T(8,128)(2,1)} %collective-permute-done.25.refs_11_), channel_id=1, source_target_pairs={{0,2},{2,0},{1,3},{3,1},{4,6},{6,4},{5,7},{7,5},{8,10},{10,8},{9,1... | collective-permute-start | bytes 1572872 | tf_op jit(solution)/shard_map/ppermute | solution.py:1079
  149.0 16.0 %collective-permute-start.29 = (bf16[256,1024]{1,0:T(8,128)(2,1)}, bf16[256,1024]{1,0:T(8,128)(2,1)S(1)}, u32[]{:S(2)}, u32[]{:S(2)}) collective-permute-start(bf16[256,1024]{1,0:T(8,128)(2,1)} %collective-permute-done.24.refs_10_), channel_id=1, source_target_pairs={{0,2},{2,0},{1,3},{3,1},{4,6},{6,4},{5,7},{7,5},{8,10},{10,8},{9,1... | collective-permute-start | bytes 1572872 | tf_op jit(solution)/shard_map/ppermute | solution.py:1079
  149.1 15.9 %collective-permute-start.28 = (bf16[256,1024]{1,0:T(8,128)(2,1)}, bf16[256,1024]{1,0:T(8,128)(2,1)S(1)}, u32[]{:S(2)}, u32[]{:S(2)}) collective-permute-start(bf16[256,1024]{1,0:T(8,128)(2,1)} %collective-permute-done.14.refs_9_), channel_id=1, source_target_pairs={{0,2},{2,0},{1,3},{3,1},{4,6},{6,4},{5,7},{7,5},{8,10},{10,8},{9,1... | collective-permute-start | bytes 1572872 | tf_op jit(solution)/shard_map/ppermute | solution.py:1079
  149.6 15.5 %collective-permute-start.27 = (bf16[1024,256]{1,0:T(8,128)(2,1)}, bf16[1024,256]{1,0:T(8,128)(2,1)S(1)}, u32[]{:S(2)}, u32[]{:S(2)}) collective-permute-start(bf16[1024,256]{1,0:T(8,128)(2,1)} %collective-permute-done.13.refs_8_), channel_id=1, source_target_pairs={{0,2},{2,0},{1,3},{3,1},{4,6},{6,4},{5,7},{7,5},{8,10},{10,8},{9,1... | collective-permute-start | bytes 1572872 | tf_op jit(solution)/shard_map/ppermute | solution.py:1079
  149.7 15.4 %collective-permute-start.32 = (bf16[256,1024]{1,0:T(8,128)(2,1)S(1)}, bf16[256,1024]{1,0:T(8,128)(2,1)S(1)}, u32[]{:S(2)}, u32[]{:S(2)}) collective-permute-start(bf16[256,1024]{1,0:T(8,128)(2,1)S(1)} %collective-permute-done.31.refs_12_), channel_id=1, source_target_pairs={{0,2},{2,0},{1,3},{3,1},{4,6},{6,4},{5,7},{7,5},{8,10},{10,8},{9,1... | collective-permute-start | bytes 1572872 | tf_op jit(solution)/shard_map/ppermute | solution.py:1079
  195.5 18.0 %collective-permute-start.35 = (bf16[16,3968]{1,0:T(8,128)(2,1)S(1)}, bf16[16,3968]{1,0:T(8,128)(2,1)S(1)}, u32[]{:S(2)}, u32[]{:S(2)}) collective-permute-start(bf16[16,3968]{1,0:T(8,128)(2,1)S(1)} %maximum_maximum_fusion), channel_id=1, source_target_pairs={{0,1},{1,0},{2,3},{3,2},{4,5},{5,4},{6,7},{7,6},{8,9},{9,8},{10,11... | collective-permute-start | bytes 380936 | tf_op jit(solution)/shard_map/ppermute | solution.py:1079
  209.8 35.8 %collective-permute-start.34 = (bf16[688,1024]{1,0:T(8,128)(2,1)S(1)}, bf16[688,1024]{1,0:T(8,128)(2,1)}, u32[]{:S(2)}, u32[]{:S(2)}) collective-permute-start(bf16[688,1024]{1,0:T(8,128)(2,1)S(1)} %copy-done.6), channel_id=1, source_target_pairs={{1,2},{2,1},{5,6},{6,5},{9,10},{10,9},{13,14},{14,13},{17,18},{18,... | collective-permute-start | bytes 4227080 | tf_op jit(solution)/shard_map/ppermute | solution.py:1075
  213.6 16.8 %collective-permute-start.38 = (bf16[2,16,3968]{2,1,0:T(8,128)(2,1)S(1)}, bf16[2,16,3968]{2,1,0:T(8,128)(2,1)S(1)}, u32[]{:S(2)}, u32[]{:S(2)}) collective-permute-start(bf16[2,16,3968]{2,1,0:T(8,128)(2,1)S(1)} %maximum_select_fusion.3), channel_id=1, source_target_pairs={{0,16},{16,0},{1,17},{17,1},{2,18},{18,2},{3,19},{19,3},{4,20},{20... | collective-permute-start | bytes 761864 | tf_op jit(solution)/shard_map/ppermute | solution.py:1079
  230.5 14.9 %collective-permute-start.39 = (bf16[4,16,3968]{2,1,0:T(8,128)(2,1)S(1)}, bf16[4,16,3968]{2,1,0:T(8,128)(2,1)S(1)}, u32[]{:S(2)}, u32[]{:S(2)}) collective-permute-start(bf16[4,16,3968]{2,1,0:T(8,128)(2,1)S(1)} %maximum_select_fusion.1), channel_id=1, source_target_pairs={{0,8},{8,0},{1,9},{9,1},{2,10},{10,2},{3,11},{11,3},{4,12},{12,4},... | collective-permute-start | bytes 1523720 | tf_op jit(solution)/shard_map/ppermute | solution.py:1079
  230.7 29.7 %collective-permute-start.36 = (bf16[2,688,256]{2,1,0:T(8,128)(2,1)}, bf16[2,688,256]{2,1,0:T(8,128)(2,1)S(1)}, u32[]{:S(2)}, u32[]{:S(2)}) collective-permute-start(bf16[2,688,256]{2,1,0:T(8,128)(2,1)} %get-tuple-element.203), channel_id=1, source_target_pairs={{0,2},{2,0},{1,3},{3,1},{4,6},{6,4},{5,7},{7,5},{8,10},{10,8},{9,1... | collective-permute-start | bytes 2113544 | tf_op jit(solution)/shard_map/ppermute | solution.py:1079
  230.8 29.7 %collective-permute-start.37 = (bf16[2,688,256]{2,1,0:T(8,128)(2,1)}, bf16[2,688,256]{2,1,0:T(8,128)(2,1)S(1)}, u32[]{:S(2)}, u32[]{:S(2)}) collective-permute-start(bf16[2,688,256]{2,1,0:T(8,128)(2,1)} %get-tuple-element.204), channel_id=1, source_target_pairs={{0,2},{2,0},{1,3},{3,1},{4,6},{6,4},{5,7},{7,5},{8,10},{10,8},{9,1... | collective-permute-start | bytes 2113544 | tf_op jit(solution)/shard_map/ppermute | solution.py:1079
  245.3 15.2 %collective-permute-start.40 = (bf16[2,688,256]{2,1,0:T(8,128)(2,1)}, bf16[2,688,256]{2,1,0:T(8,128)(2,1)S(1)}, u32[]{:S(2)}, u32[]{:S(2)}) collective-permute-start(bf16[2,688,256]{2,1,0:T(8,128)(2,1)} %get-tuple-element.215), channel_id=1, source_target_pairs={{0,2},{2,0},{1,3},{3,1},{4,6},{6,4},{5,7},{7,5},{8,10},{10,8},{9,1... | collective-permute-start | bytes 2113544 | tf_op jit(solution)/shard_map/ppermute | solution.py:1079
  270.4 29.9 %collective-permute-start.46 = (bf16[8,16,3968]{2,1,0:T(8,128)(2,1)S(1)}, bf16[8,16,3968]{2,1,0:T(8,128)(2,1)S(1)}, u32[]{:S(2)}, u32[]{:S(2)}) collective-permute-start(bf16[8,16,3968]{2,1,0:T(8,128)(2,1)S(1)} %maximum_select_fusion.refs_0_), channel_id=1, source_target_pairs={{0,4},{4,0},{1,5},{5,1},{2,6},{6,2},{3,7},{7,3},{8,12},{12,8},{9,1... | collective-permute-start | bytes 3047432 | tf_op jit(solution)/shard_map/ppermute | solution.py:1079
  295.2 15.0 %collective-permute-start.45 = (bf16[344,1024]{1,0:T(8,128)(2,1)}, bf16[344,1024]{1,0:T(8,128)(2,1)S(1)}, u32[]{:S(2)}, u32[]{:S(2)}) collective-permute-start(bf16[344,1024]{1,0:T(8,128)(2,1)} %qkv_rows.3), channel_id=1, source_target_pairs={{1,2},{2,1},{5,6},{6,5},{9,10},{10,9},{13,14},{14,13},{17,18},{18,... | collective-permute-start | bytes 2113544 | tf_op jit(solution)/shard_map/ppermute | solution.py:1075
  (60 other events, 442.9 us)

commit v4 on v3

--- a/solution.py
+++ b/solution.py
@@ -646,7 +646,7 @@
         for copy in fetch(arrays, nears, w_b, sem, scal[2], 0, arrays[0].shape[1]):
             copy.wait()
 
-    ranked = dotg(mix_a[...], pad_rows(oa_a[...]), 1, 1) + dotg(mix_b[...], pad_rows(oa_b[...]), 1, 1)
+    ranked = dotg(mix_a[...], pad_rows(oa_a[...]), 1, 1) + dotg(mix_b[...], pad_rows(oa_b[:, -oa_a.shape[1] :]), 1, 1)
     ranked = two_terms(ranked, rank)
     rank_out[...] = ranked
     terms = dotg(mix_a[...], w_a[...], 1, 0) + dotg(mix_b[...], w_b[...], 1, 0)
@@ -710,7 +710,7 @@
     wu, wd, ubs, das, hidden, grad_pre, sem = rest[6:]
     width = wu.shape[1]
     rank = ub.shape[0]
-    size = ub.shape[1] // PARTS
+    size = gub_out.shape[1] // PARTS
     pieces = width // size
     chunks = width // step
     waits = [[] for _ in range(chunks)]
@@ -724,10 +724,10 @@
             copy = pltpu.make_async_copy(source, target, sem.at[which, piece])
             copy.start()
             waits[piece * size // step].append(copy)
-    def place(piece):
+    def place(piece, first=0):
         if nears is None:
             return pl.ds(piece * size, size)
-        return pl.ds(pl.multiple_of((scal[2] ^ nears[piece]) * size, size), size)
+        return pl.ds(pl.multiple_of((scal[2] ^ nears[piece]) * size + first, size), size)
 
     if nears is None:
         grad_low = (scale_two[...] * (cot[...].astype(F32) * row_mask(scal, cot.shape[0]))).astype(BF)
@@ -740,7 +740,7 @@
     for piece in range(pieces):
         at = slice(piece * size, (piece + 1) * size)
         ubs[0:rank, at] = ub[:, place(piece)]
-        das[0:rank, at] = da[:, place(piece)]
+        das[0:rank, at] = da[:, place(piece, da.shape[1] // 2)]
     up_turned = rank_up[...].T[0:rank]
     grad_turned = grad_rank[...].T[0:rank]
 
@@ -786,6 +786,7 @@
 def mlp(scal, n2, rank_up, ub, da, ups, downs, grads, nears=None, earlier=()):
     rows, width = n2.shape
     rank, half = ub.shape[-2:]
+    half = half if nears is None else half // 2
     units = half if nears is None else len(nears) * half // PARTS
     step = min(512, units)
     sums = jax.ShapeDtypeStruct((rows, width), BF)
@@ -816,12 +817,12 @@
     )(scal, n2, rank_up, ub, da, *ups, *downs, *grads, *earlier)
 
 
-def mlp_other(scal, n2, rank_up, ub, da, up, down, grads, earlier):
+def mlp_other(scal, n2, rank_up, tables, up, down, grads, earlier):
     for odd in range(2):
         ups, nears = up.held(odd)
         downs, same = down.held(odd)
         assert nears == same
-        earlier = mlp(scal, n2, rank_up, ub, da, ups, downs, grads, nears, tuple(earlier))
+        earlier = mlp(scal, n2, rank_up, tables, tables, ups, downs, grads, nears, tuple(earlier))
     return earlier
 
 
@@ -867,7 +868,7 @@
         dotg(grad_attn, w_a[...], 1, 1) + dotg(grad_rank, pad_rows(oa_a[...]), 1, 0)
     ).astype(BF)
     grad_b[...] = (
-        dotg(grad_attn, w_b[...], 1, 1) + dotg(grad_rank, pad_rows(oa_b[...]), 1, 0)
+        dotg(grad_attn, w_b[...], 1, 1) + dotg(grad_rank, pad_rows(oa_b[:, -oa_a.shape[1] :]), 1, 0)
     ).astype(BF)
     rank_turned = grad_rank.T[0:rank]
     add(goa_a, dotg(rank_turned, mix_a[...], 1, 0))
@@ -906,15 +907,18 @@
         first += piece.shape[-1]
 
 
-def qkv_tables_kernel(count, *refs):
-    sides, refs = (refs[: 3 * count], refs[3 * count : 6 * count]), refs[6 * count :]
+def qkv_tables_kernel(counts, *refs):
+    sides = []
+    for count in counts:
+        sides.append((refs[:count], refs[count : 2 * count], refs[2 * count : 3 * count]))
+        refs = refs[3 * count :]
     scal, qb_a, qb_b, n1, rank_in, total_a, total_b, rank_out, kept, sent, gqb_a, gqb_b, gqa = refs
     rank = qb_a.shape[0]
     third = qb_a.shape[1] // 3
     rank_turned = rank_in[...].T[0:rank]
     ranked = None
     for side, qb, total, table in zip(sides, (qb_a, qb_b), (total_a, total_b), (gqb_a, gqb_b)):
-        queries, owns, gots = side[:count], side[count : 2 * count], side[2 * count :]
+        queries, owns, gots = side
         for (piece, at), own, got in zip(columns_of(queries), owns, gots):
             for c in range(3):
                 if c == 0:
@@ -942,12 +946,12 @@
 def qkv_tables(scal, side_a, side_b, qb_a, qb_b, n1, rank_in):
     rows, width = n1.shape
     rank, columns = qb_a.shape
-    count = len(side_a) // 3
+    pieces = [piece for side in (side_a, side_b) for group in side for piece in group]
     total = jax.ShapeDtypeStruct((2, rows, columns // 3), BF)
     share = columns + width // 2
     return pl.pallas_call(
-        functools.partial(qkv_tables_kernel, count),
-        in_specs=[whole()] * (6 * count) + [scalars()] + [whole()] * 4,
+        functools.partial(qkv_tables_kernel, (len(side_a[0]), len(side_b[0]))),
+        in_specs=[whole()] * len(pieces) + [scalars()] + [whole()] * 4,
         out_specs=[whole()] * 5,
         out_shape=[total, total, jax.ShapeDtypeStruct((rows, PAD), BF)]
         + [jax.ShapeDtypeStruct((rank, share), F32), jax.ShapeDtypeStruct((rank, share), BF)],
@@ -955,18 +959,18 @@
         compiler_params=params(),
         cost_estimate=cost(7e-6 * 1e15, 14e6),
         name="qkv_tables",
-    )(*side_a, *side_b, scal, qb_a, qb_b, n1, rank_in)
-
-
-def qkv_rows_kernel(count, *refs):
-    grads_a, grads_b, refs = refs[: count + 1], refs[count + 1 : 2 * count + 2], refs[2 * count + 2 :]
+    )(*pieces, scal, qb_a, qb_b, n1, rank_in)
+
+
+def qkv_rows_kernel(count_a, count_b, *refs):
+    grads_a, grads_b, refs = refs[:count_a], refs[count_a : count_a + count_b], refs[count_a + count_b :]
     w_a, w_b, ranked, qa, tok, gain, grad_res, out = refs
     grad = dotg(ranked[...], pad_twice(qa[...]), 1, 0)
     for grads, w in ((grads_a, w_a), (grads_b, w_b)):
-        for piece, at in columns_of(grads[:count]):
+        for piece, at in columns_of(grads[:-1]):
             grad = grad + dotg(piece[...], w[0, :, at], 1, 1)
         for c in (1, 2):
-            grad = grad + dotg(grads[count][c - 1], w[c], 1, 1)
+            grad = grad + dotg(grads[-1][c - 1], w[c], 1, 1)
     unit, scale = norm_stats(tok[...].astype(F32))
     out[...] = (grad_res[...].astype(F32) + norm_grad(unit, scale, grad * gain[...])).astype(BF)
 
@@ -978,7 +982,7 @@
     deep = lambda array: pl.BlockSpec((2, block, array.shape[2]), lambda step: (0, block_at, 0))
     specs = [flat(array) if array.ndim == 2 else deep(array) for array in grads_a + grads_b]
     return pl.pallas_call(
-        functools.partial(qkv_rows_kernel, len(grads_a) - 1),
+        functools.partial(qkv_rows_kernel, len(grads_a), len(grads_b)),
         grid=(1,),
         in_specs=specs
         + [whole(), whole(), flat(ranked), whole(), flat(tok), whole(), flat(grad_res)],
@@ -1032,7 +1036,7 @@
         ],
         scratch_shapes=[pltpu.VMEM((adapters, rank, columns), F32)],
         compiler_params=params(),
-        cost_estimate=cost(2e-6 * 1e15, 1e6),
+        cost_estimate=cost((20e-6 if ids is None else 1e-6) * 1e15, 1e6),
         name="gather_images",
     )(flag.astype(jnp.int32)[None], *given, *pair)
 
@@ -1059,14 +1063,14 @@
         write(other, own)
 
 
-def finish(core, cut, spans, places, own, other, shapes):
+def finish(core, cut, spans, places, own, other, shapes, seconds=1e-6):
     return pl.pallas_call(
         functools.partial(finish_kernel, cut, spans, places),
         in_specs=[scalars(), whole(), whole()],
         out_specs=[whole()] * len(shapes),
         out_shape=[jax.ShapeDtypeStruct(shape, F32) for shape in shapes],
         compiler_params=params(),
-        cost_estimate=cost(2e-6 * 1e15, 4e6),
+        cost_estimate=cost(seconds * 1e15, 1e6),
         name="finish",
     )(core, own, other)
 
@@ -1167,9 +1171,9 @@
         self.other = flip("core")(self.dense)
         return ids
 
-    def finish(self, spans, places, shapes):
+    def finish(self, spans, places, shapes, *seconds):
         core = self.core.astype(jnp.int32)[None]
-        return finish(core, self.cut, spans, places, self.dense, self.other, shapes)
+        return finish(core, self.cut, spans, places, self.dense, self.other, shapes, *seconds)
 
 
 def quad_body(
@@ -1202,21 +1206,21 @@
     flat = lambda table: jnp.swapaxes(table, 0, 1).reshape(rank, 3 * third)
     half_qkv.hop(0, "x")
     half_qkv.hop(0, "zb")
-    adapter, adapter_other = after((adapter, adapter_other), half_qkv.parts[2])
     packed_first = jnp.concatenate([flat(pick(qkv_b, adapter_other)), pick(out_a, adapter_other)], axis=1)
     packed = jnp.concatenate([pick(table, adapter_other) for table in (up_b, down_a)], axis=1)
     qa, oa = pick(qkv_a, adapter), pick(out_a, adapter)
     qb = flat(pick(qkv_b, adapter))
     gain_one, gain_two, scale_one, scale_two = (v.reshape(1, width) for v in (gain_one, gain_two, scale_one, scale_two))
 
-    qb_other, oa_other = jnp.split(flip("tensor")(packed_first), (3 * third,), axis=1)
-    half_up.over_tensor(half_qkv.parts[4], qb_other)
+    other_tables = flip("tensor")(packed_first)
+    half_up.over_tensor(half_qkv.parts[4], other_tables)
     half_qkv.last_hop()
-    tok_swapped = after(tok_swapped, half_qkv.parts[2], half_qkv.parts[4], qb_other, scal)
+    half_qkv.parts[6] = after(half_qkv.parts[6], scal, qa, qb, other_tables, half_up.mine)
+    tok_swapped = after(tok_swapped, half_qkv.parts[2], half_qkv.parts[4], other_tables, scal, half_out.mine, half_down.mine)
     tok, n1, rank_qkv, q_a, own_a = qkv_local(scal, tok_here, tok_swapped, gain_one, w3, qa, qb)
     half_qkv.pairs_over_cores()
     kv_a = flip("core")(own_a)
-    q_b, own_b, w3_other = qkv_other(scal, after(n1, half_up.parts[0]), rank_qkv, qb_other, half_qkv)
+    q_b, own_b, w3_other = qkv_other(scal, after(n1, half_up.parts[0]), rank_qkv, other_tables, half_qkv)
     kv_b = flip("core")(own_b)
     half_out.over_tensor(own_b)
     half_up.hop(0, "x", own_b)
@@ -1231,10 +1235,10 @@
     half_down.hop(0, "x", mix_b)
     half_down.hop(0, "zb", mix_b)
     residual, n2, rank_out, rank_up, out_other = branch(
-        scal, after(mix_a, half_up.parts[6], half_down.parts[0]), mix_b, tok, w_out, half_out, oa, oa_other, out_b, scale_one, gain_two, up_a
+        scal, after(mix_a, half_up.parts[6], half_down.parts[0]), mix_b, tok, w_out, half_out, oa, other_tables, out_b, scale_one, gain_two, up_a
     )
     half_down.hop(2, "zb", n2)
-    ub_other, da_other = jnp.split(flip("tensor")(after(packed, n2)), 2, axis=1)
+    other_units = flip("tensor")(after(packed, n2))
     for near in (0, 2, 4):
         half_up.hop(near, "core", n2)
     cot = jnp.where(core == tensor, cotangent[0], cot_swapped)
@@ -1246,12 +1250,12 @@
     for near in (0, 2, 4, 6):
         half_down.hop(near, "core", m)
     m, g, rd, gru, gub_b, gda_b = mlp_other(
-        scal, n2, rank_up, ub_other, da_other, half_up, half_down, [grad_mlp, grad_rank], (m, g, rd, gru)
+        scal, n2, rank_up, other_units, half_up, half_down, [grad_mlp, grad_rank], (m, g, rd, gru)
     )
     layer, grad_res, grad_a, grad_b, goa_a, goa_b, gob, gua, gdb = middle(
         scal,
         (residual, m, g, rd, gru, cot, mix_a, mix_b, rank_out, n2, grad_mlp),
-        (down_b, up_a, scale_two, gain_two, scale_one, w_out, out_other, oa, oa_other, out_b),
+        (down_b, up_a, scale_two, gain_two, scale_one, w_out, out_other, oa, other_tables, out_b),
     )
     shares = Sum.shares(
         jnp.concatenate([goa_a, gub_a, gda_a], axis=1),
@@ -1262,60 +1266,63 @@
     early = Sum(*shares, third // 2 + units, adapter, core, tensor)
     early.over_cores()
 
-    def back(queries, own, kv, mixed, grad, logs, piece, *others):
-        queries = after(queries, *others) if others else queries
-        grad_queries, kept, sent = attend_back(scal, queries, own, kv, mixed, grad, logs, piece, 2)
-        return grad_queries, kept, flip("core")(sent)
+    def back(queries, own, kv, mixed, grad, logs, piece, pieces, *others):
+        return attend_back(scal, after(queries, *others), own, kv, mixed, grad, logs, piece, pieces)
+
+    def exchanged(back, *others):
+        return back[0], back[1], flip("core")(after(back[2], *others) if others else back[2])
+
 
     side_a = (q_a, own_a, kv_a, mix_a, grad_a, logs_a)
     side_b = (q_b, own_b, kv_b, mix_b, grad_b, logs_b)
     early.start_pair()
-    back_1 = back(*side_a, 0, early.send)
+    back_1 = back(*side_a, 0, 2, early.send)
     early.arrive(back_1[0])
     early.start("hi")
-    back_2 = back(*side_a, 1, early.images)
+    back_1 = exchanged(back_1, early.images)
     layer_swapped = swap(after(layer, back_1[0]))
+    back_2 = back(*side_a, 1, 2, early.images)
     early.arrive(back_2[0])
     early.start("zb")
-    back_3 = back(*side_b, 0, early.images)
+    back_2 = exchanged(back_2, early.images)
+    back_3 = back(*side_b, 0, 2, early.images)
     early.arrive(back_3[0])
     early.start("x")
-    back_4 = back(*side_b, 1, early.images, layer_swapped)
+    back_3 = exchanged(back_3, early.images)
+    back_4 = exchanged(back(*side_b, 1, 2, early.images, layer_swapped))
     kv_sum_a, kv_sum_b, ranked, kept, sent = qkv_tables(
         scal,
-        [part for pair in zip(back_1, back_2) for part in pair],
-        [part for pair in zip(back_3, back_4) for part in pair],
-        qb, qb_other, n1, rank_qkv,
-    )
-    late = Sum(kept, sent, 3 * third // 2, None, core, tensor)
+        [list(pair) for pair in zip(back_1, back_2)],
+        [list(pair) for pair in zip(back_3, back_4)],
+        qb, other_tables, n1, rank_qkv,
+    )
+    early.arrive(kept)
+    late = Sum(kept, after(sent, early.pair[1]), 3 * third // 2, None, core, tensor)
     late.over_cores()
     late.start_pair()
-    grads = (
-        [back_1[0], back_2[0], kv_sum_a], [back_3[0], back_4[0], kv_sum_b],
-        w3, w3_other, ranked, qa, tok, gain_one, grad_res,
-    )
-    upper = qkv_rows(0, 2, grads[0], grads[1], after(w3, late.send), *grads[3:])
-    upper_swapped = swap(upper)
-    late.arrive(upper)
+    early.arrive(late.send)
+    ids = early.over_adapters(None, adapters)
+    late.arrive(early.dense)
     late.start("hi")
-    lower = qkv_rows(1, 2, grads[0], grads[1], after(w3, late.images), *grads[3:])
-    lower_swapped = swap(lower)
-    late.arrive(lower, upper_swapped)
+    grad_rows = qkv_rows(
+        0, 1, [back_1[0], back_2[0], kv_sum_a], [back_3[0], back_4[0], kv_sum_b],
+        after(w3, late.images), w3_other, ranked, qa, tok, gain_one, grad_res,
+    )
+    late.arrive(grad_rows)
+    grad_rows_swapped = swap(after(grad_rows, late.pair[1]))
+    early.other = after(early.other, grad_rows)
     late.start("zb")
     late.start("x")
-    early.arrive(lower, late.images)
-    ids = early.over_adapters(None, adapters)
+    late.arrive(grad_rows_swapped)
     in_place_already = core == tensor
-    grad_tokens = jnp.concatenate(
-        [jnp.where(in_place_already, *rows) for rows in ((upper, upper_swapped), (lower, lower_swapped))], axis=0
-    ).astype(F32)
+    grad_tokens = jnp.where(in_place_already, grad_rows, grad_rows_swapped).astype(F32)
     layer_out = jnp.where(in_place_already, layer, layer_swapped)
     late.over_adapters(ids, adapters)
     ends = (0, third, third + units, third + 2 * units)
     spans = [(False, ends[k], ends[k + 1]) for k in range(3)] + [(True, k * width, (k + 1) * width) for k in range(3)]
     widths = (third, units, units, width, width, width)
     sum_oa, sum_ub, sum_da, sum_ob, sum_ua, sum_db = early.finish(
-        spans, [(k, None) for k in range(6)], [(adapters, rank, size) for size in widths]
+        spans, [(k, None) for k in range(6)], [(adapters, rank, size) for size in widths], 20e-6
     )
     sum_qb, sum_qa = late.finish(
         [(False, c * third, (c + 1) * third) for c in range(3)] + [(True, 0, width)],

time: 326 us -> 319 us (0.979)
  waiting for transfers between devices: 13.4 us -> 23.9 us
  starting transfers between devices: 55.8 us -> 46.1 us
  local copies, waits for them, and re-layouts: 23.2 us -> 19.1 us
    ppermute x47, waiting for transfers between devices: 11.6 us -> 21.4 us  [flip(): return lambda array: lax.ppermute(array, axis, FLIP)]
    ppermute x47, starting transfers between devices: 40.4 us -> 33.8 us  [flip(): return lambda array: lax.ppermute(array, axis, FLIP)]
    pallas_call x3 -> x2, Pallas kernels: 22.3 us -> 19 us  [the longest x1 12.2 us: qkv_rows(): pl.pallas_call(functools.partial(qkv_rows_kernel, len(grads_a), len(grads...]
    ppermute x5 -> x4, starting transfers between devices: 15.5 us -> 12.3 us  [swap(): return lax.ppermute(rows, ('core', 'tensor'), SWAP)]
    unnamed x86 -> x80, local copies, waits for them, and re-layouts: 9.63 us -> 7.31 us
  transfers between devices with their start and end apart: 52 -> 51, of which waited for: 7 -> 10; matrix products, arithmetic and copies ran while one was open for 7% -> 6% of each run, Pallas kernels for 55% -> 57%
where the time goes in v4:
time: 319 us; the launch traced here: 314 us
  Pallas kernels  208 us (65%)
  starting transfers between devices  46.1 us (14%)
  waiting for transfers between devices  23.9 us (7%)
  local copies, waits for them, and re-layouts  19.1 us (6%)
  other arithmetic  8.66 us (3%)
  between operations  7.55 us (2%)
    pallas_call x4, Pallas kernels, attend_back(): pl.pallas_call(attend_back_kernel, grid=(pairs,), in_specs=[scalars(), fl...  57 us
    pallas_call x3, Pallas kernels, mlp(): pl.pallas_call(functools.partial(mlp_kernel, nears, step, len(earlier)),...  53.1 us
    ppermute x47, starting transfers between devices, flip(): return lambda array: lax.ppermute(array, axis, FLIP)  33.8 us
    pallas_call x2, Pallas kernels, attend(): pl.pallas_call(attend_kernel, grid=(pairs,), in_specs=[scalars(), flat, t...  29.9 us
    ppermute x47, waiting for transfers between devices, flip(): return lambda array: lax.ppermute(array, axis, FLIP)  21.4 us
    ppermute x4, starting transfers between devices, swap(): return lax.ppermute(rows, ('core', 'tensor'), SWAP)  12.3 us
    pallas_call x1, Pallas kernels, qkv_rows(): pl.pallas_call(functools.partial(qkv_rows_kernel, len(grads_a), len(grads...  12.2 us
    pallas_call x1, Pallas kernels, middle(): pl.pallas_call(middle_kernel, grid=(blocks,), in_specs=[scalars()] + [blo...  11.6 us
  transfers between devices with their start and end apart: 51, of which 10 were waited for; matrix products, arithmetic and copies ran while one was open for 6% of the time, Pallas kernels for 57%

profile of v4, /device:TPU:1, one launch (start us, length us, event | category | flops | bytes accessed | tf_op | source)
XLA Modules:
  0.0 313.7 jit_solution(13912675203583340570)
XLA Ops:
  1.8 2.1 collective-permute-start.2
  21.7 3.5 %collective-permute-done.3 = bf16[3,128,512]{2,1,0:T(8,128)(2,1)S(1)} collective-permute-done((bf16[3,128,512]{2,1,0:T(8,128)(2,1)S(1)}, bf16[3,128,512]{2,1,0:T(8,128)(2,1)S(1)}, u32[]{:S(2)}, u32[]{:S(2)}) %collective-permute-start.3) | collective-permute-done | bytes 393248 | tf_op jit(solution)/shard_map/ppermute | solution.py:1083
  32.5 1.9 collective-permute-start.10
  36.6 9.7 %qkv_local.1 = (bf16[688,1024]{1,0:T(8,128)(2,1)}, bf16[688,1024]{1,0:T(8,128)(2,1)}, bf16[688,128]{1,0:T(8,128)(2,1)}, bf16[688,512]{1,0:T(8,128)(2,1)}, bf16[2,688,512]{2,1,0:T(8,128)(2,1)}) custom-call(s32[5]{0:T(128)} %stack.50.scal.refs_0_.refs_12_, bf16[688,1024]{1,0:T(8,128)(2,1)} %bitcast.96, bf16[688,1024]{1,0:T(8,128)(2,1)} %collective-permute-done.1.swapped, ...), custom_call_target="tpu_custom_call" | custom-call | flops 1750000000 | bytes 200000 | tf_op jit(solution)/shard_map/qkv_local/pallas_call | solution.py:402
  46.6 3.4 %collective-permute-done.6.refs_5_ = bf16[1024,256]{1,0:T(8,128)(2,1)} collective-permute-done((bf16[1024,256]{1,0:T(8,128)(2,1)S(1)}, bf16[1024,256]{1,0:T(8,128)(2,1)}, u32[]{:S(2)}, u32[]{:S(2)}) %collective-permute-start.6) | collective-permute-done | bytes 524320 | tf_op jit(solution)/shard_map/ppermute | solution.py:1083
  51.1 7.8 %qkv_other.1 = (bf16[688,512]{1,0:T(8,128)(2,1)}, bf16[2,688,512]{2,1,0:T(8,128)(2,1)}, bf16[3,1024,512]{2,1,0:T(8,128)(2,1)}) custom-call(s32[5]{0:T(128)} %stack.50.scal.refs_0_.refs_12_, bf16[688,1024]{1,0:T(8,128)(2,1)} %get-tuple-element.135.n1.refs_15_, bf16[688,128]{1,0:T(8,128)(2,1)} %get-tuple-element.136.rank.refs_16_, ...), custom_call_target="tpu_custom_call" | custom-call | flops 1750000000 | bytes 250000 | tf_op jit(solution)/shard_map/qkv_other/pallas_call | solution.py:454
  62.2 4.7 %collective-permute-start.26 = (bf16[688,1024]{1,0:T(8,128)(2,1)S(1)}, bf16[688,1024]{1,0:T(8,128)(2,1)S(1)}, u32[]{:S(2)}, u32[]{:S(2)}) collective-permute-start(bf16[688,1024]{1,0:T(8,128)(2,1)S(1)} %bitcast.71), channel_id=1, source_target_pairs={{1,2},{2,1},{5,6},{6,5},{9,10},{10,9},{13,14},{14,13},{17,18},{18,... | collective-permute-start | bytes 4227080 | tf_op jit(solution)/shard_map/ppermute | solution.py:1079
  66.9 15.0 %attend.2 = (bf16[688,512]{1,0:T(8,128)(2,1)}, f32[688,512]{1,0:T(8,128)}) custom-call(s32[5]{0:T(128)} %stack.50.scal.refs_0_.refs_12_, bf16[688,512]{1,0:T(8,128)(2,1)} %get-tuple-element.204.q_ref, bf16[2,688,512]{2,1,0:T(8,128)(2,1)} %get-tuple-element.140.k_ref.v_ref, bf16[2,688,512]{2,1,0:T(8,128)(2,1)} %get-tuple-element.140.k_ref.v_ref, ...), custom_call_target="tpu_custom_call" | custom-call | flops 4000000000 | bytes 150000 | tf_op jit(solution)/shard_map/attend/pallas_call | solution.py:534
  84.5 15.0 %attend.3 = (bf16[688,512]{1,0:T(8,128)(2,1)}, f32[688,512]{1,0:T(8,128)}) custom-call(s32[5]{0:T(128)} %stack.50.scal.refs_0_.refs_12_, bf16[688,512]{1,0:T(8,128)(2,1)} %get-tuple-element.218.q_ref, bf16[2,688,512]{2,1,0:T(8,128)(2,1)} %get-tuple-element.138.k_ref.v_ref, bf16[2,688,512]{2,1,0:T(8,128)(2,1)} %get-tuple-element.138.k_ref.v_ref, ...), custom_call_target="tpu_custom_call" | custom-call | flops 4000000000 | bytes 150000 | tf_op jit(solution)/shard_map/attend/pallas_call | solution.py:534
  104.1 8.7 %branch.1 = (bf16[688,1024]{1,0:T(8,128)(2,1)}, bf16[688,1024]{1,0:T(8,128)(2,1)}, bf16[688,128]{1,0:T(8,128)(2,1)}, bf16[688,128]{1,0:T(8,128)(2,1)}, bf16[512,1024]{1,0:T(8,128)(2,1)}) custom-call(s32[5]{0:T(128)} %stack.50.scal.refs_0_.refs_12_, bf16[688,512]{1,0:T(8,128)(2,1)} %get-tuple-element.145.mix_a.mixed_ref, ...), custom_call_target="tpu_custom_call" | custom-call | flops 2000000000 | bytes 400000 | tf_op jit(solution)/shard_map/branch/pallas_call | solution.py:675
  116.2 24.4 %mlp.3 = (bf16[688,1024]{1,0:T(8,128)(2,1)}, bf16[688,128]{1,0:T(8,128)(2,1)}, bf16[688,1024]{1,0:T(8,128)(2,1)}, bf16[688,1024]{1,0:T(8,128)(2,1)}, f32[688,128...) custom-call(s32[5]{0:T(128)} %stack.50.scal.refs_0_.refs_12_, ...), custom_call_target="tpu_custom_call" | custom-call | flops 6249999872 | bytes 500000 | tf_op jit(solution)/shard_map/mlp/pallas_call | solution.py:797
  143.8 14.2 %mlp.4 = (bf16[688,1024]{1,0:T(8,128)(2,1)}, bf16[688,1024]{1,0:T(8,128)(2,1)}, f32[688,128]{1,0:T(8,128)}, f32[688,128]{1,0:T(8,128)}, f32[16,2048]{1,0:T(8,128)}, /*index=5*/f32[16,2048]{1,0:T(8,128)}) custom-call(s32[5]{0:T(128)} %stack.50.scal.refs_0_.refs_12_, bf16[688,1024]{1,0:T(8,128)(2,1)} %get-tuple-element.162.refs_1_.n2, ...), custom_call_target="tpu_custom_call" | custom-call | flops 3124999936 | bytes 500000 | tf_op jit(solution)/shard_map/mlp/pallas_call | solution.py:797
  159.2 14.5 %mlp.5 = (bf16[688,1024]{1,0:T(8,128)(2,1)}, bf16[688,1024]{1,0:T(8,128)(2,1)}, f32[688,128]{1,0:T(8,128)}, f32[688,128]{1,0:T(8,128)}, f32[16,2048]{1,0:T(8,128)}, /*index=5*/f32[16,2048]{1,0:T(8,128)}) custom-call(s32[5]{0:T(128)} %stack.50.scal.refs_0_.refs_12_, bf16[688,1024]{1,0:T(8,128)(2,1)} %get-tuple-element.162.refs_1_.n2, ...), custom_call_target="tpu_custom_call" | custom-call | flops 3124999936 | bytes 500000 | tf_op jit(solution)/shard_map/mlp/pallas_call | solution.py:797
  173.7 11.6 %middle.1 = (bf16[688,1024]{1,0:T(8,128)(2,1)}, bf16[688,1024]{1,0:T(8,128)(2,1)}, bf16[688,512]{1,0:T(8,128)(2,1)}, bf16[688,512]{1,0:T(8,128)(2,1)}, f32[16,51...) custom-call(s32[5]{0:T(128)} %stack.50.scal.refs_0_.refs_12_, ...), custom_call_target="tpu_custom_call" | custom-call | flops 2249999872 | bytes 500000 | tf_op jit(solution)/shard_map/middle/pallas_call | solution.py:887
  188.9 14.2 %attend_back.4 = (bf16[688,256]{1,0:T(8,128)(2,1)}, bf16[2,688,256]{2,1,0:T(8,128)(2,1)}, bf16[2,688,256]{2,1,0:T(8,128)(2,1)}) custom-call(s32[5]{0:T(128)} %stack.50.scal.refs_0_.refs_12_, bf16[688,512]{1,0:T(8,128)(2,1)} %get-tuple-element.204.q_ref, bf16[2,688,512]{2,1,0:T(8,128)(2,1)} %get-tuple-element.140.k_ref.v_ref, ...), custom_call_target="tpu_custom_call" | custom-call | flops 3249999872 | bytes 225000 | tf_op jit(solution)/shard_map/attend_back/pallas_call | solution.py:619
  203.1 3.1 collective-permute-start.34
  206.3 2.4 collective-permute-start.37
  208.6 14.5 %attend_back.5 = (bf16[688,256]{1,0:T(8,128)(2,1)}, bf16[2,688,256]{2,1,0:T(8,128)(2,1)}, bf16[2,688,256]{2,1,0:T(8,128)(2,1)}) custom-call(s32[5]{0:T(128)} %stack.50.scal.refs_0_.refs_12_, bf16[688,512]{1,0:T(8,128)(2,1)} %get-tuple-element.204.q_ref, bf16[2,688,512]{2,1,0:T(8,128)(2,1)} %get-tuple-element.140.k_ref.v_ref, ...), custom_call_target="tpu_custom_call" | custom-call | flops 3249999872 | bytes 225000 | tf_op jit(solution)/shard_map/attend_back/pallas_call | solution.py:619
  224.7 14.1 %attend_back.6 = (bf16[688,256]{1,0:T(8,128)(2,1)}, bf16[2,688,256]{2,1,0:T(8,128)(2,1)}, bf16[2,688,256]{2,1,0:T(8,128)(2,1)}) custom-call(s32[5]{0:T(128)} %stack.50.scal.refs_0_.refs_12_, bf16[688,512]{1,0:T(8,128)(2,1)} %get-tuple-element.218.q_ref, bf16[2,688,512]{2,1,0:T(8,128)(2,1)} %get-tuple-element.138.k_ref.v_ref, ...), custom_call_target="tpu_custom_call" | custom-call | flops 3249999872 | bytes 225000 | tf_op jit(solution)/shard_map/attend_back/pallas_call | solution.py:619
  241.3 14.3 %attend_back.7 = (bf16[688,256]{1,0:T(8,128)(2,1)}, bf16[2,688,256]{2,1,0:T(8,128)(2,1)}, bf16[2,688,256]{2,1,0:T(8,128)(2,1)}) custom-call(s32[5]{0:T(128)} %stack.50.scal.refs_0_.refs_12_, bf16[688,512]{1,0:T(8,128)(2,1)} %get-tuple-element.218.q_ref, bf16[2,688,512]{2,1,0:T(8,128)(2,1)} %get-tuple-element.138.k_ref.v_ref, ...), custom_call_target="tpu_custom_call" | custom-call | flops 3249999872 | bytes 225000 | tf_op jit(solution)/shard_map/attend_back/pallas_call | solution.py:619
  255.9 2.2 collective-permute-done.41.refs_11_
  258.1 6.7 %qkv_tables.1 = (bf16[2,688,512]{2,1,0:T(8,128)(2,1)}, bf16[2,688,512]{2,1,0:T(8,128)(2,1)}, bf16[688,128]{1,0:T(8,128)(2,1)}, f32[16,2048]{1,0:T(8,128)}, bf16[16,2048]{1,0:T(8,128)(2,1)}) custom-call(bf16[688,256]{1,0:T(8,128)(2,1)} %get-tuple-element.201.refs_0_, bf16[688,256]{1,0:T(8,128)(2,1)} %get-tuple-element.205.refs_1_, ...), custom_call_target="tpu_custom_call" | custom-call | flops 1750000000 | bytes 350000 | tf_op jit(solution)/shard_map/qkv_tables/pallas_call | solution.py:952
  268.6 3.5 %gather_images.2 = (bf16[8,16,3840]{2,1,0:T(8,128)(2,1)}, s32[16]{0:T(128)}) custom-call(s32[1]{0:T(128)} %bitcast.39.flag, bf16[8,16,3968]{2,1,0:T(8,128)(2,1)} %copy-done.5, bf16[8,16,3968]{2,1,0:T(8,128)(2,1)} %collective-permute-done.42.refs_1_), custom_call_target="tpu_custom_call" | custom-call | flops 5000000000 | bytes 25000 | tf_op jit(solution)/shard_map/gather_images/pallas_call | solution.py:1029
  272.8 12.2 %qkv_rows.1 = bf16[688,1024]{1,0:T(8,128)(2,1)} custom-call(bf16[688,256]{1,0:T(8,128)(2,1)} %get-tuple-element.201.refs_0_, bf16[688,256]{1,0:T(8,128)(2,1)} %get-tuple-element.205.refs_1_, bf16[2,688,512]{2,1,0:T(8,128)(2,1)} %get-tuple-element.225.refs_2_, bf16[688,256]{1,0:T(8,128)(2,1)} %get-tuple-element.216.refs_6_.refs_3_, ...), custom_call_target="tpu_custom_call" | custom-call | flops 3000000000 | bytes 400000 | tf_op jit(solution)/shard_map/qkv_rows/pallas_call | solution.py:984
  285.0 2.6 collective-permute-start.46
  289.8 4.0 %collective-permute-done.47 = bf16[4,16,1280]{2,1,0:T(8,128)(2,1)S(1)} collective-permute-done((bf16[4,16,1280]{2,1,0:T(8,128)(2,1)S(1)}, bf16[4,16,1280]{2,1,0:T(8,128)(2,1)S(1)}, u32[]{:S(2)}, u32[]{:S(2)}) %collective-permute-start.47) | collective-permute-done | bytes 163872 | tf_op jit(solution)/shard_map/ppermute | solution.py:1083
  295.6 3.8 %finish.3 = (f32[8,16,512]{2,1,0:T(8,128)}, f32[8,16,2048]{2,1,0:T(8,128)}, f32[8,16,2048]{2,1,0:T(8,128)}, f32[8,16,1024]{2,1,0:T(8,128)}, f32[8,16,1024]{2,1,0:T(8,128)}, /*index=5*/f32[8,16,1024]{2,1,0:T(8,128)}) custom-call(s32[1]{0:T(128)} %bitcast.core, bf16[8,16,3840]{2,1,0:T(8,128)(2,1)} %get-tuple-element.232.own, bf16[8,16,3840]{2,1,0:T(8,128)(2,1)} %copy-done.22), custom_call_target="tpu_custom_call" | custom-call | flops 5000000000 | bytes 25000 | tf_op jit(solution)/shard_map/finish/pallas_call | solution.py:1067
  299.3 3.5 %collective-permute-done.48.refs_2_ = bf16[8,16,1280]{2,1,0:T(8,128)(2,1)S(1)} collective-permute-done((bf16[8,16,1280]{2,1,0:T(8,128)(2,1)S(1)}, bf16[8,16,1280]{2,1,0:T(8,128)(2,1)S(1)}, u32[]{:S(2)}, u32[]{:S(2)}) %collective-permute-start.48) | collective-permute-done | bytes 327712 | tf_op jit(solution)/shard_map/ppermute | solution.py:1083
  302.8 2.4 collective-permute-done.46
  305.3 2.0 gather_images.3
  307.4 3.1 %bitcast_convert_fusion = f32[1,688,1024]{2,1,0:T(8,128)} fusion(bf16[688,1024]{1,0:T(8,128)(2,1)S(1)} %copy-done.2, bf16[688,1024]{1,0:T(8,128)(2,1)} %collective-permute-done.46, pred[]{:T(512)S(6)} %eq.24), kind=kLoop, calls=%fused_computation | loop fusion | flops 1409024 | bytes 5636097 | tf_op jit(solution)/shard_map/broadcast_in_dim | solution.py:1335
  311.3 2.2 finish.2
  (223 shorter events, 58.7 us)
Async XLA Ops:
  6.2 30.3 %collective-permute-start.1 = (bf16[688,1024]{1,0:T(8,128)(2,1)}, bf16[688,1024]{1,0:T(8,128)(2,1)}, u32[]{:S(2)}, u32[]{:S(2)}) collective-permute-start(bf16[688,1024]{1,0:T(8,128)(2,1)} %bitcast.95), channel_id=1, source_target_pairs={{1,2},{2,1},{5,6},{6,5},{9,10},{10,9},{13,14},{14,13},{17,18},{18,... | collective-permute-start | bytes 4227080 | tf_op jit(solution)/shard_map/ppermute | solution.py:1079
  28.8 21.2 %collective-permute-start.9 = (bf16[2,3,128,512]{3,2,1,0:T(8,128)(2,1)S(1)}, bf16[2,3,128,512]{3,2,1,0:T(8,128)(2,1)S(1)}, u32[]{:S(2)}, u32[]{:S(2)}) collective-permute-start(bf16[2,3,128,512]{3,2,1,0:T(8,128)(2,1)S(1)} %pad_maximum_fusion.rest_0_), channel_id=1, source_target_pairs={{0,2},{2,0},{1,3},{3,1},{4,6},{6,4},{5,7},{7,5},{8,10},{10,8},{9,1... | collective-permute-start | bytes 2359304 | tf_op jit(solution)/shard_map/ppermute | solution.py:1083
  32.5 17.5 %collective-permute-start.10 = (bf16[2,3,128,512]{3,2,1,0:T(8,128)(2,1)S(1)}, bf16[2,3,128,512]{3,2,1,0:T(8,128)(2,1)S(1)}, u32[]{:S(2)}, u32[]{:S(2)}) collective-permute-start(bf16[2,3,128,512]{3,2,1,0:T(8,128)(2,1)S(1)} %pad_maximum_fusion.1.rest_1_), channel_id=1, source_target_pairs={{0,2},{2,0},{1,3},{3,1},{4,6},{6,4},{5,7},{7,5},{8,10},{10,8},{9,1... | collective-permute-start | bytes 2359304 | tf_op jit(solution)/shard_map/ppermute | solution.py:1083
  46.3 15.9 %collective-permute-start.11 = (bf16[2,688,512]{2,1,0:T(8,128)(2,1)}, bf16[2,688,512]{2,1,0:T(8,128)(2,1)}, u32[]{:S(2)}, u32[]{:S(2)}) collective-permute-start(bf16[2,688,512]{2,1,0:T(8,128)(2,1)} %get-tuple-element.140.k_ref.v_ref), channel_id=1, source_target_pairs={{0,2},{2,0},{1,3},{3,1},{4,6},{6,4},{5,7},{7,5},{8,10},{10,8},{9,1... | collective-permute-start | bytes 4227080 | tf_op jit(solution)/shard_map/ppermute | solution.py:1083
  58.9 25.6 %collective-permute-start.16 = (bf16[2,688,512]{2,1,0:T(8,128)(2,1)}, bf16[2,688,512]{2,1,0:T(8,128)(2,1)}, u32[]{:S(2)}, u32[]{:S(2)}) collective-permute-start(bf16[2,688,512]{2,1,0:T(8,128)(2,1)} %get-tuple-element.138.k_ref.v_ref), channel_id=1, source_target_pairs={{0,2},{2,0},{1,3},{3,1},{4,6},{6,4},{5,7},{7,5},{8,10},{10,8},{9,1... | collective-permute-start | bytes 4227080 | tf_op jit(solution)/shard_map/ppermute | solution.py:1083
  60.0 21.9 %collective-permute-start.12 = (bf16[1024,256]{1,0:T(8,128)(2,1)}, bf16[1024,256]{1,0:T(8,128)(2,1)S(1)}, u32[]{:S(2)}, u32[]{:S(2)}) collective-permute-start(bf16[1024,256]{1,0:T(8,128)(2,1)} %collective-permute-done.6.refs_5_), channel_id=1, source_target_pairs={{0,8},{8,0},{1,9},{9,1},{2,10},{10,2},{3,11},{11,3},{4,12},{12,4},... | collective-permute-start | bytes 1572872 | tf_op jit(solution)/shard_map/ppermute | solution.py:1083
  61.8 21.1 %collective-permute-start.15 = (bf16[1024,256]{1,0:T(8,128)(2,1)}, bf16[1024,256]{1,0:T(8,128)(2,1)S(1)}, u32[]{:S(2)}, u32[]{:S(2)}) collective-permute-start(bf16[1024,256]{1,0:T(8,128)(2,1)} %collective-permute-done.6.refs_5_), channel_id=1, source_target_pairs={{0,4},{4,0},{1,5},{5,1},{2,6},{6,2},{3,7},{7,3},{8,12},{12,8},{9,1... | collective-permute-start | bytes 1572872 | tf_op jit(solution)/shard_map/ppermute | solution.py:1083
  62.2 20.7 %collective-permute-start.17 = (bf16[128,1024]{1,0:T(8,128)(2,1)S(1)}, bf16[128,1024]{1,0:T(8,128)(2,1)S(1)}, u32[]{:S(2)}, u32[]{:S(2)}) collective-permute-start(bf16[128,1024]{1,0:T(8,128)(2,1)S(1)} %constant_dynamic-slice_fusion.5), channel_id=1, source_target_pairs={{0,1},{1,0},{2,3},{3,2},{4,5},{5,4},{6,7},{7,6},{8,9},{9,8},{10,11... | collective-permute-start | bytes 786440 | tf_op jit(solution)/shard_map/ppermute | solution.py:1083
  62.2 39.8 %collective-permute-start.26 = (bf16[688,1024]{1,0:T(8,128)(2,1)S(1)}, bf16[688,1024]{1,0:T(8,128)(2,1)S(1)}, u32[]{:S(2)}, u32[]{:S(2)}) collective-permute-start(bf16[688,1024]{1,0:T(8,128)(2,1)S(1)} %bitcast.71), channel_id=1, source_target_pairs={{1,2},{2,1},{5,6},{6,5},{9,10},{10,9},{13,14},{14,13},{17,18},{18,... | collective-permute-start | bytes 4227080 | tf_op jit(solution)/shard_map/ppermute | solution.py:1079
  81.9 18.5 %collective-permute-start.14 = (bf16[256,1024]{1,0:T(8,128)(2,1)S(1)}, bf16[256,1024]{1,0:T(8,128)(2,1)S(1)}, u32[]{:S(2)}, u32[]{:S(2)}) collective-permute-start(bf16[256,1024]{1,0:T(8,128)(2,1)S(1)} %constant_dynamic-slice_fusion.4), channel_id=1, source_target_pairs={{0,1},{1,0},{2,3},{3,2},{4,5},{5,4},{6,7},{7,6},{8,9},{9,8},{10,11... | collective-permute-start | bytes 1572872 | tf_op jit(solution)/shard_map/ppermute | solution.py:1083
  82.9 16.5 %collective-permute-start.18 = (bf16[128,1024]{1,0:T(8,128)(2,1)S(1)}, bf16[128,1024]{1,0:T(8,128)(2,1)S(1)}, u32[]{:S(2)}, u32[]{:S(2)}) collective-permute-start(bf16[128,1024]{1,0:T(8,128)(2,1)S(1)} %collective-permute-done.17), channel_id=1, source_target_pairs={{0,4},{4,0},{1,5},{5,1},{2,6},{6,2},{3,7},{7,3},{8,12},{12,8},{9,1... | collective-permute-start | bytes 786440 | tf_op jit(solution)/shard_map/ppermute | solution.py:1083
  84.0 19.3 %collective-permute-start.13 = (bf16[1024,256]{1,0:T(8,128)(2,1)S(1)}, bf16[1024,256]{1,0:T(8,128)(2,1)}, u32[]{:S(2)}, u32[]{:S(2)}) collective-permute-start(bf16[1024,256]{1,0:T(8,128)(2,1)S(1)} %collective-permute-done.12.refs_7_), channel_id=1, source_target_pairs={{0,4},{4,0},{1,5},{5,1},{2,6},{6,2},{3,7},{7,3},{8,12},{12,8},{9,1... | collective-permute-start | bytes 1572872 | tf_op jit(solution)/shard_map/ppermute | solution.py:1083
  112.9 28.4 %collective-permute-start.20 = (bf16[16,4096]{1,0:T(8,128)(2,1)S(1)}, bf16[16,4096]{1,0:T(8,128)(2,1)}, u32[]{:S(2)}, u32[]{:S(2)}) collective-permute-start(bf16[16,4096]{1,0:T(8,128)(2,1)S(1)} %pad_maximum_fusion.5), channel_id=1, source_target_pairs={{0,1},{1,0},{2,3},{3,2},{4,5},{5,4},{6,7},{7,6},{8,9},{9,8},{10,11... | collective-permute-start | bytes 393224 | tf_op jit(solution)/shard_map/ppermute | solution.py:1083
  113.5 27.8 %collective-permute-start.23 = (bf16[1024,256]{1,0:T(8,128)(2,1)S(1)}, bf16[1024,256]{1,0:T(8,128)(2,1)S(1)}, u32[]{:S(2)}, u32[]{:S(2)}) collective-permute-start(bf16[1024,256]{1,0:T(8,128)(2,1)S(1)} %collective-permute-done.12.refs_7_), channel_id=1, source_target_pairs={{0,2},{2,0},{1,3},{3,1},{4,6},{6,4},{5,7},{7,5},{8,10},{10,8},{9,1... | collective-permute-start | bytes 1572872 | tf_op jit(solution)/shard_map/ppermute | solution.py:1083
  114.8 27.0 %collective-permute-start.22 = (bf16[1024,256]{1,0:T(8,128)(2,1)S(1)}, bf16[1024,256]{1,0:T(8,128)(2,1)S(1)}, u32[]{:S(2)}, u32[]{:S(2)}) collective-permute-start(bf16[1024,256]{1,0:T(8,128)(2,1)S(1)} %collective-permute-done.15.refs_6_), channel_id=1, source_target_pairs={{0,2},{2,0},{1,3},{3,1},{4,6},{6,4},{5,7},{7,5},{8,10},{10,8},{9,1... | collective-permute-start | bytes 1572872 | tf_op jit(solution)/shard_map/ppermute | solution.py:1083
  114.9 27.9 %collective-permute-start.21 = (bf16[1024,256]{1,0:T(8,128)(2,1)}, bf16[1024,256]{1,0:T(8,128)(2,1)}, u32[]{:S(2)}, u32[]{:S(2)}) collective-permute-start(bf16[1024,256]{1,0:T(8,128)(2,1)} %collective-permute-done.6.refs_5_), channel_id=1, source_target_pairs={{0,2},{2,0},{1,3},{3,1},{4,6},{6,4},{5,7},{7,5},{8,10},{10,8},{9,1... | collective-permute-start | bytes 1572872 | tf_op jit(solution)/shard_map/ppermute | solution.py:1083
  115.3 25.4 %collective-permute-start.31 = (bf16[256,1024]{1,0:T(8,128)(2,1)S(1)}, bf16[256,1024]{1,0:T(8,128)(2,1)}, u32[]{:S(2)}, u32[]{:S(2)}) collective-permute-start(bf16[256,1024]{1,0:T(8,128)(2,1)S(1)} %collective-permute-done.24.refs_10_), channel_id=1, source_target_pairs={{0,8},{8,0},{1,9},{9,1},{2,10},{10,2},{3,11},{11,3},{4,12},{12,4},... | collective-permute-start | bytes 1572872 | tf_op jit(solution)/shard_map/ppermute | solution.py:1083
  140.7 17.4 %collective-permute-start.30 = (bf16[256,1024]{1,0:T(8,128)(2,1)}, bf16[256,1024]{1,0:T(8,128)(2,1)}, u32[]{:S(2)}, u32[]{:S(2)}) collective-permute-start(bf16[256,1024]{1,0:T(8,128)(2,1)} %collective-permute-done.25.refs_11_), channel_id=1, source_target_pairs={{0,2},{2,0},{1,3},{3,1},{4,6},{6,4},{5,7},{7,5},{8,10},{10,8},{9,1... | collective-permute-start | bytes 1572872 | tf_op jit(solution)/shard_map/ppermute | solution.py:1083
  141.2 16.8 %collective-permute-start.29 = (bf16[256,1024]{1,0:T(8,128)(2,1)S(1)}, bf16[256,1024]{1,0:T(8,128)(2,1)S(1)}, u32[]{:S(2)}, u32[]{:S(2)}) collective-permute-start(bf16[256,1024]{1,0:T(8,128)(2,1)S(1)} %collective-permute-done.24.refs_10_), channel_id=1, source_target_pairs={{0,2},{2,0},{1,3},{3,1},{4,6},{6,4},{5,7},{7,5},{8,10},{10,8},{9,1... | collective-permute-start | bytes 1572872 | tf_op jit(solution)/shard_map/ppermute | solution.py:1083
  141.3 16.7 %collective-permute-start.28 = (bf16[256,1024]{1,0:T(8,128)(2,1)S(1)}, bf16[256,1024]{1,0:T(8,128)(2,1)S(1)}, u32[]{:S(2)}, u32[]{:S(2)}) collective-permute-start(bf16[256,1024]{1,0:T(8,128)(2,1)S(1)} %collective-permute-done.14.refs_9_), channel_id=1, source_target_pairs={{0,2},{2,0},{1,3},{3,1},{4,6},{6,4},{5,7},{7,5},{8,10},{10,8},{9,1... | collective-permute-start | bytes 1572872 | tf_op jit(solution)/shard_map/ppermute | solution.py:1083
  142.6 15.5 %collective-permute-start.27 = (bf16[1024,256]{1,0:T(8,128)(2,1)}, bf16[1024,256]{1,0:T(8,128)(2,1)S(1)}, u32[]{:S(2)}, u32[]{:S(2)}) collective-permute-start(bf16[1024,256]{1,0:T(8,128)(2,1)} %collective-permute-done.13.refs_8_), channel_id=1, source_target_pairs={{0,2},{2,0},{1,3},{3,1},{4,6},{6,4},{5,7},{7,5},{8,10},{10,8},{9,1... | collective-permute-start | bytes 1572872 | tf_op jit(solution)/shard_map/ppermute | solution.py:1083
  142.7 15.4 %collective-permute-start.32 = (bf16[256,1024]{1,0:T(8,128)(2,1)}, bf16[256,1024]{1,0:T(8,128)(2,1)}, u32[]{:S(2)}, u32[]{:S(2)}) collective-permute-start(bf16[256,1024]{1,0:T(8,128)(2,1)} %collective-permute-done.31.refs_12_), channel_id=1, source_target_pairs={{0,2},{2,0},{1,3},{3,1},{4,6},{6,4},{5,7},{7,5},{8,10},{10,8},{9,1... | collective-permute-start | bytes 1572872 | tf_op jit(solution)/shard_map/ppermute | solution.py:1083
  188.2 18.0 %collective-permute-start.35 = (bf16[16,3968]{1,0:T(8,128)(2,1)S(1)}, bf16[16,3968]{1,0:T(8,128)(2,1)S(1)}, u32[]{:S(2)}, u32[]{:S(2)}) collective-permute-start(bf16[16,3968]{1,0:T(8,128)(2,1)S(1)} %maximum_maximum_fusion), channel_id=1, source_target_pairs={{0,1},{1,0},{2,3},{3,2},{4,5},{5,4},{6,7},{7,6},{8,9},{9,8},{10,11... | collective-permute-start | bytes 380936 | tf_op jit(solution)/shard_map/ppermute | solution.py:1083
  203.1 38.2 %collective-permute-start.34 = (bf16[688,1024]{1,0:T(8,128)(2,1)S(1)}, bf16[688,1024]{1,0:T(8,128)(2,1)S(1)}, u32[]{:S(2)}, u32[]{:S(2)}) collective-permute-start(bf16[688,1024]{1,0:T(8,128)(2,1)S(1)} %copy-done.4), channel_id=1, source_target_pairs={{1,2},{2,1},{5,6},{6,5},{9,10},{10,9},{13,14},{14,13},{17,18},{18,... | collective-permute-start | bytes 4227080 | tf_op jit(solution)/shard_map/ppermute | solution.py:1079
  206.3 16.8 %collective-permute-start.37 = (bf16[2,16,3968]{2,1,0:T(8,128)(2,1)S(1)}, bf16[2,16,3968]{2,1,0:T(8,128)(2,1)S(1)}, u32[]{:S(2)}, u32[]{:S(2)}) collective-permute-start(bf16[2,16,3968]{2,1,0:T(8,128)(2,1)S(1)} %maximum_select_fusion.3), channel_id=1, source_target_pairs={{0,16},{16,0},{1,17},{17,1},{2,18},{18,2},{3,19},{19,3},{4,20},{20... | collective-permute-start | bytes 761864 | tf_op jit(solution)/shard_map/ppermute | solution.py:1083
  223.2 15.7 %collective-permute-start.39 = (bf16[4,16,3968]{2,1,0:T(8,128)(2,1)S(1)}, bf16[4,16,3968]{2,1,0:T(8,128)(2,1)}, u32[]{:S(2)}, u32[]{:S(2)}) collective-permute-start(bf16[4,16,3968]{2,1,0:T(8,128)(2,1)S(1)} %maximum_select_fusion.1), channel_id=1, source_target_pairs={{0,8},{8,0},{1,9},{9,1},{2,10},{10,2},{3,11},{11,3},{4,12},{12,4},... | collective-permute-start | bytes 1523720 | tf_op jit(solution)/shard_map/ppermute | solution.py:1083
  224.2 31.6 %collective-permute-start.36 = (bf16[2,688,256]{2,1,0:T(8,128)(2,1)}, bf16[2,688,256]{2,1,0:T(8,128)(2,1)S(1)}, u32[]{:S(2)}, u32[]{:S(2)}) collective-permute-start(bf16[2,688,256]{2,1,0:T(8,128)(2,1)} %get-tuple-element.209), channel_id=1, source_target_pairs={{0,2},{2,0},{1,3},{3,1},{4,6},{6,4},{5,7},{7,5},{8,10},{10,8},{9,1... | collective-permute-start | bytes 2113544 | tf_op jit(solution)/shard_map/ppermute | solution.py:1083
  224.2 31.6 %collective-permute-start.38 = (bf16[2,688,256]{2,1,0:T(8,128)(2,1)}, bf16[2,688,256]{2,1,0:T(8,128)(2,1)S(1)}, u32[]{:S(2)}, u32[]{:S(2)}) collective-permute-start(bf16[2,688,256]{2,1,0:T(8,128)(2,1)} %get-tuple-element.212), channel_id=1, source_target_pairs={{0,2},{2,0},{1,3},{3,1},{4,6},{6,4},{5,7},{7,5},{8,10},{10,8},{9,1... | collective-permute-start | bytes 2113544 | tf_op jit(solution)/shard_map/ppermute | solution.py:1083
  240.3 24.6 %collective-permute-start.42 = (bf16[8,16,3968]{2,1,0:T(8,128)(2,1)S(1)}, bf16[8,16,3968]{2,1,0:T(8,128)(2,1)}, u32[]{:S(2)}, u32[]{:S(2)}) collective-permute-start(bf16[8,16,3968]{2,1,0:T(8,128)(2,1)S(1)} %maximum_select_fusion.refs_0_), channel_id=1, source_target_pairs={{0,4},{4,0},{1,5},{5,1},{2,6},{6,2},{3,7},{7,3},{8,12},{12,8},{9,1... | collective-permute-start | bytes 3047432 | tf_op jit(solution)/shard_map/ppermute | solution.py:1083
  241.0 14.9 %collective-permute-start.40 = (bf16[2,688,256]{2,1,0:T(8,128)(2,1)}, bf16[2,688,256]{2,1,0:T(8,128)(2,1)S(1)}, u32[]{:S(2)}, u32[]{:S(2)}) collective-permute-start(bf16[2,688,256]{2,1,0:T(8,128)(2,1)} %get-tuple-element.223), channel_id=1, source_target_pairs={{0,2},{2,0},{1,3},{3,1},{4,6},{6,4},{5,7},{7,5},{8,10},{10,8},{9,1... | collective-permute-start | bytes 2113544 | tf_op jit(solution)/shard_map/ppermute | solution.py:1083
  272.1 22.5 %collective-permute-start.50 = (bf16[8,16,3840]{2,1,0:T(8,128)(2,1)}, bf16[8,16,3840]{2,1,0:T(8,128)(2,1)S(1)}, u32[]{:S(2)}, u32[]{:S(2)}) collective-permute-start(bf16[8,16,3840]{2,1,0:T(8,128)(2,1)} %get-tuple-element.232.own), channel_id=1, source_target_pairs={{0,2},{2,0},{1,3},{3,1},{4,6},{6,4},{5,7},{7,5},{8,10},{10,8},{9,1... | collective-permute-start | bytes 2949128 | tf_op jit(solution)/shard_map/ppermute | solution.py:1083
  285.0 20.3 %collective-permute-start.46 = (bf16[688,1024]{1,0:T(8,128)(2,1)}, bf16[688,1024]{1,0:T(8,128)(2,1)}, u32[]{:S(2)}, u32[]{:S(2)}) collective-permute-start(bf16[688,1024]{1,0:T(8,128)(2,1)} %qkv_rows.1), channel_id=1, source_target_pairs={{1,2},{2,1},{5,6},{6,5},{9,10},{10,9},{13,14},{14,13},{17,18},{18,... | collective-permute-start | bytes 4227080 | tf_op jit(solution)/shard_map/ppermute | solution.py:1079
  (56 other events, 490.8 us)

commit v5 on v4

--- a/solution.py
+++ b/solution.py
@@ -427,7 +427,7 @@
         ],
         scratch_shapes=[pltpu.VMEM((rows, PAD), BF), pltpu.SemaphoreType.DMA((1,))],
         compiler_params=params(dimension_semantics=("arbitrary",)),
-        cost_estimate=cost(7e-6 * 1e15, 8e6),
+        cost_estimate=cost(1e-7 * 1e15, 1e5),
         name="qkv_local",
     )(scal, tok, swapped, gain, w, qa, qb)
 
@@ -694,11 +694,9 @@
     )(scal, mix_a, mix_b, tok, w_a, oa_a, oa_b, ob, scale_one, gain_two, ua, *arrays)
 
 
-def mlp_kernel(nears, step, more, *refs):
+def mlp_kernel(nears, counts, step, more, *refs):
     scal, n2, rank_up, ub, da = refs[:5]
-    count = 1 if nears is None else len(nears)
-    ups, downs = refs[5 : 5 + count], refs[5 + count : 5 + 2 * count]
-    rest = refs[5 + 2 * count :]
+    ups, downs, rest = refs[5 : 5 + counts[0]], refs[5 + counts[0] : 5 + sum(counts)], refs[5 + sum(counts) :]
     if nears is None:
         cot, scale_two, dbs, grad_mlp, grad_rank = rest[:5]
         earlier, rest = (), rest[5:]
@@ -719,7 +717,8 @@
         if nears is None:
             sources = ups[0].at[:, at], downs[0].at[at]
         else:
-            sources = ups[piece], downs[piece]
+            last = counts[0] - 1
+            sources = ups[piece] if piece < last else ups[last].at[piece - last], downs[piece]
         for which, (source, target) in enumerate(zip(sources, (wu.at[:, at], wd.at[at]))):
             copy = pltpu.make_async_copy(source, target, sem.at[which, piece])
             copy.start()
@@ -733,8 +732,6 @@
         grad_low = (scale_two[...] * (cot[...].astype(F32) * row_mask(scal, cot.shape[0]))).astype(BF)
         grad_mlp[...] = grad_low
         grad_rank[...] = dotg(grad_low, pad_rows(db[...]), 1, 1).astype(BF)
-    if more == 6:
-        gub_out[...], gda_out[...] = earlier[4][...], earlier[5][...]
     ubs[...] = jnp.zeros_like(ubs)
     das[...] = jnp.zeros_like(das)
     for piece in range(pieces):
@@ -795,10 +792,10 @@
     low = jax.ShapeDtypeStruct((rows, width), BF)
     first = [low, jax.ShapeDtypeStruct((rows, PAD), BF)] if nears is None else []
     return pl.pallas_call(
-        functools.partial(mlp_kernel, nears, step, len(earlier)),
+        functools.partial(mlp_kernel, nears, (len(ups), len(downs)), step, len(earlier)),
         in_specs=[scalars()]
         + [whole()] * 4
-        + [in_place()] * (2 * len(ups))
+        + [in_place()] * (len(ups) + len(downs))
         + [whole()] * (len(grads) + len(earlier)),
         out_specs=[whole()] * (len(first) + 6),
         out_shape=first + [sums, sums, ranked, ranked, table, table],
@@ -815,15 +812,6 @@
         cost_estimate=cost(25e-6 * units / half * 1e15, 20e6),
         name="mlp",
     )(scal, n2, rank_up, ub, da, *ups, *downs, *grads, *earlier)
-
-
-def mlp_other(scal, n2, rank_up, tables, up, down, grads, earlier):
-    for odd in range(2):
-        ups, nears = up.held(odd)
-        downs, same = down.held(odd)
-        assert nears == same
-        earlier = mlp(scal, n2, rank_up, tables, tables, ups, downs, grads, nears, tuple(earlier))
-    return earlier
 
 
 def middle_kernel(
@@ -1113,10 +1101,6 @@
         self.pairs = even + [flip("core")(array) for array in even]
         self.names = self.nears + tuple(near + 1 for near in self.nears)
 
-    def held(self, odd):
-        names = tuple(near + odd for near in self.nears)
-        return [self.parts[near] for near in names], names
-
 
 def half_columns(array, index):
     size = array.shape[1] // 2
@@ -1204,6 +1188,7 @@
     qkv_b, out_b, up_b, down_b = (jnp.swapaxes(table, -1, -2) for table in (qkv_b, out_b, up_b, down_b))
     pick = lambda table, index: lax.dynamic_index_in_dim(table, index, 0, False)
     flat = lambda table: jnp.swapaxes(table, 0, 1).reshape(rank, 3 * third)
+    half_qkv.parts[0] = after(half_qkv.parts[0], half_out.mine, half_up.mine, half_down.mine)
     half_qkv.hop(0, "x")
     half_qkv.hop(0, "zb")
     packed_first = jnp.concatenate([flat(pick(qkv_b, adapter_other)), pick(out_a, adapter_other)], axis=1)
@@ -1213,7 +1198,7 @@
     gain_one, gain_two, scale_one, scale_two = (v.reshape(1, width) for v in (gain_one, gain_two, scale_one, scale_two))
 
     other_tables = flip("tensor")(packed_first)
-    half_up.over_tensor(half_qkv.parts[4], other_tables)
+    half_up.over_tensor(half_qkv.parts[4])
     half_qkv.last_hop()
     half_qkv.parts[6] = after(half_qkv.parts[6], scal, qa, qb, other_tables, half_up.mine)
     tok_swapped = after(tok_swapped, half_qkv.parts[2], half_qkv.parts[4], other_tables, scal, half_out.mine, half_down.mine)
@@ -1238,19 +1223,22 @@
         scal, after(mix_a, half_up.parts[6], half_down.parts[0]), mix_b, tok, w_out, half_out, oa, other_tables, out_b, scale_one, gain_two, up_a
     )
     half_down.hop(2, "zb", n2)
-    other_units = flip("tensor")(after(packed, n2))
-    for near in (0, 2, 4):
-        half_up.hop(near, "core", n2)
+    other_units = flip("tensor")(after(packed, mix_b))
+    evens = (0, 2, 4, 6)
+    ups = after([half_up.parts[near] for near in evens], mix_b)
+    ups_odd = flip("core")(jnp.stack(ups))
+    for near in evens[:3]:
+        half_down.hop(near, "core", n2)
     cot = jnp.where(core == tensor, cotangent[0], cot_swapped)
     grad_mlp, grad_rank, m, g, rd, gru, gub_a, gda_a = mlp(
-        scal, after(n2, half_down.parts[2], half_down.parts[4]), rank_up, up_b, down_a, [w_up], [w_down],
+        scal, after(n2, half_down.parts[2], half_down.parts[4], other_units), rank_up, up_b, down_a, [w_up], [w_down],
         [cot, scale_two, down_b],
     )
-    half_up.hop(6, "core", m)
-    for near in (0, 2, 4, 6):
-        half_down.hop(near, "core", m)
-    m, g, rd, gru, gub_b, gda_b = mlp_other(
-        scal, n2, rank_up, other_units, half_up, half_down, [grad_mlp, grad_rank], (m, g, rd, gru)
+    half_down.hop(6, "core", m)
+    nears = evens + tuple(near + 1 for near in evens)
+    m, g, rd, gru, gub_b, gda_b = mlp(
+        scal, n2, rank_up, other_units, other_units, [*ups, ups_odd], [half_down.parts[near] for near in nears],
+        [grad_mlp, grad_rank], nears, (m, g, rd, gru),
     )
     layer, grad_res, grad_a, grad_b, goa_a, goa_b, gob, gua, gdb = middle(
         scal,

time: 319 us -> 318 us (level)
  Pallas kernels: 208 us -> 204 us
  starting transfers between devices: 46.1 us -> 42.4 us
    pallas_call x3 -> x2, Pallas kernels: 53.1 us -> 48.9 us  [mlp(): pl.pallas_call(functools.partial(mlp_kernel, nears, (len(ups), len(downs)...]
    ppermute x47 -> x44, starting transfers between devices: 33.8 us -> 30.6 us  [flip(): return lambda array: lax.ppermute(array, axis, FLIP)]
    ppermute x47 -> x44, waiting for transfers between devices: 21.4 us -> 23.1 us  [flip(): return lambda array: lax.ppermute(array, axis, FLIP)]
    unnamed x80 -> x88, local copies, waits for them, and re-layouts: 7.31 us -> 6.99 us
  transfers between devices with their start and end apart: 51 -> 48, of which waited for: 10 -> 13; matrix products, arithmetic and copies ran while one was open for 6% -> 8% of each run, Pallas kernels for 57% -> 52%
where the time goes in v5:
time: 318 us; the launch traced here: 313 us
  Pallas kernels  204 us (64%)
  starting transfers between devices  42.4 us (13%)
  waiting for transfers between devices  26.5 us (8%)
  local copies, waits for them, and re-layouts  21.5 us (7%)
  other arithmetic  10.3 us (3%)
  between operations  7.64 us (2%)
    pallas_call x4, Pallas kernels, attend_back(): pl.pallas_call(attend_back_kernel, grid=(pairs,), in_specs=[scalars(), fl...  56.8 us
    pallas_call x2, Pallas kernels, mlp(): pl.pallas_call(functools.partial(mlp_kernel, nears, (len(ups), len(downs)...  48.9 us
    ppermute x44, starting transfers between devices, flip(): return lambda array: lax.ppermute(array, axis, FLIP)  30.6 us
    pallas_call x2, Pallas kernels, attend(): pl.pallas_call(attend_kernel, grid=(pairs,), in_specs=[scalars(), flat, t...  29.8 us
    ppermute x44, waiting for transfers between devices, flip(): return lambda array: lax.ppermute(array, axis, FLIP)  23.1 us
    pallas_call x1, Pallas kernels, qkv_rows(): pl.pallas_call(functools.partial(qkv_rows_kernel, len(grads_a), len(grads...  12.4 us
    ppermute x4, starting transfers between devices, swap(): return lax.ppermute(rows, ('core', 'tensor'), SWAP)  11.7 us
    pallas_call x1, Pallas kernels, middle(): pl.pallas_call(middle_kernel, grid=(blocks,), in_specs=[scalars()] + [blo...  11.6 us
  transfers between devices with their start and end apart: 48, of which 13 were waited for; matrix products, arithmetic and copies ran while one was open for 8% of the time, Pallas kernels for 52%

profile of v5, /device:TPU:1, one launch (start us, length us, event | category | flops | bytes accessed | tf_op | source)
XLA Modules:
  0.0 312.7 jit_solution(14330671913711126530)
XLA Ops:
  1.8 2.1 collective-permute-start.2
  23.4 2.0 stack.65.scal.refs_0_.refs_12_
  25.4 3.1 collective-permute-done.3
  32.1 3.2 %collective-permute-done.7 = bf16[3,64,512]{2,1,0:T(8,128)(2,1)S(1)} collective-permute-done((bf16[3,64,512]{2,1,0:T(8,128)(2,1)S(1)}, bf16[3,64,512]{2,1,0:T(8,128)(2,1)S(1)}, u32[]{:S(2)}, u32[]{:S(2)}) %collective-permute-start.7) | collective-permute-done | bytes 196640 | tf_op jit(solution)/shard_map/ppermute | solution.py:1071
  38.7 9.7 %qkv_local.1 = (bf16[688,1024]{1,0:T(8,128)(2,1)}, bf16[688,1024]{1,0:T(8,128)(2,1)}, bf16[688,128]{1,0:T(8,128)(2,1)}, bf16[688,512]{1,0:T(8,128)(2,1)}, bf16[2,688,512]{2,1,0:T(8,128)(2,1)}) custom-call(s32[5]{0:T(128)} %stack.65.scal.refs_0_.refs_12_, bf16[688,1024]{1,0:T(8,128)(2,1)} %bitcast.77, bf16[688,1024]{1,0:T(8,128)(2,1)} %copy-done.5, ...), custom_call_target="tpu_custom_call" | custom-call | flops 25000000 | bytes 2500 | tf_op jit(solution)/shard_map/qkv_local/pallas_call | solution.py:402
  48.6 2.6 collective-permute-done.6.refs_5_
  52.1 7.8 %qkv_other.1 = (bf16[688,512]{1,0:T(8,128)(2,1)}, bf16[2,688,512]{2,1,0:T(8,128)(2,1)}, bf16[3,1024,512]{2,1,0:T(8,128)(2,1)}) custom-call(s32[5]{0:T(128)} %stack.65.scal.refs_0_.refs_12_, bf16[688,1024]{1,0:T(8,128)(2,1)} %get-tuple-element.130.n1.refs_15_, bf16[688,128]{1,0:T(8,128)(2,1)} %get-tuple-element.131.rank.refs_16_, ...), custom_call_target="tpu_custom_call" | custom-call | flops 1750000000 | bytes 250000 | tf_op jit(solution)/shard_map/qkv_other/pallas_call | solution.py:454
  63.6 4.6 %collective-permute-start.28 = (bf16[688,1024]{1,0:T(8,128)(2,1)S(1)}, bf16[688,1024]{1,0:T(8,128)(2,1)S(1)}, u32[]{:S(2)}, u32[]{:S(2)}) collective-permute-start(bf16[688,1024]{1,0:T(8,128)(2,1)S(1)} %bitcast.75), channel_id=1, source_target_pairs={{1,2},{2,1},{5,6},{6,5},{9,10},{10,9},{13,14},{14,13},{17,18},{18,... | collective-permute-start | bytes 4227080 | tf_op jit(solution)/shard_map/ppermute | solution.py:1067
  68.2 14.9 %attend.2 = (bf16[688,512]{1,0:T(8,128)(2,1)}, f32[688,512]{1,0:T(8,128)}) custom-call(s32[5]{0:T(128)} %stack.65.scal.refs_0_.refs_12_, bf16[688,512]{1,0:T(8,128)(2,1)} %get-tuple-element.192.q_ref, bf16[2,688,512]{2,1,0:T(8,128)(2,1)} %get-tuple-element.135.k_ref.v_ref, bf16[2,688,512]{2,1,0:T(8,128)(2,1)} %get-tuple-element.135.k_ref.v_ref, ...), custom_call_target="tpu_custom_call" | custom-call | flops 4000000000 | bytes 150000 | tf_op jit(solution)/shard_map/attend/pallas_call | solution.py:534
  86.4 14.9 %attend.3 = (bf16[688,512]{1,0:T(8,128)(2,1)}, f32[688,512]{1,0:T(8,128)}) custom-call(s32[5]{0:T(128)} %stack.65.scal.refs_0_.refs_12_, bf16[688,512]{1,0:T(8,128)(2,1)} %get-tuple-element.206.q_ref, bf16[2,688,512]{2,1,0:T(8,128)(2,1)} %get-tuple-element.133.k_ref.v_ref, bf16[2,688,512]{2,1,0:T(8,128)(2,1)} %get-tuple-element.133.k_ref.v_ref, ...), custom_call_target="tpu_custom_call" | custom-call | flops 4000000000 | bytes 150000 | tf_op jit(solution)/shard_map/attend/pallas_call | solution.py:534
  109.8 9.1 %branch.1 = (bf16[688,1024]{1,0:T(8,128)(2,1)}, bf16[688,1024]{1,0:T(8,128)(2,1)}, bf16[688,128]{1,0:T(8,128)(2,1)}, bf16[688,128]{1,0:T(8,128)(2,1)}, bf16[512,1024]{1,0:T(8,128)(2,1)}) custom-call(s32[5]{0:T(128)} %stack.65.scal.refs_0_.refs_12_, bf16[688,512]{1,0:T(8,128)(2,1)} %get-tuple-element.140.mix_a.mixed_ref, ...), custom_call_target="tpu_custom_call" | custom-call | flops 2000000000 | bytes 400000 | tf_op jit(solution)/shard_map/branch/pallas_call | solution.py:675
  121.4 24.3 %mlp.2 = (bf16[688,1024]{1,0:T(8,128)(2,1)}, bf16[688,128]{1,0:T(8,128)(2,1)}, bf16[688,1024]{1,0:T(8,128)(2,1)}, bf16[688,1024]{1,0:T(8,128)(2,1)}, f32[688,128...) custom-call(s32[5]{0:T(128)} %stack.65.scal.refs_0_.refs_12_, ...), custom_call_target="tpu_custom_call" | custom-call | flops 6249999872 | bytes 500000 | tf_op jit(solution)/shard_map/mlp/pallas_call | solution.py:794
  147.9 24.7 %mlp.3 = (bf16[688,1024]{1,0:T(8,128)(2,1)}, bf16[688,1024]{1,0:T(8,128)(2,1)}, f32[688,128]{1,0:T(8,128)}, f32[688,128]{1,0:T(8,128)}, f32[16,2048]{1,0:T(8,128)}, /*index=5*/f32[16,2048]{1,0:T(8,128)}) custom-call(s32[5]{0:T(128)} %stack.65.scal.refs_0_.refs_12_, bf16[688,1024]{1,0:T(8,128)(2,1)} %get-tuple-element.161.refs_1_.n2, ...), custom_call_target="tpu_custom_call" | custom-call | flops 6249999872 | bytes 500000 | tf_op jit(solution)/shard_map/mlp/pallas_call | solution.py:794
  172.6 11.6 %middle.1 = (bf16[688,1024]{1,0:T(8,128)(2,1)}, bf16[688,1024]{1,0:T(8,128)(2,1)}, bf16[688,512]{1,0:T(8,128)(2,1)}, bf16[688,512]{1,0:T(8,128)(2,1)}, f32[16,51...) custom-call(s32[5]{0:T(128)} %stack.65.scal.refs_0_.refs_12_, ...), custom_call_target="tpu_custom_call" | custom-call | flops 2249999872 | bytes 500000 | tf_op jit(solution)/shard_map/middle/pallas_call | solution.py:875
  188.0 14.2 %attend_back.4 = (bf16[688,256]{1,0:T(8,128)(2,1)}, bf16[2,688,256]{2,1,0:T(8,128)(2,1)}, bf16[2,688,256]{2,1,0:T(8,128)(2,1)}) custom-call(s32[5]{0:T(128)} %stack.65.scal.refs_0_.refs_12_, bf16[688,512]{1,0:T(8,128)(2,1)} %get-tuple-element.192.q_ref, bf16[2,688,512]{2,1,0:T(8,128)(2,1)} %get-tuple-element.135.k_ref.v_ref, ...), custom_call_target="tpu_custom_call" | custom-call | flops 3249999872 | bytes 225000 | tf_op jit(solution)/shard_map/attend_back/pallas_call | solution.py:619
  202.2 3.0 collective-permute-start.31
  205.3 2.4 collective-permute-start.34
  207.7 14.2 %attend_back.5 = (bf16[688,256]{1,0:T(8,128)(2,1)}, bf16[2,688,256]{2,1,0:T(8,128)(2,1)}, bf16[2,688,256]{2,1,0:T(8,128)(2,1)}) custom-call(s32[5]{0:T(128)} %stack.65.scal.refs_0_.refs_12_, bf16[688,512]{1,0:T(8,128)(2,1)} %get-tuple-element.192.q_ref, bf16[2,688,512]{2,1,0:T(8,128)(2,1)} %get-tuple-element.135.k_ref.v_ref, ...), custom_call_target="tpu_custom_call" | custom-call | flops 3249999872 | bytes 225000 | tf_op jit(solution)/shard_map/attend_back/pallas_call | solution.py:619
  222.8 14.0 %attend_back.6 = (bf16[688,256]{1,0:T(8,128)(2,1)}, bf16[2,688,256]{2,1,0:T(8,128)(2,1)}, bf16[2,688,256]{2,1,0:T(8,128)(2,1)}) custom-call(s32[5]{0:T(128)} %stack.65.scal.refs_0_.refs_12_, bf16[688,512]{1,0:T(8,128)(2,1)} %get-tuple-element.206.q_ref, bf16[2,688,512]{2,1,0:T(8,128)(2,1)} %get-tuple-element.133.k_ref.v_ref, ...), custom_call_target="tpu_custom_call" | custom-call | flops 3249999872 | bytes 225000 | tf_op jit(solution)/shard_map/attend_back/pallas_call | solution.py:619
  239.8 14.3 %attend_back.7 = (bf16[688,256]{1,0:T(8,128)(2,1)}, bf16[2,688,256]{2,1,0:T(8,128)(2,1)}, bf16[2,688,256]{2,1,0:T(8,128)(2,1)}) custom-call(s32[5]{0:T(128)} %stack.65.scal.refs_0_.refs_12_, bf16[688,512]{1,0:T(8,128)(2,1)} %get-tuple-element.206.q_ref, bf16[2,688,512]{2,1,0:T(8,128)(2,1)} %get-tuple-element.133.k_ref.v_ref, ...), custom_call_target="tpu_custom_call" | custom-call | flops 3249999872 | bytes 225000 | tf_op jit(solution)/shard_map/attend_back/pallas_call | solution.py:619
  254.5 2.2 collective-permute-done.38.refs_11_
  256.7 6.7 %qkv_tables.1 = (bf16[2,688,512]{2,1,0:T(8,128)(2,1)}, bf16[2,688,512]{2,1,0:T(8,128)(2,1)}, bf16[688,128]{1,0:T(8,128)(2,1)}, f32[16,2048]{1,0:T(8,128)}, bf16[16,2048]{1,0:T(8,128)(2,1)}) custom-call(bf16[688,256]{1,0:T(8,128)(2,1)} %get-tuple-element.189.refs_0_, bf16[688,256]{1,0:T(8,128)(2,1)} %get-tuple-element.193.refs_1_, ...), custom_call_target="tpu_custom_call" | custom-call | flops 1750000000 | bytes 350000 | tf_op jit(solution)/shard_map/qkv_tables/pallas_call | solution.py:940
  267.4 3.5 %gather_images.2 = (bf16[8,16,3840]{2,1,0:T(8,128)(2,1)}, s32[16]{0:T(128)}) custom-call(s32[1]{0:T(128)} %bitcast.43.flag, bf16[8,16,3968]{2,1,0:T(8,128)(2,1)} %copy-done.6, bf16[8,16,3968]{2,1,0:T(8,128)(2,1)} %collective-permute-done.39.refs_1_), custom_call_target="tpu_custom_call" | custom-call | flops 5000000000 | bytes 25000 | tf_op jit(solution)/shard_map/gather_images/pallas_call | solution.py:1017
  271.5 12.4 %qkv_rows.1 = bf16[688,1024]{1,0:T(8,128)(2,1)} custom-call(bf16[688,256]{1,0:T(8,128)(2,1)} %get-tuple-element.189.refs_0_, bf16[688,256]{1,0:T(8,128)(2,1)} %get-tuple-element.193.refs_1_, bf16[2,688,512]{2,1,0:T(8,128)(2,1)} %get-tuple-element.213.refs_2_, bf16[688,256]{1,0:T(8,128)(2,1)} %get-tuple-element.204.refs_6_.refs_3_, ...), custom_call_target="tpu_custom_call" | custom-call | flops 3000000000 | bytes 400000 | tf_op jit(solution)/shard_map/qkv_rows/pallas_call | solution.py:972
  283.9 2.3 collective-permute-start.43
  288.4 3.9 %collective-permute-done.44 = bf16[4,16,1280]{2,1,0:T(8,128)(2,1)S(1)} collective-permute-done((bf16[4,16,1280]{2,1,0:T(8,128)(2,1)S(1)}, bf16[4,16,1280]{2,1,0:T(8,128)(2,1)S(1)}, u32[]{:S(2)}, u32[]{:S(2)}) %collective-permute-start.44) | collective-permute-done | bytes 163872 | tf_op jit(solution)/shard_map/ppermute | solution.py:1071
  294.0 3.8 %finish.3 = (f32[8,16,512]{2,1,0:T(8,128)}, f32[8,16,2048]{2,1,0:T(8,128)}, f32[8,16,2048]{2,1,0:T(8,128)}, f32[8,16,1024]{2,1,0:T(8,128)}, f32[8,16,1024]{2,1,0:T(8,128)}, /*index=5*/f32[8,16,1024]{2,1,0:T(8,128)}) custom-call(s32[1]{0:T(128)} %bitcast.core, bf16[8,16,3840]{2,1,0:T(8,128)(2,1)} %get-tuple-element.220.own, bf16[8,16,3840]{2,1,0:T(8,128)(2,1)} %copy-done.33), custom_call_target="tpu_custom_call" | custom-call | flops 5000000000 | bytes 25000 | tf_op jit(solution)/shard_map/finish/pallas_call | solution.py:1055
  297.8 3.1 collective-permute-done.45.refs_2_
  300.9 3.4 %collective-permute-done.43 = bf16[688,1024]{1,0:T(8,128)(2,1)} collective-permute-done((bf16[688,1024]{1,0:T(8,128)(2,1)}, bf16[688,1024]{1,0:T(8,128)(2,1)}, u32[]{:S(2)}, u32[]{:S(2)}) %collective-permute-start.43) | collective-permute-done | bytes 1409056 | tf_op jit(solution)/shard_map/ppermute | solution.py:1067
  304.2 2.0 gather_images.3
  306.4 3.1 %bitcast_convert_fusion = f32[1,688,1024]{2,1,0:T(8,128)} fusion(bf16[688,1024]{1,0:T(8,128)(2,1)S(1)} %copy-done.2, bf16[688,1024]{1,0:T(8,128)(2,1)} %collective-permute-done.43, pred[]{:T(512)S(6)} %eq.24), kind=kLoop, calls=%fused_computation.1 | loop fusion | flops 1409024 | bytes 5636097 | tf_op jit(solution)/shard_map/broadcast_in_dim | solution.py:1323
  310.2 2.2 finish.2
  (225 shorter events, 59.9 us)
Async XLA Ops:
  1.8 16.2 %collective-permute-start.2 = (bf16[3,128,512]{2,1,0:T(8,128)(2,1)S(1)}, bf16[3,128,512]{2,1,0:T(8,128)(2,1)S(1)}, u32[]{:S(2)}, u32[]{:S(2)}) collective-permute-start(bf16[3,128,512]{2,1,0:T(8,128)(2,1)S(1)} %dynamic-slice_bitcast_fusion), channel_id=1, source_target_pairs={{0,1},{1,0},{2,3},{3,2},{4,5},{5,4},{6,7},{7,6},{8,9},{9,8},{10,11... | collective-permute-start | bytes 1179656 | tf_op jit(solution)/shard_map/ppermute | solution.py:1071
  6.2 31.3 %collective-permute-start.1 = (bf16[688,1024]{1,0:T(8,128)(2,1)}, bf16[688,1024]{1,0:T(8,128)(2,1)S(1)}, u32[]{:S(2)}, u32[]{:S(2)}) collective-permute-start(bf16[688,1024]{1,0:T(8,128)(2,1)} %bitcast.76), channel_id=1, source_target_pairs={{1,2},{2,1},{5,6},{6,5},{9,10},{10,9},{13,14},{14,13},{17,18},{18,... | collective-permute-start | bytes 4227080 | tf_op jit(solution)/shard_map/ppermute | solution.py:1067
  22.8 13.9 %collective-permute-start.5 = (bf16[16,2048]{1,0:T(8,128)(2,1)S(1)}, bf16[16,2048]{1,0:T(8,128)(2,1)S(1)}, u32[]{:S(2)}, u32[]{:S(2)}) collective-permute-start(bf16[16,2048]{1,0:T(8,128)(2,1)S(1)} %pad_maximum_fusion.7), channel_id=1, source_target_pairs={{0,1},{1,0},{2,3},{3,2},{4,5},{5,4},{6,7},{7,6},{8,9},{9,8},{10,11... | collective-permute-start | bytes 196616 | tf_op jit(solution)/shard_map/ppermute | solution.py:1071
  31.8 19.3 %collective-permute-start.9 = (bf16[2,3,128,512]{3,2,1,0:T(8,128)(2,1)S(1)}, bf16[2,3,128,512]{3,2,1,0:T(8,128)(2,1)S(1)}, u32[]{:S(2)}, u32[]{:S(2)}) collective-permute-start(bf16[2,3,128,512]{3,2,1,0:T(8,128)(2,1)S(1)} %pad_maximum_fusion.1.rest_0_), channel_id=1, source_target_pairs={{0,2},{2,0},{1,3},{3,1},{4,6},{6,4},{5,7},{7,5},{8,10},{10,8},{9,1... | collective-permute-start | bytes 2359304 | tf_op jit(solution)/shard_map/ppermute | solution.py:1071
  36.8 14.4 %collective-permute-start.10 = (bf16[2,3,128,512]{3,2,1,0:T(8,128)(2,1)S(1)}, bf16[2,3,128,512]{3,2,1,0:T(8,128)(2,1)}, u32[]{:S(2)}, u32[]{:S(2)}) collective-permute-start(bf16[2,3,128,512]{3,2,1,0:T(8,128)(2,1)S(1)} %pad_maximum_fusion.2.rest_1_), channel_id=1, source_target_pairs={{0,2},{2,0},{1,3},{3,1},{4,6},{6,4},{5,7},{7,5},{8,10},{10,8},{9,1... | collective-permute-start | bytes 2359304 | tf_op jit(solution)/shard_map/ppermute | solution.py:1071
  48.4 15.2 %collective-permute-start.11 = (bf16[2,688,512]{2,1,0:T(8,128)(2,1)}, bf16[2,688,512]{2,1,0:T(8,128)(2,1)}, u32[]{:S(2)}, u32[]{:S(2)}) collective-permute-start(bf16[2,688,512]{2,1,0:T(8,128)(2,1)} %get-tuple-element.135.k_ref.v_ref), channel_id=1, source_target_pairs={{0,2},{2,0},{1,3},{3,1},{4,6},{6,4},{5,7},{7,5},{8,10},{10,8},{9,1... | collective-permute-start | bytes 4227080 | tf_op jit(solution)/shard_map/ppermute | solution.py:1071
  59.9 26.5 %collective-permute-start.16 = (bf16[2,688,512]{2,1,0:T(8,128)(2,1)}, bf16[2,688,512]{2,1,0:T(8,128)(2,1)}, u32[]{:S(2)}, u32[]{:S(2)}) collective-permute-start(bf16[2,688,512]{2,1,0:T(8,128)(2,1)} %get-tuple-element.133.k_ref.v_ref), channel_id=1, source_target_pairs={{0,2},{2,0},{1,3},{3,1},{4,6},{6,4},{5,7},{7,5},{8,10},{10,8},{9,1... | collective-permute-start | bytes 4227080 | tf_op jit(solution)/shard_map/ppermute | solution.py:1071
  60.8 22.3 %collective-permute-start.12 = (bf16[1024,256]{1,0:T(8,128)(2,1)}, bf16[1024,256]{1,0:T(8,128)(2,1)S(1)}, u32[]{:S(2)}, u32[]{:S(2)}) collective-permute-start(bf16[1024,256]{1,0:T(8,128)(2,1)} %collective-permute-done.6.refs_5_), channel_id=1, source_target_pairs={{0,8},{8,0},{1,9},{9,1},{2,10},{10,2},{3,11},{11,3},{4,12},{12,4},... | collective-permute-start | bytes 1572872 | tf_op jit(solution)/shard_map/ppermute | solution.py:1071
  63.6 22.5 %collective-permute-start.15 = (bf16[1024,256]{1,0:T(8,128)(2,1)}, bf16[1024,256]{1,0:T(8,128)(2,1)S(1)}, u32[]{:S(2)}, u32[]{:S(2)}) collective-permute-start(bf16[1024,256]{1,0:T(8,128)(2,1)} %collective-permute-done.6.refs_5_), channel_id=1, source_target_pairs={{0,4},{4,0},{1,5},{5,1},{2,6},{6,2},{3,7},{7,3},{8,12},{12,8},{9,1... | collective-permute-start | bytes 1572872 | tf_op jit(solution)/shard_map/ppermute | solution.py:1071
  63.6 22.6 %collective-permute-start.17 = (bf16[128,1024]{1,0:T(8,128)(2,1)S(1)}, bf16[128,1024]{1,0:T(8,128)(2,1)S(1)}, u32[]{:S(2)}, u32[]{:S(2)}) collective-permute-start(bf16[128,1024]{1,0:T(8,128)(2,1)S(1)} %copy-done.18), channel_id=1, source_target_pairs={{0,1},{1,0},{2,3},{3,2},{4,5},{5,4},{6,7},{7,6},{8,9},{9,8},{10,11... | collective-permute-start | bytes 786440 | tf_op jit(solution)/shard_map/ppermute | solution.py:1071
  63.6 42.9 %collective-permute-start.28 = (bf16[688,1024]{1,0:T(8,128)(2,1)S(1)}, bf16[688,1024]{1,0:T(8,128)(2,1)S(1)}, u32[]{:S(2)}, u32[]{:S(2)}) collective-permute-start(bf16[688,1024]{1,0:T(8,128)(2,1)S(1)} %bitcast.75), channel_id=1, source_target_pairs={{1,2},{2,1},{5,6},{6,5},{9,10},{10,9},{13,14},{14,13},{17,18},{18,... | collective-permute-start | bytes 4227080 | tf_op jit(solution)/shard_map/ppermute | solution.py:1067
  83.1 18.2 %collective-permute-start.13 = (bf16[1024,256]{1,0:T(8,128)(2,1)S(1)}, bf16[1024,256]{1,0:T(8,128)(2,1)}, u32[]{:S(2)}, u32[]{:S(2)}) collective-permute-start(bf16[1024,256]{1,0:T(8,128)(2,1)S(1)} %collective-permute-done.12.refs_7_), channel_id=1, source_target_pairs={{0,4},{4,0},{1,5},{5,1},{2,6},{6,2},{3,7},{7,3},{8,12},{12,8},{9,1... | collective-permute-start | bytes 1572872 | tf_op jit(solution)/shard_map/ppermute | solution.py:1071
  86.1 18.6 %collective-permute-start.14 = (bf16[256,1024]{1,0:T(8,128)(2,1)S(1)}, bf16[256,1024]{1,0:T(8,128)(2,1)}, u32[]{:S(2)}, u32[]{:S(2)}) collective-permute-start(bf16[256,1024]{1,0:T(8,128)(2,1)S(1)} %copy-done.13), channel_id=1, source_target_pairs={{0,1},{1,0},{2,3},{3,2},{4,5},{5,4},{6,7},{7,6},{8,9},{9,8},{10,11... | collective-permute-start | bytes 1572872 | tf_op jit(solution)/shard_map/ppermute | solution.py:1071
  86.2 15.1 %collective-permute-start.18 = (bf16[128,1024]{1,0:T(8,128)(2,1)S(1)}, bf16[128,1024]{1,0:T(8,128)(2,1)S(1)}, u32[]{:S(2)}, u32[]{:S(2)}) collective-permute-start(bf16[128,1024]{1,0:T(8,128)(2,1)S(1)} %collective-permute-done.17), channel_id=1, source_target_pairs={{0,4},{4,0},{1,5},{5,1},{2,6},{6,2},{3,7},{7,3},{8,12},{12,8},{9,1... | collective-permute-start | bytes 786440 | tf_op jit(solution)/shard_map/ppermute | solution.py:1071
  103.7 44.1 %collective-permute-start.21 = (bf16[4,1024,256]{2,1,0:T(8,128)(2,1)S(1)}, bf16[4,1024,256]{2,1,0:T(8,128)(2,1)}, u32[]{:S(2)}, u32[]{:S(2)}) collective-permute-start(bf16[4,1024,256]{2,1,0:T(8,128)(2,1)S(1)} %pad_maximum_fusion), channel_id=1, source_target_pairs={{0,2},{2,0},{1,3},{3,1},{4,6},{6,4},{5,7},{7,5},{8,10},{10,8},{9,1... | collective-permute-start | bytes 6291464 | tf_op jit(solution)/shard_map/ppermute | solution.py:1071
  104.8 14.8 %collective-permute-start.22 = (bf16[256,1024]{1,0:T(8,128)(2,1)}, bf16[256,1024]{1,0:T(8,128)(2,1)}, u32[]{:S(2)}, u32[]{:S(2)}) collective-permute-start(bf16[256,1024]{1,0:T(8,128)(2,1)} %collective-permute-done.14.refs_10_), channel_id=1, source_target_pairs={{0,4},{4,0},{1,5},{5,1},{2,6},{6,2},{3,7},{7,3},{8,12},{12,8},{9,1... | collective-permute-start | bytes 1572872 | tf_op jit(solution)/shard_map/ppermute | solution.py:1071
  106.3 15.0 %collective-permute-start.23 = (bf16[256,1024]{1,0:T(8,128)(2,1)}, bf16[256,1024]{1,0:T(8,128)(2,1)}, u32[]{:S(2)}, u32[]{:S(2)}) collective-permute-start(bf16[256,1024]{1,0:T(8,128)(2,1)} %collective-permute-done.14.refs_10_), channel_id=1, source_target_pairs={{0,8},{8,0},{1,9},{9,1},{2,10},{10,2},{3,11},{11,3},{4,12},{12,4},... | collective-permute-start | bytes 1572872 | tf_op jit(solution)/shard_map/ppermute | solution.py:1071
  106.5 14.4 %collective-permute-start.20 = (bf16[16,4096]{1,0:T(8,128)(2,1)S(1)}, bf16[16,4096]{1,0:T(8,128)(2,1)S(1)}, u32[]{:S(2)}, u32[]{:S(2)}) collective-permute-start(bf16[16,4096]{1,0:T(8,128)(2,1)S(1)} %pad_maximum_fusion.6), channel_id=1, source_target_pairs={{0,1},{1,0},{2,3},{3,2},{4,5},{5,4},{6,7},{7,6},{8,9},{9,8},{10,11... | collective-permute-start | bytes 393224 | tf_op jit(solution)/shard_map/ppermute | solution.py:1071
  118.9 28.0 %collective-permute-start.25 = (bf16[256,1024]{1,0:T(8,128)(2,1)}, bf16[256,1024]{1,0:T(8,128)(2,1)S(1)}, u32[]{:S(2)}, u32[]{:S(2)}) collective-permute-start(bf16[256,1024]{1,0:T(8,128)(2,1)} %collective-permute-done.14.refs_10_), channel_id=1, source_target_pairs={{0,2},{2,0},{1,3},{3,1},{4,6},{6,4},{5,7},{7,5},{8,10},{10,8},{9,1... | collective-permute-start | bytes 1572872 | tf_op jit(solution)/shard_map/ppermute | solution.py:1071
  119.6 26.1 %collective-permute-start.24 = (bf16[256,1024]{1,0:T(8,128)(2,1)}, bf16[256,1024]{1,0:T(8,128)(2,1)S(1)}, u32[]{:S(2)}, u32[]{:S(2)}) collective-permute-start(bf16[256,1024]{1,0:T(8,128)(2,1)} %collective-permute-done.22.refs_11_), channel_id=1, source_target_pairs={{0,8},{8,0},{1,9},{9,1},{2,10},{10,2},{3,11},{11,3},{4,12},{12,4},... | collective-permute-start | bytes 1572872 | tf_op jit(solution)/shard_map/ppermute | solution.py:1071
  120.9 26.0 %collective-permute-start.26 = (bf16[256,1024]{1,0:T(8,128)(2,1)}, bf16[256,1024]{1,0:T(8,128)(2,1)}, u32[]{:S(2)}, u32[]{:S(2)}) collective-permute-start(bf16[256,1024]{1,0:T(8,128)(2,1)} %collective-permute-done.22.refs_11_), channel_id=1, source_target_pairs={{0,2},{2,0},{1,3},{3,1},{4,6},{6,4},{5,7},{7,5},{8,10},{10,8},{9,1... | collective-permute-start | bytes 1572872 | tf_op jit(solution)/shard_map/ppermute | solution.py:1071
  121.3 25.6 %collective-permute-start.27 = (bf16[256,1024]{1,0:T(8,128)(2,1)}, bf16[256,1024]{1,0:T(8,128)(2,1)}, u32[]{:S(2)}, u32[]{:S(2)}) collective-permute-start(bf16[256,1024]{1,0:T(8,128)(2,1)} %collective-permute-done.23.refs_12_), channel_id=1, source_target_pairs={{0,2},{2,0},{1,3},{3,1},{4,6},{6,4},{5,7},{7,5},{8,10},{10,8},{9,1... | collective-permute-start | bytes 1572872 | tf_op jit(solution)/shard_map/ppermute | solution.py:1071
  187.0 18.2 %collective-permute-start.32 = (bf16[16,3968]{1,0:T(8,128)(2,1)S(1)}, bf16[16,3968]{1,0:T(8,128)(2,1)S(1)}, u32[]{:S(2)}, u32[]{:S(2)}) collective-permute-start(bf16[16,3968]{1,0:T(8,128)(2,1)S(1)} %maximum_maximum_fusion), channel_id=1, source_target_pairs={{0,1},{1,0},{2,3},{3,2},{4,5},{5,4},{6,7},{7,6},{8,9},{9,8},{10,11... | collective-permute-start | bytes 380936 | tf_op jit(solution)/shard_map/ppermute | solution.py:1071
  202.2 37.6 %collective-permute-start.31 = (bf16[688,1024]{1,0:T(8,128)(2,1)S(1)}, bf16[688,1024]{1,0:T(8,128)(2,1)S(1)}, u32[]{:S(2)}, u32[]{:S(2)}) collective-permute-start(bf16[688,1024]{1,0:T(8,128)(2,1)S(1)} %copy-done.4), channel_id=1, source_target_pairs={{1,2},{2,1},{5,6},{6,5},{9,10},{10,9},{13,14},{14,13},{17,18},{18,... | collective-permute-start | bytes 4227080 | tf_op jit(solution)/shard_map/ppermute | solution.py:1067
  205.3 16.6 %collective-permute-start.34 = (bf16[2,16,3968]{2,1,0:T(8,128)(2,1)S(1)}, bf16[2,16,3968]{2,1,0:T(8,128)(2,1)S(1)}, u32[]{:S(2)}, u32[]{:S(2)}) collective-permute-start(bf16[2,16,3968]{2,1,0:T(8,128)(2,1)S(1)} %maximum_select_fusion.3), channel_id=1, source_target_pairs={{0,16},{16,0},{1,17},{17,1},{2,18},{18,2},{3,19},{19,3},{4,20},{20... | collective-permute-start | bytes 761864 | tf_op jit(solution)/shard_map/ppermute | solution.py:1071
  222.0 14.8 %collective-permute-start.36 = (bf16[4,16,3968]{2,1,0:T(8,128)(2,1)S(1)}, bf16[4,16,3968]{2,1,0:T(8,128)(2,1)}, u32[]{:S(2)}, u32[]{:S(2)}) collective-permute-start(bf16[4,16,3968]{2,1,0:T(8,128)(2,1)S(1)} %maximum_select_fusion.1), channel_id=1, source_target_pairs={{0,8},{8,0},{1,9},{9,1},{2,10},{10,2},{3,11},{11,3},{4,12},{12,4},... | collective-permute-start | bytes 1523720 | tf_op jit(solution)/shard_map/ppermute | solution.py:1071
  222.3 32.2 %collective-permute-start.33 = (bf16[2,688,256]{2,1,0:T(8,128)(2,1)}, bf16[2,688,256]{2,1,0:T(8,128)(2,1)S(1)}, u32[]{:S(2)}, u32[]{:S(2)}) collective-permute-start(bf16[2,688,256]{2,1,0:T(8,128)(2,1)} %get-tuple-element.197), channel_id=1, source_target_pairs={{0,2},{2,0},{1,3},{3,1},{4,6},{6,4},{5,7},{7,5},{8,10},{10,8},{9,1... | collective-permute-start | bytes 2113544 | tf_op jit(solution)/shard_map/ppermute | solution.py:1071
  222.3 32.2 %collective-permute-start.35 = (bf16[2,688,256]{2,1,0:T(8,128)(2,1)}, bf16[2,688,256]{2,1,0:T(8,128)(2,1)S(1)}, u32[]{:S(2)}, u32[]{:S(2)}) collective-permute-start(bf16[2,688,256]{2,1,0:T(8,128)(2,1)} %get-tuple-element.200), channel_id=1, source_target_pairs={{0,2},{2,0},{1,3},{3,1},{4,6},{6,4},{5,7},{7,5},{8,10},{10,8},{9,1... | collective-permute-start | bytes 2113544 | tf_op jit(solution)/shard_map/ppermute | solution.py:1071
  238.2 25.2 %collective-permute-start.39 = (bf16[8,16,3968]{2,1,0:T(8,128)(2,1)S(1)}, bf16[8,16,3968]{2,1,0:T(8,128)(2,1)}, u32[]{:S(2)}, u32[]{:S(2)}) collective-permute-start(bf16[8,16,3968]{2,1,0:T(8,128)(2,1)S(1)} %maximum_select_fusion.refs_0_), channel_id=1, source_target_pairs={{0,4},{4,0},{1,5},{5,1},{2,6},{6,2},{3,7},{7,3},{8,12},{12,8},{9,1... | collective-permute-start | bytes 3047432 | tf_op jit(solution)/shard_map/ppermute | solution.py:1071
  239.5 14.9 %collective-permute-start.37 = (bf16[2,688,256]{2,1,0:T(8,128)(2,1)}, bf16[2,688,256]{2,1,0:T(8,128)(2,1)S(1)}, u32[]{:S(2)}, u32[]{:S(2)}) collective-permute-start(bf16[2,688,256]{2,1,0:T(8,128)(2,1)} %get-tuple-element.211), channel_id=1, source_target_pairs={{0,2},{2,0},{1,3},{3,1},{4,6},{6,4},{5,7},{7,5},{8,10},{10,8},{9,1... | collective-permute-start | bytes 2113544 | tf_op jit(solution)/shard_map/ppermute | solution.py:1071
  270.9 22.2 %collective-permute-start.47 = (bf16[8,16,3840]{2,1,0:T(8,128)(2,1)}, bf16[8,16,3840]{2,1,0:T(8,128)(2,1)S(1)}, u32[]{:S(2)}, u32[]{:S(2)}) collective-permute-start(bf16[8,16,3840]{2,1,0:T(8,128)(2,1)} %get-tuple-element.220.own), channel_id=1, source_target_pairs={{0,2},{2,0},{1,3},{3,1},{4,6},{6,4},{5,7},{7,5},{8,10},{10,8},{9,1... | collective-permute-start | bytes 2949128 | tf_op jit(solution)/shard_map/ppermute | solution.py:1071
  283.9 20.3 %collective-permute-start.43 = (bf16[688,1024]{1,0:T(8,128)(2,1)}, bf16[688,1024]{1,0:T(8,128)(2,1)}, u32[]{:S(2)}, u32[]{:S(2)}) collective-permute-start(bf16[688,1024]{1,0:T(8,128)(2,1)} %qkv_rows.1), channel_id=1, source_target_pairs={{1,2},{2,1},{5,6},{6,5},{9,10},{10,9},{13,14},{14,13},{17,18},{18,... | collective-permute-start | bytes 4227080 | tf_op jit(solution)/shard_map/ppermute | solution.py:1067
  (57 other events, 444.2 us)

commit v6 on v5

--- a/solution.py
+++ b/solution.py
@@ -1192,7 +1192,6 @@
     half_qkv.hop(0, "x")
     half_qkv.hop(0, "zb")
     packed_first = jnp.concatenate([flat(pick(qkv_b, adapter_other)), pick(out_a, adapter_other)], axis=1)
-    packed = jnp.concatenate([pick(table, adapter_other) for table in (up_b, down_a)], axis=1)
     qa, oa = pick(qkv_a, adapter), pick(out_a, adapter)
     qb = flat(pick(qkv_b, adapter))
     gain_one, gain_two, scale_one, scale_two = (v.reshape(1, width) for v in (gain_one, gain_two, scale_one, scale_two))
@@ -1205,7 +1204,9 @@
     tok, n1, rank_qkv, q_a, own_a = qkv_local(scal, tok_here, tok_swapped, gain_one, w3, qa, qb)
     half_qkv.pairs_over_cores()
     kv_a = flip("core")(own_a)
-    q_b, own_b, w3_other = qkv_other(scal, after(n1, half_up.parts[0]), rank_qkv, other_tables, half_qkv)
+    later_other = after(adapter_other, n1)
+    packed = jnp.concatenate([pick(table, later_other) for table in (up_b, down_a)], axis=1)
+    q_b, own_b, w3_other = qkv_other(scal, after(n1, half_up.parts[0], packed), rank_qkv, other_tables, half_qkv)
     kv_b = flip("core")(own_b)
     half_out.over_tensor(own_b)
     half_up.hop(0, "x", own_b)

time: 318 us -> 319 us (level)
  waiting for transfers between devices: 26.5 us -> 22.2 us
  other arithmetic: 10.3 us -> 13.9 us
    ppermute x44, waiting for transfers between devices: 23.1 us -> 18.9 us  [flip(): return lambda array: lax.ppermute(array, axis, FLIP)]
    unnamed x88 -> x80, local copies, waits for them, and re-layouts: 6.99 us -> 7.47 us
  transfers between devices with their start and end apart: 48 -> 48, of which waited for: 13 -> 10; matrix products, arithmetic and copies ran while one was open for 8% -> 8% of each run, Pallas kernels for 52% -> 52%
where the time goes in v6:
time: 319 us; the launch traced here: 314 us
  Pallas kernels  204 us (64%)
  starting transfers between devices  42.5 us (13%)
  waiting for transfers between devices  22.2 us (7%)
  local copies, waits for them, and re-layouts  21.4 us (7%)
  other arithmetic  13.9 us (4%)
  between operations  9.24 us (3%)
    pallas_call x4, Pallas kernels, attend_back(): pl.pallas_call(attend_back_kernel, grid=(pairs,), in_specs=[scalars(), fl...  56.8 us
    pallas_call x2, Pallas kernels, mlp(): pl.pallas_call(functools.partial(mlp_kernel, nears, (len(ups), len(downs)...  48.9 us
    ppermute x44, starting transfers between devices, flip(): return lambda array: lax.ppermute(array, axis, FLIP)  30.5 us
    pallas_call x2, Pallas kernels, attend(): pl.pallas_call(attend_kernel, grid=(pairs,), in_specs=[scalars(), flat, t...  29.8 us
    ppermute x44, waiting for transfers between devices, flip(): return lambda array: lax.ppermute(array, axis, FLIP)  18.9 us
    pallas_call x1, Pallas kernels, qkv_rows(): pl.pallas_call(functools.partial(qkv_rows_kernel, len(grads_a), len(grads...  12.5 us
    ppermute x4, starting transfers between devices, swap(): return lax.ppermute(rows, ('core', 'tensor'), SWAP)  12 us
    pallas_call x1, Pallas kernels, middle(): pl.pallas_call(middle_kernel, grid=(blocks,), in_specs=[scalars()] + [blo...  11.6 us
  transfers between devices with their start and end apart: 48, of which 10 were waited for; matrix products, arithmetic and copies ran while one was open for 8% of the time, Pallas kernels for 52%

profile of v6, /device:TPU:1, one launch (start us, length us, event | category | flops | bytes accessed | tf_op | source)
XLA Modules:
  0.0 313.6 jit_solution(6380202765467670901)
XLA Ops:
  1.8 2.1 collective-permute-start.2
  6.2 1.9 collective-permute-start.1
  8.2 1.9 constant_dynamic-slice_fusion.3
  25.8 3.2 %collective-permute-done.3 = bf16[3,128,512]{2,1,0:T(8,128)(2,1)S(1)} collective-permute-done((bf16[3,128,512]{2,1,0:T(8,128)(2,1)S(1)}, bf16[3,128,512]{2,1,0:T(8,128)(2,1)S(1)}, u32[]{:S(2)}, u32[]{:S(2)}) %collective-permute-start.3) | collective-permute-done | bytes 393248 | tf_op jit(solution)/shard_map/ppermute | solution.py:1071
  33.4 2.4 collective-permute-done.7
  39.9 9.7 %qkv_local.1 = (bf16[688,1024]{1,0:T(8,128)(2,1)}, bf16[688,1024]{1,0:T(8,128)(2,1)}, bf16[688,128]{1,0:T(8,128)(2,1)}, bf16[688,512]{1,0:T(8,128)(2,1)}, bf16[2,688,512]{2,1,0:T(8,128)(2,1)}) custom-call(s32[5]{0:T(128)} %stack.65.scal.refs_0_.refs_12_, bf16[688,1024]{1,0:T(8,128)(2,1)} %bitcast.77, bf16[688,1024]{1,0:T(8,128)(2,1)} %copy-done.5, ...), custom_call_target="tpu_custom_call" | custom-call | flops 25000000 | bytes 2500 | tf_op jit(solution)/shard_map/qkv_local/pallas_call | solution.py:402
  54.8 7.8 %qkv_other.1 = (bf16[688,512]{1,0:T(8,128)(2,1)}, bf16[2,688,512]{2,1,0:T(8,128)(2,1)}, bf16[3,1024,512]{2,1,0:T(8,128)(2,1)}) custom-call(s32[5]{0:T(128)} %stack.65.scal.refs_0_.refs_12_, bf16[688,1024]{1,0:T(8,128)(2,1)} %get-tuple-element.132.n1.refs_15_, bf16[688,128]{1,0:T(8,128)(2,1)} %get-tuple-element.133.rank.refs_16_, ...), custom_call_target="tpu_custom_call" | custom-call | flops 1750000000 | bytes 250000 | tf_op jit(solution)/shard_map/qkv_other/pallas_call | solution.py:454
  64.6 4.8 %collective-permute-start.28 = (bf16[688,1024]{1,0:T(8,128)(2,1)S(1)}, bf16[688,1024]{1,0:T(8,128)(2,1)S(1)}, u32[]{:S(2)}, u32[]{:S(2)}) collective-permute-start(bf16[688,1024]{1,0:T(8,128)(2,1)S(1)} %bitcast.75), channel_id=1, source_target_pairs={{1,2},{2,1},{5,6},{6,5},{9,10},{10,9},{13,14},{14,13},{17,18},{18,... | collective-permute-start | bytes 4227080 | tf_op jit(solution)/shard_map/ppermute | solution.py:1067
  69.3 14.9 %attend.2 = (bf16[688,512]{1,0:T(8,128)(2,1)}, f32[688,512]{1,0:T(8,128)}) custom-call(s32[5]{0:T(128)} %stack.65.scal.refs_0_.refs_12_, bf16[688,512]{1,0:T(8,128)(2,1)} %get-tuple-element.194.q_ref, bf16[2,688,512]{2,1,0:T(8,128)(2,1)} %get-tuple-element.137.k_ref.v_ref, bf16[2,688,512]{2,1,0:T(8,128)(2,1)} %get-tuple-element.137.k_ref.v_ref, ...), custom_call_target="tpu_custom_call" | custom-call | flops 4000000000 | bytes 150000 | tf_op jit(solution)/shard_map/attend/pallas_call | solution.py:534
  87.1 14.9 %attend.3 = (bf16[688,512]{1,0:T(8,128)(2,1)}, f32[688,512]{1,0:T(8,128)}) custom-call(s32[5]{0:T(128)} %stack.65.scal.refs_0_.refs_12_, bf16[688,512]{1,0:T(8,128)(2,1)} %get-tuple-element.208.q_ref, bf16[2,688,512]{2,1,0:T(8,128)(2,1)} %get-tuple-element.135.k_ref.v_ref, bf16[2,688,512]{2,1,0:T(8,128)(2,1)} %get-tuple-element.135.k_ref.v_ref, ...), custom_call_target="tpu_custom_call" | custom-call | flops 4000000000 | bytes 150000 | tf_op jit(solution)/shard_map/attend/pallas_call | solution.py:534
  110.3 9.1 %branch.1 = (bf16[688,1024]{1,0:T(8,128)(2,1)}, bf16[688,1024]{1,0:T(8,128)(2,1)}, bf16[688,128]{1,0:T(8,128)(2,1)}, bf16[688,128]{1,0:T(8,128)(2,1)}, bf16[512,1024]{1,0:T(8,128)(2,1)}) custom-call(s32[5]{0:T(128)} %stack.65.scal.refs_0_.refs_12_, bf16[688,512]{1,0:T(8,128)(2,1)} %get-tuple-element.142.mix_a.mixed_ref, ...), custom_call_target="tpu_custom_call" | custom-call | flops 2000000000 | bytes 400000 | tf_op jit(solution)/shard_map/branch/pallas_call | solution.py:675
  122.1 24.3 %mlp.2 = (bf16[688,1024]{1,0:T(8,128)(2,1)}, bf16[688,128]{1,0:T(8,128)(2,1)}, bf16[688,1024]{1,0:T(8,128)(2,1)}, bf16[688,1024]{1,0:T(8,128)(2,1)}, f32[688,128...) custom-call(s32[5]{0:T(128)} %stack.65.scal.refs_0_.refs_12_, ...), custom_call_target="tpu_custom_call" | custom-call | flops 6249999872 | bytes 500000 | tf_op jit(solution)/shard_map/mlp/pallas_call | solution.py:794
  148.6 24.6 %mlp.3 = (bf16[688,1024]{1,0:T(8,128)(2,1)}, bf16[688,1024]{1,0:T(8,128)(2,1)}, f32[688,128]{1,0:T(8,128)}, f32[688,128]{1,0:T(8,128)}, f32[16,2048]{1,0:T(8,128)}, /*index=5*/f32[16,2048]{1,0:T(8,128)}) custom-call(s32[5]{0:T(128)} %stack.65.scal.refs_0_.refs_12_, bf16[688,1024]{1,0:T(8,128)(2,1)} %get-tuple-element.163.refs_1_.n2, ...), custom_call_target="tpu_custom_call" | custom-call | flops 6249999872 | bytes 500000 | tf_op jit(solution)/shard_map/mlp/pallas_call | solution.py:794
  173.3 11.6 %middle.1 = (bf16[688,1024]{1,0:T(8,128)(2,1)}, bf16[688,1024]{1,0:T(8,128)(2,1)}, bf16[688,512]{1,0:T(8,128)(2,1)}, bf16[688,512]{1,0:T(8,128)(2,1)}, f32[16,51...) custom-call(s32[5]{0:T(128)} %stack.65.scal.refs_0_.refs_12_, ...), custom_call_target="tpu_custom_call" | custom-call | flops 2249999872 | bytes 500000 | tf_op jit(solution)/shard_map/middle/pallas_call | solution.py:875
  188.8 14.2 %attend_back.4 = (bf16[688,256]{1,0:T(8,128)(2,1)}, bf16[2,688,256]{2,1,0:T(8,128)(2,1)}, bf16[2,688,256]{2,1,0:T(8,128)(2,1)}) custom-call(s32[5]{0:T(128)} %stack.65.scal.refs_0_.refs_12_, bf16[688,512]{1,0:T(8,128)(2,1)} %get-tuple-element.194.q_ref, bf16[2,688,512]{2,1,0:T(8,128)(2,1)} %get-tuple-element.137.k_ref.v_ref, ...), custom_call_target="tpu_custom_call" | custom-call | flops 3249999872 | bytes 225000 | tf_op jit(solution)/shard_map/attend_back/pallas_call | solution.py:619
  203.0 3.0 collective-permute-start.31
  206.0 2.4 collective-permute-start.34
  208.4 14.3 %attend_back.5 = (bf16[688,256]{1,0:T(8,128)(2,1)}, bf16[2,688,256]{2,1,0:T(8,128)(2,1)}, bf16[2,688,256]{2,1,0:T(8,128)(2,1)}) custom-call(s32[5]{0:T(128)} %stack.65.scal.refs_0_.refs_12_, bf16[688,512]{1,0:T(8,128)(2,1)} %get-tuple-element.194.q_ref, bf16[2,688,512]{2,1,0:T(8,128)(2,1)} %get-tuple-element.137.k_ref.v_ref, ...), custom_call_target="tpu_custom_call" | custom-call | flops 3249999872 | bytes 225000 | tf_op jit(solution)/shard_map/attend_back/pallas_call | solution.py:619
  223.7 14.1 %attend_back.6 = (bf16[688,256]{1,0:T(8,128)(2,1)}, bf16[2,688,256]{2,1,0:T(8,128)(2,1)}, bf16[2,688,256]{2,1,0:T(8,128)(2,1)}) custom-call(s32[5]{0:T(128)} %stack.65.scal.refs_0_.refs_12_, bf16[688,512]{1,0:T(8,128)(2,1)} %get-tuple-element.208.q_ref, bf16[2,688,512]{2,1,0:T(8,128)(2,1)} %get-tuple-element.135.k_ref.v_ref, ...), custom_call_target="tpu_custom_call" | custom-call | flops 3249999872 | bytes 225000 | tf_op jit(solution)/shard_map/attend_back/pallas_call | solution.py:619
  240.7 14.3 %attend_back.7 = (bf16[688,256]{1,0:T(8,128)(2,1)}, bf16[2,688,256]{2,1,0:T(8,128)(2,1)}, bf16[2,688,256]{2,1,0:T(8,128)(2,1)}) custom-call(s32[5]{0:T(128)} %stack.65.scal.refs_0_.refs_12_, bf16[688,512]{1,0:T(8,128)(2,1)} %get-tuple-element.208.q_ref, bf16[2,688,512]{2,1,0:T(8,128)(2,1)} %get-tuple-element.135.k_ref.v_ref, ...), custom_call_target="tpu_custom_call" | custom-call | flops 3249999872 | bytes 225000 | tf_op jit(solution)/shard_map/attend_back/pallas_call | solution.py:619
  255.4 2.2 collective-permute-done.38.refs_11_
  257.6 6.7 %qkv_tables.1 = (bf16[2,688,512]{2,1,0:T(8,128)(2,1)}, bf16[2,688,512]{2,1,0:T(8,128)(2,1)}, bf16[688,128]{1,0:T(8,128)(2,1)}, f32[16,2048]{1,0:T(8,128)}, bf16[16,2048]{1,0:T(8,128)(2,1)}) custom-call(bf16[688,256]{1,0:T(8,128)(2,1)} %get-tuple-element.191.refs_0_, bf16[688,256]{1,0:T(8,128)(2,1)} %get-tuple-element.195.refs_1_, ...), custom_call_target="tpu_custom_call" | custom-call | flops 1750000000 | bytes 350000 | tf_op jit(solution)/shard_map/qkv_tables/pallas_call | solution.py:940
  268.2 3.5 %gather_images.2 = (bf16[8,16,3840]{2,1,0:T(8,128)(2,1)}, s32[16]{0:T(128)}) custom-call(s32[1]{0:T(128)} %bitcast.43.flag, bf16[8,16,3968]{2,1,0:T(8,128)(2,1)} %copy-done.6, bf16[8,16,3968]{2,1,0:T(8,128)(2,1)} %collective-permute-done.39.refs_1_), custom_call_target="tpu_custom_call" | custom-call | flops 5000000000 | bytes 25000 | tf_op jit(solution)/shard_map/gather_images/pallas_call | solution.py:1017
  272.3 12.5 %qkv_rows.1 = bf16[688,1024]{1,0:T(8,128)(2,1)} custom-call(bf16[688,256]{1,0:T(8,128)(2,1)} %get-tuple-element.191.refs_0_, bf16[688,256]{1,0:T(8,128)(2,1)} %get-tuple-element.195.refs_1_, bf16[2,688,512]{2,1,0:T(8,128)(2,1)} %get-tuple-element.215.refs_2_, bf16[688,256]{1,0:T(8,128)(2,1)} %get-tuple-element.206.refs_6_.refs_3_, ...), custom_call_target="tpu_custom_call" | custom-call | flops 3000000000 | bytes 400000 | tf_op jit(solution)/shard_map/qkv_rows/pallas_call | solution.py:972
  284.8 2.3 collective-permute-start.43
  289.2 3.9 %collective-permute-done.44 = bf16[4,16,1280]{2,1,0:T(8,128)(2,1)S(1)} collective-permute-done((bf16[4,16,1280]{2,1,0:T(8,128)(2,1)S(1)}, bf16[4,16,1280]{2,1,0:T(8,128)(2,1)S(1)}, u32[]{:S(2)}, u32[]{:S(2)}) %collective-permute-start.44) | collective-permute-done | bytes 163872 | tf_op jit(solution)/shard_map/ppermute | solution.py:1071
  295.0 3.8 %finish.3 = (f32[8,16,512]{2,1,0:T(8,128)}, f32[8,16,2048]{2,1,0:T(8,128)}, f32[8,16,2048]{2,1,0:T(8,128)}, f32[8,16,1024]{2,1,0:T(8,128)}, f32[8,16,1024]{2,1,0:T(8,128)}, /*index=5*/f32[8,16,1024]{2,1,0:T(8,128)}) custom-call(s32[1]{0:T(128)} %bitcast.core, bf16[8,16,3840]{2,1,0:T(8,128)(2,1)} %get-tuple-element.222.own, bf16[8,16,3840]{2,1,0:T(8,128)(2,1)} %copy-done.29), custom_call_target="tpu_custom_call" | custom-call | flops 5000000000 | bytes 25000 | tf_op jit(solution)/shard_map/finish/pallas_call | solution.py:1055
  298.7 3.1 collective-permute-done.45.refs_2_
  301.9 3.2 %collective-permute-done.43 = bf16[688,1024]{1,0:T(8,128)(2,1)} collective-permute-done((bf16[688,1024]{1,0:T(8,128)(2,1)}, bf16[688,1024]{1,0:T(8,128)(2,1)}, u32[]{:S(2)}, u32[]{:S(2)}) %collective-permute-start.43) | collective-permute-done | bytes 1409056 | tf_op jit(solution)/shard_map/ppermute | solution.py:1067
  305.1 2.0 gather_images.3
  307.2 3.1 %bitcast_convert_fusion = f32[1,688,1024]{2,1,0:T(8,128)} fusion(bf16[688,1024]{1,0:T(8,128)(2,1)S(1)} %copy-done.2, bf16[688,1024]{1,0:T(8,128)(2,1)} %collective-permute-done.43, pred[]{:T(512)S(6)} %eq.24), kind=kLoop, calls=%fused_computation.1 | loop fusion | flops 1409024 | bytes 5636097 | tf_op jit(solution)/shard_map/broadcast_in_dim | solution.py:1324
  311.1 2.2 finish.2
  (217 shorter events, 60.3 us)
Async XLA Ops:
  1.8 16.7 %collective-permute-start.2 = (bf16[3,128,512]{2,1,0:T(8,128)(2,1)S(1)}, bf16[3,128,512]{2,1,0:T(8,128)(2,1)S(1)}, u32[]{:S(2)}, u32[]{:S(2)}) collective-permute-start(bf16[3,128,512]{2,1,0:T(8,128)(2,1)S(1)} %dynamic-slice_bitcast_fusion), channel_id=1, source_target_pairs={{0,1},{1,0},{2,3},{3,2},{4,5},{5,4},{6,7},{7,6},{8,9},{9,8},{10,11... | collective-permute-start | bytes 1179656 | tf_op jit(solution)/shard_map/ppermute | solution.py:1071
  6.2 32.5 %collective-permute-start.1 = (bf16[688,1024]{1,0:T(8,128)(2,1)}, bf16[688,1024]{1,0:T(8,128)(2,1)S(1)}, u32[]{:S(2)}, u32[]{:S(2)}) collective-permute-start(bf16[688,1024]{1,0:T(8,128)(2,1)} %bitcast.76), channel_id=1, source_target_pairs={{1,2},{2,1},{5,6},{6,5},{9,10},{10,9},{13,14},{14,13},{17,18},{18,... | collective-permute-start | bytes 4227080 | tf_op jit(solution)/shard_map/ppermute | solution.py:1067
  23.4 13.7 %collective-permute-start.5 = (bf16[16,2048]{1,0:T(8,128)(2,1)S(1)}, bf16[16,2048]{1,0:T(8,128)(2,1)S(1)}, u32[]{:S(2)}, u32[]{:S(2)}) collective-permute-start(bf16[16,2048]{1,0:T(8,128)(2,1)S(1)} %pad_maximum_fusion.7), channel_id=1, source_target_pairs={{0,1},{1,0},{2,3},{3,2},{4,5},{5,4},{6,7},{7,6},{8,9},{9,8},{10,11... | collective-permute-start | bytes 196616 | tf_op jit(solution)/shard_map/ppermute | solution.py:1071
  32.3 21.6 %collective-permute-start.6 = (bf16[1024,256]{1,0:T(8,128)(2,1)}, bf16[1024,256]{1,0:T(8,128)(2,1)}, u32[]{:S(2)}, u32[]{:S(2)}) collective-permute-start(bf16[1024,256]{1,0:T(8,128)(2,1)} %constant_dynamic-slice_fusion.4), channel_id=1, source_target_pairs={{0,1},{1,0},{2,3},{3,2},{4,5},{5,4},{6,7},{7,6},{8,9},{9,8},{10,11... | collective-permute-start | bytes 1572872 | tf_op jit(solution)/shard_map/ppermute | solution.py:1071
  35.8 18.1 %collective-permute-start.9 = (bf16[2,3,128,512]{3,2,1,0:T(8,128)(2,1)S(1)}, bf16[2,3,128,512]{3,2,1,0:T(8,128)(2,1)}, u32[]{:S(2)}, u32[]{:S(2)}) collective-permute-start(bf16[2,3,128,512]{3,2,1,0:T(8,128)(2,1)S(1)} %pad_maximum_fusion.1.rest_0_), channel_id=1, source_target_pairs={{0,2},{2,0},{1,3},{3,1},{4,6},{6,4},{5,7},{7,5},{8,10},{10,8},{9,1... | collective-permute-start | bytes 2359304 | tf_op jit(solution)/shard_map/ppermute | solution.py:1071
  38.1 15.8 %collective-permute-start.10 = (bf16[2,3,128,512]{3,2,1,0:T(8,128)(2,1)}, bf16[2,3,128,512]{3,2,1,0:T(8,128)(2,1)S(1)}, u32[]{:S(2)}, u32[]{:S(2)}) collective-permute-start(bf16[2,3,128,512]{3,2,1,0:T(8,128)(2,1)} %pad_maximum_fusion.2.rest_1_), channel_id=1, source_target_pairs={{0,2},{2,0},{1,3},{3,1},{4,6},{6,4},{5,7},{7,5},{8,10},{10,8},{9,1... | collective-permute-start | bytes 2359304 | tf_op jit(solution)/shard_map/ppermute | solution.py:1071
  62.6 23.4 %collective-permute-start.16 = (bf16[2,688,512]{2,1,0:T(8,128)(2,1)}, bf16[2,688,512]{2,1,0:T(8,128)(2,1)S(1)}, u32[]{:S(2)}, u32[]{:S(2)}) collective-permute-start(bf16[2,688,512]{2,1,0:T(8,128)(2,1)} %get-tuple-element.135.k_ref.v_ref), channel_id=1, source_target_pairs={{0,2},{2,0},{1,3},{3,1},{4,6},{6,4},{5,7},{7,5},{8,10},{10,8},{9,1... | collective-permute-start | bytes 4227080 | tf_op jit(solution)/shard_map/ppermute | solution.py:1071
  63.2 21.1 %collective-permute-start.12 = (bf16[1024,256]{1,0:T(8,128)(2,1)}, bf16[1024,256]{1,0:T(8,128)(2,1)S(1)}, u32[]{:S(2)}, u32[]{:S(2)}) collective-permute-start(bf16[1024,256]{1,0:T(8,128)(2,1)} %collective-permute-done.6.refs_5_), channel_id=1, source_target_pairs={{0,8},{8,0},{1,9},{9,1},{2,10},{10,2},{3,11},{11,3},{4,12},{12,4},... | collective-permute-start | bytes 1572872 | tf_op jit(solution)/shard_map/ppermute | solution.py:1071
  64.4 21.1 %collective-permute-start.15 = (bf16[1024,256]{1,0:T(8,128)(2,1)}, bf16[1024,256]{1,0:T(8,128)(2,1)S(1)}, u32[]{:S(2)}, u32[]{:S(2)}) collective-permute-start(bf16[1024,256]{1,0:T(8,128)(2,1)} %collective-permute-done.6.refs_5_), channel_id=1, source_target_pairs={{0,4},{4,0},{1,5},{5,1},{2,6},{6,2},{3,7},{7,3},{8,12},{12,8},{9,1... | collective-permute-start | bytes 1572872 | tf_op jit(solution)/shard_map/ppermute | solution.py:1071
  64.6 21.0 %collective-permute-start.17 = (bf16[128,1024]{1,0:T(8,128)(2,1)S(1)}, bf16[128,1024]{1,0:T(8,128)(2,1)}, u32[]{:S(2)}, u32[]{:S(2)}) collective-permute-start(bf16[128,1024]{1,0:T(8,128)(2,1)S(1)} %copy-done.18), channel_id=1, source_target_pairs={{0,1},{1,0},{2,3},{3,2},{4,5},{5,4},{6,7},{7,6},{8,9},{9,8},{10,11... | collective-permute-start | bytes 786440 | tf_op jit(solution)/shard_map/ppermute | solution.py:1071
  64.6 42.8 %collective-permute-start.28 = (bf16[688,1024]{1,0:T(8,128)(2,1)S(1)}, bf16[688,1024]{1,0:T(8,128)(2,1)S(1)}, u32[]{:S(2)}, u32[]{:S(2)}) collective-permute-start(bf16[688,1024]{1,0:T(8,128)(2,1)S(1)} %bitcast.75), channel_id=1, source_target_pairs={{1,2},{2,1},{5,6},{6,5},{9,10},{10,9},{13,14},{14,13},{17,18},{18,... | collective-permute-start | bytes 4227080 | tf_op jit(solution)/shard_map/ppermute | solution.py:1067
  84.3 17.8 %collective-permute-start.13 = (bf16[1024,256]{1,0:T(8,128)(2,1)S(1)}, bf16[1024,256]{1,0:T(8,128)(2,1)}, u32[]{:S(2)}, u32[]{:S(2)}) collective-permute-start(bf16[1024,256]{1,0:T(8,128)(2,1)S(1)} %collective-permute-done.12.refs_7_), channel_id=1, source_target_pairs={{0,4},{4,0},{1,5},{5,1},{2,6},{6,2},{3,7},{7,3},{8,12},{12,8},{9,1... | collective-permute-start | bytes 1572872 | tf_op jit(solution)/shard_map/ppermute | solution.py:1071
  85.5 20.4 %collective-permute-start.14 = (bf16[256,1024]{1,0:T(8,128)(2,1)S(1)}, bf16[256,1024]{1,0:T(8,128)(2,1)}, u32[]{:S(2)}, u32[]{:S(2)}) collective-permute-start(bf16[256,1024]{1,0:T(8,128)(2,1)S(1)} %copy-done.12), channel_id=1, source_target_pairs={{0,1},{1,0},{2,3},{3,2},{4,5},{5,4},{6,7},{7,6},{8,9},{9,8},{10,11... | collective-permute-start | bytes 1572872 | tf_op jit(solution)/shard_map/ppermute | solution.py:1071
  85.6 19.2 %collective-permute-start.18 = (bf16[128,1024]{1,0:T(8,128)(2,1)}, bf16[128,1024]{1,0:T(8,128)(2,1)}, u32[]{:S(2)}, u32[]{:S(2)}) collective-permute-start(bf16[128,1024]{1,0:T(8,128)(2,1)} %collective-permute-done.17), channel_id=1, source_target_pairs={{0,4},{4,0},{1,5},{5,1},{2,6},{6,2},{3,7},{7,3},{8,12},{12,8},{9,1... | collective-permute-start | bytes 786440 | tf_op jit(solution)/shard_map/ppermute | solution.py:1071
  103.8 44.8 %collective-permute-start.21 = (bf16[4,1024,256]{2,1,0:T(8,128)(2,1)S(1)}, bf16[4,1024,256]{2,1,0:T(8,128)(2,1)}, u32[]{:S(2)}, u32[]{:S(2)}) collective-permute-start(bf16[4,1024,256]{2,1,0:T(8,128)(2,1)S(1)} %pad_maximum_fusion), channel_id=1, source_target_pairs={{0,2},{2,0},{1,3},{3,1},{4,6},{6,4},{5,7},{7,5},{8,10},{10,8},{9,1... | collective-permute-start | bytes 6291464 | tf_op jit(solution)/shard_map/ppermute | solution.py:1071
  105.9 14.5 %collective-permute-start.22 = (bf16[256,1024]{1,0:T(8,128)(2,1)}, bf16[256,1024]{1,0:T(8,128)(2,1)}, u32[]{:S(2)}, u32[]{:S(2)}) collective-permute-start(bf16[256,1024]{1,0:T(8,128)(2,1)} %collective-permute-done.14.refs_10_), channel_id=1, source_target_pairs={{0,4},{4,0},{1,5},{5,1},{2,6},{6,2},{3,7},{7,3},{8,12},{12,8},{9,1... | collective-permute-start | bytes 1572872 | tf_op jit(solution)/shard_map/ppermute | solution.py:1071
  107.1 15.0 %collective-permute-start.23 = (bf16[256,1024]{1,0:T(8,128)(2,1)}, bf16[256,1024]{1,0:T(8,128)(2,1)}, u32[]{:S(2)}, u32[]{:S(2)}) collective-permute-start(bf16[256,1024]{1,0:T(8,128)(2,1)} %collective-permute-done.14.refs_10_), channel_id=1, source_target_pairs={{0,8},{8,0},{1,9},{9,1},{2,10},{10,2},{3,11},{11,3},{4,12},{12,4},... | collective-permute-start | bytes 1572872 | tf_op jit(solution)/shard_map/ppermute | solution.py:1071
  107.3 14.3 %collective-permute-start.20 = (bf16[16,4096]{1,0:T(8,128)(2,1)S(1)}, bf16[16,4096]{1,0:T(8,128)(2,1)S(1)}, u32[]{:S(2)}, u32[]{:S(2)}) collective-permute-start(bf16[16,4096]{1,0:T(8,128)(2,1)S(1)} %copy-done.19), channel_id=1, source_target_pairs={{0,1},{1,0},{2,3},{3,2},{4,5},{5,4},{6,7},{7,6},{8,9},{9,8},{10,11... | collective-permute-start | bytes 393224 | tf_op jit(solution)/shard_map/ppermute | solution.py:1071
  119.4 28.1 %collective-permute-start.25 = (bf16[256,1024]{1,0:T(8,128)(2,1)}, bf16[256,1024]{1,0:T(8,128)(2,1)S(1)}, u32[]{:S(2)}, u32[]{:S(2)}) collective-permute-start(bf16[256,1024]{1,0:T(8,128)(2,1)} %collective-permute-done.14.refs_10_), channel_id=1, source_target_pairs={{0,2},{2,0},{1,3},{3,1},{4,6},{6,4},{5,7},{7,5},{8,10},{10,8},{9,1... | collective-permute-start | bytes 1572872 | tf_op jit(solution)/shard_map/ppermute | solution.py:1071
  120.4 26.0 %collective-permute-start.24 = (bf16[256,1024]{1,0:T(8,128)(2,1)}, bf16[256,1024]{1,0:T(8,128)(2,1)S(1)}, u32[]{:S(2)}, u32[]{:S(2)}) collective-permute-start(bf16[256,1024]{1,0:T(8,128)(2,1)} %collective-permute-done.22.refs_11_), channel_id=1, source_target_pairs={{0,8},{8,0},{1,9},{9,1},{2,10},{10,2},{3,11},{11,3},{4,12},{12,4},... | collective-permute-start | bytes 1572872 | tf_op jit(solution)/shard_map/ppermute | solution.py:1071
  121.6 26.0 %collective-permute-start.26 = (bf16[256,1024]{1,0:T(8,128)(2,1)}, bf16[256,1024]{1,0:T(8,128)(2,1)}, u32[]{:S(2)}, u32[]{:S(2)}) collective-permute-start(bf16[256,1024]{1,0:T(8,128)(2,1)} %collective-permute-done.22.refs_11_), channel_id=1, source_target_pairs={{0,2},{2,0},{1,3},{3,1},{4,6},{6,4},{5,7},{7,5},{8,10},{10,8},{9,1... | collective-permute-start | bytes 1572872 | tf_op jit(solution)/shard_map/ppermute | solution.py:1071
  122.0 25.5 %collective-permute-start.27 = (bf16[256,1024]{1,0:T(8,128)(2,1)}, bf16[256,1024]{1,0:T(8,128)(2,1)}, u32[]{:S(2)}, u32[]{:S(2)}) collective-permute-start(bf16[256,1024]{1,0:T(8,128)(2,1)} %collective-permute-done.23.refs_12_), channel_id=1, source_target_pairs={{0,2},{2,0},{1,3},{3,1},{4,6},{6,4},{5,7},{7,5},{8,10},{10,8},{9,1... | collective-permute-start | bytes 1572872 | tf_op jit(solution)/shard_map/ppermute | solution.py:1071
  187.8 18.2 %collective-permute-start.32 = (bf16[16,3968]{1,0:T(8,128)(2,1)S(1)}, bf16[16,3968]{1,0:T(8,128)(2,1)S(1)}, u32[]{:S(2)}, u32[]{:S(2)}) collective-permute-start(bf16[16,3968]{1,0:T(8,128)(2,1)S(1)} %maximum_maximum_fusion), channel_id=1, source_target_pairs={{0,1},{1,0},{2,3},{3,2},{4,5},{5,4},{6,7},{7,6},{8,9},{9,8},{10,11... | collective-permute-start | bytes 380936 | tf_op jit(solution)/shard_map/ppermute | solution.py:1071
  203.0 37.7 %collective-permute-start.31 = (bf16[688,1024]{1,0:T(8,128)(2,1)S(1)}, bf16[688,1024]{1,0:T(8,128)(2,1)S(1)}, u32[]{:S(2)}, u32[]{:S(2)}) collective-permute-start(bf16[688,1024]{1,0:T(8,128)(2,1)S(1)} %copy-done.4), channel_id=1, source_target_pairs={{1,2},{2,1},{5,6},{6,5},{9,10},{10,9},{13,14},{14,13},{17,18},{18,... | collective-permute-start | bytes 4227080 | tf_op jit(solution)/shard_map/ppermute | solution.py:1067
  206.0 16.7 %collective-permute-start.34 = (bf16[2,16,3968]{2,1,0:T(8,128)(2,1)S(1)}, bf16[2,16,3968]{2,1,0:T(8,128)(2,1)S(1)}, u32[]{:S(2)}, u32[]{:S(2)}) collective-permute-start(bf16[2,16,3968]{2,1,0:T(8,128)(2,1)S(1)} %maximum_select_fusion.3), channel_id=1, source_target_pairs={{0,16},{16,0},{1,17},{17,1},{2,18},{18,2},{3,19},{19,3},{4,20},{20... | collective-permute-start | bytes 761864 | tf_op jit(solution)/shard_map/ppermute | solution.py:1071
  222.8 15.0 %collective-permute-start.36 = (bf16[4,16,3968]{2,1,0:T(8,128)(2,1)S(1)}, bf16[4,16,3968]{2,1,0:T(8,128)(2,1)}, u32[]{:S(2)}, u32[]{:S(2)}) collective-permute-start(bf16[4,16,3968]{2,1,0:T(8,128)(2,1)S(1)} %maximum_select_fusion.1), channel_id=1, source_target_pairs={{0,8},{8,0},{1,9},{9,1},{2,10},{10,2},{3,11},{11,3},{4,12},{12,4},... | collective-permute-start | bytes 1523720 | tf_op jit(solution)/shard_map/ppermute | solution.py:1071
  223.2 32.1 %collective-permute-start.33 = (bf16[2,688,256]{2,1,0:T(8,128)(2,1)}, bf16[2,688,256]{2,1,0:T(8,128)(2,1)S(1)}, u32[]{:S(2)}, u32[]{:S(2)}) collective-permute-start(bf16[2,688,256]{2,1,0:T(8,128)(2,1)} %get-tuple-element.199), channel_id=1, source_target_pairs={{0,2},{2,0},{1,3},{3,1},{4,6},{6,4},{5,7},{7,5},{8,10},{10,8},{9,1... | collective-permute-start | bytes 2113544 | tf_op jit(solution)/shard_map/ppermute | solution.py:1071
  223.2 32.1 %collective-permute-start.35 = (bf16[2,688,256]{2,1,0:T(8,128)(2,1)}, bf16[2,688,256]{2,1,0:T(8,128)(2,1)S(1)}, u32[]{:S(2)}, u32[]{:S(2)}) collective-permute-start(bf16[2,688,256]{2,1,0:T(8,128)(2,1)} %get-tuple-element.202), channel_id=1, source_target_pairs={{0,2},{2,0},{1,3},{3,1},{4,6},{6,4},{5,7},{7,5},{8,10},{10,8},{9,1... | collective-permute-start | bytes 2113544 | tf_op jit(solution)/shard_map/ppermute | solution.py:1071
  239.2 25.1 %collective-permute-start.39 = (bf16[8,16,3968]{2,1,0:T(8,128)(2,1)S(1)}, bf16[8,16,3968]{2,1,0:T(8,128)(2,1)}, u32[]{:S(2)}, u32[]{:S(2)}) collective-permute-start(bf16[8,16,3968]{2,1,0:T(8,128)(2,1)S(1)} %maximum_select_fusion.refs_0_), channel_id=1, source_target_pairs={{0,4},{4,0},{1,5},{5,1},{2,6},{6,2},{3,7},{7,3},{8,12},{12,8},{9,1... | collective-permute-start | bytes 3047432 | tf_op jit(solution)/shard_map/ppermute | solution.py:1071
  240.4 14.9 %collective-permute-start.37 = (bf16[2,688,256]{2,1,0:T(8,128)(2,1)}, bf16[2,688,256]{2,1,0:T(8,128)(2,1)S(1)}, u32[]{:S(2)}, u32[]{:S(2)}) collective-permute-start(bf16[2,688,256]{2,1,0:T(8,128)(2,1)} %get-tuple-element.213), channel_id=1, source_target_pairs={{0,2},{2,0},{1,3},{3,1},{4,6},{6,4},{5,7},{7,5},{8,10},{10,8},{9,1... | collective-permute-start | bytes 2113544 | tf_op jit(solution)/shard_map/ppermute | solution.py:1071
  271.7 22.3 %collective-permute-start.47 = (bf16[8,16,3840]{2,1,0:T(8,128)(2,1)}, bf16[8,16,3840]{2,1,0:T(8,128)(2,1)S(1)}, u32[]{:S(2)}, u32[]{:S(2)}) collective-permute-start(bf16[8,16,3840]{2,1,0:T(8,128)(2,1)} %get-tuple-element.222.own), channel_id=1, source_target_pairs={{0,2},{2,0},{1,3},{3,1},{4,6},{6,4},{5,7},{7,5},{8,10},{10,8},{9,1... | collective-permute-start | bytes 2949128 | tf_op jit(solution)/shard_map/ppermute | solution.py:1071
  284.8 20.3 %collective-permute-start.43 = (bf16[688,1024]{1,0:T(8,128)(2,1)}, bf16[688,1024]{1,0:T(8,128)(2,1)}, u32[]{:S(2)}, u32[]{:S(2)}) collective-permute-start(bf16[688,1024]{1,0:T(8,128)(2,1)} %qkv_rows.1), channel_id=1, source_target_pairs={{1,2},{2,1},{5,6},{6,5},{9,10},{10,9},{13,14},{14,13},{17,18},{18,... | collective-permute-start | bytes 4227080 | tf_op jit(solution)/shard_map/ppermute | solution.py:1067
  (53 other events, 413.0 us)
